TPU v7x, 32 devices: a whole 2x2x4 slice. The times are simulated.
32 devices in a mesh: dp: 16 (over z, x, core), mp: 2 (over y).
Axes of the slice: x: 2, y: 2, z: 4, core: 2. Of those that a mesh axis runs over, the one named last changes fastest.
Arguments:
- enc_in: bfloat16 [32, 128, 768], P('dp'), may hold values from -6 to 6
- dec_in: bfloat16 [32, 64, 768], P('dp'), may hold values from -6 to 6
- cotangent: bfloat16 [32, 64, 768], P('dp'), may hold values from -6 to 6
- patch_counts: int32 [32], P('dp'), may hold values from 32 to 128, as said below
- table_lengths: int32 [32], P('dp'), may hold values from 40 to 64, as said below
- enc_qkv: bfloat16 [3, 768, 768], P(None, None, 'mp'), may hold values from -0.21875 to 0.21875
- enc_attn_out: bfloat16 [768, 768], P('mp'), may hold values from -1.25 to 1.25
- enc_mlp_in: bfloat16 [2, 768, 2048], P(None, None, 'mp'), may hold values from -0.21875 to 0.21875
- enc_mlp_out: bfloat16 [2048, 768], P('mp'), may hold values from -0.125 to 0.125
- enc_gains: float32 [3, 768], replicated, may hold values from 0.5 to 1.5
- dec_self_qkv: bfloat16 [3, 768, 768], P(None, None, 'mp'), may hold values from -0.21875 to 0.21875
- dec_self_out: bfloat16 [768, 768], P('mp'), may hold values from -1.25 to 1.25
- dec_cross_qkv: bfloat16 [3, 768, 768], P(None, None, 'mp'), may hold values from -0.21875 to 0.21875
- dec_cross_out: bfloat16 [768, 768], P('mp'), may hold values from -1.25 to 1.25
- dec_mlp_in: bfloat16 [2, 768, 2048], P(None, None, 'mp'), may hold values from -0.21875 to 0.21875
- dec_mlp_out: bfloat16 [2048, 768], P('mp'), may hold values from -0.125 to 0.125
- dec_gains: float32 [3, 768], replicated, may hold values from 0.5 to 1.5
Outputs:
- dec_out: bfloat16 [32, 64, 768], P('dp')
- enc_in_grad: bfloat16 [32, 128, 768], P('dp')
- dec_in_grad: bfloat16 [32, 64, 768], P('dp')
- enc_qkv_grad: float32 [3, 768, 768], P(None, 'dp', 'mp')
- enc_attn_out_grad: float32 [768, 768], P('mp', 'dp')
- enc_mlp_in_grad: float32 [2, 768, 2048], P(None, 'dp', 'mp')
- enc_mlp_out_grad: float32 [2048, 768], P('mp', 'dp')
- enc_gains_grad: float32 [3, 768], P(None, 'dp')
- dec_self_qkv_grad: float32 [3, 768, 768], P(None, 'dp', 'mp')
- dec_self_out_grad: float32 [768, 768], P('mp', 'dp')
- dec_cross_qkv_grad: float32 [3, 768, 768], P(None, 'dp', 'mp')
- dec_cross_out_grad: float32 [768, 768], P('mp', 'dp')
- dec_mlp_in_grad: float32 [2, 768, 2048], P(None, 'dp', 'mp')
- dec_mlp_out_grad: float32 [2048, 768], P('mp', 'dp')
- dec_gains_grad: float32 [3, 768], P(None, 'dp')
Inputs may be any that keep to these rules, and one draw needn't show every extreme that they name: `patch_counts`: rows at or past a plot's count are padding that no query reads as a key; some plot has exactly 128 and another exactly 32. `table_lengths`: rows at or past a plot's length are padding that no query reads as a key; some plot has exactly 64 and another exactly 40.
All inputs are finite; a program needn't handle non-finite values.
Results may differ from a plain program's by a relative error of at most 0.02.
Values sent between devices are 32-bit elements; how exact they have to be, the bound alone decides.
No kernel may reach another device: no remote copies, remote signals or barrier semaphores. Data moves between devices by JAX's collectives and lax.ppermute only.
A program may use at most 192 MiB of HBM per device.

v0:
```python
import jax
import jax.numpy as jnp
from jax import lax
from jax.sharding import PartitionSpec as P

HEAD_DIM = 64


EPSILON = 1e-06
NEG_LARGE = -1e30


def project(left, right):
    return jnp.dot(left, right, preferred_element_type=jnp.float32)


def project_back(left, right):
    return jnp.einsum("sd,ed->se", left, right, preferred_element_type=jnp.float32)


def outer_sum(left, right):
    return jnp.einsum("sd,se->de", left, right, preferred_element_type=jnp.float32)


def norm_rows(hidden, gain):
    scaling = lax.rsqrt(jnp.mean(hidden * hidden, -1, keepdims=True) + EPSILON)
    return (hidden * scaling * gain, scaling)


def norm_back(grad, hidden, scaling, gain):
    normed = hidden * scaling
    grad_hat = grad * gain
    grad_in = scaling * (grad_hat - normed * jnp.mean(grad_hat * normed, -1, keepdims=True))
    return (grad_in, jnp.sum(grad * normed, 0))


def heads_of(tensor):
    return tensor.reshape(tensor.shape[0], -1, HEAD_DIM)


def scores_of(query, keys, allowed):
    raw_scores = jnp.einsum(
        "qhd,khd->hqk", heads_of(query), heads_of(keys), preferred_element_type=jnp.float32
    ) * HEAD_DIM ** (-0.5)
    return jnp.where(allowed[None], raw_scores, NEG_LARGE)


def attend_fwd(query, keys, values, allowed):
    scores = scores_of(query, keys, allowed)
    row_max = jnp.max(scores, -1, keepdims=True)
    expon = jnp.exp(scores - row_max)
    row_sum = jnp.sum(expon, -1, keepdims=True)
    soft_low = (expon / row_sum).astype(jnp.bfloat16)
    mixed_heads = jnp.einsum(
        "hqk,khd->qhd", soft_low, heads_of(values), preferred_element_type=jnp.float32
    )
    return (mixed_heads.reshape(query.shape[0], -1), row_max + jnp.log(row_sum))


def attend_back(query, keys, values, allowed, log_sum, grad_out):
    scores = scores_of(query, keys, allowed)
    soft = jnp.exp(scores - log_sum)
    grad_heads = heads_of(grad_out)
    grad_values = jnp.einsum(
        "hqk,qhd->khd", soft.astype(jnp.bfloat16), grad_heads, preferred_element_type=jnp.float32
    )
    grad_soft = jnp.einsum(
        "qhd,khd->hqk", grad_heads, heads_of(values), preferred_element_type=jnp.float32
    )
    grad_scores = (soft * (grad_soft - jnp.sum(soft * grad_soft, -1, keepdims=True))).astype(
        jnp.bfloat16
    )
    factor = HEAD_DIM ** (-0.5)
    grad_query = (
        jnp.einsum("hqk,khd->qhd", grad_scores, heads_of(keys), preferred_element_type=jnp.float32)
        * factor
    )
    grad_keys = (
        jnp.einsum("hqk,qhd->khd", grad_scores, heads_of(query), preferred_element_type=jnp.float32)
        * factor
    )
    grad_query = grad_query.reshape(query.shape[0], -1).astype(jnp.bfloat16)
    grad_keys = grad_keys.reshape(keys.shape[0], -1).astype(jnp.bfloat16)
    grad_values = grad_values.reshape(keys.shape[0], -1).astype(jnp.bfloat16)
    return (grad_query, grad_keys, grad_values)


def attention_fwd(normed_q, normed_kv, stacked, allowed):
    query = project(normed_q, stacked[0]).astype(jnp.bfloat16)
    keys = project(normed_kv, stacked[1]).astype(jnp.bfloat16)
    values = project(normed_kv, stacked[2]).astype(jnp.bfloat16)
    attended, log_sum = attend_fwd(query, keys, values, allowed)
    attended = attended.astype(jnp.bfloat16)
    return (attended, (query, keys, values, log_sum, attended))


def attention_back(grad, normed_q, normed_kv, stacked, out_weight, saved, allowed):
    query, keys, values, log_sum, attended = saved
    grad_low = grad.astype(jnp.bfloat16)
    grad_out_weight = outer_sum(attended, grad_low)
    grad_attended = project_back(grad_low, out_weight).astype(jnp.bfloat16)
    grad_query, grad_keys, grad_values = attend_back(
        query, keys, values, allowed, log_sum, grad_attended
    )
    grad_stack = jnp.stack(
        [
            outer_sum(normed_q, grad_query),
            outer_sum(normed_kv, grad_keys),
            outer_sum(normed_kv, grad_values),
        ]
    )
    from_query = project_back(grad_query, stacked[0])
    from_memory = project_back(grad_keys, stacked[1]) + project_back(grad_values, stacked[2])
    return (grad_stack, grad_out_weight, from_query, from_memory)


def gated(gate_pre, up_pre):
    return jax.nn.gelu(gate_pre, approximate=True) * up_pre


def mlp_fwd(normed, inner):
    gate_pre = project(normed, inner[0])
    up_pre = project(normed, inner[1])
    hidden_low = gated(gate_pre, up_pre).astype(jnp.bfloat16)
    return (hidden_low, (gate_pre, up_pre, hidden_low))


def mlp_back(grad, normed, inner, outer, saved):
    gate_pre, up_pre, hidden_low = saved
    grad_low = grad.astype(jnp.bfloat16)
    grad_outer = outer_sum(hidden_low, grad_low)
    grad_hidden = project_back(grad_low, outer)
    unused, pull = jax.vjp(gated, gate_pre, up_pre)
    grad_gate, grad_up = pull(grad_hidden)
    grad_gate = grad_gate.astype(jnp.bfloat16)
    grad_up = grad_up.astype(jnp.bfloat16)
    grad_inner = jnp.stack([outer_sum(normed, grad_gate), outer_sum(normed, grad_up)])
    grad_normed = project_back(grad_gate, inner[0]) + project_back(grad_up, inner[1])
    return (grad_inner, grad_outer, grad_normed)


def branch_sum(partial_sum):
    return lax.psum(partial_sum, "mp")


def input_sum(partial_sum):
    return lax.psum(partial_sum, "mp")


def body(
    enc_in,
    dec_in,
    cotangent,
    patch_counts,
    table_lengths,
    enc_qkv,
    enc_attn_out,
    enc_mlp_in,
    enc_mlp_out,
    enc_gains,
    dec_self_qkv,
    dec_self_out,
    dec_cross_qkv,
    dec_cross_out,
    dec_mlp_in,
    dec_mlp_out,
    dec_gains,
):
    micro = enc_in.shape[0]
    enc_len = enc_in.shape[1]
    dec_len = dec_in.shape[1]
    enc_pos = jnp.arange(enc_len)
    dec_pos = jnp.arange(dec_len)
    enc_params = (enc_qkv, enc_attn_out, enc_mlp_in, enc_mlp_out, enc_gains)
    dec_params = (
        dec_self_qkv,
        dec_self_out,
        dec_cross_qkv,
        dec_cross_out,
        dec_mlp_in,
        dec_mlp_out,
        dec_gains,
    )
    enc_accum = [jnp.zeros(weight.shape, jnp.float32) for weight in enc_params]
    dec_accum = [jnp.zeros(weight.shape, jnp.float32) for weight in dec_params]
    outputs = []
    enc_grads = []
    dec_grads = []
    for step in range(micro):
        patches = patch_counts[step]
        table = table_lengths[step]
        enc_allowed = jnp.broadcast_to(enc_pos[None, :] < patches, (enc_len, enc_len))
        self_allowed = (dec_pos[None, :] <= dec_pos[:, None]) & (dec_pos[None, :] < table)
        cross_allowed = jnp.broadcast_to(enc_pos[None, :] < patches, (dec_len, enc_len))
        state_zero = enc_in[step].astype(jnp.float32)
        normed, scale_zero = norm_rows(state_zero, enc_gains[0])
        enc_norm_zero = normed.astype(jnp.bfloat16)
        attended, enc_attn_saved = attention_fwd(enc_norm_zero, enc_norm_zero, enc_qkv, enc_allowed)
        state_one = state_zero + branch_sum(project(attended, enc_attn_out))
        normed, scale_one = norm_rows(state_one, enc_gains[1])
        enc_norm_one = normed.astype(jnp.bfloat16)
        hidden_low, enc_mlp_saved = mlp_fwd(enc_norm_one, enc_mlp_in)
        state_two = state_one + branch_sum(project(hidden_low, enc_mlp_out))
        normed, scale_two = norm_rows(state_two, enc_gains[2])
        memory = normed.astype(jnp.bfloat16)
        stream_zero = dec_in[step].astype(jnp.float32)
        normed, dscale_zero = norm_rows(stream_zero, dec_gains[0])
        dec_norm_zero = normed.astype(jnp.bfloat16)
        attended, self_saved = attention_fwd(
            dec_norm_zero, dec_norm_zero, dec_self_qkv, self_allowed
        )
        stream_one = stream_zero + branch_sum(project(attended, dec_self_out))
        normed, dscale_one = norm_rows(stream_one, dec_gains[1])
        dec_norm_one = normed.astype(jnp.bfloat16)
        attended, cross_saved = attention_fwd(dec_norm_one, memory, dec_cross_qkv, cross_allowed)
        stream_two = stream_one + branch_sum(project(attended, dec_cross_out))
        normed, dscale_two = norm_rows(stream_two, dec_gains[2])
        dec_norm_two = normed.astype(jnp.bfloat16)
        hidden_low, dec_mlp_saved = mlp_fwd(dec_norm_two, dec_mlp_in)
        stream_three = stream_two + branch_sum(project(hidden_low, dec_mlp_out))
        outputs.append(stream_three.astype(jnp.bfloat16))
        grad = cotangent[step].astype(jnp.float32)
        grad_inner, grad_outer, partial_grad = mlp_back(
            grad, dec_norm_two, dec_mlp_in, dec_mlp_out, dec_mlp_saved
        )
        grad_in, gain_two = norm_back(input_sum(partial_grad), stream_two, dscale_two, dec_gains[2])
        grad = grad + grad_in
        dec_accum[4] = dec_accum[4] + grad_inner
        dec_accum[5] = dec_accum[5] + grad_outer
        grad_stack, grad_out_weight, from_query, from_memory = attention_back(
            grad, dec_norm_one, memory, dec_cross_qkv, dec_cross_out, cross_saved, cross_allowed
        )
        full_query, full_memory = lax.psum((from_query, from_memory), "mp")
        grad_in, gain_one = norm_back(full_query, stream_one, dscale_one, dec_gains[1])
        grad = grad + grad_in
        dec_accum[2] = dec_accum[2] + grad_stack
        dec_accum[3] = dec_accum[3] + grad_out_weight
        grad_stack, grad_out_weight, from_query, from_memory = attention_back(
            grad, dec_norm_zero, dec_norm_zero, dec_self_qkv, dec_self_out, self_saved, self_allowed
        )
        grad_in, gain_zero = norm_back(
            input_sum(from_query + from_memory), stream_zero, dscale_zero, dec_gains[0]
        )
        grad = grad + grad_in
        dec_accum[0] = dec_accum[0] + grad_stack
        dec_accum[1] = dec_accum[1] + grad_out_weight
        dec_accum[6] = dec_accum[6] + jnp.stack([gain_zero, gain_one, gain_two])
        dec_grads.append(grad.astype(jnp.bfloat16))
        back_state, egain_two = norm_back(full_memory, state_two, scale_two, enc_gains[2])
        grad_inner, grad_outer, partial_grad = mlp_back(
            back_state, enc_norm_one, enc_mlp_in, enc_mlp_out, enc_mlp_saved
        )
        grad_in, egain_one = norm_back(input_sum(partial_grad), state_one, scale_one, enc_gains[1])
        back_state = back_state + grad_in
        enc_accum[2] = enc_accum[2] + grad_inner
        enc_accum[3] = enc_accum[3] + grad_outer
        grad_stack, grad_out_weight, from_query, from_memory = attention_back(
            back_state,
            enc_norm_zero,
            enc_norm_zero,
            enc_qkv,
            enc_attn_out,
            enc_attn_saved,
            enc_allowed,
        )
        grad_in, egain_zero = norm_back(
            input_sum(from_query + from_memory), state_zero, scale_zero, enc_gains[0]
        )
        back_state = back_state + grad_in
        enc_accum[0] = enc_accum[0] + grad_stack
        enc_accum[1] = enc_accum[1] + grad_out_weight
        enc_accum[4] = enc_accum[4] + jnp.stack([egain_zero, egain_one, egain_two])
        enc_grads.append(back_state.astype(jnp.bfloat16))
    reduced = tuple(
        lax.psum_scatter(tuple(enc_accum + dec_accum), "dp", scatter_dimension=1, tiled=True)
    )
    return (jnp.stack(outputs), jnp.stack(enc_grads), jnp.stack(dec_grads)) + reduced


def solution(mesh):
    placed = (
        P("dp", None, None),
        P("dp", None, None),
        P("dp", None, None),
        P("dp"),
        P("dp"),
        P(None, None, "mp"),
        P("mp", None),
        P(None, None, "mp"),
        P("mp", None),
        P(),
        P(None, None, "mp"),
        P("mp", None),
        P(None, None, "mp"),
        P("mp", None),
        P(None, None, "mp"),
        P("mp", None),
        P(),
    )
    return jax.shard_map(
        body,
        mesh=mesh,
        in_specs=placed,
        out_specs=(
            P("dp", None, None),
            P("dp", None, None),
            P("dp", None, None),
            P(None, "dp", "mp"),
            P("mp", "dp"),
            P(None, "dp", "mp"),
            P("mp", "dp"),
            P(None, "dp"),
            P(None, "dp", "mp"),
            P("mp", "dp"),
            P(None, "dp", "mp"),
            P("mp", "dp"),
            P(None, "dp", "mp"),
            P("mp", "dp"),
            P(None, "dp"),
        ),
        check_vma=False,
    )
```

profile of v0, /device:TPU:0, one launch (start us, length us, event | category | flops | bytes accessed | tf_op | source)
XLA Modules:
  0.0 1253.8 jit_solution(1905144356962491317)
XLA Ops:
  33.0 26.2 %all-reduce.27.cloned.1.call-done = (f32[128,768]{1,0:T(8,128)}, f32[128,768]{1,0:T(8,128)}) async-done(((f32[128,768]{1,0:T(8,128)}, f32[128,768]{1,0:T(8,128)}), (f32[128,768]{1,0:T(8,128)}, f32[128,768]{1,0:T(8,128)})) %all-reduce.27.cloned.1.call-update) | async-done | bytes 786448 | tf_op jit(solution)/shard_map/psum | solution.py:143
  67.5 2.2 fusion.287
  69.7 41.0 %all-reduce.25.cloned.1.call-done = (f32[64,768]{1,0:T(8,128)}, f32[128,768]{1,0:T(8,128)}, f32[64,768]{1,0:T(8,128)}, f32[128,768]{1,0:T(8,128)}) async-done(((f32[64,768]{1,0:T(8,128)}, f32[128,768]{1,0:T(8,128)}, f32[64,768]{1,0:T(8,128)}, f32[128,768]{1,0:T(8,128)}), (f32[64,768]{1,0:T(8,128)}, f32[128,768]{1,0:T(8,128)}, f32[64,768]{1,0:T(8,128)}, f32[128,768]{1,0:T(8,128)})) %all-reduce.25.cloned.1.call-update) | async-done | bytes 1179664 | tf_op jit(solution)/shard_map/psum | solution.py:143
  142.0 2.2 fusion.291
  144.2 22.3 %all-reduce.23.cloned.1.call-done = (f32[64,768]{1,0:T(8,128)}, f32[64,768]{1,0:T(8,128)}) async-done(((f32[64,768]{1,0:T(8,128)}, f32[64,768]{1,0:T(8,128)}), (f32[64,768]{1,0:T(8,128)}, f32[64,768]{1,0:T(8,128)})) %all-reduce.23.cloned.1.call-update) | async-done | bytes 393232 | tf_op jit(solution)/shard_map/psum | solution.py:143
  181.1 23.4 %all-reduce.21.cloned.1.call-done = (f32[64,768]{1,0:T(8,128)}, f32[64,768]{1,0:T(8,128)}) async-done(((f32[64,768]{1,0:T(8,128)}, f32[64,768]{1,0:T(8,128)}), (f32[64,768]{1,0:T(8,128)}, f32[64,768]{1,0:T(8,128)})) %all-reduce.21.cloned.1.call-update) | async-done | bytes 393232 | tf_op jit(solution)/shard_map/psum | solution.py:147
  206.6 2.1 multiply_add_fusion.5
  213.8 2.5 multiply_reduce_fusion.22
  240.8 23.4 %all-reduce.19.cloned.1.call-done = (f32[128,768]{1,0:T(8,128)}, f32[128,768]{1,0:T(8,128)}) async-done(((f32[128,768]{1,0:T(8,128)}, f32[128,768]{1,0:T(8,128)}), (f32[128,768]{1,0:T(8,128)}, f32[128,768]{1,0:T(8,128)})) %all-reduce.19.cloned.1.call-update) | async-done | bytes 786448 | tf_op jit(solution)/shard_map/psum | solution.py:233
  266.2 2.3 multiply_reduce_fusion
  280.0 39.7 %all-reduce.17.cloned.1.call-done = (f32[128,768]{1,0:T(8,128)}, f32[128,768]{1,0:T(8,128)}, f32[64,768]{1,0:T(8,128)}, f32[64,768]{1,0:T(8,128)}) async-done(((f32[128,768]{1,0:T(8,128)}, f32[128,768]{1,0:T(8,128)}, f32[64,768]{1,0:T(8,128)}, f32[64,768]{1,0:T(8,128)}), (f32[128,768]{1,0:T(8,128)}, f32[128,768]{1,0:T(8,128)}, f32[64,768]{1,0:T(8,128)}, f32[64,768]{1,0:T(8,128)})) %all-reduce.17.cloned.1.call-update) | async-done | bytes 1179664 | tf_op jit(solution)/shard_map/psum | solution.py:147
  358.4 51.8 %all-reduce.15.cloned.1.call-done = (f32[64,768]{1,0:T(8,128)}, f32[64,768]{1,0:T(8,128)}, f32[128,768]{1,0:T(8,128)}, f32[128,768]{1,0:T(8,128)}, f32[64,768]{1,0:T(8,128)}, /*index=5*/f32[64,768]{1,0:T(8,128)}) async-done(((f32[64,768]{1,0:T(8,128)}, f32[64,768]{1,0:T(8,128)}, f32[128,768]{1,0:T(8,128)}, f32[128,768]{1,0:T(8,128)}, f32[64,768]{1,0:T(8,128)}, /*index=5*/f32[64,768]{1,0:T(8,128)}), ...) | async-done | bytes 1572880 | tf_op jit(solution)/shard_map/psum | solution.py:143
  420.9 2.3 convolution_add_fusion.3
  424.2 2.3 convolution_add_fusion
  430.7 2.2 maximum_add_fusion.4
  434.7 2.4 convolution_add_fusion.1
  440.6 2.3 maximum_add_fusion.2
  446.4 2.3 maximum_add_fusion.3
  452.7 3.6 maximum_add_fusion.1
  460.6 3.7 maximum_add_fusion
  468.3 2.6 reduce-scatter.39.cloned.1.call-done
  472.3 56.8 %reduce-scatter.37.cloned.1.call-done = f32[48,3]{1,0:T(8,128)} async-done(((f32[768,3]{1,0:T(8,128)}), f32[48,3]{1,0:T(8,128)}) %reduce-scatter.37.cloned.1.call-update) | async-done | bytes 592
  530.5 60.1 %reduce-scatter.31.cloned.1.call-done = f32[384,48]{0,1:T(8,128)} async-done(((f32[384,768]{0,1:T(8,128)}), f32[384,48]{0,1:T(8,128)}) %reduce-scatter.31.cloned.1.call-update) | async-done | bytes 73744 | tf_op jit(solution)/shard_map/reduce_scatter | solution.py:275
  590.6 61.6 %reduce-scatter.19.cloned.1.call-done = f32[384,48]{0,1:T(8,128)} async-done(((f32[384,768]{0,1:T(8,128)}), f32[384,48]{0,1:T(8,128)}) %reduce-scatter.19.cloned.1.call-update) | async-done | bytes 73744 | tf_op jit(solution)/shard_map/reduce_scatter | solution.py:275
  652.2 61.4 %reduce-scatter.27.cloned.1.call-done = f32[384,48]{0,1:T(8,128)} async-done(((f32[384,768]{0,1:T(8,128)}), f32[384,48]{0,1:T(8,128)}) %reduce-scatter.27.cloned.1.call-update) | async-done | bytes 73744 | tf_op jit(solution)/shard_map/reduce_scatter | solution.py:275
  713.7 70.2 %reduce-scatter.35.cloned.1.call-done = f32[1024,48]{0,1:T(8,128)} async-done(((f32[1024,768]{0,1:T(8,128)}), f32[1024,48]{0,1:T(8,128)}) %reduce-scatter.35.cloned.1.call-update) | async-done | bytes 196624 | tf_op jit(solution)/shard_map/reduce_scatter | solution.py:275
  783.9 71.9 %reduce-scatter.29.cloned.1.call-done = f32[3,48,384]{2,1,0:T(8,128)} async-done(((f32[3,768,384]{2,1,0:T(8,128)}), f32[3,48,384]{2,1,0:T(8,128)}) %reduce-scatter.29.cloned.1.call-update) | async-done | bytes 221200 | tf_op jit(solution)/shard_map/reduce_scatter | solution.py:275
  855.8 69.9 %reduce-scatter.23.cloned.1.call-done = f32[1024,48]{0,1:T(8,128)} async-done(((f32[1024,768]{0,1:T(8,128)}), f32[1024,48]{0,1:T(8,128)}) %reduce-scatter.23.cloned.1.call-update) | async-done | bytes 196624 | tf_op jit(solution)/shard_map/reduce_scatter | solution.py:275
  925.6 71.8 %reduce-scatter.17.cloned.1.call-done = f32[3,48,384]{2,1,0:T(8,128)} async-done(((f32[3,768,384]{2,1,0:T(8,128)}), f32[3,48,384]{2,1,0:T(8,128)}) %reduce-scatter.17.cloned.1.call-update) | async-done | bytes 221200 | tf_op jit(solution)/shard_map/reduce_scatter | solution.py:275
  997.4 71.6 %reduce-scatter.25.cloned.1.call-done = f32[3,48,384]{2,1,0:T(8,128)} async-done(((f32[3,768,384]{2,1,0:T(8,128)}), f32[3,48,384]{2,1,0:T(8,128)}) %reduce-scatter.25.cloned.1.call-update) | async-done | bytes 221200 | tf_op jit(solution)/shard_map/reduce_scatter | solution.py:275
  1069.0 89.1 %reduce-scatter.33.cloned.1.call-done = f32[2,48,1024]{2,1,0:T(8,128)} async-done(((f32[2,768,1024]{2,1,0:T(8,128)}), f32[2,48,1024]{2,1,0:T(8,128)}) %reduce-scatter.33.cloned.1.call-update) | async-done | bytes 393232 | tf_op jit(solution)/shard_map/reduce_scatter | solution.py:275
  1158.1 88.9 %reduce-scatter.21.cloned.1.call-done = f32[2,48,1024]{2,1,0:T(8,128)} async-done(((f32[2,768,1024]{2,1,0:T(8,128)}), f32[2,48,1024]{2,1,0:T(8,128)}) %reduce-scatter.21.cloned.1.call-update) | async-done | bytes 393232 | tf_op jit(solution)/shard_map/reduce_scatter | solution.py:275
  (835 shorter events, 199.7 us)
Async XLA Ops:
  7.2 57.6 %copy-start = (bf16[1024,768]{1,0:T(8,128)(2,1)S(1)}, bf16[1024,768]{1,0:T(8,128)(2,1)}, u32[]{:S(2)}) copy-start(bf16[1024,768]{1,0:T(8,128)(2,1)} %param.25) | copy-start | bytes 4718596
  7.2 52.0 %all-reduce.27.cloned.1.call-start = ((), (), s32[]{:S(2)}) async-start(), calls=%async_computation.30 | async-start | bytes 1572864 | tf_op jit(solution)/shard_map/psum | solution.py:143
  21.9 88.8 %all-reduce.25.cloned.1.call-start = ((), (), s32[]{:S(2)}) async-start(), calls=%async_computation.29 | async-start | bytes 2359296 | tf_op jit(solution)/shard_map/psum | solution.py:143
  67.1 99.4 %all-reduce.23.cloned.1.call-start = ((), (), s32[]{:S(2)}) async-start(), calls=%async_computation.28 | async-start | bytes 786432 | tf_op jit(solution)/shard_map/psum | solution.py:143
  140.4 64.1 %all-reduce.21.cloned.1.call-start = ((), (), s32[]{:S(2)}) async-start(), calls=%async_computation.27 | async-start | bytes 786432 | tf_op jit(solution)/shard_map/psum | solution.py:147
  178.5 85.7 %all-reduce.19.cloned.1.call-start = ((), (), s32[]{:S(2)}) async-start(), calls=%async_computation.26 | async-start | bytes 1572864 | tf_op jit(solution)/shard_map/psum | solution.py:233
  229.6 90.1 %all-reduce.17.cloned.1.call-start = ((), (), s32[]{:S(2)}) async-start(), calls=%async_computation.25 | async-start | bytes 2359296 | tf_op jit(solution)/shard_map/psum | solution.py:147
  276.1 134.1 %all-reduce.15.cloned.1.call-start = ((), (), s32[]{:S(2)}) async-start(), calls=%async_computation.24 | async-start | bytes 3145728 | tf_op jit(solution)/shard_map/psum | solution.py:143
  276.6 47.2 %copy-start.195 = (f32[6,64]{1,0:T(8,128)}, f32[6,64]{1,0:T(8,128)S(1)}, u32[]{:S(2)}) copy-start(f32[6,64]{1,0:T(8,128)S(1)} %log_add_fusion.1) | copy-start | bytes 4612
  278.9 44.2 %copy-start.23 = (bf16[384,768]{1,0:T(8,128)(2,1)S(1)}, bf16[384,768]{1,0:T(8,128)(2,1)}, u32[]{:S(2)}) copy-start(bf16[384,768]{1,0:T(8,128)(2,1)} %param.28) | copy-start | bytes 1769476
  278.9 44.7 %copy-start.40 = (f32[6,64,64]{1,2,0:T(8,128)S(1)}, f32[6,64,64]{1,2,0:T(8,128)}, u32[]{:S(2)}) copy-start(f32[6,64,64]{1,2,0:T(8,128)} %copy-done.39) | copy-start | bytes 294916
  280.0 43.6 %copy-start.156 = (bf16[64,6,64]{2,1,0:T(8,128)(2,1)S(1)}, bf16[64,6,64]{2,1,0:T(8,128)(2,1)}, u32[]{:S(2)}) copy-start(bf16[64,6,64]{2,1,0:T(8,128)(2,1)} %copy-done.155) | copy-start | bytes 147460
  357.6 52.6 %copy-start.211 = (f32[128]{0:T(128)S(1)}, f32[128]{0:T(128)}, u32[]{:S(2)}) copy-start(f32[128]{0:T(128)} %copy-done.210) | copy-start | bytes 1540
  357.6 52.6 %copy-start.215 = (f32[128]{0:T(128)S(1)}, f32[128]{0:T(128)}, u32[]{:S(2)}) copy-start(f32[128]{0:T(128)} %copy-done.214) | copy-start | bytes 1540
  357.7 54.5 %copy-start.19 = (bf16[2,64,768]{2,1,0:T(8,128)(2,1)S(1)}, bf16[2,64,768]{2,1,0:T(8,128)(2,1)}, u32[]{:S(2)}) copy-start(bf16[2,64,768]{2,1,0:T(8,128)(2,1)} %param.18) | copy-start | bytes 589828
  357.7 54.5 %copy-start.206 = (f32[64]{0:T(128)S(1)}, f32[64]{0:T(128)}, u32[]{:S(2)}) copy-start(f32[64]{0:T(128)} %copy-done.205) | copy-start | bytes 772
  357.7 54.5 %copy-start.208 = (f32[64]{0:T(128)S(1)}, f32[64]{0:T(128)}, u32[]{:S(2)}) copy-start(f32[64]{0:T(128)} %copy-done.207) | copy-start | bytes 772
  357.7 113.2 %reduce-scatter.39.cloned.1.call-start = ((), (), s32[]{:S(2)}) async-start(), calls=%async_computation.23 | async-start | bytes 417792
  358.3 57.9 %copy-start.63 = (f32[64,768]{1,0:T(8,128)S(1)}, f32[64,768]{1,0:T(8,128)}, u32[]{:S(2)}) copy-start(f32[64,768]{1,0:T(8,128)} %copy-done.61) | copy-start | bytes 589828
  358.3 57.9 %copy-start.172 = (bf16[6,64,64]{2,1,0:T(8,128)(2,1)S(1)}, bf16[6,64,64]{2,1,0:T(8,128)(2,1)}, u32[]{:S(2)}) copy-start(bf16[6,64,64]{2,1,0:T(8,128)(2,1)} %copy-done.171) | copy-start | bytes 147460
  415.1 113.9 %reduce-scatter.37.cloned.1.call-start = ((), (), s32[]{:S(2)}) async-start(), calls=%async_computation.22 | async-start | bytes 417792
  416.2 174.4 %reduce-scatter.31.cloned.1.call-start = ((), (), s32[]{:S(2)}) async-start(), calls=%async_computation.19 | async-start | bytes 1253376 | tf_op jit(solution)/shard_map/reduce_scatter | solution.py:275
  417.7 234.5 %reduce-scatter.19.cloned.1.call-start = ((), (), s32[]{:S(2)}) async-start(), calls=%async_computation.13 | async-start | bytes 1253376 | tf_op jit(solution)/shard_map/reduce_scatter | solution.py:275
  420.0 293.7 %reduce-scatter.27.cloned.1.call-start = ((), (), s32[]{:S(2)}) async-start(), calls=%async_computation.17 | async-start | bytes 1253376 | tf_op jit(solution)/shard_map/reduce_scatter | solution.py:275
  423.3 360.6 %reduce-scatter.35.cloned.1.call-start = ((), (), s32[]{:S(2)}) async-start(), calls=%async_computation.21 | async-start | bytes 3342336 | tf_op jit(solution)/shard_map/reduce_scatter | solution.py:275
  426.6 429.2 %reduce-scatter.29.cloned.1.call-start = ((), (), s32[]{:S(2)}) async-start(), calls=%async_computation.18 | async-start | bytes 3760128 | tf_op jit(solution)/shard_map/reduce_scatter | solution.py:275
  433.0 492.6 %reduce-scatter.23.cloned.1.call-start = ((), (), s32[]{:S(2)}) async-start(), calls=%async_computation.15 | async-start | bytes 3342336 | tf_op jit(solution)/shard_map/reduce_scatter | solution.py:275
  437.1 560.3 %reduce-scatter.17.cloned.1.call-start = ((), (), s32[]{:S(2)}) async-start(), calls=%async_computation.12 | async-start | bytes 3760128 | tf_op jit(solution)/shard_map/reduce_scatter | solution.py:275
  443.0 626.1 %reduce-scatter.25.cloned.1.call-start = ((), (), s32[]{:S(2)}) async-start(), calls=%async_computation.16 | async-start | bytes 3760128 | tf_op jit(solution)/shard_map/reduce_scatter | solution.py:275
  448.7 709.4 %reduce-scatter.33.cloned.1.call-start = ((), (), s32[]{:S(2)}) async-start(), calls=%async_computation.20 | async-start | bytes 6684672 | tf_op jit(solution)/shard_map/reduce_scatter | solution.py:275
  456.4 790.7 %reduce-scatter.21.cloned.1.call-start = ((), (), s32[]{:S(2)}) async-start(), calls=%async_computation.14 | async-start | bytes 6684672 | tf_op jit(solution)/shard_map/reduce_scatter | solution.py:275
  466.4 780.6 %copy-start.1 = (bf16[1024,768]{1,0:T(8,128)(2,1)S(1)}, bf16[1024,768]{1,0:T(8,128)(2,1)}, u32[]{:S(2)}) copy-start(bf16[1024,768]{1,0:T(8,128)(2,1)} %param.25) | copy-start | bytes 4718596
  (250 other events, 968.2 us)
Sparse Core Ops, SparseCore 0:
  22.0 37.2 all-reduce.26
  67.2 43.4 all-reduce.24
  140.6 25.8 all-reduce.22
  178.6 25.8 all-reduce.20
  229.7 34.4 all-reduce.18
  276.2 43.4 all-reduce.16
  357.8 52.3 all-reduce.14
  415.2 55.5 reduce-scatter.38
  474.4 54.6 reduce-scatter.36
  533.5 57.0 reduce-scatter.30
  595.2 56.9 reduce-scatter.18
  656.7 56.9 reduce-scatter.26
  718.5 65.2 reduce-scatter.34
  788.7 67.0 reduce-scatter.28
  860.5 65.1 reduce-scatter.22
  930.4 66.9 reduce-scatter.16
  1002.2 66.8 reduce-scatter.24
  1073.9 84.1 reduce-scatter.32
  1162.6 84.3 reduce-scatter.20
where the time goes:
time: 1260 us; the launch traced here: 1250 us
  waiting for transfers between devices  1000 us (79%)
  matrix products  125 us (10%)
  other arithmetic  59.7 us (5%)
  local copies, waits for them, and re-layouts  45.6 us (4%)
  between operations  17.8 us (1%)
    reduce_scatter x10, waiting for transfers between devices, body(): lax.psum_scatter(tuple(enc_accum + dec_accum), 'dp', scatter_dimension=1,...  717 us
    psum x4, waiting for transfers between devices, branch_sum(): return lax.psum(partial_sum, 'mp')  141 us
    psum x2, waiting for transfers between devices, input_sum(): return lax.psum(partial_sum, 'mp')  63.1 us
    unnamed x21, waiting for transfers between devices  59.7 us
    dot_general x36, matrix products, project_back(): jnp.einsum('sd,ed->se', left, right, preferred_element_type=jnp.float32)  36.4 us
    dot_general x36, matrix products, project(): return jnp.dot(left, right, preferred_element_type=jnp.float32)  33.6 us
  transfers between devices with their start and end apart: 19, of which 19 were waited for; matrix products, arithmetic and copies ran while one was open for 6% of the time, Pallas kernels for 0%

commit v1 on v0

--- a/solution.py
+++ b/solution.py
@@ -139,12 +139,43 @@
     return (grad_inner, grad_outer, grad_normed)
 
 
-def branch_sum(partial_sum):
+def pair_sum(partial_sum):
+    shards = lax.axis_size("mp")
+    if shards == 2:
+        return partial_sum + lax.ppermute(partial_sum, "mp", [(0, 1), (1, 0)])
     return lax.psum(partial_sum, "mp")
 
 
-def input_sum(partial_sum):
-    return lax.psum(partial_sum, "mp")
+branch_sum = pair_sum
+input_sum = pair_sum
+
+
+def scatter_sum(grads, cut_dims):
+    shards = lax.axis_size("dp")
+    me = lax.axis_index("dp")
+    bits = shards.bit_length() - 1
+    rows = []
+    for grad, cut in zip(grads, cut_dims):
+        moved = jnp.moveaxis(grad, cut, 0)
+        rows.append(moved.reshape(moved.shape[0], -1))
+    total = jnp.concatenate(rows, 1)
+    width = total.shape[1]
+    total = total.reshape((2,) * bits + (-1, width))
+    for bit in range(bits):
+        axis = bits - 1 - bit
+        mine = (me >> bit) & 1
+        sent = lax.dynamic_index_in_dim(total, 1 - mine, axis, keepdims=False)
+        kept = lax.dynamic_index_in_dim(total, mine, axis, keepdims=False)
+        total = kept + lax.ppermute(sent, "dp", [(i, i ^ (1 << bit)) for i in range(shards)])
+    outs = []
+    at = 0
+    for grad, cut in zip(grads, cut_dims):
+        moved = jnp.moveaxis(grad, cut, 0)
+        size = moved.size // moved.shape[0]
+        piece = lax.slice_in_dim(total, at, at + size, axis=1).reshape((total.shape[0],) + moved.shape[1:])
+        at += size
+        outs.append(jnp.moveaxis(piece, 0, cut))
+    return outs
 
 
 def body(
@@ -230,7 +261,7 @@
         grad_stack, grad_out_weight, from_query, from_memory = attention_back(
             grad, dec_norm_one, memory, dec_cross_qkv, dec_cross_out, cross_saved, cross_allowed
         )
-        full_query, full_memory = lax.psum((from_query, from_memory), "mp")
+        full_query, full_memory = pair_sum(from_query), pair_sum(from_memory)
         grad_in, gain_one = norm_back(full_query, stream_one, dscale_one, dec_gains[1])
         grad = grad + grad_in
         dec_accum[2] = dec_accum[2] + grad_stack
@@ -271,8 +302,14 @@
         enc_accum[1] = enc_accum[1] + grad_out_weight
         enc_accum[4] = enc_accum[4] + jnp.stack([egain_zero, egain_one, egain_two])
         enc_grads.append(back_state.astype(jnp.bfloat16))
+    dec_mlp = scatter_sum(dec_accum[4:6], (1, 1))
+    dec_cross = scatter_sum(dec_accum[2:4], (1, 1))
+    dec_self = scatter_sum(dec_accum[0:2], (1, 1))
+    enc_mlp = scatter_sum(enc_accum[2:4], (1, 1))
+    enc_attn = scatter_sum(enc_accum[0:2], (1, 1))
+    gains = scatter_sum([enc_accum[4], dec_accum[6]], (1, 1))
     reduced = tuple(
-        lax.psum_scatter(tuple(enc_accum + dec_accum), "dp", scatter_dimension=1, tiled=True)
+        enc_attn + enc_mlp + gains[:1] + dec_self + dec_cross + dec_mlp + gains[1:]
     )
     return (jnp.stack(outputs), jnp.stack(enc_grads), jnp.stack(dec_grads)) + reduced
 

time: 1260 us -> 686 us (0.54)
  waiting for transfers between devices: 1000 us -> 236 us
  local copies, waits for them, and re-layouts: 45.6 us -> 137 us
  starting transfers between devices: 1.79 us -> 49.9 us
  other arithmetic: 59.7 us -> 102 us
  matrix products: 125 us -> 144 us
  between operations: 17.8 us -> 4.8 us
    reduce_scatter x10 -> x0, waiting for transfers between devices: 717 us -> none  [body(): lax.psum_scatter(tuple(enc_accum + dec_accum), 'dp', scatter_dimension=1,...]
    ppermute x0 -> x46, waiting for transfers between devices: none -> 236 us  [the longest x24 214 us: scatter_sum(): lax.ppermute(sent, 'dp', [(i, i ^ 1 << bit) for i in range(shards)])]
    psum x7 -> x0, waiting for transfers between devices: 228 us -> none  [the longest x4 141 us: branch_sum(): return lax.psum(partial_sum, 'mp')]
    unnamed x21 -> x0, waiting for transfers between devices: 59.7 us -> none
    ppermute x0 -> x46, starting transfers between devices: none -> 49.9 us  [the longest x24 26 us: scatter_sum(): lax.ppermute(sent, 'dp', [(i, i ^ 1 << bit) for i in range(shards)])]
    concatenate x0 -> x5, local copies, waits for them, and re-layouts: none -> 39.2 us  [scatter_sum(): total = jnp.concatenate(rows, 1)]
    transpose x0 -> x11, local copies, waits for them, and re-layouts: none -> 38.3 us  [the longest x5 34.4 us: scatter_sum(): moved = jnp.moveaxis(grad, cut, 0)]
    squeeze x0 -> x5, other arithmetic: none -> 15.2 us  [scatter_sum(): sent = lax.dynamic_index_in_dim(total, 1 - mine, axis, keepdims=False)]
  transfers between devices with their start and end apart: 19 -> 46, of which waited for: 19 -> 17; matrix products, arithmetic and copies ran while one was open for 6% -> 50% of each run, Pallas kernels for 0% -> 0%
where the time goes in v1:
time: 686 us; the launch traced here: 674 us
  waiting for transfers between devices  236 us (34%)
  matrix products  144 us (21%)
  local copies, waits for them, and re-layouts  137 us (20%)
  other arithmetic  102 us (15%)
  starting transfers between devices  49.9 us (7%)
    ppermute x24, waiting for transfers between devices, scatter_sum(): lax.ppermute(sent, 'dp', [(i, i ^ 1 << bit) for i in range(shards)])  214 us
    concatenate x5, local copies, waits for them, and re-layouts, scatter_sum(): total = jnp.concatenate(rows, 1)  39.2 us
    dot_general x36, matrix products, outer_sum(): jnp.einsum('sd,se->de', left, right, preferred_element_type=jnp.float32)  38.6 us
    dot_general x36, matrix products, project_back(): jnp.einsum('sd,ed->se', left, right, preferred_element_type=jnp.float32)  37.2 us
    transpose x5, local copies, waits for them, and re-layouts, scatter_sum(): moved = jnp.moveaxis(grad, cut, 0)  34.4 us
    dot_general x36, matrix products, project(): return jnp.dot(left, right, preferred_element_type=jnp.float32)  30.7 us
    ppermute x24, starting transfers between devices, scatter_sum(): lax.ppermute(sent, 'dp', [(i, i ^ 1 << bit) for i in range(shards)])  26 us
    add x24, other arithmetic, scatter_sum(): kept + lax.ppermute(sent, 'dp', [(i, i ^ 1 << bit) for i in range(shards)])  25 us
  transfers between devices with their start and end apart: 46, of which 17 were waited for; matrix products, arithmetic and copies ran while one was open for 50% of the time, Pallas kernels for 0%

profile of v1, /device:TPU:0, one launch (start us, length us, event | category | flops | bytes accessed | tf_op | source)
XLA Modules:
  0.0 673.5 jit_solution(12832645752052465551)
XLA Ops:
  10.7 3.0 collective-permute-start
  61.4 7.8 %collective-permute-done.2 = f32[128,768]{1,0:T(8,128)S(1)} collective-permute-done((f32[128,768]{1,0:T(8,128)S(1)}, f32[128,768]{1,0:T(8,128)S(1)}, u32[]{:S(2)}, u32[]{:S(2)}) %collective-permute-start.2) | collective-permute-done | bytes 393248 | tf_op jit(solution)/shard_map/ppermute | solution.py:145
  69.4 6.2 collective-permute-done.7
  110.7 3.6 collective-permute-done.10
  122.8 3.7 fusion.1
  126.5 10.3 %copy.335 = f32[768,2,1024]{2,1,0:T(2,128)} copy(f32[768,2,1024]{2,0,1:T(8,128)} %fusion.1) | data formatting | bytes 12582912 | tf_op jit(solution)/shard_map/transpose | solution.py:159
  136.8 9.5 %concatenate.56 = f32[2,2,2,2,48,2048]{5,4,3,2,1,0:T(8,128)} reshape(f32[768,2,1024]{2,1,0:T(2,128)} %copy.335) | data formatting | bytes 12582912 | tf_op jit(solution)/shard_map/concatenate | solution.py:161
  197.2 4.7 copy.334
  201.9 6.9 %concatenate.53 = f32[2,2,2,2,48,1152]{5,4,3,2,1,0:T(8,128)} reshape(f32[768,3,384]{2,1,0:T(4,128)} %copy.334) | data formatting | bytes 7077888 | tf_op jit(solution)/shard_map/concatenate | solution.py:161
  210.7 3.3 fusion.16
  215.3 4.5 collective-permute-done.18
  272.8 4.7 copy.333
  277.4 6.6 concatenate.50
  285.8 3.7 fusion.21
  313.4 3.6 fusion
  317.0 10.2 %copy.325 = f32[768,2,1024]{2,1,0:T(2,128)} copy(f32[768,2,1024]{2,0,1:T(8,128)} %fusion) | data formatting | bytes 12582912 | tf_op jit(solution)/shard_map/transpose | solution.py:159
  327.2 9.4 %concatenate.46 = f32[2,2,2,2,48,2048]{5,4,3,2,1,0:T(8,128)} reshape(f32[768,2,1024]{2,1,0:T(2,128)} %copy.325) | data formatting | bytes 12582912 | tf_op jit(solution)/shard_map/concatenate | solution.py:161
  370.3 4.5 copy.324
  374.8 6.7 concatenate.43
  382.3 3.2 fusion.26
  413.5 20.5 %collective-permute-done.39 = f32[2,2,48,1536]{3,2,1,0:T(8,128)S(1)} collective-permute-done((f32[2,2,48,1536]{3,2,1,0:T(8,128)S(1)}, f32[2,2,48,1536]{3,2,1,0:T(8,128)S(1)}, u32[]{:S(2)}, u32[]{:S(2)}) %collective-permute-start.39) | collective-permute-done | bytes 1179680 | tf_op jit(solution)/shard_map/ppermute | solution.py:169
  435.7 23.6 %collective-permute-done.35 = f32[2,2,48,1536]{3,2,1,0:T(8,128)S(1)} collective-permute-done((f32[2,2,48,1536]{3,2,1,0:T(8,128)S(1)}, f32[2,2,48,1536]{3,2,1,0:T(8,128)S(1)}, u32[]{:S(2)}, u32[]{:S(2)}) %collective-permute-start.35) | collective-permute-done | bytes 1179680 | tf_op jit(solution)/shard_map/ppermute | solution.py:169
  461.1 2.7 collective-permute-start.41
  463.7 20.5 %collective-permute-done.23 = f32[2,2,48,1536]{3,2,1,0:T(8,128)S(1)} collective-permute-done((f32[2,2,48,1536]{3,2,1,0:T(8,128)S(1)}, f32[2,2,48,1536]{3,2,1,0:T(8,128)S(1)}, u32[]{:S(2)}, u32[]{:S(2)}) %collective-permute-start.23) | collective-permute-done | bytes 1179680 | tf_op jit(solution)/shard_map/ppermute | solution.py:169
  490.9 4.8 fusion.6
  500.6 5.3 collective-permute-done.24
  507.1 3.1 fusion.11
  518.5 10.7 %collective-permute-done.25 = f32[48,1536]{1,0:T(8,128)S(1)} collective-permute-done((f32[48,1536]{1,0:T(8,128)S(1)}, f32[48,1536]{1,0:T(8,128)S(1)}, u32[]{:S(2)}, u32[]{:S(2)}) %collective-permute-start.25) | collective-permute-done | bytes 294944 | tf_op jit(solution)/shard_map/ppermute | solution.py:169
  529.3 24.3 %collective-permute-done.43 = f32[2,2,48,3072]{3,2,1,0:T(8,128)} collective-permute-done((f32[2,2,48,3072]{3,2,1,0:T(8,128)}, f32[2,2,48,3072]{3,2,1,0:T(8,128)}, u32[]{:S(2)}, u32[]{:S(2)}) %collective-permute-start.43) | collective-permute-done | bytes 2359328 | tf_op jit(solution)/shard_map/ppermute | solution.py:169
  557.7 44.7 %collective-permute-done.27 = f32[2,2,48,3072]{3,2,1,0:T(8,128)} collective-permute-done((f32[2,2,48,3072]{3,2,1,0:T(8,128)}, f32[2,2,48,3072]{3,2,1,0:T(8,128)}, u32[]{:S(2)}, u32[]{:S(2)}) %collective-permute-start.27) | collective-permute-done | bytes 2359328 | tf_op jit(solution)/shard_map/ppermute | solution.py:169
  610.4 34.5 %collective-permute-done.28 = f32[2,48,3072]{2,1,0:T(8,128)} collective-permute-done((f32[2,48,3072]{2,1,0:T(8,128)S(1)}, f32[2,48,3072]{2,1,0:T(8,128)}, u32[]{:S(2)}, u32[]{:S(2)}) %collective-permute-start.28) | collective-permute-done | bytes 1179680 | tf_op jit(solution)/shard_map/ppermute | solution.py:169
  648.1 23.4 %collective-permute-done.29 = f32[48,3072]{1,0:T(8,128)S(1)} collective-permute-done((f32[48,3072]{1,0:T(8,128)S(1)}, f32[48,3072]{1,0:T(8,128)S(1)}, u32[]{:S(2)}, u32[]{:S(2)}) %collective-permute-start.29) | collective-permute-done | bytes 589856 | tf_op jit(solution)/shard_map/ppermute | solution.py:169
  (926 shorter events, 334.4 us)
Async XLA Ops:
  10.7 30.3 %collective-permute-start = (f32[64,768]{1,0:T(8,128)}, f32[64,768]{1,0:T(8,128)}, u32[]{:S(2)}, u32[]{:S(2)}) collective-permute-start(f32[64,768]{1,0:T(8,128)} %fusion.407), channel_id=1, source_target_pairs={{0,1},{1,0},{2,3},{3,2},{4,5},{5,4},{6,7},{7,6},{8,9},{9,8},{10,11... | collective-permute-start | bytes 589832 | tf_op jit(solution)/shard_map/ppermute | solution.py:145
  17.3 23.8 %collective-permute-start.5 = (f32[64,768]{1,0:T(8,128)}, f32[64,768]{1,0:T(8,128)}, u32[]{:S(2)}, u32[]{:S(2)}) collective-permute-start(f32[64,768]{1,0:T(8,128)} %fusion.412), channel_id=1, source_target_pairs={{0,1},{1,0},{2,3},{3,2},{4,5},{5,4},{6,7},{7,6},{8,9},{9,8},{10,11... | collective-permute-start | bytes 589832 | tf_op jit(solution)/shard_map/ppermute | solution.py:145
  23.3 29.4 %collective-permute-start.1 = (f32[128,768]{1,0:T(8,128)}, f32[128,768]{1,0:T(8,128)}, u32[]{:S(2)}, u32[]{:S(2)}) collective-permute-start(f32[128,768]{1,0:T(8,128)} %fusion.408), channel_id=1, source_target_pairs={{0,1},{1,0},{2,3},{3,2},{4,5},{5,4},{6,7},{7,6},{8,9},{9,8},{10,11... | collective-permute-start | bytes 1179656 | tf_op jit(solution)/shard_map/ppermute | solution.py:145
  109.5 45.1 %collective-permute-start.4 = (f32[64,768]{1,0:T(8,128)}, f32[64,768]{1,0:T(8,128)}, u32[]{:S(2)}, u32[]{:S(2)}) collective-permute-start(f32[64,768]{1,0:T(8,128)} %fusion.411), channel_id=1, source_target_pairs={{0,1},{1,0},{2,3},{3,2},{4,5},{5,4},{6,7},{7,6},{8,9},{9,8},{10,11... | collective-permute-start | bytes 589832 | tf_op jit(solution)/shard_map/ppermute | solution.py:145
  119.1 33.8 %collective-permute-start.14 = (f32[64,768]{1,0:T(8,128)}, f32[64,768]{1,0:T(8,128)}, u32[]{:S(2)}, u32[]{:S(2)}) collective-permute-start(f32[64,768]{1,0:T(8,128)} %fusion.73), channel_id=1, source_target_pairs={{0,1},{1,0},{2,3},{3,2},{4,5},{5,4},{6,7},{7,6},{8,9},{9,8},{10,11... | collective-permute-start | bytes 589832 | tf_op jit(solution)/shard_map/ppermute | solution.py:145
  121.5 33.2 %collective-permute-start.9 = (f32[64,768]{1,0:T(8,128)}, f32[64,768]{1,0:T(8,128)}, u32[]{:S(2)}, u32[]{:S(2)}) collective-permute-start(f32[64,768]{1,0:T(8,128)} %fusion.416), channel_id=1, source_target_pairs={{0,1},{1,0},{2,3},{3,2},{4,5},{5,4},{6,7},{7,6},{8,9},{9,8},{10,11... | collective-permute-start | bytes 589832 | tf_op jit(solution)/shard_map/ppermute | solution.py:145
  152.8 338.1 %collective-permute-start.42 = (f32[2,2,2,48,3072]{4,3,2,1,0:T(8,128)}, f32[2,2,2,48,3072]{4,3,2,1,0:T(8,128)}, u32[]{:S(2)}, u32[]{:S(2)}) collective-permute-start(f32[2,2,2,48,3072]{4,3,2,1,0:T(8,128)} %fusion.3), channel_id=1, source_target_pairs={{0,2},{2,0},{4,6},{6,4},{8,10},{10,8},{12,14},{14,12},{16,18},{18,... | collective-permute-start | bytes 14155784 | tf_op jit(solution)/shard_map/ppermute | solution.py:169
  191.2 102.9 %collective-permute-start.15 = (f32[128,768]{1,0:T(8,128)}, f32[128,768]{1,0:T(8,128)}, u32[]{:S(2)}, u32[]{:S(2)}) collective-permute-start(f32[128,768]{1,0:T(8,128)} %convolution_add_fusion.7), channel_id=1, source_target_pairs={{0,1},{1,0},{2,3},{3,2},{4,5},{5,4},{6,7},{7,6},{8,9},{9,8},{10,11... | collective-permute-start | bytes 1179656 | tf_op jit(solution)/shard_map/ppermute | solution.py:145
  194.1 97.4 %collective-permute-start.11 = (f32[128,768]{1,0:T(8,128)}, f32[128,768]{1,0:T(8,128)}, u32[]{:S(2)}, u32[]{:S(2)}) collective-permute-start(f32[128,768]{1,0:T(8,128)} %convolution_add_fusion.10), channel_id=1, source_target_pairs={{0,1},{1,0},{2,3},{3,2},{4,5},{5,4},{6,7},{7,6},{8,9},{9,8},{10,11... | collective-permute-start | bytes 1179656 | tf_op jit(solution)/shard_map/ppermute | solution.py:145
  194.7 26.9 %collective-permute-start.20 = (f32[64,768]{1,0:T(8,128)}, f32[64,768]{1,0:T(8,128)}, u32[]{:S(2)}, u32[]{:S(2)}) collective-permute-start(f32[64,768]{1,0:T(8,128)} %fusion.122), channel_id=1, source_target_pairs={{0,1},{1,0},{2,3},{3,2},{4,5},{5,4},{6,7},{7,6},{8,9},{9,8},{10,11... | collective-permute-start | bytes 589832 | tf_op jit(solution)/shard_map/ppermute | solution.py:145
  196.1 23.7 %collective-permute-start.18 = (f32[64,768]{1,0:T(8,128)}, f32[64,768]{1,0:T(8,128)}, u32[]{:S(2)}, u32[]{:S(2)}) collective-permute-start(f32[64,768]{1,0:T(8,128)} %fusion.124), channel_id=1, source_target_pairs={{0,1},{1,0},{2,3},{3,2},{4,5},{5,4},{6,7},{7,6},{8,9},{9,8},{10,11... | collective-permute-start | bytes 589832 | tf_op jit(solution)/shard_map/ppermute | solution.py:145
  219.8 183.1 %collective-permute-start.38 = (f32[2,2,2,48,1536]{4,3,2,1,0:T(8,128)}, f32[2,2,2,48,1536]{4,3,2,1,0:T(8,128)}, u32[]{:S(2)}, u32[]{:S(2)}) collective-permute-start(f32[2,2,2,48,1536]{4,3,2,1,0:T(8,128)} %fusion.16), channel_id=1, source_target_pairs={{0,2},{2,0},{4,6},{6,4},{8,10},{10,8},{12,14},{14,12},{16,18},{18,... | collective-permute-start | bytes 7077896 | tf_op jit(solution)/shard_map/ppermute | solution.py:169
  265.8 43.1 %collective-permute-start.19 = (f32[64,768]{1,0:T(8,128)}, f32[64,768]{1,0:T(8,128)}, u32[]{:S(2)}, u32[]{:S(2)}) collective-permute-start(f32[64,768]{1,0:T(8,128)} %fusion.77), channel_id=1, source_target_pairs={{0,1},{1,0},{2,3},{3,2},{4,5},{5,4},{6,7},{7,6},{8,9},{9,8},{10,11... | collective-permute-start | bytes 589832 | tf_op jit(solution)/shard_map/ppermute | solution.py:145
  294.1 112.5 %collective-permute-start.34 = (f32[2,2,2,48,1536]{4,3,2,1,0:T(8,128)}, f32[2,2,2,48,1536]{4,3,2,1,0:T(8,128)}, u32[]{:S(2)}, u32[]{:S(2)}) collective-permute-start(f32[2,2,2,48,1536]{4,3,2,1,0:T(8,128)} %fusion.21), channel_id=1, source_target_pairs={{0,2},{2,0},{4,6},{6,4},{8,10},{10,8},{12,14},{14,12},{16,18},{18,... | collective-permute-start | bytes 7077896 | tf_op jit(solution)/shard_map/ppermute | solution.py:169
  308.9 40.0 %collective-permute-start.16 = (f32[128,768]{1,0:T(8,128)}, f32[128,768]{1,0:T(8,128)}, u32[]{:S(2)}, u32[]{:S(2)}) collective-permute-start(f32[128,768]{1,0:T(8,128)} %fusion.67), channel_id=1, source_target_pairs={{0,1},{1,0},{2,3},{3,2},{4,5},{5,4},{6,7},{7,6},{8,9},{9,8},{10,11... | collective-permute-start | bytes 1179656 | tf_op jit(solution)/shard_map/ppermute | solution.py:145
  310.4 36.7 %collective-permute-start.12 = (f32[128,768]{1,0:T(8,128)S(1)}, f32[128,768]{1,0:T(8,128)}, u32[]{:S(2)}, u32[]{:S(2)}) collective-permute-start(f32[128,768]{1,0:T(8,128)S(1)} %fusion.64), channel_id=1, source_target_pairs={{0,1},{1,0},{2,3},{3,2},{4,5},{5,4},{6,7},{7,6},{8,9},{9,8},{10,11... | collective-permute-start | bytes 1179656 | tf_op jit(solution)/shard_map/ppermute | solution.py:145
  385.5 24.6 %collective-permute-start.22 = (f32[2,2,2,48,1536]{4,3,2,1,0:T(8,128)}, f32[2,2,2,48,1536]{4,3,2,1,0:T(8,128)}, u32[]{:S(2)}, u32[]{:S(2)}) collective-permute-start(f32[2,2,2,48,1536]{4,3,2,1,0:T(8,128)} %fusion.26), channel_id=1, source_target_pairs={{0,2},{2,0},{4,6},{6,4},{8,10},{10,8},{12,14},{14,12},{16,18},{18,... | collective-permute-start | bytes 7077896 | tf_op jit(solution)/shard_map/ppermute | solution.py:169
  402.3 104.8 %collective-permute-start.26 = (f32[2,2,2,48,3072]{4,3,2,1,0:T(8,128)}, f32[2,2,2,48,3072]{4,3,2,1,0:T(8,128)}, u32[]{:S(2)}, u32[]{:S(2)}) collective-permute-start(f32[2,2,2,48,3072]{4,3,2,1,0:T(8,128)} %fusion.8), channel_id=1, source_target_pairs={{0,2},{2,0},{4,6},{6,4},{8,10},{10,8},{12,14},{14,12},{16,18},{18,... | collective-permute-start | bytes 14155784 | tf_op jit(solution)/shard_map/ppermute | solution.py:169
  405.2 28.8 %collective-permute-start.39 = (f32[2,2,48,1536]{3,2,1,0:T(8,128)S(1)}, f32[2,2,48,1536]{3,2,1,0:T(8,128)S(1)}, u32[]{:S(2)}, u32[]{:S(2)}) collective-permute-start(f32[2,2,48,1536]{3,2,1,0:T(8,128)S(1)} %dynamic-slice_bitcast_fusion.3), channel_id=1, source_target_pairs={{0,4},{2,6},{4,0},{6,2},{8,12},{10,14},{12,8},{14,10},{16,20},{18,... | collective-permute-start | bytes 3538952 | tf_op jit(solution)/shard_map/ppermute | solution.py:169
  408.8 50.4 %collective-permute-start.35 = (f32[2,2,48,1536]{3,2,1,0:T(8,128)S(1)}, f32[2,2,48,1536]{3,2,1,0:T(8,128)S(1)}, u32[]{:S(2)}, u32[]{:S(2)}) collective-permute-start(f32[2,2,48,1536]{3,2,1,0:T(8,128)S(1)} %dynamic-slice_bitcast_fusion.4), channel_id=1, source_target_pairs={{0,4},{2,6},{4,0},{6,2},{8,12},{10,14},{12,8},{14,10},{16,20},{18,... | collective-permute-start | bytes 3538952 | tf_op jit(solution)/shard_map/ppermute | solution.py:169
  412.2 72.0 %collective-permute-start.23 = (f32[2,2,48,1536]{3,2,1,0:T(8,128)S(1)}, f32[2,2,48,1536]{3,2,1,0:T(8,128)S(1)}, u32[]{:S(2)}, u32[]{:S(2)}) collective-permute-start(f32[2,2,48,1536]{3,2,1,0:T(8,128)S(1)} %dynamic-slice_bitcast_fusion.6), channel_id=1, source_target_pairs={{0,4},{2,6},{4,0},{6,2},{8,12},{10,14},{12,8},{14,10},{16,20},{18,... | collective-permute-start | bytes 3538952 | tf_op jit(solution)/shard_map/ppermute | solution.py:169
  434.2 26.8 %collective-permute-start.40 = (f32[2,48,1536]{2,1,0:T(8,128)S(1)}, f32[2,48,1536]{2,1,0:T(8,128)S(1)}, u32[]{:S(2)}, u32[]{:S(2)}) collective-permute-start(f32[2,48,1536]{2,1,0:T(8,128)S(1)} %dynamic-slice_bitcast_fusion.8), channel_id=1, source_target_pairs={{0,8},{2,10},{4,12},{6,14},{8,0},{10,2},{12,4},{14,6},{16,24},{18,... | collective-permute-start | bytes 1769480 | tf_op jit(solution)/shard_map/ppermute | solution.py:169
  459.5 26.5 %collective-permute-start.36 = (f32[2,48,1536]{2,1,0:T(8,128)S(1)}, f32[2,48,1536]{2,1,0:T(8,128)S(1)}, u32[]{:S(2)}, u32[]{:S(2)}) collective-permute-start(f32[2,48,1536]{2,1,0:T(8,128)S(1)} %dynamic-slice_bitcast_fusion.9), channel_id=1, source_target_pairs={{0,8},{2,10},{4,12},{6,14},{8,0},{10,2},{12,4},{14,6},{16,24},{18,... | collective-permute-start | bytes 1769480 | tf_op jit(solution)/shard_map/ppermute | solution.py:169
  461.1 28.3 %collective-permute-start.41 = (f32[48,1536]{1,0:T(8,128)S(1)}, f32[48,1536]{1,0:T(8,128)S(1)}, u32[]{:S(2)}, u32[]{:S(2)}) collective-permute-start(f32[48,1536]{1,0:T(8,128)S(1)} %dynamic-slice_bitcast_fusion.12), channel_id=1, source_target_pairs={{0,16},{2,18},{4,20},{6,22},{8,24},{10,26},{12,28},{14,30},{16,0},... | collective-permute-start | bytes 884744 | tf_op jit(solution)/shard_map/ppermute | solution.py:169
  484.4 21.5 %collective-permute-start.24 = (f32[2,48,1536]{2,1,0:T(8,128)S(1)}, f32[2,48,1536]{2,1,0:T(8,128)}, u32[]{:S(2)}, u32[]{:S(2)}) collective-permute-start(f32[2,48,1536]{2,1,0:T(8,128)S(1)} %dynamic-slice_bitcast_fusion.11), channel_id=1, source_target_pairs={{0,8},{2,10},{4,12},{6,14},{8,0},{10,2},{12,4},{14,6},{16,24},{18,... | collective-permute-start | bytes 1769480 | tf_op jit(solution)/shard_map/ppermute | solution.py:169
  486.8 29.3 %collective-permute-start.37 = (f32[48,1536]{1,0:T(8,128)}, f32[48,1536]{1,0:T(8,128)}, u32[]{:S(2)}, u32[]{:S(2)}) collective-permute-start(f32[48,1536]{1,0:T(8,128)} %dynamic-slice_bitcast_fusion.13), channel_id=1, source_target_pairs={{0,16},{2,18},{4,20},{6,22},{8,24},{10,26},{12,28},{14,30},{16,0},... | collective-permute-start | bytes 884744 | tf_op jit(solution)/shard_map/ppermute | solution.py:169
  499.1 54.5 %collective-permute-start.43 = (f32[2,2,48,3072]{3,2,1,0:T(8,128)}, f32[2,2,48,3072]{3,2,1,0:T(8,128)}, u32[]{:S(2)}, u32[]{:S(2)}) collective-permute-start(f32[2,2,48,3072]{3,2,1,0:T(8,128)} %dynamic-slice_bitcast_fusion), channel_id=1, source_target_pairs={{0,4},{2,6},{4,0},{6,2},{8,12},{10,14},{12,8},{14,10},{16,20},{18,... | collective-permute-start | bytes 7077896 | tf_op jit(solution)/shard_map/ppermute | solution.py:169
  513.0 89.4 %collective-permute-start.27 = (f32[2,2,48,3072]{3,2,1,0:T(8,128)}, f32[2,2,48,3072]{3,2,1,0:T(8,128)}, u32[]{:S(2)}, u32[]{:S(2)}) collective-permute-start(f32[2,2,48,3072]{3,2,1,0:T(8,128)} %dynamic-slice_bitcast_fusion.1), channel_id=1, source_target_pairs={{0,4},{2,6},{4,0},{6,2},{8,12},{10,14},{12,8},{14,10},{16,20},{18,... | collective-permute-start | bytes 7077896 | tf_op jit(solution)/shard_map/ppermute | solution.py:169
  556.4 51.5 %collective-permute-start.44 = (f32[2,48,3072]{2,1,0:T(8,128)S(1)}, f32[2,48,3072]{2,1,0:T(8,128)}, u32[]{:S(2)}, u32[]{:S(2)}) collective-permute-start(f32[2,48,3072]{2,1,0:T(8,128)S(1)} %dynamic-slice_bitcast_fusion.2), channel_id=1, source_target_pairs={{0,8},{2,10},{4,12},{6,14},{8,0},{10,2},{12,4},{14,6},{16,24},{18,... | collective-permute-start | bytes 3538952 | tf_op jit(solution)/shard_map/ppermute | solution.py:169
  605.9 39.0 %collective-permute-start.28 = (f32[2,48,3072]{2,1,0:T(8,128)S(1)}, f32[2,48,3072]{2,1,0:T(8,128)}, u32[]{:S(2)}, u32[]{:S(2)}) collective-permute-start(f32[2,48,3072]{2,1,0:T(8,128)S(1)} %dynamic-slice_bitcast_fusion.5), channel_id=1, source_target_pairs={{0,8},{2,10},{4,12},{6,14},{8,0},{10,2},{12,4},{14,6},{16,24},{18,... | collective-permute-start | bytes 3538952 | tf_op jit(solution)/shard_map/ppermute | solution.py:169
  609.8 36.6 %collective-permute-start.45 = (f32[48,3072]{1,0:T(8,128)S(1)}, f32[48,3072]{1,0:T(8,128)S(1)}, u32[]{:S(2)}, u32[]{:S(2)}) collective-permute-start(f32[48,3072]{1,0:T(8,128)S(1)} %dynamic-slice_bitcast_fusion.7), channel_id=1, source_target_pairs={{0,16},{2,18},{4,20},{6,22},{8,24},{10,26},{12,28},{14,30},{16,0},... | collective-permute-start | bytes 1769480 | tf_op jit(solution)/shard_map/ppermute | solution.py:169
  646.4 25.1 %collective-permute-start.29 = (f32[48,3072]{1,0:T(8,128)S(1)}, f32[48,3072]{1,0:T(8,128)S(1)}, u32[]{:S(2)}, u32[]{:S(2)}) collective-permute-start(f32[48,3072]{1,0:T(8,128)S(1)} %dynamic-slice_bitcast_fusion.10), channel_id=1, source_target_pairs={{0,16},{2,18},{4,20},{6,22},{8,24},{10,26},{12,28},{14,30},{16,0},... | collective-permute-start | bytes 1769480 | tf_op jit(solution)/shard_map/ppermute | solution.py:169
  (265 other events, 1557.7 us)

commit v2 on v0

v2 whole, which is shorter than its diff:
```python
import functools

import jax
import jax.numpy as jnp
from jax import lax
from jax.experimental import pallas as pl
from jax.experimental.pallas import tpu as pltpu
from jax.sharding import PartitionSpec as P

HEAD_DIM = 64
PAIR = 2 * HEAD_DIM
EPSILON = 1e-06
NEG_LARGE = -1e30
SCALE = HEAD_DIM ** (-0.5)
BF = jnp.bfloat16
F32 = jnp.float32
MIB = 1024 * 1024


def mm(left, right):
    return jnp.dot(left, right, preferred_element_type=F32)


def mm_nt(left, right):
    return lax.dot_general(left, right, (((1,), (1,)), ((), ())), preferred_element_type=F32)


def mm_tn(left, right):
    return lax.dot_general(left, right, (((0,), (0,)), ((), ())), preferred_element_type=F32)


def norm(hidden, gain):
    scaling = lax.rsqrt(jnp.mean(hidden * hidden, -1, keepdims=True) + EPSILON)
    return (hidden * scaling * gain).astype(BF)


def norm_back(grad, hidden, gain):
    scaling = lax.rsqrt(jnp.mean(hidden * hidden, -1, keepdims=True) + EPSILON)
    normed = hidden * scaling
    grad_hat = grad * gain
    grad_in = scaling * (grad_hat - normed * jnp.mean(grad_hat * normed, -1, keepdims=True))
    return grad_in, jnp.sum(grad * normed, 0, keepdims=True)


def gelu_parts(gate):
    slope = 0.7978845608028654
    square = gate * gate
    bent = jnp.tanh(slope * gate * (1.0 + 0.044715 * square))
    half = 0.5 * (1.0 + bent)
    value = gate * half
    rise = half + 0.5 * gate * (1.0 - bent * bent) * slope * (1.0 + 0.134145 * square)
    return value, rise


def stack_heads(pair):
    lane = lax.broadcasted_iota(jnp.int32, pair.shape, 1)
    zero = jnp.zeros_like(pair)
    return jnp.concatenate(
        [jnp.where(lane < HEAD_DIM, pair, zero), jnp.where(lane < HEAD_DIM, zero, pair)], 0
    )


def merge_heads(stacked):
    rows = stacked.shape[0] // 2
    lane = lax.broadcasted_iota(jnp.int32, (rows, PAIR), 1)
    return jnp.where(lane < HEAD_DIM, stacked[:rows], stacked[rows:])


def soft_of(stacked_query, keys, bias):
    scores = mm_nt(stacked_query, keys) * SCALE + bias
    expon = jnp.exp(scores - jnp.max(scores, -1, keepdims=True))
    return expon / jnp.sum(expon, -1, keepdims=True)


def pair_fwd(query, keys, values, bias):
    soft = soft_of(stack_heads(query), keys, bias)
    return merge_heads(mm(soft.astype(BF), values)).astype(BF)


def pair_back(query, keys, values, grad_out, bias):
    queries = stack_heads(query)
    soft = soft_of(queries, keys, bias)
    grads = stack_heads(grad_out)
    grad_values = mm_tn(soft.astype(BF), grads)
    grad_soft = mm_nt(grads, values)
    grad_scores = (
        soft * (grad_soft - jnp.sum(soft * grad_soft, -1, keepdims=True))
    ).astype(BF)
    grad_query = merge_heads(mm(grad_scores, keys)) * SCALE
    grad_keys = mm_tn(grad_scores, queries) * SCALE
    return grad_query.astype(BF), grad_keys.astype(BF), grad_values.astype(BF)


def length_bias(count, rows, length):
    col = lax.broadcasted_iota(jnp.int32, (2 * rows, length), 1)
    return jnp.where(col < count, 0.0, NEG_LARGE).astype(F32)


def causal_bias(counts, plots, length):
    shape = (plots * length, plots * length)
    row = lax.broadcasted_iota(jnp.int32, shape, 0)
    col = lax.broadcasted_iota(jnp.int32, shape, 1)
    bias = jnp.full(shape, NEG_LARGE, F32)
    for plot in range(plots):
        low = plot * length
        inside = (row >= low) & (row < low + length) & (col >= low)
        inside = inside & (col <= row) & (col < low + counts[plot])
        bias = jnp.where(inside, 0.0, bias)
    return jnp.concatenate([bias, bias], 0)


def pairs_of(width):
    return [slice(at, at + PAIR) for at in range(0, width, PAIR)]


def put(ref, at, value):
    ref[:, at : at + value.shape[1]] = value.astype(ref.dtype)
    return at + value.shape[1]


def put_both(send_ref, keep_ref, at, value):
    put(send_ref, at, value)
    return put(keep_ref, at, value)


def put_cut(send_ref, keep_ref, at, value, order_ref):
    ordered = mm(value, order_ref[...])
    half = ordered.shape[1] // 2
    put(send_ref, at, ordered[:, :half])
    return put(keep_ref, at, ordered[:, half:])


def self_fwd_kernel(causal, length, counts, state, gain, stacked, outer, part, normed_ref, qkv_ref, mixed_ref):
    rows = state.shape[0]
    width = outer.shape[0]
    normed = norm(state[...].astype(F32), gain[...])
    normed_ref[...] = normed
    for which in range(3):
        qkv_ref[:, which * width : (which + 1) * width] = mm(normed, stacked[which]).astype(BF)
    plots = rows // length
    if causal:
        spans = [slice(0, rows)]
        biases = [causal_bias(counts, plots, length)]
    else:
        spans = [slice(p * length, (p + 1) * length) for p in range(plots)]
        biases = [length_bias(counts[p], length, length) for p in range(plots)]
    for span, bias in zip(spans, biases):
        for cols in pairs_of(width):
            mixed_ref[span, cols] = pair_fwd(
                qkv_ref[span, cols],
                qkv_ref[span, width + cols.start : width + cols.stop],
                qkv_ref[span, 2 * width + cols.start : 2 * width + cols.stop],
                bias,
            )
    part[...] = mm(mixed_ref[...], outer[...])


def enc_mlp_fwd_kernel(state, own, other, gain, inner, outer, part, state_ref, normed_ref, gate_ref, up_ref, hidden_ref):
    full = state[...].astype(F32) + own[...] + other[...]
    state_ref[...] = full
    normed_ref[...] = norm(full, gain[...])
    width = outer.shape[0]
    step = 256
    for at in range(0, width, step):
        cols = slice(at, at + step)
        gate = mm(normed_ref[...], inner[0, :, cols])
        up = mm(normed_ref[...], inner[1, :, cols])
        gate_ref[:, cols] = gate
        up_ref[:, cols] = up
        value, _ = gelu_parts(gate)
        hidden_ref[:, cols] = (value * up).astype(BF)
    part[...] = mm(hidden_ref[...], outer[...])


def cross_fwd_kernel(
    length, counts, enc_state, enc_own, enc_other, enc_gain, dec_state, dec_own, dec_other, dec_gain, stacked, outer,
    part, enc_ref, memory_ref, dec_ref, normed_ref, query_ref, kv_ref, mixed_ref,
):
    width = outer.shape[0]
    enc_full = enc_state[...] + enc_own[...] + enc_other[...]
    enc_ref[...] = enc_full
    memory_ref[...] = norm(enc_full, enc_gain[...])
    dec_full = dec_state[...].astype(F32) + dec_own[...] + dec_other[...]
    dec_ref[...] = dec_full
    normed_ref[...] = norm(dec_full, dec_gain[...])
    query_ref[...] = mm(normed_ref[...], stacked[0]).astype(BF)
    kv_ref[:, :width] = mm(memory_ref[...], stacked[1]).astype(BF)
    kv_ref[:, width:] = mm(memory_ref[...], stacked[2]).astype(BF)
    plots = enc_state.shape[0] // length
    rows = dec_state.shape[0] // plots
    for plot in range(plots):
        bias = length_bias(counts[plot], rows, length)
        q_span = slice(plot * rows, (plot + 1) * rows)
        k_span = slice(plot * length, (plot + 1) * length)
        for cols in pairs_of(width):
            mixed_ref[q_span, cols] = pair_fwd(
                query_ref[q_span, cols],
                kv_ref[k_span, cols],
                kv_ref[k_span, width + cols.start : width + cols.stop],
                bias,
            )
    part[...] = mm(mixed_ref[...], outer[...])


def dec_mlp_kernel(state, own, other, gain, cotangent, inner, outer, order, out_part, grad_part, state_ref, send, keep):
    full = state[...] + own[...] + other[...]
    state_ref[...] = full
    normed = norm(full, gain[...])
    width = outer.shape[0]
    at = put_cut(send, keep, 0, normed, order)
    half = at
    low = cotangent[...]
    put_cut(send, keep, half + 2 * width, low, order)
    step = 256
    for col in range(0, width, step):
        cols = slice(col, col + step)
        gate = mm(normed, inner[0, :, cols])
        up = mm(normed, inner[1, :, cols])
        value, rise = gelu_parts(gate)
        grad_hidden = mm_nt(low, outer[cols, :])
        put_both(send, keep, half + col, (grad_hidden * up * rise).astype(BF))
        put_both(send, keep, half + width + col, (grad_hidden * value).astype(BF))
        put_both(send, keep, 2 * half + 2 * width + col, (value * up).astype(BF))
    grad_part[...] = mm_nt(keep[:, half : half + width], inner[0]) + mm_nt(
        keep[:, half + width : half + 2 * width], inner[1]
    )
    out_part[...] = mm(keep[:, 2 * half + 2 * width :], outer[...])


def cross_back_kernel(
    length, counts, grad, own, other, state, gain, normed, memory, query, kv, mixed, stacked, outer, order,
    query_part, memory_part, grad_ref, gain_ref, send, keep, key_grads,
):
    grad_in, gain_ref[...] = norm_back(own[...] + other[...], state[...], gain[...])
    full = grad[...].astype(F32) + grad_in
    grad_ref[...] = full
    low = full.astype(BF)
    width = outer.shape[0]
    at = put_cut(send, keep, 0, normed[...], order)
    half = at
    at = put_cut(send, keep, half + width, low, order)
    put_both(send, keep, at, mixed[...])
    base = at + width
    grad_mixed = mm_nt(low, outer[...]).astype(BF)
    plots = kv.shape[0] // length
    rows = low.shape[0] // plots
    for plot in range(plots):
        bias = length_bias(counts[plot], rows, length)
        q_span = slice(plot * rows, (plot + 1) * rows)
        k_span = slice(plot * length, (plot + 1) * length)
        for cols in pairs_of(width):
            values = slice(width + cols.start, width + cols.stop)
            grad_query, grad_keys, grad_values = pair_back(
                query[q_span, cols], kv[k_span, cols], kv[k_span, values], grad_mixed[q_span, cols], bias
            )
            keep[q_span, half + cols.start : half + cols.stop] = grad_query
            send[q_span, half + cols.start : half + cols.stop] = grad_query.astype(F32)
            key_grads[k_span, cols] = grad_keys
            key_grads[k_span, values] = grad_values
    query_part[...] = mm_nt(keep[:, half : half + width], stacked[0])
    memory_part[...] = mm_nt(key_grads[:, :width], stacked[1]) + mm_nt(key_grads[:, width:], stacked[2])
    ordered = mm(memory[...], order[...])
    folds = kv.shape[0] // low.shape[0]
    for fold in range(folds):
        span = slice(fold * low.shape[0], (fold + 1) * low.shape[0])
        put(send, base, ordered[span, :half])
        put(keep, base, ordered[span, half:])
        base = put_both(send, keep, base + half, key_grads[span, :])


def self_back_kernel(
    causal, length, counts, grad, own, other, state, gain, normed, qkv, mixed, stacked, outer, order,
    part, grad_ref, gain_ref, send, keep,
):
    grad_in, gain_ref[...] = norm_back(own[...] + other[...], state[...], gain[...])
    full = grad[...] + grad_in
    grad_ref[...] = full
    low = full.astype(BF)
    width = outer.shape[0]
    half = put_cut(send, keep, 0, normed[...], order)
    at = put_cut(send, keep, half + 3 * width, low, order)
    put_both(send, keep, at, mixed[...])
    grad_mixed = mm_nt(low, outer[...]).astype(BF)
    rows = low.shape[0]
    plots = rows // length
    if causal:
        spans = [slice(0, rows)]
        biases = [causal_bias(counts, plots, length)]
    else:
        spans = [slice(p * length, (p + 1) * length) for p in range(plots)]
        biases = [length_bias(counts[p], length, length) for p in range(plots)]
    for span, bias in zip(spans, biases):
        for cols in pairs_of(width):
            grads = pair_back(
                qkv[span, cols],
                qkv[span, width + cols.start : width + cols.stop],
                qkv[span, 2 * width + cols.start : 2 * width + cols.stop],
                grad_mixed[span, cols],
                bias,
            )
            for which, piece in enumerate(grads):
                start = half + which * width + cols.start
                keep[span, start : start + PAIR] = piece
                send[span, start : start + PAIR] = piece.astype(F32)
    total = mm_nt(keep[:, half : half + width], stacked[0])
    total += mm_nt(keep[:, half + width : half + 2 * width], stacked[1])
    total += mm_nt(keep[:, half + 2 * width : half + 3 * width], stacked[2])
    part[...] = total


def enc_mlp_back_kernel(
    own, other, state, gain, normed, gate_ref, up_ref, hidden, inner, outer, order,
    part, grad_ref, gain_ref, send, keep,
):
    full, gain_ref[...] = norm_back(own[...] + other[...], state[...], gain[...])
    grad_ref[...] = full
    low = full.astype(BF)
    width = outer.shape[0]
    half = put_cut(send, keep, 0, normed[...], order)
    at = put_cut(send, keep, half + 2 * width, low, order)
    put_both(send, keep, at, hidden[...])
    step = 256
    for col in range(0, width, step):
        cols = slice(col, col + step)
        value, rise = gelu_parts(gate_ref[:, cols])
        grad_hidden = mm_nt(low, outer[cols, :])
        put_both(send, keep, half + col, (grad_hidden * up_ref[:, cols] * rise).astype(BF))
        put_both(send, keep, half + width + col, (grad_hidden * value).astype(BF))
    part[...] = mm_nt(keep[:, half : half + width], inner[0]) + mm_nt(
        keep[:, half + width : half + 2 * width], inner[1]
    )


def last_kernel(
    enc_grad, enc_own, enc_other, enc_state, enc_gain, dec_grad, dec_own, dec_other, dec_state, dec_gain,
    enc_ref, enc_gain_ref, dec_ref, dec_gain_ref,
):
    grad_in, enc_gain_ref[...] = norm_back(
        enc_own[...] + enc_other[...], enc_state[...].astype(F32), enc_gain[...]
    )
    enc_ref[...] = (enc_grad[...] + grad_in).astype(BF)
    grad_in, dec_gain_ref[...] = norm_back(
        dec_own[...] + dec_other[...], dec_state[...].astype(F32), dec_gain[...]
    )
    dec_ref[...] = (dec_grad[...] + grad_in).astype(BF)


def weight_kernel(segments, keep, recv, send_out, keep_out):
    started = set()
    for cut, cut_width, first, columns, target in segments:
        left = jnp.concatenate([keep[:, cut : cut + cut_width], recv[:, cut : cut + cut_width].astype(BF)], 0)
        half = cut_width // 2
        step = 512 if columns % 512 == 0 else 384
        for at in range(0, columns, step):
            cols = slice(first + at, first + at + step)
            right = jnp.concatenate([keep[:, cols], recv[:, cols].astype(BF)], 0)
            total = mm_tn(left, right)
            into = slice(target + at, target + at + step)
            if target in started:
                send_out[:, into] += total[:half]
                keep_out[:, into] += total[half:]
            else:
                send_out[:, into] = total[:half]
                keep_out[:, into] = total[half:]
        started.add(target)


SMEM = pl.BlockSpec(memory_space=pltpu.SMEM)
VMEM = pl.BlockSpec(memory_space=pltpu.VMEM)


def call(kernel, outs, args, flops, name, scalars=0, scratch=(), limit=40):
    shapes = [jax.ShapeDtypeStruct(shape, kind) for shape, kind in outs]
    moved = sum(a.size * a.dtype.itemsize for a in args) + sum(
        s.size * jnp.dtype(s.dtype).itemsize for s in shapes
    )
    return pl.pallas_call(
        kernel,
        out_shape=shapes,
        in_specs=[SMEM] * scalars + [VMEM] * (len(args) - scalars),
        out_specs=[VMEM] * len(shapes),
        scratch_shapes=list(scratch),
        compiler_params=pltpu.CompilerParams(vmem_limit_bytes=limit * MIB),
        cost_estimate=pl.CostEstimate(flops=int(flops), bytes_accessed=int(moved), transcendentals=0),
        name=name,
    )(*args)


def pair_other(part):
    return lax.ppermute(part, "mp", [(0, 1), (1, 0)])


def swap(value, bit):
    shards = lax.axis_size("dp")
    return lax.ppermute(value, "dp", [(i, i ^ (1 << bit)) for i in range(shards)])


def feature_order(features, bits_order):
    shards = lax.axis_size("dp")
    me = lax.axis_index("dp")
    block = features // shards
    column = jnp.arange(features, dtype=jnp.int32)
    place = column // block
    owner = jnp.zeros_like(column)
    count = len(bits_order)
    for at, bit in enumerate(bits_order):
        own = (place >> (count - 1 - at)) & 1
        owner = owner | ((((me >> bit) & 1) ^ (1 - own)) << bit)
    source = owner * block + column % block
    return (jnp.arange(features, dtype=jnp.int32)[:, None] == source[None, :]).astype(BF)


def halve(sent, kept, bits_order):
    bits = list(bits_order[1:])
    total = kept + swap(sent, bits[0])
    for bit in bits[1:]:
        rows = total.shape[0] // 2
        total = total[rows:] + swap(total[:rows], bit)
    return total


def weight_sums(send, keep, segments, columns, bits_order, name):
    recv = swap(send, 0)
    rows = segments[0][1] // 2
    flops = sum(2 * 2 * keep.shape[0] * s[1] * s[3] for s in segments)
    sent, kept = call(
        functools.partial(weight_kernel, segments),
        [((rows, columns), F32), ((rows, columns), F32)],
        [keep, recv],
        flops,
        name,
    )
    return halve(sent, kept, bits_order)


def body(
    enc_in, dec_in, cotangent, patch_counts, table_lengths, enc_qkv, enc_attn_out, enc_mlp_in, enc_mlp_out, enc_gains,
    dec_self_qkv, dec_self_out, dec_cross_qkv, dec_cross_out, dec_mlp_in, dec_mlp_out, dec_gains,
):
    plots, enc_len, features = enc_in.shape
    dec_len = dec_in.shape[1]
    enc_rows, dec_rows = plots * enc_len, plots * dec_len
    heads = enc_attn_out.shape[0]
    units = enc_mlp_out.shape[0]
    half = features // 2
    bits = lax.axis_size("dp").bit_length() - 1
    plain = tuple(range(bits))
    turned = (0, 2, 1) + tuple(range(3, bits))
    order = feature_order(features, plain)
    order_turned = feature_order(features, turned)
    x0 = enc_in.reshape(enc_rows, features)
    y0 = dec_in.reshape(dec_rows, features)
    top = cotangent.reshape(dec_rows, features)
    eg = [enc_gains[i : i + 1] for i in range(3)]
    dg = [dec_gains[i : i + 1] for i in range(3)]
    enc_wide, dec_wide = ((enc_rows, features), F32), ((dec_rows, features), F32)
    enc_low, dec_low = ((enc_rows, features), BF), ((dec_rows, features), BF)
    gain_row = ((1, features), F32)
    attn_flops = 2 * features * heads

    part_e1, u_e0, qkv_e, mixed_e = call(
        functools.partial(self_fwd_kernel, False, enc_len),
        [enc_wide, enc_low, ((enc_rows, 3 * heads), BF), ((enc_rows, heads), BF)],
        [patch_counts, x0, eg[0], enc_qkv, enc_attn_out],
        4 * enc_rows * attn_flops, "enc_attn_fwd", 1,
    )
    other_e1 = pair_other(part_e1)
    part_d1, u_d0, qkv_d, mixed_d = call(
        functools.partial(self_fwd_kernel, True, dec_len),
        [dec_wide, dec_low, ((dec_rows, 3 * heads), BF), ((dec_rows, heads), BF)],
        [table_lengths, y0, dg[0], dec_self_qkv, dec_self_out],
        4 * dec_rows * attn_flops, "dec_self_fwd", 1,
    )
    other_d1 = pair_other(part_d1)
    part_e2, x1, u_e1, gate, up, hidden = call(
        enc_mlp_fwd_kernel,
        [enc_wide, enc_wide, enc_low, ((enc_rows, units), F32), ((enc_rows, units), F32), ((enc_rows, units), BF)],
        [x0, part_e1, other_e1, eg[1], enc_mlp_in, enc_mlp_out],
        6 * enc_rows * features * units, "enc_mlp_fwd",
    )
    other_e2 = pair_other(part_e2)
    part_d2, x2, memory, y1, u_d1, query, kv, mixed_c = call(
        functools.partial(cross_fwd_kernel, enc_len),
        [dec_wide, enc_wide, enc_low, dec_wide, dec_low, ((dec_rows, heads), BF), ((enc_rows, 2 * heads), BF),
         ((dec_rows, heads), BF)],
        [patch_counts, x1, part_e2, other_e2, eg[2], y0, part_d1, other_d1, dg[1], dec_cross_qkv, dec_cross_out],
        2 * (dec_rows + enc_rows) * attn_flops, "cross_fwd", 1,
    )
    other_d2 = pair_other(part_d2)
    wide = 2 * half + 3 * units
    part_out, part_g3, y2, send_m, keep_m = call(
        dec_mlp_kernel,
        [dec_wide, dec_wide, dec_wide, ((dec_rows, wide), F32), ((dec_rows, wide), BF)],
        [y1, part_d2, other_d2, dg[2], top, dec_mlp_in, dec_mlp_out, order],
        12 * dec_rows * features * units, "dec_mlp",
    )
    other_g3 = pair_other(part_g3)
    wide = 2 * half + 2 * heads + (enc_rows // dec_rows) * (half + 2 * heads)
    part_q, part_m, g2, gain_d2, send_c, keep_c = call(
        functools.partial(cross_back_kernel, enc_len),
        [dec_wide, enc_wide, dec_wide, gain_row, ((dec_rows, wide), F32), ((dec_rows, wide), BF)],
        [patch_counts, top, part_g3, other_g3, y2, dg[2], u_d1, memory, query, kv, mixed_c, dec_cross_qkv,
         dec_cross_out, order],
        2 * (dec_rows + enc_rows) * attn_flops, "cross_back", 1,
        scratch=[pltpu.VMEM((enc_rows, 2 * heads), BF)],
    )
    other_m = pair_other(part_m)
    other_q = pair_other(part_q)
    mlp_segments = (
        (0, half, half, 2 * units, 0),
        (half + 2 * units, half, 2 * half + 2 * units, units, 2 * units),
    )
    attn_segments = (
        (0, half, half, 3 * heads, 0),
        (half + 3 * heads, half, 2 * half + 3 * heads, heads, 3 * heads),
    )
    base = 2 * half + 2 * heads
    cross_segments = (
        (0, half, half, heads, 0),
        (half + heads, half, 2 * half + heads, heads, heads),
    ) + tuple(
        (base + f * (half + 2 * heads), half, base + f * (half + 2 * heads) + half, 2 * heads, 2 * heads)
        for f in range(enc_rows // dec_rows)
    )
    sum_m = weight_sums(send_m, keep_m, mlp_segments, 3 * units, plain, "dec_mlp_weights")
    wide = 2 * half + 3 * units
    part_g1, back2, gain_e2, send_f, keep_f = call(
        enc_mlp_back_kernel,
        [enc_wide, enc_wide, gain_row, ((enc_rows, wide), F32), ((enc_rows, wide), BF)],
        [part_m, other_m, x2, eg[2], u_e1, gate, up, hidden, enc_mlp_in, enc_mlp_out, order],
        6 * enc_rows * features * units, "enc_mlp_back",
    )
    other_g1 = pair_other(part_g1)
    sum_c = weight_sums(send_c, keep_c, cross_segments, 4 * heads, plain, "cross_weights")
    wide = 2 * half + 4 * heads
    part_g0, g1, gain_d1, send_s, keep_s = call(
        functools.partial(self_back_kernel, True, dec_len),
        [dec_wide, dec_wide, gain_row, ((dec_rows, wide), F32), ((dec_rows, wide), BF)],
        [table_lengths, g2, part_q, other_q, y1, dg[1], u_d0, qkv_d, mixed_d, dec_self_qkv, dec_self_out,
         order_turned],
        4 * dec_rows * attn_flops, "dec_self_back", 1,
    )
    other_g0 = pair_other(part_g0)
    sum_f = weight_sums(send_f, keep_f, mlp_segments, 3 * units, plain, "enc_mlp_weights")
    sum_s = weight_sums(send_s, keep_s, attn_segments, 4 * heads, turned, "dec_self_weights")
    part_ge, back1, gain_e1, send_a, keep_a = call(
        functools.partial(self_back_kernel, False, enc_len),
        [enc_wide, enc_wide, gain_row, ((enc_rows, wide), F32), ((enc_rows, wide), BF)],
        [patch_counts, back2, part_g1, other_g1, x1, eg[1], u_e0, qkv_e, mixed_e, enc_qkv, enc_attn_out, order],
        4 * enc_rows * attn_flops, "enc_attn_back", 1,
    )
    other_ge = pair_other(part_ge)
    sum_a = weight_sums(send_a, keep_a, attn_segments, 4 * heads, plain, "enc_attn_weights")
    enc_out, gain_e0, dec_out_grad, gain_d0 = call(
        last_kernel,
        [enc_low, gain_row, dec_low, gain_row],
        [back1, part_ge, other_ge, x0, eg[0], g1, part_g0, other_g0, y0, dg[0]],
        100, "input_grads",
    )
    dec_out = (y2 + part_out + pair_other(part_out)).astype(BF)

    gains = jnp.concatenate([gain_e0, gain_e1, gain_e2, gain_d0, gain_d1, gain_d2], 0)
    gains = gains.reshape((gains.shape[0],) + (2,) * bits + (-1,))
    me = lax.axis_index("dp")
    for bit in range(bits):
        axis = bits - bit
        mine = (me >> bit) & 1
        sent = lax.dynamic_index_in_dim(gains, 1 - mine, axis, keepdims=False)
        gains = lax.dynamic_index_in_dim(gains, mine, axis, keepdims=False) + swap(sent, bit)

    def stacked_of(total, count):
        return jnp.moveaxis(total.reshape(total.shape[0], count, -1), 1, 0)

    def attn_grads(total):
        return [stacked_of(total[:, : 3 * heads], 3), total[:, 3 * heads :].T]

    def mlp_grads(total):
        return [stacked_of(total[:, : 2 * units], 2), total[:, 2 * units :].T]

    cross_in = jnp.concatenate([sum_c[:, :heads], sum_c[:, 2 * heads :]], 1)
    cross = [stacked_of(cross_in, 3), sum_c[:, heads : 2 * heads].T]
    grads = (
        attn_grads(sum_a) + mlp_grads(sum_f) + [gains[:3]] + attn_grads(sum_s) + cross + mlp_grads(sum_m) + [gains[3:]]
    )
    return (
        dec_out.reshape(cotangent.shape),
        enc_out.reshape(enc_in.shape),
        dec_out_grad.reshape(dec_in.shape),
    ) + tuple(grads)


def solution(mesh):
    rows = P("dp", None, None)
    inner, outer = P(None, None, "mp"), P("mp", None)
    enc = (inner, outer, inner, outer, P())
    dec = (inner, outer, inner, outer, inner, outer, P())
    inner_grad, outer_grad, gain_grad = P(None, "dp", "mp"), P("mp", "dp"), P(None, "dp")
    return jax.shard_map(
        body,
        mesh=mesh,
        in_specs=(rows, rows, rows, P("dp"), P("dp")) + enc + dec,
        out_specs=(rows, rows, rows)
        + (inner_grad, outer_grad) * 2 + (gain_grad,)
        + (inner_grad, outer_grad) * 3 + (gain_grad,),
        check_vma=False,
    )
```

time: 1260 us -> 468 us (0.37)
  waiting for transfers between devices: 1000 us -> 314 us
  matrix products: 125 us -> 0 us
  Pallas kernels: 0 us -> 55.8 us
  other arithmetic: 59.7 us -> 13.3 us
  starting transfers between devices: 1.79 us -> 30.4 us
  between operations: 17.8 us -> 1.54 us
    reduce_scatter x10 -> x0, waiting for transfers between devices: 717 us -> none  [body(): lax.psum_scatter(tuple(enc_accum + dec_accum), 'dp', scatter_dimension=1,...]
    ppermute x0 -> x35, waiting for transfers between devices: none -> 314 us  [the longest x24 198 us: swap(): return lax.ppermute(value, 'dp', [(i, i ^ 1 << bit) for i in range(shards)])]
    psum x7 -> x0, waiting for transfers between devices: 228 us -> none  [the longest x4 141 us: branch_sum(): return lax.psum(partial_sum, 'mp')]
    dot_general x144 -> x0, matrix products: 125 us -> none  [the longest x36 36.4 us: project_back(): jnp.einsum('sd,ed->se', left, right, preferred_element_type=jnp.float32)]
    unnamed x21 -> x0, waiting for transfers between devices: 59.7 us -> none
    pallas_call x0 -> x15, Pallas kernels: none -> 55.8 us  [call(): pl.pallas_call(kernel, out_shape=shapes, in_specs=[SMEM] * scalars + [VME...]
    ppermute x0 -> x35, starting transfers between devices: none -> 30.4 us  [the longest x24 17.4 us: swap(): return lax.ppermute(value, 'dp', [(i, i ^ 1 << bit) for i in range(shards)])]
    reduce_sum x23 -> x0, other arithmetic: 26.8 us -> none  [the longest x9 17.1 us: norm_back(): return (grad_in, jnp.sum(grad * normed, 0))]
  transfers between devices with their start and end apart: 19 -> 35, of which waited for: 19 -> 19; matrix products, arithmetic and copies ran while one was open for 6% -> 6% of each run, Pallas kernels for 0% -> 9%
where the time goes in v2:
time: 468 us; the launch traced here: 467 us
  waiting for transfers between devices  314 us (67%)
  Pallas kernels  55.8 us (12%)
  local copies, waits for them, and re-layouts  52.5 us (11%)
  starting transfers between devices  30.4 us (6%)
  other arithmetic  13.3 us (3%)
    ppermute x24, waiting for transfers between devices, swap(): return lax.ppermute(value, 'dp', [(i, i ^ 1 << bit) for i in range(shards)])  198 us
    ppermute x11, waiting for transfers between devices, pair_other(): return lax.ppermute(part, 'mp', [(0, 1), (1, 0)])  116 us
    pallas_call x15, Pallas kernels, call(): pl.pallas_call(kernel, out_shape=shapes, in_specs=[SMEM] * scalars + [VME...  55.8 us
    unnamed x202, local copies, waits for them, and re-layouts  37.8 us
    ppermute x24, starting transfers between devices, swap(): return lax.ppermute(value, 'dp', [(i, i ^ 1 << bit) for i in range(shards)])  17.4 us
    ppermute x11, starting transfers between devices, pair_other(): return lax.ppermute(part, 'mp', [(0, 1), (1, 0)])  13 us
  transfers between devices with their start and end apart: 35, of which 19 were waited for; matrix products, arithmetic and copies ran while one was open for 6% of the time, Pallas kernels for 9%

profile of v2, /device:TPU:0, one launch (start us, length us, event | category | flops | bytes accessed | tf_op | source)
XLA Modules:
  0.0 467.4 jit_solution(14640296589531147331)
XLA Ops:
  5.7 2.3 enc_attn_fwd.1
  10.3 3.0 collective-permute-start
  13.2 17.5 %collective-permute-done.other = f32[256,768]{1,0:T(8,128)S(1)} collective-permute-done((f32[256,768]{1,0:T(8,128)S(1)}, f32[256,768]{1,0:T(8,128)S(1)}, u32[]{:S(2)}, u32[]{:S(2)}) %collective-permute-start) | collective-permute-done | bytes 786464 | tf_op jit(solution)/shard_map/ppermute | solution.py:390
  42.9 20.4 %collective-permute-done.2.dec_other = f32[128,768]{1,0:T(8,128)S(1)} collective-permute-done((f32[128,768]{1,0:T(8,128)S(1)}, f32[128,768]{1,0:T(8,128)S(1)}, u32[]{:S(2)}, u32[]{:S(2)}) %collective-permute-start.2) | collective-permute-done | bytes 393248 | tf_op jit(solution)/shard_map/ppermute | solution.py:390
  63.3 4.0 cross_fwd.1
  74.2 7.8 %collective-permute-done.3.other = f32[128,768]{1,0:T(8,128)} collective-permute-done((f32[128,768]{1,0:T(8,128)}, f32[128,768]{1,0:T(8,128)}, u32[]{:S(2)}, u32[]{:S(2)}) %collective-permute-start.3) | collective-permute-done | bytes 393248 | tf_op jit(solution)/shard_map/ppermute | solution.py:390
  86.1 3.8 dec_mlp.1
  91.8 7.4 %collective-permute-done.5.other = f32[128,768]{1,0:T(8,128)S(1)} collective-permute-done((f32[128,768]{1,0:T(8,128)S(1)}, f32[128,768]{1,0:T(8,128)S(1)}, u32[]{:S(2)}, u32[]{:S(2)}) %collective-permute-start.5) | collective-permute-done | bytes 393248 | tf_op jit(solution)/shard_map/ppermute | solution.py:390
  99.2 6.0 %cross_back.1 = (f32[128,768]{1,0:T(8,128)S(1)}, f32[256,768]{1,0:T(8,128)S(1)}, f32[128,768]{1,0:T(8,128)S(1)}, f32[1,768]{1,0:T(1,128)S(1)}, f32[128,3840]{1,0:T(8,128)}, /*index=5*/bf16[128,3840]{1,0:T(8,128)(2,1)S(1)}) custom-call(s32[2]{0:T(128)S(1)} %copy-done.89, bf16[128,768]{1,0:T(8,128)(2,1)S(1)} %bitcast.56, ...), custom_call_target="tpu_custom_call" | custom-call | flops 452984832 | bytes 10622984 | tf_op jit(solution)/shard_map/cross_back/pallas_call | solution.py:377
  109.0 21.9 %collective-permute-done.9.other = f32[128,768]{1,0:T(8,128)S(1)} collective-permute-done((f32[128,768]{1,0:T(8,128)S(1)}, f32[128,768]{1,0:T(8,128)S(1)}, u32[]{:S(2)}, u32[]{:S(2)}) %collective-permute-start.9) | collective-permute-done | bytes 393248 | tf_op jit(solution)/shard_map/ppermute | solution.py:390
  131.0 4.7 %dec_self_back.1 = (f32[128,768]{1,0:T(8,128)S(1)}, f32[128,768]{1,0:T(8,128)S(1)}, f32[1,768]{1,0:T(1,128)S(1)}, f32[128,2304]{1,0:T(8,128)}, bf16[128,2304]{1,0:T(8,128)(2,1)S(1)}) custom-call(s32[2]{0:T(128)S(1)} %copy-done.93, f32[128,768]{1,0:T(8,128)S(1)} %get-tuple-element.104.grad, f32[128,768]{1,0:T(8,128)S(1)} %get-tuple-element.105.own, ...), custom_call_target="tpu_custom_call" | custom-call | flops 301989888 | bytes 8263688 | tf_op jit(solution)/shard_map/dec_self_back/pallas_call | solution.py:377
  139.3 6.8 %enc_mlp_back.1 = (f32[256,768]{1,0:T(8,128)S(1)}, f32[256,768]{1,0:T(8,128)S(1)}, f32[1,768]{1,0:T(1,128)S(1)}, f32[256,3840]{1,0:T(8,128)}, bf16[256,3840]{1,0:T(8,128)(2,1)S(1)}) custom-call(f32[256,768]{1,0:T(8,128)S(1)} %copy-done.45, f32[256,768]{1,0:T(8,128)S(1)} %collective-permute-done.6.other, f32[256,768]{1,0:T(8,128)S(1)} %copy-done.41, ...), custom_call_target="tpu_custom_call" | custom-call | flops 1207959552 | bytes 18749440 | tf_op jit(solution)/shard_map/enc_mlp_back/pallas_call | solution.py:377
  148.4 19.0 %collective-permute-done.7.other = f32[256,768]{1,0:T(8,128)S(1)} collective-permute-done((f32[256,768]{1,0:T(8,128)S(1)}, f32[256,768]{1,0:T(8,128)S(1)}, u32[]{:S(2)}, u32[]{:S(2)}) %collective-permute-start.7) | collective-permute-done | bytes 786464 | tf_op jit(solution)/shard_map/ppermute | solution.py:390
  167.4 6.8 %enc_attn_back.1 = (f32[256,768]{1,0:T(8,128)}, f32[256,768]{1,0:T(8,128)S(1)}, f32[1,768]{1,0:T(1,128)S(1)}, f32[256,2304]{1,0:T(8,128)}, bf16[256,2304]{1,0:T(8,128)(2,1)S(1)}) custom-call(s32[2]{0:T(128)S(1)} %copy-done.89, f32[256,768]{1,0:T(8,128)S(1)} %get-tuple-element.97.grad, f32[256,768]{1,0:T(8,128)S(1)} %get-tuple-element.98.own, ...), custom_call_target="tpu_custom_call" | custom-call | flops 603979776 | bytes 12982280 | tf_op jit(solution)/shard_map/enc_attn_back/pallas_call | solution.py:377
  178.5 2.1 dec_mlp_weights.1
  180.6 21.5 %collective-permute-done.10.dec_other = f32[128,768]{1,0:T(8,128)S(1)} collective-permute-done((f32[128,768]{1,0:T(8,128)S(1)}, f32[128,768]{1,0:T(8,128)S(1)}, u32[]{:S(2)}, u32[]{:S(2)}) %collective-permute-start.10) | collective-permute-done | bytes 393248 | tf_op jit(solution)/shard_map/ppermute | solution.py:390
  206.4 2.7 input_grads.1
  214.0 2.7 cross_weights.1
  219.8 37.8 %collective-permute-done.20 = f32[6,2,2,48]{3,2,1,0:T(2,128)S(1)} collective-permute-done((f32[6,2,2,48]{3,2,1,0:T(2,128)S(1)}, f32[6,2,2,48]{3,2,1,0:T(2,128)S(1)}, u32[]{:S(2)}, u32[]{:S(2)}) %collective-permute-start.20) | collective-permute-done | bytes 4640 | tf_op jit(solution)/shard_map/ppermute | solution.py:395
  261.7 31.6 %collective-permute-done.25 = f32[96,1536]{1,0:T(8,128)S(1)} collective-permute-done((f32[96,1536]{1,0:T(8,128)S(1)}, f32[96,1536]{1,0:T(8,128)S(1)}, u32[]{:S(2)}, u32[]{:S(2)}) %collective-permute-start.25) | collective-permute-done | bytes 589856 | tf_op jit(solution)/shard_map/ppermute | solution.py:395
  294.9 2.9 collective-permute-done.22
  302.6 1.9 add.163
  306.7 4.1 collective-permute-done.26
  310.9 4.9 %enc_mlp_weights.1 = (f32[192,3072]{1,0:T(8,128)}, f32[192,3072]{1,0:T(8,128)S(1)}) custom-call(bf16[256,3840]{1,0:T(8,128)(2,1)S(1)} %copy-done.20, f32[256,3840]{1,0:T(8,128)} %collective-permute-done.15.recv), custom_call_target="tpu_custom_call" | custom-call | flops 1207959552 | bytes 10616832 | tf_op jit(solution)/shard_map/enc_mlp_weights/pallas_call | solution.py:377
  323.2 3.8 enc_attn_weights.1
  328.5 22.3 %collective-permute-done.33 = f32[96,3072]{1,0:T(8,128)} collective-permute-done((f32[96,3072]{1,0:T(8,128)}, f32[96,3072]{1,0:T(8,128)}, u32[]{:S(2)}, u32[]{:S(2)}) %collective-permute-start.33) | collective-permute-done | bytes 1179680 | tf_op jit(solution)/shard_map/ppermute | solution.py:395
  358.2 35.3 %collective-permute-done.12 = f32[192,1536]{1,0:T(8,128)} collective-permute-done((f32[192,1536]{1,0:T(8,128)}, f32[192,1536]{1,0:T(8,128)}, u32[]{:S(2)}, u32[]{:S(2)}) %collective-permute-start.12) | collective-permute-done | bytes 1179680 | tf_op jit(solution)/shard_map/ppermute | solution.py:395
  395.1 1.9 add.142
  397.1 2.1 collective-permute-start.17
  401.1 13.4 %collective-permute-done.13 = f32[96,1536]{1,0:T(8,128)S(1)} collective-permute-done((f32[96,1536]{1,0:T(8,128)S(1)}, f32[96,1536]{1,0:T(8,128)S(1)}, u32[]{:S(2)}, u32[]{:S(2)}) %collective-permute-start.13) | collective-permute-done | bytes 589856 | tf_op jit(solution)/shard_map/ppermute | solution.py:395
  415.8 24.1 %collective-permute-done.17 = f32[96,3072]{1,0:T(8,128)S(1)} collective-permute-done((f32[96,3072]{1,0:T(8,128)S(1)}, f32[96,3072]{1,0:T(8,128)S(1)}, u32[]{:S(2)}, u32[]{:S(2)}) %collective-permute-start.17) | collective-permute-done | bytes 1179680 | tf_op jit(solution)/shard_map/ppermute | solution.py:395
  442.1 23.7 %collective-permute-done.18 = f32[48,3072]{1,0:T(8,128)S(1)} collective-permute-done((f32[48,3072]{1,0:T(8,128)S(1)}, f32[48,3072]{1,0:T(8,128)S(1)}, u32[]{:S(2)}, u32[]{:S(2)}) %collective-permute-start.18) | collective-permute-done | bytes 589856 | tf_op jit(solution)/shard_map/ppermute | solution.py:395
  (315 shorter events, 95.5 us)
Async XLA Ops:
  10.3 20.5 %collective-permute-start = (f32[256,768]{1,0:T(8,128)S(1)}, f32[256,768]{1,0:T(8,128)S(1)}, u32[]{:S(2)}, u32[]{:S(2)}) collective-permute-start(f32[256,768]{1,0:T(8,128)S(1)} %get-tuple-element.77.own), channel_id=1, source_target_pairs={{0,1},{1,0},{2,3},{3,2},{4,5},{5,4},{6,7},{7,6},{8,9},{9,8},{10,11... | collective-permute-start | bytes 2359304 | tf_op jit(solution)/shard_map/ppermute | solution.py:390
  36.1 27.2 %collective-permute-start.1 = (f32[256,768]{1,0:T(8,128)S(1)}, f32[256,768]{1,0:T(8,128)S(1)}, u32[]{:S(2)}, u32[]{:S(2)}) collective-permute-start(f32[256,768]{1,0:T(8,128)S(1)} %get-tuple-element.79.enc_own), channel_id=1, source_target_pairs={{0,1},{1,0},{2,3},{3,2},{4,5},{5,4},{6,7},{7,6},{8,9},{9,8},{10,11... | collective-permute-start | bytes 2359304 | tf_op jit(solution)/shard_map/ppermute | solution.py:390
  42.4 20.9 %collective-permute-start.2 = (f32[128,768]{1,0:T(8,128)S(1)}, f32[128,768]{1,0:T(8,128)S(1)}, u32[]{:S(2)}, u32[]{:S(2)}) collective-permute-start(f32[128,768]{1,0:T(8,128)S(1)} %get-tuple-element.80.dec_own), channel_id=1, source_target_pairs={{0,1},{1,0},{2,3},{3,2},{4,5},{5,4},{6,7},{7,6},{8,9},{9,8},{10,11... | collective-permute-start | bytes 1179656 | tf_op jit(solution)/shard_map/ppermute | solution.py:390
  72.4 9.7 %collective-permute-start.3 = (f32[128,768]{1,0:T(8,128)}, f32[128,768]{1,0:T(8,128)}, u32[]{:S(2)}, u32[]{:S(2)}) collective-permute-start(f32[128,768]{1,0:T(8,128)} %get-tuple-element.82.own), channel_id=1, source_target_pairs={{0,1},{1,0},{2,3},{3,2},{4,5},{5,4},{6,7},{7,6},{8,9},{9,8},{10,11... | collective-permute-start | bytes 1179656 | tf_op jit(solution)/shard_map/ppermute | solution.py:390
  90.7 8.5 %collective-permute-start.5 = (f32[128,768]{1,0:T(8,128)S(1)}, f32[128,768]{1,0:T(8,128)S(1)}, u32[]{:S(2)}, u32[]{:S(2)}) collective-permute-start(f32[128,768]{1,0:T(8,128)S(1)} %get-tuple-element.85.own), channel_id=1, source_target_pairs={{0,1},{1,0},{2,3},{3,2},{4,5},{5,4},{6,7},{7,6},{8,9},{9,8},{10,11... | collective-permute-start | bytes 1179656 | tf_op jit(solution)/shard_map/ppermute | solution.py:390
  91.8 86.1 %collective-permute-start.31 = (f32[128,3840]{1,0:T(8,128)S(1)}, f32[128,3840]{1,0:T(8,128)S(1)}, u32[]{:S(2)}, u32[]{:S(2)}) collective-permute-start(f32[128,3840]{1,0:T(8,128)S(1)} %get-tuple-element.136), channel_id=1, source_target_pairs={{0,2},{2,0},{4,6},{6,4},{8,10},{10,8},{12,14},{14,12},{16,18},{18,... | collective-permute-start | bytes 5898248 | tf_op jit(solution)/shard_map/ppermute | solution.py:395
  106.3 31.8 %collective-permute-start.6 = (f32[256,768]{1,0:T(8,128)S(1)}, f32[256,768]{1,0:T(8,128)S(1)}, u32[]{:S(2)}, u32[]{:S(2)}) collective-permute-start(f32[256,768]{1,0:T(8,128)S(1)} %get-tuple-element.91.own), channel_id=1, source_target_pairs={{0,1},{1,0},{2,3},{3,2},{4,5},{5,4},{6,7},{7,6},{8,9},{9,8},{10,11... | collective-permute-start | bytes 2359304 | tf_op jit(solution)/shard_map/ppermute | solution.py:390
  107.3 23.6 %collective-permute-start.9 = (f32[128,768]{1,0:T(8,128)S(1)}, f32[128,768]{1,0:T(8,128)S(1)}, u32[]{:S(2)}, u32[]{:S(2)}) collective-permute-start(f32[128,768]{1,0:T(8,128)S(1)} %get-tuple-element.105.own), channel_id=1, source_target_pairs={{0,1},{1,0},{2,3},{3,2},{4,5},{5,4},{6,7},{7,6},{8,9},{9,8},{10,11... | collective-permute-start | bytes 1179656 | tf_op jit(solution)/shard_map/ppermute | solution.py:390
  138.1 36.6 %collective-permute-start.23 = (f32[128,2304]{1,0:T(8,128)}, f32[128,2304]{1,0:T(8,128)S(1)}, u32[]{:S(2)}, u32[]{:S(2)}) collective-permute-start(f32[128,2304]{1,0:T(8,128)} %get-tuple-element.128), channel_id=1, source_target_pairs={{0,2},{2,0},{4,6},{6,4},{8,10},{10,8},{12,14},{14,12},{16,18},{18,... | collective-permute-start | bytes 3538952 | tf_op jit(solution)/shard_map/ppermute | solution.py:395
  147.4 19.9 %collective-permute-start.7 = (f32[256,768]{1,0:T(8,128)S(1)}, f32[256,768]{1,0:T(8,128)S(1)}, u32[]{:S(2)}, u32[]{:S(2)}) collective-permute-start(f32[256,768]{1,0:T(8,128)S(1)} %get-tuple-element.98.own), channel_id=1, source_target_pairs={{0,1},{1,0},{2,3},{3,2},{4,5},{5,4},{6,7},{7,6},{8,9},{9,8},{10,11... | collective-permute-start | bytes 2359304 | tf_op jit(solution)/shard_map/ppermute | solution.py:390
  147.8 64.4 %collective-permute-start.27 = (f32[128,3840]{1,0:T(8,128)}, f32[128,3840]{1,0:T(8,128)}, u32[]{:S(2)}, u32[]{:S(2)}) collective-permute-start(f32[128,3840]{1,0:T(8,128)} %get-tuple-element.132), channel_id=1, source_target_pairs={{0,2},{2,0},{4,6},{6,4},{8,10},{10,8},{12,14},{14,12},{16,18},{18,... | collective-permute-start | bytes 5898248 | tf_op jit(solution)/shard_map/ppermute | solution.py:395
  148.1 162.8 %collective-permute-start.15 = (f32[256,3840]{1,0:T(8,128)}, f32[256,3840]{1,0:T(8,128)}, u32[]{:S(2)}, u32[]{:S(2)}) collective-permute-start(f32[256,3840]{1,0:T(8,128)} %get-tuple-element.118), channel_id=1, source_target_pairs={{0,2},{2,0},{4,6},{6,4},{8,10},{10,8},{12,14},{14,12},{16,18},{18,... | collective-permute-start | bytes 11796488 | tf_op jit(solution)/shard_map/ppermute | solution.py:395
  174.2 29.1 %collective-permute-start.8 = (f32[256,768]{1,0:T(8,128)}, f32[256,768]{1,0:T(8,128)}, u32[]{:S(2)}, u32[]{:S(2)}) collective-permute-start(f32[256,768]{1,0:T(8,128)} %get-tuple-element.103.enc_own), channel_id=1, source_target_pairs={{0,1},{1,0},{2,3},{3,2},{4,5},{5,4},{6,7},{7,6},{8,9},{9,8},{10,11... | collective-permute-start | bytes 2359304 | tf_op jit(solution)/shard_map/ppermute | solution.py:390
  176.4 40.4 %collective-permute-start.24 = (f32[192,1536]{1,0:T(8,128)}, f32[192,1536]{1,0:T(8,128)}, u32[]{:S(2)}, u32[]{:S(2)}) collective-permute-start(f32[192,1536]{1,0:T(8,128)} %get-tuple-element.130), channel_id=1, source_target_pairs={{0,8},{2,10},{4,12},{6,14},{8,0},{10,2},{12,4},{14,6},{16,24},{18,... | collective-permute-start | bytes 3538952 | tf_op jit(solution)/shard_map/ppermute | solution.py:395
  177.9 24.2 %collective-permute-start.10 = (f32[128,768]{1,0:T(8,128)S(1)}, f32[128,768]{1,0:T(8,128)S(1)}, u32[]{:S(2)}, u32[]{:S(2)}) collective-permute-start(f32[128,768]{1,0:T(8,128)S(1)} %copy-done.58), channel_id=1, source_target_pairs={{0,1},{1,0},{2,3},{3,2},{4,5},{5,4},{6,7},{7,6},{8,9},{9,8},{10,11... | collective-permute-start | bytes 1179656 | tf_op jit(solution)/shard_map/ppermute | solution.py:390
  202.8 99.7 %collective-permute-start.32 = (f32[192,3072]{1,0:T(8,128)}, f32[192,3072]{1,0:T(8,128)}, u32[]{:S(2)}, u32[]{:S(2)}) collective-permute-start(f32[192,3072]{1,0:T(8,128)} %get-tuple-element.138), channel_id=1, source_target_pairs={{0,4},{2,6},{4,0},{6,2},{8,12},{10,14},{12,8},{14,10},{16,20},{18,... | collective-permute-start | bytes 7077896 | tf_op jit(solution)/shard_map/ppermute | solution.py:395
  210.7 47.3 %collective-permute-start.4 = (f32[128,768]{1,0:T(8,128)}, f32[128,768]{1,0:T(8,128)S(1)}, u32[]{:S(2)}, u32[]{:S(2)}) collective-permute-start(f32[128,768]{1,0:T(8,128)} %copy-done.67), channel_id=1, source_target_pairs={{0,1},{1,0},{2,3},{3,2},{4,5},{5,4},{6,7},{7,6},{8,9},{9,8},{10,11... | collective-permute-start | bytes 1179656 | tf_op jit(solution)/shard_map/ppermute | solution.py:390
  212.2 45.3 %collective-permute-start.20 = (f32[6,2,2,48]{3,2,1,0:T(2,128)S(1)}, f32[6,2,2,48]{3,2,1,0:T(2,128)S(1)}, u32[]{:S(2)}, u32[]{:S(2)}) collective-permute-start(f32[6,2,2,48]{3,2,1,0:T(2,128)S(1)} %dynamic-slice_bitcast_fusion), channel_id=1, source_target_pairs={{0,4},{2,6},{4,0},{6,2},{8,12},{10,14},{12,8},{14,10},{16,20},{18,... | collective-permute-start | bytes 13832 | tf_op jit(solution)/shard_map/ppermute | solution.py:395
  216.7 83.2 %collective-permute-start.28 = (f32[192,1536]{1,0:T(8,128)S(1)}, f32[192,1536]{1,0:T(8,128)S(1)}, u32[]{:S(2)}, u32[]{:S(2)}) collective-permute-start(f32[192,1536]{1,0:T(8,128)S(1)} %get-tuple-element.134), channel_id=1, source_target_pairs={{0,4},{2,6},{4,0},{6,2},{8,12},{10,14},{12,8},{14,10},{16,20},{18,... | collective-permute-start | bytes 3538952 | tf_op jit(solution)/shard_map/ppermute | solution.py:395
  257.5 35.8 %collective-permute-start.25 = (f32[96,1536]{1,0:T(8,128)S(1)}, f32[96,1536]{1,0:T(8,128)S(1)}, u32[]{:S(2)}, u32[]{:S(2)}) collective-permute-start(f32[96,1536]{1,0:T(8,128)S(1)} %slice.169), channel_id=1, source_target_pairs={{0,4},{2,6},{4,0},{6,2},{8,12},{10,14},{12,8},{14,10},{16,20},{18,... | collective-permute-start | bytes 1769480 | tf_op jit(solution)/shard_map/ppermute | solution.py:395
  261.7 61.5 %collective-permute-start.11 = (f32[256,2304]{1,0:T(8,128)}, f32[256,2304]{1,0:T(8,128)}, u32[]{:S(2)}, u32[]{:S(2)}) collective-permute-start(f32[256,2304]{1,0:T(8,128)} %get-tuple-element.114), channel_id=1, source_target_pairs={{0,2},{2,0},{4,6},{6,4},{8,10},{10,8},{12,14},{14,12},{16,18},{18,... | collective-permute-start | bytes 7077896 | tf_op jit(solution)/shard_map/ppermute | solution.py:395
  297.8 13.0 %collective-permute-start.26 = (f32[48,1536]{1,0:T(8,128)S(1)}, f32[48,1536]{1,0:T(8,128)S(1)}, u32[]{:S(2)}, u32[]{:S(2)}) collective-permute-start(f32[48,1536]{1,0:T(8,128)S(1)} %slice.171), channel_id=1, source_target_pairs={{0,16},{2,18},{4,20},{6,22},{8,24},{10,26},{12,28},{14,30},{16,0},... | collective-permute-start | bytes 884744 | tf_op jit(solution)/shard_map/ppermute | solution.py:395
  300.9 20.7 %collective-permute-start.29 = (f32[96,1536]{1,0:T(8,128)}, f32[96,1536]{1,0:T(8,128)}, u32[]{:S(2)}, u32[]{:S(2)}) collective-permute-start(f32[96,1536]{1,0:T(8,128)} %slice.175), channel_id=1, source_target_pairs={{0,8},{2,10},{4,12},{6,14},{8,0},{10,2},{12,4},{14,6},{16,24},{18,... | collective-permute-start | bytes 1769480 | tf_op jit(solution)/shard_map/ppermute | solution.py:395
  306.3 44.6 %collective-permute-start.33 = (f32[96,3072]{1,0:T(8,128)}, f32[96,3072]{1,0:T(8,128)}, u32[]{:S(2)}, u32[]{:S(2)}) collective-permute-start(f32[96,3072]{1,0:T(8,128)} %slice.182), channel_id=1, source_target_pairs={{0,8},{2,10},{4,12},{6,14},{8,0},{10,2},{12,4},{14,6},{16,24},{18,... | collective-permute-start | bytes 3538952 | tf_op jit(solution)/shard_map/ppermute | solution.py:395
  315.8 79.3 %collective-permute-start.16 = (f32[192,3072]{1,0:T(8,128)}, f32[192,3072]{1,0:T(8,128)}, u32[]{:S(2)}, u32[]{:S(2)}) collective-permute-start(f32[192,3072]{1,0:T(8,128)} %get-tuple-element.120), channel_id=1, source_target_pairs={{0,4},{2,6},{4,0},{6,2},{8,12},{10,14},{12,8},{14,10},{16,20},{18,... | collective-permute-start | bytes 7077896 | tf_op jit(solution)/shard_map/ppermute | solution.py:395
  322.8 30.5 %collective-permute-start.30 = (f32[48,1536]{1,0:T(8,128)S(1)}, f32[48,1536]{1,0:T(8,128)S(1)}, u32[]{:S(2)}, u32[]{:S(2)}) collective-permute-start(f32[48,1536]{1,0:T(8,128)S(1)} %slice.177), channel_id=1, source_target_pairs={{0,16},{2,18},{4,20},{6,22},{8,24},{10,26},{12,28},{14,30},{16,0},... | collective-permute-start | bytes 884744 | tf_op jit(solution)/shard_map/ppermute | solution.py:395
  327.0 66.5 %collective-permute-start.12 = (f32[192,1536]{1,0:T(8,128)}, f32[192,1536]{1,0:T(8,128)}, u32[]{:S(2)}, u32[]{:S(2)}) collective-permute-start(f32[192,1536]{1,0:T(8,128)} %get-tuple-element.116), channel_id=1, source_target_pairs={{0,4},{2,6},{4,0},{6,2},{8,12},{10,14},{12,8},{14,10},{16,20},{18,... | collective-permute-start | bytes 3538952 | tf_op jit(solution)/shard_map/ppermute | solution.py:395
  353.3 45.9 %collective-permute-start.34 = (f32[48,3072]{1,0:T(8,128)}, f32[48,3072]{1,0:T(8,128)}, u32[]{:S(2)}, u32[]{:S(2)}) collective-permute-start(f32[48,3072]{1,0:T(8,128)} %slice.184), channel_id=1, source_target_pairs={{0,16},{2,18},{4,20},{6,22},{8,24},{10,26},{12,28},{14,30},{16,0},... | collective-permute-start | bytes 1769480 | tf_op jit(solution)/shard_map/ppermute | solution.py:395
  395.0 19.5 %collective-permute-start.13 = (f32[96,1536]{1,0:T(8,128)S(1)}, f32[96,1536]{1,0:T(8,128)S(1)}, u32[]{:S(2)}, u32[]{:S(2)}) collective-permute-start(f32[96,1536]{1,0:T(8,128)S(1)} %slice.157), channel_id=1, source_target_pairs={{0,8},{2,10},{4,12},{6,14},{8,0},{10,2},{12,4},{14,6},{16,24},{18,... | collective-permute-start | bytes 1769480 | tf_op jit(solution)/shard_map/ppermute | solution.py:395
  397.1 42.8 %collective-permute-start.17 = (f32[96,3072]{1,0:T(8,128)S(1)}, f32[96,3072]{1,0:T(8,128)S(1)}, u32[]{:S(2)}, u32[]{:S(2)}) collective-permute-start(f32[96,3072]{1,0:T(8,128)S(1)} %slice.163), channel_id=1, source_target_pairs={{0,8},{2,10},{4,12},{6,14},{8,0},{10,2},{12,4},{14,6},{16,24},{18,... | collective-permute-start | bytes 3538952 | tf_op jit(solution)/shard_map/ppermute | solution.py:395
  414.6 26.1 %collective-permute-start.14 = (f32[48,1536]{1,0:T(8,128)S(1)}, f32[48,1536]{1,0:T(8,128)S(1)}, u32[]{:S(2)}, u32[]{:S(2)}) collective-permute-start(f32[48,1536]{1,0:T(8,128)S(1)} %slice.159), channel_id=1, source_target_pairs={{0,16},{2,18},{4,20},{6,22},{8,24},{10,26},{12,28},{14,30},{16,0},... | collective-permute-start | bytes 884744 | tf_op jit(solution)/shard_map/ppermute | solution.py:395
  440.1 25.7 %collective-permute-start.18 = (f32[48,3072]{1,0:T(8,128)S(1)}, f32[48,3072]{1,0:T(8,128)S(1)}, u32[]{:S(2)}, u32[]{:S(2)}) collective-permute-start(f32[48,3072]{1,0:T(8,128)S(1)} %slice.165), channel_id=1, source_target_pairs={{0,16},{2,18},{4,20},{6,22},{8,24},{10,26},{12,28},{14,30},{16,0},... | collective-permute-start | bytes 1769480 | tf_op jit(solution)/shard_map/ppermute | solution.py:395
  (102 other events, 1034.9 us)

commit v3 on v2

v3 whole, which is shorter than its diff:
```python
import functools

import jax
import jax.numpy as jnp
from jax import lax
from jax.experimental import pallas as pl
from jax.experimental.pallas import tpu as pltpu
from jax.sharding import PartitionSpec as P

HEAD_DIM = 64
PAIR = 2 * HEAD_DIM
EPSILON = 1e-06
NEG_LARGE = -1e30
SCALE = HEAD_DIM ** (-0.5)
BF = jnp.bfloat16
F32 = jnp.float32
MIB = 1024 * 1024


def mm(left, right):
    return jnp.dot(left, right, preferred_element_type=F32)


def mm_nt(left, right):
    return lax.dot_general(left, right, (((1,), (1,)), ((), ())), preferred_element_type=F32)


def mm_tn(left, right):
    return lax.dot_general(left, right, (((0,), (0,)), ((), ())), preferred_element_type=F32)


def norm(hidden, gain):
    scaling = lax.rsqrt(jnp.mean(hidden * hidden, -1, keepdims=True) + EPSILON)
    return (hidden * scaling * gain).astype(BF)


def norm_back(grad, hidden, gain):
    scaling = lax.rsqrt(jnp.mean(hidden * hidden, -1, keepdims=True) + EPSILON)
    normed = hidden * scaling
    grad_hat = grad * gain
    grad_in = scaling * (grad_hat - normed * jnp.mean(grad_hat * normed, -1, keepdims=True))
    return grad_in, jnp.sum(grad * normed, 0, keepdims=True)


def gelu_parts(gate):
    slope = 0.7978845608028654
    square = gate * gate
    bent = jnp.tanh(slope * gate * (1.0 + 0.044715 * square))
    half = 0.5 * (1.0 + bent)
    value = gate * half
    rise = half + 0.5 * gate * (1.0 - bent * bent) * slope * (1.0 + 0.134145 * square)
    return value, rise


def stack_heads(pair):
    lane = lax.broadcasted_iota(jnp.int32, pair.shape, 1)
    zero = jnp.zeros_like(pair)
    return jnp.concatenate(
        [jnp.where(lane < HEAD_DIM, pair, zero), jnp.where(lane < HEAD_DIM, zero, pair)], 0
    )


def merge_heads(stacked):
    rows = stacked.shape[0] // 2
    lane = lax.broadcasted_iota(jnp.int32, (rows, PAIR), 1)
    return jnp.where(lane < HEAD_DIM, stacked[:rows], stacked[rows:])


def soft_of(stacked_query, keys, bias):
    scores = mm_nt(stacked_query, keys) * SCALE + bias
    expon = jnp.exp(scores - jnp.max(scores, -1, keepdims=True))
    return expon / jnp.sum(expon, -1, keepdims=True)


def pair_fwd(query, keys, values, bias):
    soft = soft_of(stack_heads(query), keys, bias)
    return merge_heads(mm(soft.astype(BF), values)).astype(BF)


def pair_back(query, keys, values, grad_out, bias):
    queries = stack_heads(query)
    soft = soft_of(queries, keys, bias)
    grads = stack_heads(grad_out)
    grad_values = mm_tn(soft.astype(BF), grads)
    grad_soft = mm_nt(grads, values)
    grad_scores = (
        soft * (grad_soft - jnp.sum(soft * grad_soft, -1, keepdims=True))
    ).astype(BF)
    grad_query = merge_heads(mm(grad_scores, keys)) * SCALE
    grad_keys = mm_tn(grad_scores, queries) * SCALE
    return grad_query.astype(BF), grad_keys.astype(BF), grad_values.astype(BF)


def length_bias(count, rows, length):
    col = lax.broadcasted_iota(jnp.int32, (2 * rows, length), 1)
    return jnp.where(col < count, 0.0, NEG_LARGE).astype(F32)


def causal_bias(counts, plots, length):
    shape = (plots * length, plots * length)
    row = lax.broadcasted_iota(jnp.int32, shape, 0)
    col = lax.broadcasted_iota(jnp.int32, shape, 1)
    bias = jnp.full(shape, NEG_LARGE, F32)
    for plot in range(plots):
        low = plot * length
        inside = (row >= low) & (row < low + length) & (col >= low)
        inside = inside & (col <= row) & (col < low + counts[plot])
        bias = jnp.where(inside, 0.0, bias)
    return jnp.concatenate([bias, bias], 0)


def pairs_of(width):
    return [slice(at, at + PAIR) for at in range(0, width, PAIR)]


def put(ref, at, value):
    last = at + value.shape[1]
    ref[:, at:last] = value.astype(ref.dtype)
    ref.flush(at, last)
    return last


def put_both(send, keep, at, value):
    put(send, at, value)
    return put(keep, at, value)


def put_cut(send, keep, at, value, order):
    ordered = mm(value, order[...])
    half = ordered.shape[1] // 2
    put(send, at, ordered[:, :half])
    return put(keep, at, ordered[:, half:])


def keys_of(causal, length, rows, counts):
    plots = rows // length
    if causal:
        return [(slice(0, rows), causal_bias(counts, plots, length))]
    return [(slice(p * length, (p + 1) * length), length_bias(counts[p], length, length)) for p in range(plots)]


def self_fwd_kernel(causal, length, counts, state, gain, stacked, outer, part, normed_ref, qkv, mixed):
    rows, width = state.shape[0], outer.shape[0]
    normed = norm(state[...].astype(F32), gain[0:1, :])
    normed_ref[...] = normed
    normed_ref.flush()
    for which in range(3):
        put(qkv, which * width, mm(normed, stacked[which]))
    for span, bias in keys_of(causal, length, rows, counts):
        for cols in pairs_of(width):
            mixed[span, cols] = pair_fwd(
                qkv[span, cols],
                qkv[span, width + cols.start : width + cols.stop],
                qkv[span, 2 * width + cols.start : 2 * width + cols.stop],
                bias,
            )
    mixed.flush()
    part[...] = mm(mixed[...], outer[...])


def enc_mlp_fwd_kernel(state, own, other, gain, inner, outer, part, state_ref, normed, gate_ref, up_ref, hidden):
    full = state[...].astype(F32) + own[...] + other[...]
    state_ref[...] = full
    normed[...] = norm(full, gain[1:2, :])
    flush(state_ref, normed)
    width = outer.shape[0]
    step = 256
    for at in range(0, width, step):
        cols = slice(at, at + step)
        gate = mm(normed[...], inner[0, :, cols])
        up = mm(normed[...], inner[1, :, cols])
        value, _ = gelu_parts(gate)
        put(gate_ref, at, gate)
        put(up_ref, at, up)
        put(hidden, at, value * up)
    part[...] = mm(hidden[...], outer[...])


def cross_fwd_kernel(
    length, counts, enc_state, enc_own, enc_other, enc_gain, dec_state, dec_own, dec_other, dec_gain, stacked, outer,
    part, enc_ref, memory, dec_ref, normed, query, kv, mixed,
):
    width = outer.shape[0]
    dec_full = dec_state[...].astype(F32) + dec_own[...] + dec_other[...]
    dec_ref[...] = dec_full
    normed[...] = norm(dec_full, dec_gain[1:2, :])
    flush(dec_ref, normed)
    put(query, 0, mm(normed[...], stacked[0]))
    enc_full = enc_state[...] + enc_own[...] + enc_other[...]
    enc_ref[...] = enc_full
    memory[...] = norm(enc_full, enc_gain[2:3, :])
    flush(enc_ref, memory)
    put(kv, 0, mm(memory[...], stacked[1]))
    put(kv, width, mm(memory[...], stacked[2]))
    plots = enc_state.shape[0] // length
    rows = dec_state.shape[0] // plots
    for plot in range(plots):
        bias = length_bias(counts[plot], rows, length)
        q_span = slice(plot * rows, (plot + 1) * rows)
        k_span = slice(plot * length, (plot + 1) * length)
        for cols in pairs_of(width):
            mixed[q_span, cols] = pair_fwd(
                query[q_span, cols],
                kv[k_span, cols],
                kv[k_span, width + cols.start : width + cols.stop],
                bias,
            )
    mixed.flush()
    part[...] = mm(mixed[...], outer[...])


def dec_mlp_kernel(
    state, own, other, gain, cotangent, inner, outer, order, order_outer, part, state_ref, send, keep
):
    full = state[...] + own[...] + other[...]
    state_ref[...] = full
    state_ref.flush()
    normed = norm(full, gain[2:3, :])
    low = cotangent[...]
    width, half = outer.shape[0], order.shape[0] // 2
    step = 256
    for col in range(0, width, step):
        cols = slice(col, col + step)
        gate = mm(normed, inner[0, :, cols])
        up = mm(normed, inner[1, :, cols])
        value, rise = gelu_parts(gate)
        grad_hidden = mm_nt(low, outer[cols, :])
        put_both(send, keep, half + col, (grad_hidden * up * rise).astype(BF))
        put_both(send, keep, half + width + col, (grad_hidden * value).astype(BF))
        put_both(send, keep, 2 * half + 2 * width + col, (value * up).astype(BF))
    part[...] = mm_nt(keep[:, half : half + width], inner[0]) + mm_nt(
        keep[:, half + width : half + 2 * width], inner[1]
    )
    part.flush()
    put_cut(send, keep, 0, normed, order)
    put_cut(send, keep, half + 2 * width, low, order_outer)


def out_part_kernel(keep, outer, part):
    part[...] = mm(keep[:, keep.shape[1] - outer.shape[0] :], outer[...])


def query_part_kernel(keep, stacked, part):
    half = stacked.shape[1] // 2
    part[...] = mm_nt(keep[:, half : half + stacked.shape[2]], stacked[0])


def cross_back_kernel(
    length, counts, own, other, state, gain, grad, outer, query, kv, stacked, order, normed, memory, mixed,
    part, grad_ref, gain_ref, send, keep, key_grads,
):
    grad_in, gain_ref[...] = norm_back(own[...] + other[...], state[...], gain[2:3, :])
    full = grad[...].astype(F32) + grad_in
    grad_ref[...] = full
    flush(gain_ref, grad_ref)
    low = full.astype(BF)
    width, half = outer.shape[0], order.shape[0] // 2
    grad_mixed = mm_nt(low, outer[...]).astype(BF)
    plots = kv.shape[0] // length
    rows = low.shape[0] // plots
    for plot in range(plots):
        bias = length_bias(counts[plot], rows, length)
        q_span = slice(plot * rows, (plot + 1) * rows)
        k_span = slice(plot * length, (plot + 1) * length)
        for cols in pairs_of(width):
            values = slice(width + cols.start, width + cols.stop)
            grad_query, grad_keys, grad_values = pair_back(
                query[q_span, cols], kv[k_span, cols], kv[k_span, values], grad_mixed[q_span, cols], bias
            )
            keep[q_span, half + cols.start : half + cols.stop] = grad_query
            send[q_span, half + cols.start : half + cols.stop] = grad_query.astype(F32)
            key_grads[k_span, cols] = grad_keys
            key_grads[k_span, values] = grad_values
    send.flush(half, half + width)
    keep.flush(half, half + width)
    part[...] = mm_nt(key_grads[:, :width], stacked[1]) + mm_nt(key_grads[:, width:], stacked[2])
    part.flush()
    put_cut(send, keep, 0, normed[...], order)
    at = put_cut(send, keep, half + width, low, order)
    base = put_both(send, keep, at, mixed[...])
    ordered = mm(memory[...], order[...])
    for fold in range(kv.shape[0] // low.shape[0]):
        span = slice(fold * low.shape[0], (fold + 1) * low.shape[0])
        put(send, base, ordered[span, :half])
        put(keep, base, ordered[span, half:])
        base = put_both(send, keep, base + half, key_grads[span, :])


def self_back_kernel(
    causal, length, counts, own, other, state, gain, grad, outer, qkv, stacked, order, normed, mixed,
    part, grad_ref, gain_ref, send, keep,
):
    grad_in, gain_ref[...] = norm_back(own[...] + other[...], state[...], gain[1:2, :])
    full = grad[...] + grad_in
    grad_ref[...] = full
    flush(gain_ref, grad_ref)
    low = full.astype(BF)
    width, half = outer.shape[0], order.shape[0] // 2
    grad_mixed = mm_nt(low, outer[...]).astype(BF)
    for span, bias in keys_of(causal, length, low.shape[0], counts):
        for cols in pairs_of(width):
            grads = pair_back(
                qkv[span, cols],
                qkv[span, width + cols.start : width + cols.stop],
                qkv[span, 2 * width + cols.start : 2 * width + cols.stop],
                grad_mixed[span, cols],
                bias,
            )
            for which, piece in enumerate(grads):
                start = half + which * width + cols.start
                keep[span, start : start + PAIR] = piece
                send[span, start : start + PAIR] = piece.astype(F32)
    send.flush(half, half + 3 * width)
    keep.flush(half, half + 3 * width)
    total = mm_nt(keep[:, half : half + width], stacked[0])
    total += mm_nt(keep[:, half + width : half + 2 * width], stacked[1])
    total += mm_nt(keep[:, half + 2 * width : half + 3 * width], stacked[2])
    part[...] = total
    part.flush()
    put_cut(send, keep, 0, normed[...], order)
    at = put_cut(send, keep, half + 3 * width, low, order)
    put_both(send, keep, at, mixed[...])


def enc_mlp_back_kernel(
    own, other, state, gain, outer, gate, up, inner, order, order_outer, normed, hidden,
    part, grad_ref, gain_ref, send, keep,
):
    full, gain_ref[...] = norm_back(own[...] + other[...], state[...], gain[2:3, :])
    grad_ref[...] = full
    flush(gain_ref, grad_ref)
    low = full.astype(BF)
    width, half = outer.shape[0], order.shape[0] // 2
    step = 256
    for col in range(0, width, step):
        cols = slice(col, col + step)
        value, rise = gelu_parts(gate[:, cols])
        grad_hidden = mm_nt(low, outer[cols, :])
        put_both(send, keep, half + col, (grad_hidden * up[:, cols] * rise).astype(BF))
        put_both(send, keep, half + width + col, (grad_hidden * value).astype(BF))
    part[...] = mm_nt(keep[:, half : half + width], inner[0]) + mm_nt(
        keep[:, half + width : half + 2 * width], inner[1]
    )
    part.flush()
    put_cut(send, keep, 0, normed[...], order)
    at = put_cut(send, keep, half + 2 * width, low, order_outer)
    put_both(send, keep, at, hidden[...])


def last_kernel(
    enc_own, enc_other, enc_state, enc_gain, enc_grad, dec_own, dec_other, dec_state, dec_gain, dec_grad,
    enc_ref, enc_gain_ref, dec_ref, dec_gain_ref,
):
    grad_in, enc_gain_ref[...] = norm_back(
        enc_own[...] + enc_other[...], enc_state[...].astype(F32), enc_gain[0:1, :]
    )
    enc_ref[...] = (enc_grad[...] + grad_in).astype(BF)
    flush(enc_ref, enc_gain_ref)
    grad_in, dec_gain_ref[...] = norm_back(
        dec_own[...] + dec_other[...], dec_state[...].astype(F32), dec_gain[0:1, :]
    )
    dec_ref[...] = (dec_grad[...] + grad_in).astype(BF)


def weight_kernel(segments, keep, recv, *outs):
    last_of = {(group, target): at for at, (_, _, _, _, group, target) in enumerate(segments)}
    started = set()
    for number, (cut, cut_width, first, columns, group, target) in enumerate(segments):
        send_out, keep_out = outs[2 * group], outs[2 * group + 1]
        left = jnp.concatenate([keep[:, cut : cut + cut_width], recv[:, cut : cut + cut_width].astype(BF)], 0)
        half = cut_width // 2
        step = 512 if columns % 512 == 0 else 384
        for at in range(0, columns, step):
            cols = slice(first + at, first + at + step)
            right = jnp.concatenate([keep[:, cols], recv[:, cols].astype(BF)], 0)
            total = mm_tn(left, right)
            into = slice(target + at, target + at + step)
            if (group, target) in started:
                total += jnp.concatenate([send_out[:, into], keep_out[:, into]], 0)
            send_out[:, into] = total[:half]
            keep_out[:, into] = total[half:]
            if last_of[group, target] == number:
                send_out.flush(into.start, into.stop)
                keep_out.flush(into.start, into.stop)
        started.add((group, target))


def halve_kernel(kept, recv, send_out, keep_out):
    rows = send_out.shape[0]
    send_out[...] = kept[:rows] + recv[:rows]
    send_out.flush()
    keep_out[...] = kept[rows:] + recv[rows:]


SMEM = pl.BlockSpec(memory_space=pltpu.SMEM)
VMEM = pl.BlockSpec(memory_space=pltpu.VMEM)
ANY = pl.BlockSpec(memory_space=pl.ANY)


COST = {
    "enc_attn_fwd": 2.3, "dec_self_fwd": 2.5, "enc_mlp_fwd": 1.7, "cross_fwd": 4.2, "dec_mlp": 2.7,
    "dec_mlp_weights": 0.8, "cross_back": 4.6, "enc_mlp_back": 3.0, "cross_weights": 0.8, "enc_attn_back": 6.8,
    "query_part": 0.3, "enc_mlp_weights": 2.4, "dec_self_back": 4.8, "dec_self_weights": 0.6,
    "enc_attn_weights": 2.8, "dec_out_part": 0.4, "input_grads": 3.0, "halve": 1.0,
}
COST_SCALE = 1.0
VMEM_LIMIT = 8


class Stored:
    def __init__(self, ref):
        self.ref = ref
        self.shape, self.dtype = ref.shape, ref.dtype

    def __getitem__(self, at):
        return self.ref[at]

    def __setitem__(self, at, value):
        self.ref[at] = value

    def flush(self, first=0, last=None):
        pass


def flush(*refs):
    for ref in refs:
        ref.flush()


class Line:
    def __init__(self):
        self.last = None

    def call(self, kernel, outs, args, name, scratch=()):
        shapes = [jax.ShapeDtypeStruct(*out) for out in outs]
        count, made = len(args), len(outs)
        in_specs = [VMEM if a.ndim > 1 else SMEM for a in args]
        if self.last is not None:
            args = list(args) + [self.last]
            in_specs.append(ANY)
        total = len(args)

        def run(*refs):
            stored = [Stored(ref) for ref in refs[total : total + made]]
            kernel(*refs[:count], *stored, *refs[total + made :])

        cost = COST[name] * COST_SCALE
        results = pl.pallas_call(
            run,
            out_shape=shapes,
            in_specs=in_specs,
            out_specs=[VMEM] * made,
            scratch_shapes=list(scratch),
            compiler_params=pltpu.CompilerParams(vmem_limit_bytes=VMEM_LIMIT * MIB),
            cost_estimate=pl.CostEstimate(
                flops=int(cost * 1.15e9), bytes_accessed=int(cost * 3.69e6), transcendentals=0
            ),
            name=name,
        )(*args)
        self.last = min(results, key=lambda r: r.size)
        return results


def pair_other(part):
    return lax.ppermute(part, "mp", [(0, 1), (1, 0)])


def swap(value, bit):
    shards = lax.axis_size("dp")
    return lax.ppermute(value, "dp", [(i, i ^ (1 << bit)) for i in range(shards)])


def feature_order(features, bits_order):
    shards = lax.axis_size("dp")
    me = lax.axis_index("dp")
    block = features // shards
    column = jnp.arange(features, dtype=jnp.int32)
    place = column // block
    owner = jnp.zeros_like(column)
    count = len(bits_order)
    for at, bit in enumerate(bits_order):
        own = (place >> (count - 1 - at)) & 1
        owner = owner | ((((me >> bit) & 1) ^ (1 - own)) << bit)
    source = owner * block + column % block
    return (jnp.arange(features, dtype=jnp.int32)[:, None] == source[None, :]).astype(BF)


class Halving:
    def __init__(self, sent, kept, bits_order):
        self.bits = list(bits_order[1:])
        self.kept = kept
        self.flying = swap(sent, self.bits[0])
        self.steps = 1

    def step(self, line):
        rows, columns = self.kept.shape[0] // 2, self.kept.shape[1]
        shape = ((rows, columns), F32)
        sent, self.kept = line.call(halve_kernel, [shape, shape], [self.kept, self.flying], "halve")
        self.flying = swap(sent, self.bits[self.steps])
        self.steps += 1

    def finish(self):
        total = self.kept + self.flying
        for bit in self.bits[self.steps :]:
            rows = total.shape[0] // 2
            total = total[rows:] + swap(total[:rows], bit)
        return total


def body(
    enc_in, dec_in, cotangent, patch_counts, table_lengths, enc_qkv, enc_attn_out, enc_mlp_in, enc_mlp_out, enc_gains,
    dec_self_qkv, dec_self_out, dec_cross_qkv, dec_cross_out, dec_mlp_in, dec_mlp_out, dec_gains,
):
    plots, enc_len, features = enc_in.shape
    dec_len = dec_in.shape[1]
    enc_rows, dec_rows = plots * enc_len, plots * dec_len
    heads = enc_attn_out.shape[0]
    units = enc_mlp_out.shape[0]
    half = features // 2
    bits = lax.axis_size("dp").bit_length() - 1
    plain = tuple(range(bits))
    turned = (0, 2, 1) + tuple(range(3, bits))
    order = feature_order(features, plain)
    order_turned = feature_order(features, turned)
    x0 = enc_in.reshape(enc_rows, features)
    y0 = dec_in.reshape(dec_rows, features)
    top = cotangent.reshape(dec_rows, features)
    enc_wide, dec_wide = ((enc_rows, features), F32), ((dec_rows, features), F32)
    enc_low, dec_low = ((enc_rows, features), BF), ((dec_rows, features), BF)
    gain_row = ((1, features), F32)
    quarter = half // 2
    line = Line()

    def group(columns):
        return [((quarter, columns), F32)] * 2

    mlp_groups = group(2 * units) + group(units)

    mlp_segments = (
        (0, half, half, 2 * units, 0, 0),
        (half + 2 * units, half, 2 * half + 2 * units, units, 1, 0),
    )
    attn_segments = (
        (0, half, half, 3 * heads, 0, 0),
        (half + 3 * heads, half, 2 * half + 3 * heads, heads, 0, 3 * heads),
    )
    base, fold_width = 2 * half + 2 * heads, half + 2 * heads
    folds = enc_rows // dec_rows
    cross_segments = (
        (0, half, half, heads, 0, 0),
        (half + heads, half, 2 * half + heads, heads, 0, heads),
    ) + tuple(
        (base + f * fold_width, half, base + f * fold_width + half, 2 * heads, 0, 2 * heads) for f in range(folds)
    )
    attn_group = group(4 * heads)
    mlp_wide = 2 * half + 3 * units
    attn_wide = 2 * half + 4 * heads
    cross_wide = base + folds * fold_width
    order_m, order_mo, order_f, order_fo, order_c, order_s, order_a = (
        order, order_turned, order, order, order, order_turned, order
    )
    bits_m, bits_mo, bits_f, bits_fo, bits_c, bits_s, bits_a = plain, turned, plain, plain, plain, turned, plain

    part_e1, u_e0, qkv_e, mixed_e = line.call(
        functools.partial(self_fwd_kernel, False, enc_len),
        [enc_wide, enc_low, ((enc_rows, 3 * heads), BF), ((enc_rows, heads), BF)],
        [patch_counts, x0, enc_gains, enc_qkv, enc_attn_out], "enc_attn_fwd",
    )
    other_e1 = pair_other(part_e1)
    part_d1, u_d0, qkv_d, mixed_d = line.call(
        functools.partial(self_fwd_kernel, True, dec_len),
        [dec_wide, dec_low, ((dec_rows, 3 * heads), BF), ((dec_rows, heads), BF)],
        [table_lengths, y0, dec_gains, dec_self_qkv, dec_self_out], "dec_self_fwd",
    )
    other_d1 = pair_other(part_d1)
    part_e2, x1, u_e1, gate, up, hidden = line.call(
        enc_mlp_fwd_kernel,
        [enc_wide, enc_wide, enc_low, ((enc_rows, units), F32), ((enc_rows, units), F32),
         ((enc_rows, units), BF)],
        [x0, part_e1, other_e1, enc_gains, enc_mlp_in, enc_mlp_out], "enc_mlp_fwd",
    )
    other_e2 = pair_other(part_e2)
    part_d2, x2, memory, y1, u_d1, query, kv, mixed_c = line.call(
        functools.partial(cross_fwd_kernel, enc_len),
        [dec_wide, enc_wide, enc_low, dec_wide, dec_low, ((dec_rows, heads), BF),
         ((enc_rows, 2 * heads), BF), ((dec_rows, heads), BF)],
        [patch_counts, x1, part_e2, other_e2, enc_gains, y0, part_d1, other_d1, dec_gains, dec_cross_qkv, dec_cross_out],
        "cross_fwd",
    )
    other_d2 = pair_other(part_d2)
    part_g3, y2, send_m, keep_m = line.call(
        dec_mlp_kernel,
        [dec_wide, dec_wide, ((dec_rows, mlp_wide), F32), ((dec_rows, mlp_wide), BF)],
        [y1, part_d2, other_d2, dec_gains, top, dec_mlp_in, dec_mlp_out, order_m, order_mo], "dec_mlp",
    )
    other_g3 = pair_other(part_g3)
    recv_m = swap(send_m, 0)
    products = line.call(
        functools.partial(weight_kernel, mlp_segments), mlp_groups, [keep_m, recv_m], "dec_mlp_weights"
    )
    sum_mo = Halving(products[2], products[3], bits_mo)
    sum_m = Halving(products[0], products[1], bits_m)
    part_m, g2, gain_d2, send_c, keep_c = line.call(
        functools.partial(cross_back_kernel, enc_len),
        [enc_wide, dec_wide, gain_row, ((dec_rows, cross_wide), F32), ((dec_rows, cross_wide), BF)],
        [patch_counts, part_g3, other_g3, y2, dec_gains, top, dec_cross_out, query, kv, dec_cross_qkv, order_c, u_d1,
         memory, mixed_c],
        "cross_back", scratch=[pltpu.VMEM((enc_rows, 2 * heads), BF)],
    )
    other_m = pair_other(part_m)
    recv_c = swap(send_c, 0)
    sum_mo.step(line)
    sum_m.step(line)
    part_g1, back2, gain_e2, send_f, keep_f = line.call(
        enc_mlp_back_kernel,
        [enc_wide, enc_wide, gain_row, ((enc_rows, mlp_wide), F32), ((enc_rows, mlp_wide), BF)],
        [part_m, other_m, x2, enc_gains, enc_mlp_out, gate, up, enc_mlp_in, order_f, order_fo, u_e1, hidden],
        "enc_mlp_back",
    )
    other_g1 = pair_other(part_g1)
    recv_f = swap(send_f, 0)
    products = line.call(
        functools.partial(weight_kernel, cross_segments), attn_group, [keep_c, recv_c], "cross_weights"
    )
    sum_c = Halving(products[0], products[1], bits_c)
    sum_mo.step(line)
    part_ge, back1, gain_e1, send_a, keep_a = line.call(
        functools.partial(self_back_kernel, False, enc_len),
        [enc_wide, enc_wide, gain_row, ((enc_rows, attn_wide), F32), ((enc_rows, attn_wide), BF)],
        [patch_counts, part_g1, other_g1, x1, enc_gains, back2, enc_attn_out, qkv_e, enc_qkv, order_a, u_e0, mixed_e],
        "enc_attn_back",
    )
    recv_a = swap(send_a, 0)
    (part_q,) = line.call(query_part_kernel, [dec_wide], [keep_c, dec_cross_qkv], "query_part")
    other_q = pair_other(part_q)
    other_ge = pair_other(part_ge)
    products = line.call(
        functools.partial(weight_kernel, mlp_segments), mlp_groups, [keep_f, recv_f], "enc_mlp_weights"
    )
    sum_fo = Halving(products[2], products[3], bits_fo)
    sum_f = Halving(products[0], products[1], bits_f)
    sum_m.step(line)
    sum_c.step(line)
    part_g0, g1, gain_d1, send_s, keep_s = line.call(
        functools.partial(self_back_kernel, True, dec_len),
        [dec_wide, dec_wide, gain_row, ((dec_rows, attn_wide), F32), ((dec_rows, attn_wide), BF)],
        [table_lengths, part_q, other_q, y1, dec_gains, g2, dec_self_out, qkv_d, dec_self_qkv, order_s, u_d0, mixed_d],
        "dec_self_back",
    )
    other_g0 = pair_other(part_g0)
    recv_s = swap(send_s, 0)
    products = line.call(
        functools.partial(weight_kernel, attn_segments), attn_group, [keep_s, recv_s], "dec_self_weights"
    )
    sum_s = Halving(products[0], products[1], bits_s)
    sum_c.step(line)
    sum_fo.step(line)
    products = line.call(
        functools.partial(weight_kernel, attn_segments), attn_group, [keep_a, recv_a], "enc_attn_weights"
    )
    sum_a = Halving(products[0], products[1], bits_a)
    (part_out,) = line.call(out_part_kernel, [dec_wide], [keep_m, dec_mlp_out], "dec_out_part")
    other_out = pair_other(part_out)
    enc_out, gain_e0, dec_out_grad, gain_d0 = line.call(
        last_kernel,
        [enc_low, gain_row, dec_low, gain_row],
        [part_ge, other_ge, x0, enc_gains, back1, part_g0, other_g0, y0, dec_gains, g1], "input_grads",
    )
    dec_out = (y2 + part_out + other_out).astype(BF)
    sum_f.step(line)
    sum_s.step(line)
    sum_fo.step(line)
    sum_a.step(line)
    sum_f.step(line)
    sum_s.step(line)
    sum_a.step(line)
    total_m, total_mo, total_c, total_s, total_f, total_fo, total_a = [
        group.finish() for group in (sum_m, sum_mo, sum_c, sum_s, sum_f, sum_fo, sum_a)
    ]

    gains = jnp.concatenate([gain_e0, gain_e1, gain_e2, gain_d0, gain_d1, gain_d2], 0)
    gains = gains.reshape((gains.shape[0],) + (2,) * bits + (-1,))
    me = lax.axis_index("dp")
    for bit in range(bits):
        axis = bits - bit
        mine = (me >> bit) & 1
        sent = lax.dynamic_index_in_dim(gains, 1 - mine, axis, keepdims=False)
        gains = lax.dynamic_index_in_dim(gains, mine, axis, keepdims=False) + swap(sent, bit)

    def stacked_of(total, count):
        return jnp.moveaxis(total.reshape(total.shape[0], count, -1), 1, 0)

    def attn_grads(total):
        return [stacked_of(total[:, : 3 * heads], 3), total[:, 3 * heads :].T]

    cross_in = jnp.concatenate([total_c[:, :heads], total_c[:, 2 * heads :]], 1)
    cross = [stacked_of(cross_in, 3), total_c[:, heads : 2 * heads].T]
    grads = (
        attn_grads(total_a) + [stacked_of(total_f, 2), total_fo.T] + [gains[:3]]
        + attn_grads(total_s) + cross + [stacked_of(total_m, 2), total_mo.T] + [gains[3:]]
    )
    return (
        dec_out.reshape(cotangent.shape),
        enc_out.reshape(enc_in.shape),
        dec_out_grad.reshape(dec_in.shape),
    ) + tuple(grads)


def solution(mesh):
    rows = P("dp", None, None)
    inner, outer = P(None, None, "mp"), P("mp", None)
    enc = (inner, outer, inner, outer, P())
    dec = (inner, outer, inner, outer, inner, outer, P())
    inner_grad, outer_grad, gain_grad = P(None, "dp", "mp"), P("mp", "dp"), P(None, "dp")
    return jax.shard_map(
        body,
        mesh=mesh,
        in_specs=(rows, rows, rows, P("dp"), P("dp")) + enc + dec,
        out_specs=(rows, rows, rows)
        + (inner_grad, outer_grad) * 2 + (gain_grad,)
        + (inner_grad, outer_grad) * 3 + (gain_grad,),
        check_vma=False,
    )
```

time: 468 us -> 358 us (0.76)
  waiting for transfers between devices: 314 us -> 212 us
  starting transfers between devices: 30.4 us -> 42.4 us
  local copies, waits for them, and re-layouts: 52.5 us -> 41 us
  other arithmetic: 13.3 us -> 6.05 us
    ppermute x24 -> x30, waiting for transfers between devices: 198 us -> 145 us  [swap(): return lax.ppermute(value, 'dp', [(i, i ^ 1 << bit) for i in range(shards)])]
    ppermute x11, waiting for transfers between devices: 116 us -> 67 us  [pair_other(): return lax.ppermute(part, 'mp', [(0, 1), (1, 0)])]
    add x15 -> x5, other arithmetic: 10.9 us -> 1.32 us  [finish(): total = self.kept + self.flying]
    ppermute x24 -> x30, starting transfers between devices: 17.4 us -> 27 us  [swap(): return lax.ppermute(value, 'dp', [(i, i ^ 1 << bit) for i in range(shards)])]
    slice x15 -> x2, local copies, waits for them, and re-layouts: 4.73 us -> 0.01 us  [body(): cross_in = jnp.concatenate([total_c[:, :heads], total_c[:, 2 * heads:]], 1)]
    unnamed x202 -> x206, local copies, waits for them, and re-layouts: 37.8 us -> 34.7 us
    pallas_call x15 -> x31, Pallas kernels: 55.8 us -> 53.4 us  [call(): pl.pallas_call(run, out_shape=shapes, in_specs=in_specs, out_specs=[VMEM]...]
  transfers between devices with their start and end apart: 35 -> 41, of which waited for: 19 -> 23; matrix products, arithmetic and copies ran while one was open for 6% -> 4% of each run, Pallas kernels for 9% -> 10%
where the time goes in v3:
time: 358 us; the launch traced here: 357 us
  waiting for transfers between devices  212 us (59%)
  Pallas kernels  53.4 us (15%)
  starting transfers between devices  42.4 us (12%)
  local copies, waits for them, and re-layouts  41 us (11%)
  other arithmetic  6.05 us (2%)
    ppermute x30, waiting for transfers between devices, swap(): return lax.ppermute(value, 'dp', [(i, i ^ 1 << bit) for i in range(shards)])  145 us
    ppermute x11, waiting for transfers between devices, pair_other(): return lax.ppermute(part, 'mp', [(0, 1), (1, 0)])  67 us
    pallas_call x31, Pallas kernels, call(): pl.pallas_call(run, out_shape=shapes, in_specs=in_specs, out_specs=[VMEM]...  53.4 us
    unnamed x206, local copies, waits for them, and re-layouts  34.7 us
    ppermute x30, starting transfers between devices, swap(): return lax.ppermute(value, 'dp', [(i, i ^ 1 << bit) for i in range(shards)])  27 us
    ppermute x11, starting transfers between devices, pair_other(): return lax.ppermute(part, 'mp', [(0, 1), (1, 0)])  15.4 us
  transfers between devices with their start and end apart: 41, of which 23 were waited for; matrix products, arithmetic and copies ran while one was open for 4% of the time, Pallas kernels for 10%

profile of v3, /device:TPU:0, one launch (start us, length us, event | category | flops | bytes accessed | tf_op | source)
XLA Modules:
  0.0 356.6 jit_solution(9738659744405975947)
XLA Ops:
  9.4 3.0 collective-permute-start
  12.5 2.5 dec_self_fwd.1
  15.0 14.9 %collective-permute-done.refs_2_ = f32[256,768]{1,0:T(8,128)S(1)} collective-permute-done((f32[256,768]{1,0:T(8,128)S(1)}, f32[256,768]{1,0:T(8,128)S(1)}, u32[]{:S(2)}, u32[]{:S(2)}) %collective-permute-start) | collective-permute-done | bytes 786464 | tf_op jit(solution)/shard_map/ppermute | solution.py:465
  30.0 2.7 enc_mlp_fwd.1
  39.1 25.3 %collective-permute-done.2.refs_7_ = f32[128,768]{1,0:T(8,128)S(1)} collective-permute-done((f32[128,768]{1,0:T(8,128)}, f32[128,768]{1,0:T(8,128)S(1)}, u32[]{:S(2)}, u32[]{:S(2)}) %collective-permute-start.2) | collective-permute-done | bytes 393248 | tf_op jit(solution)/shard_map/ppermute | solution.py:465
  69.8 4.4 %cross_fwd.1 = (f32[128,768]{1,0:T(8,128)S(1)}, f32[256,768]{1,0:T(8,128)S(1)}, bf16[256,768]{1,0:T(8,128)(2,1)S(1)}, f32[128,768]{1,0:T(8,128)S(1)}, bf16[128,7...) custom-call(s32[2]{0:T(128)S(1)} %copy-done.55, ...), custom_call_target="tpu_custom_call" | custom-call | flops 4830000128 | bytes 15498000 | tf_op jit(solution)/shard_map/cross_fwd/pallas_call | solution.py:448
  76.6 7.1 %collective-permute-done.3.refs_2_ = f32[128,768]{1,0:T(8,128)S(1)} collective-permute-done((f32[128,768]{1,0:T(8,128)S(1)}, f32[128,768]{1,0:T(8,128)S(1)}, u32[]{:S(2)}, u32[]{:S(2)}) %collective-permute-start.3) | collective-permute-done | bytes 393248 | tf_op jit(solution)/shard_map/ppermute | solution.py:465
  86.2 4.0 %collective-permute-done.5.refs_1_ = f32[128,3840]{1,0:T(8,128)S(1)} collective-permute-done((f32[128,3840]{1,0:T(8,128)S(1)}, f32[128,3840]{1,0:T(8,128)S(1)}, u32[]{:S(2)}, u32[]{:S(2)}) %collective-permute-start.5) | collective-permute-done | bytes 1966112 | tf_op jit(solution)/shard_map/ppermute | solution.py:470
  95.2 7.8 %collective-permute-done.4.refs_2_ = f32[128,768]{1,0:T(8,128)S(1)} collective-permute-done((f32[128,768]{1,0:T(8,128)S(1)}, f32[128,768]{1,0:T(8,128)S(1)}, u32[]{:S(2)}, u32[]{:S(2)}) %collective-permute-start.4) | collective-permute-done | bytes 393248 | tf_op jit(solution)/shard_map/ppermute | solution.py:465
  103.0 4.7 %cross_back.1 = (f32[256,768]{1,0:T(8,128)S(1)}, f32[128,768]{1,0:T(8,128)S(1)}, f32[1,768]{1,0:T(1,128)S(1)}, f32[128,3840]{1,0:T(8,128)S(1)}, bf16[128,3840]{1,0:T(8,128)(2,1)S(1)}) custom-call(s32[2]{0:T(128)S(1)} %copy-done.56, f32[128,768]{1,0:T(8,128)S(1)} %get-tuple-element.118.refs_2_.refs_1_, f32[128,768]{1,0:T(8,128)S(1)} %collective-permute-done.4.refs_2_, ...), custom_call_target="tpu_custom_call" | custom-call | flops 5289999872 | bytes 16974000 | tf_op jit(solution)/shard_map/cross_back/pallas_call | solution.py:448
  109.4 3.3 collective-permute-done.8.refs_1_
  112.8 14.7 %collective-permute-done.7.refs_1_ = f32[192,2048]{1,0:T(8,128)S(1)} collective-permute-done((f32[192,2048]{1,0:T(8,128)S(1)}, f32[192,2048]{1,0:T(8,128)S(1)}, u32[]{:S(2)}, u32[]{:S(2)}) %collective-permute-start.7) | collective-permute-done | bytes 1572896 | tf_op jit(solution)/shard_map/ppermute | solution.py:470
  129.7 2.9 enc_mlp_back.1
  137.4 4.9 %collective-permute-done.11.refs_1_ = f32[128,3840]{1,0:T(8,128)S(1)} collective-permute-done((f32[128,3840]{1,0:T(8,128)S(1)}, f32[128,3840]{1,0:T(8,128)S(1)}, u32[]{:S(2)}, u32[]{:S(2)}) %collective-permute-start.11) | collective-permute-done | bytes 1966112 | tf_op jit(solution)/shard_map/ppermute | solution.py:470
  145.2 7.5 %collective-permute-done.9.refs_2_ = f32[256,768]{1,0:T(8,128)S(1)} collective-permute-done((f32[256,768]{1,0:T(8,128)S(1)}, f32[256,768]{1,0:T(8,128)S(1)}, u32[]{:S(2)}, u32[]{:S(2)}) %collective-permute-start.9) | collective-permute-done | bytes 786464 | tf_op jit(solution)/shard_map/ppermute | solution.py:465
  152.8 6.9 %enc_attn_back.1 = (f32[256,768]{1,0:T(8,128)}, f32[256,768]{1,0:T(8,128)S(1)}, f32[1,768]{1,0:T(1,128)S(1)}, f32[256,2304]{1,0:T(8,128)}, bf16[256,2304]{1,0:T(8,128)(2,1)S(1)}) custom-call(s32[2]{0:T(128)S(1)} %copy-done.56, f32[256,768]{1,0:T(8,128)S(1)} %get-tuple-element.137.refs_1_, f32[256,768]{1,0:T(8,128)S(1)} %collective-permute-done.9.refs_2_, ...), custom_call_target="tpu_custom_call" | custom-call | flops 7820000256 | bytes 25092000 | tf_op jit(solution)/shard_map/enc_attn_back/pallas_call | solution.py:448
  165.8 5.4 %collective-permute-done.15.refs_1_ = f32[192,1536]{1,0:T(8,128)S(1)} collective-permute-done((f32[192,1536]{1,0:T(8,128)S(1)}, f32[192,1536]{1,0:T(8,128)S(1)}, u32[]{:S(2)}, u32[]{:S(2)}) %collective-permute-start.15) | collective-permute-done | bytes 1179680 | tf_op jit(solution)/shard_map/ppermute | solution.py:470
  173.3 4.3 %dec_self_back.1 = (f32[128,768]{1,0:T(8,128)}, f32[128,768]{1,0:T(8,128)S(1)}, f32[1,768]{1,0:T(1,128)S(1)}, f32[128,2304]{1,0:T(8,128)S(1)}, bf16[128,2304]{1,0:T(8,128)(2,1)S(1)}) custom-call(s32[2]{0:T(128)S(1)} %copy-done.58, f32[128,768]{1,0:T(8,128)S(1)} %query_part.1.refs_2_.refs_1_, f32[128,768]{1,0:T(8,128)S(1)} %collective-permute-done.18.refs_2_, ...), custom_call_target="tpu_custom_call" | custom-call | flops 5520000000 | bytes 17712000 | tf_op jit(solution)/shard_map/dec_self_back/pallas_call | solution.py:448
  186.8 9.1 %collective-permute-done.17.refs_1_ = f32[96,1536]{1,0:T(8,128)S(1)} collective-permute-done((f32[96,1536]{1,0:T(8,128)}, f32[96,1536]{1,0:T(8,128)S(1)}, u32[]{:S(2)}, u32[]{:S(2)}) %collective-permute-start.17) | collective-permute-done | bytes 589856 | tf_op jit(solution)/shard_map/ppermute | solution.py:470
  201.6 2.8 enc_attn_weights.1
  205.5 4.4 %collective-permute-done.22.refs_6_ = f32[128,768]{1,0:T(8,128)S(1)} collective-permute-done((f32[128,768]{1,0:T(8,128)}, f32[128,768]{1,0:T(8,128)S(1)}, u32[]{:S(2)}, u32[]{:S(2)}) %collective-permute-start.22) | collective-permute-done | bytes 393248 | tf_op jit(solution)/shard_map/ppermute | solution.py:465
  209.9 2.9 input_grads.1
  215.4 2.6 collective-permute-start.40
  218.8 31.7 %collective-permute-done.34 = f32[6,2,2,48]{3,2,1,0:T(2,128)S(1)} collective-permute-done((f32[6,2,2,48]{3,2,1,0:T(2,128)S(1)}, f32[6,2,2,48]{3,2,1,0:T(2,128)S(1)}, u32[]{:S(2)}, u32[]{:S(2)}) %collective-permute-start.34) | collective-permute-done | bytes 4640 | tf_op jit(solution)/shard_map/ppermute | solution.py:470
  251.0 7.4 %collective-permute-done.35 = f32[6,2,48]{2,1,0:T(2,128)S(1)} collective-permute-done((f32[6,2,48]{2,1,0:T(2,128)S(1)}, f32[6,2,48]{2,1,0:T(2,128)S(1)}, u32[]{:S(2)}, u32[]{:S(2)}) %collective-permute-start.35) | collective-permute-done | bytes 2336 | tf_op jit(solution)/shard_map/ppermute | solution.py:470
  262.3 2.9 collective-permute-start.38
  266.2 10.6 %collective-permute-done.38 = f32[48,1536]{1,0:T(8,128)S(1)} collective-permute-done((f32[48,1536]{1,0:T(8,128)S(1)}, f32[48,1536]{1,0:T(8,128)S(1)}, u32[]{:S(2)}, u32[]{:S(2)}) %collective-permute-start.38) | collective-permute-done | bytes 294944 | tf_op jit(solution)/shard_map/ppermute | solution.py:470
  279.1 2.5 halve.21
  298.4 16.4 %collective-permute-done.29.refs_1_ = f32[96,2048]{1,0:T(8,128)S(1)} collective-permute-done((f32[96,2048]{1,0:T(8,128)}, f32[96,2048]{1,0:T(8,128)S(1)}, u32[]{:S(2)}, u32[]{:S(2)}) %collective-permute-start.29) | collective-permute-done | bytes 786464 | tf_op jit(solution)/shard_map/ppermute | solution.py:470
  318.0 7.0 %collective-permute-done.27.refs_1_ = f32[96,1536]{1,0:T(8,128)S(1)} collective-permute-done((f32[96,1536]{1,0:T(8,128)S(1)}, f32[96,1536]{1,0:T(8,128)S(1)}, u32[]{:S(2)}, u32[]{:S(2)}) %collective-permute-start.27) | collective-permute-done | bytes 589856 | tf_op jit(solution)/shard_map/ppermute | solution.py:470
  325.9 22.1 %collective-permute-done.31 = f32[48,2048]{1,0:T(8,128)S(1)} collective-permute-done((f32[48,2048]{1,0:T(8,128)S(1)}, f32[48,2048]{1,0:T(8,128)S(1)}, u32[]{:S(2)}, u32[]{:S(2)}) %collective-permute-start.31) | collective-permute-done | bytes 393248 | tf_op jit(solution)/shard_map/ppermute | solution.py:470
  351.8 2.5 collective-permute-done.30
  (323 shorter events, 103.8 us)
Async XLA Ops:
  9.4 20.5 %collective-permute-start = (f32[256,768]{1,0:T(8,128)S(1)}, f32[256,768]{1,0:T(8,128)S(1)}, u32[]{:S(2)}, u32[]{:S(2)}) collective-permute-start(f32[256,768]{1,0:T(8,128)S(1)} %get-tuple-element.107.refs_1_), channel_id=1, source_target_pairs={{0,1},{1,0},{2,3},{3,2},{4,5},{5,4},{6,7},{7,6},{8,9},{9,8},{10,11... | collective-permute-start | bytes 2359304 | tf_op jit(solution)/shard_map/ppermute | solution.py:465
  37.1 27.4 %collective-permute-start.1 = (f32[256,768]{1,0:T(8,128)}, f32[256,768]{1,0:T(8,128)}, u32[]{:S(2)}, u32[]{:S(2)}) collective-permute-start(f32[256,768]{1,0:T(8,128)} %get-tuple-element.111.refs_2_.refs_11_), channel_id=1, source_target_pairs={{0,1},{1,0},{2,3},{3,2},{4,5},{5,4},{6,7},{7,6},{8,9},{9,8},{10,11... | collective-permute-start | bytes 2359304 | tf_op jit(solution)/shard_map/ppermute | solution.py:465
  38.8 25.6 %collective-permute-start.2 = (f32[128,768]{1,0:T(8,128)}, f32[128,768]{1,0:T(8,128)S(1)}, u32[]{:S(2)}, u32[]{:S(2)}) collective-permute-start(f32[128,768]{1,0:T(8,128)} %get-tuple-element.112.refs_6_), channel_id=1, source_target_pairs={{0,1},{1,0},{2,3},{3,2},{4,5},{5,4},{6,7},{7,6},{8,9},{9,8},{10,11... | collective-permute-start | bytes 1179656 | tf_op jit(solution)/shard_map/ppermute | solution.py:465
  91.0 36.5 %collective-permute-start.7 = (f32[192,2048]{1,0:T(8,128)S(1)}, f32[192,2048]{1,0:T(8,128)S(1)}, u32[]{:S(2)}, u32[]{:S(2)}) collective-permute-start(f32[192,2048]{1,0:T(8,128)S(1)} %get-tuple-element.132), channel_id=1, source_target_pairs={{0,4},{2,6},{4,0},{6,2},{8,12},{10,14},{12,8},{14,10},{16,20},{18,... | collective-permute-start | bytes 4718600 | tf_op jit(solution)/shard_map/ppermute | solution.py:470
  93.7 19.0 %collective-permute-start.8 = (f32[192,1024]{1,0:T(8,128)S(1)}, f32[192,1024]{1,0:T(8,128)S(1)}, u32[]{:S(2)}, u32[]{:S(2)}) collective-permute-start(f32[192,1024]{1,0:T(8,128)S(1)} %get-tuple-element.124.refs_14_), channel_id=1, source_target_pairs={{0,8},{2,10},{4,12},{6,14},{8,0},{10,2},{12,4},{14,6},{16,24},{18,... | collective-permute-start | bytes 2359304 | tf_op jit(solution)/shard_map/ppermute | solution.py:470
  107.8 19.9 %collective-permute-start.6 = (f32[256,768]{1,0:T(8,128)S(1)}, f32[256,768]{1,0:T(8,128)S(1)}, u32[]{:S(2)}, u32[]{:S(2)}) collective-permute-start(f32[256,768]{1,0:T(8,128)S(1)} %get-tuple-element.125.refs_0_), channel_id=1, source_target_pairs={{0,1},{1,0},{2,3},{3,2},{4,5},{5,4},{6,7},{7,6},{8,9},{9,8},{10,11... | collective-permute-start | bytes 2359304 | tf_op jit(solution)/shard_map/ppermute | solution.py:465
  132.6 29.4 %collective-permute-start.13 = (f32[256,3840]{1,0:T(8,128)S(1)}, f32[256,3840]{1,0:T(8,128)S(1)}, u32[]{:S(2)}, u32[]{:S(2)}) collective-permute-start(f32[256,3840]{1,0:T(8,128)S(1)} %get-tuple-element.150), channel_id=1, source_target_pairs={{0,2},{2,0},{4,6},{6,4},{8,10},{10,8},{12,14},{14,12},{16,18},{18,... | collective-permute-start | bytes 11796488 | tf_op jit(solution)/shard_map/ppermute | solution.py:470
  133.2 19.5 %collective-permute-start.9 = (f32[256,768]{1,0:T(8,128)S(1)}, f32[256,768]{1,0:T(8,128)S(1)}, u32[]{:S(2)}, u32[]{:S(2)}) collective-permute-start(f32[256,768]{1,0:T(8,128)S(1)} %get-tuple-element.137.refs_1_), channel_id=1, source_target_pairs={{0,1},{1,0},{2,3},{3,2},{4,5},{5,4},{6,7},{7,6},{8,9},{9,8},{10,11... | collective-permute-start | bytes 2359304 | tf_op jit(solution)/shard_map/ppermute | solution.py:465
  135.8 28.5 %collective-permute-start.16 = (f32[96,2048]{1,0:T(8,128)S(1)}, f32[96,2048]{1,0:T(8,128)S(1)}, u32[]{:S(2)}, u32[]{:S(2)}) collective-permute-start(f32[96,2048]{1,0:T(8,128)S(1)} %get-tuple-element.136.refs_12_), channel_id=1, source_target_pairs={{0,8},{2,10},{4,12},{6,14},{8,0},{10,2},{12,4},{14,6},{16,24},{18,... | collective-permute-start | bytes 2359304 | tf_op jit(solution)/shard_map/ppermute | solution.py:470
  143.1 28.1 %collective-permute-start.15 = (f32[192,1536]{1,0:T(8,128)S(1)}, f32[192,1536]{1,0:T(8,128)S(1)}, u32[]{:S(2)}, u32[]{:S(2)}) collective-permute-start(f32[192,1536]{1,0:T(8,128)S(1)} %get-tuple-element.145.refs_2_), channel_id=1, source_target_pairs={{0,4},{2,6},{4,0},{6,2},{8,12},{10,14},{12,8},{14,10},{16,20},{18,... | collective-permute-start | bytes 3538952 | tf_op jit(solution)/shard_map/ppermute | solution.py:470
  160.9 12.1 %collective-permute-start.18 = (f32[128,768]{1,0:T(8,128)S(1)}, f32[128,768]{1,0:T(8,128)S(1)}, u32[]{:S(2)}, u32[]{:S(2)}) collective-permute-start(f32[128,768]{1,0:T(8,128)S(1)} %query_part.1.refs_2_.refs_1_), channel_id=1, source_target_pairs={{0,1},{1,0},{2,3},{3,2},{4,5},{5,4},{6,7},{7,6},{8,9},{9,8},{10,11... | collective-permute-start | bytes 1179656 | tf_op jit(solution)/shard_map/ppermute | solution.py:465
  162.0 39.6 %collective-permute-start.12 = (f32[256,2304]{1,0:T(8,128)}, f32[256,2304]{1,0:T(8,128)}, u32[]{:S(2)}, u32[]{:S(2)}) collective-permute-start(f32[256,2304]{1,0:T(8,128)} %get-tuple-element.148), channel_id=1, source_target_pairs={{0,2},{2,0},{4,6},{6,4},{8,10},{10,8},{12,14},{14,12},{16,18},{18,... | collective-permute-start | bytes 7077896 | tf_op jit(solution)/shard_map/ppermute | solution.py:470
  179.2 20.3 %collective-permute-start.14 = (f32[192,1024]{1,0:T(8,128)}, f32[192,1024]{1,0:T(8,128)}, u32[]{:S(2)}, u32[]{:S(2)}) collective-permute-start(f32[192,1024]{1,0:T(8,128)} %get-tuple-element.153.refs_2_), channel_id=1, source_target_pairs={{0,4},{2,6},{4,0},{6,2},{8,12},{10,14},{12,8},{14,10},{16,20},{18,... | collective-permute-start | bytes 2359304 | tf_op jit(solution)/shard_map/ppermute | solution.py:470
  180.3 15.7 %collective-permute-start.17 = (f32[96,1536]{1,0:T(8,128)}, f32[96,1536]{1,0:T(8,128)S(1)}, u32[]{:S(2)}, u32[]{:S(2)}) collective-permute-start(f32[96,1536]{1,0:T(8,128)} %get-tuple-element.158.refs_12_), channel_id=1, source_target_pairs={{0,8},{2,10},{4,12},{6,14},{8,0},{10,2},{12,4},{14,6},{16,24},{18,... | collective-permute-start | bytes 1769480 | tf_op jit(solution)/shard_map/ppermute | solution.py:470
  181.9 23.6 %collective-permute-start.21 = (f32[256,768]{1,0:T(8,128)}, f32[256,768]{1,0:T(8,128)}, u32[]{:S(2)}, u32[]{:S(2)}) collective-permute-start(f32[256,768]{1,0:T(8,128)} %get-tuple-element.169.refs_0_), channel_id=1, source_target_pairs={{0,1},{1,0},{2,3},{3,2},{4,5},{5,4},{6,7},{7,6},{8,9},{9,8},{10,11... | collective-permute-start | bytes 2359304 | tf_op jit(solution)/shard_map/ppermute | solution.py:465
  183.4 26.5 %collective-permute-start.22 = (f32[128,768]{1,0:T(8,128)}, f32[128,768]{1,0:T(8,128)S(1)}, u32[]{:S(2)}, u32[]{:S(2)}) collective-permute-start(f32[128,768]{1,0:T(8,128)} %get-tuple-element.171.refs_5_), channel_id=1, source_target_pairs={{0,1},{1,0},{2,3},{3,2},{4,5},{5,4},{6,7},{7,6},{8,9},{9,8},{10,11... | collective-permute-start | bytes 1179656 | tf_op jit(solution)/shard_map/ppermute | solution.py:465
  213.2 65.9 %collective-permute-start.26 = (f32[192,2048]{1,0:T(8,128)}, f32[192,2048]{1,0:T(8,128)}, u32[]{:S(2)}, u32[]{:S(2)}) collective-permute-start(f32[192,2048]{1,0:T(8,128)} %copy-done.26), channel_id=1, source_target_pairs={{0,4},{2,6},{4,0},{6,2},{8,12},{10,14},{12,8},{14,10},{16,20},{18,... | collective-permute-start | bytes 4718600 | tf_op jit(solution)/shard_map/ppermute | solution.py:470
  214.4 36.1 %collective-permute-start.34 = (f32[6,2,2,48]{3,2,1,0:T(2,128)S(1)}, f32[6,2,2,48]{3,2,1,0:T(2,128)S(1)}, u32[]{:S(2)}, u32[]{:S(2)}) collective-permute-start(f32[6,2,2,48]{3,2,1,0:T(2,128)S(1)} %dynamic-slice_bitcast_fusion), channel_id=1, source_target_pairs={{0,4},{2,6},{4,0},{6,2},{8,12},{10,14},{12,8},{14,10},{16,20},{18,... | collective-permute-start | bytes 13832 | tf_op jit(solution)/shard_map/ppermute | solution.py:470
  215.4 44.2 %collective-permute-start.40 = (f32[48,1024]{1,0:T(8,128)}, f32[48,1024]{1,0:T(8,128)S(1)}, u32[]{:S(2)}, u32[]{:S(2)}) collective-permute-start(f32[48,1024]{1,0:T(8,128)} %copy-done.47), channel_id=1, source_target_pairs={{0,16},{2,18},{4,20},{6,22},{8,24},{10,26},{12,28},{14,30},{16,0},... | collective-permute-start | bytes 589832 | tf_op jit(solution)/shard_map/ppermute | solution.py:470
  218.0 42.4 %collective-permute-start.39 = (f32[48,2048]{1,0:T(8,128)S(1)}, f32[48,2048]{1,0:T(8,128)}, u32[]{:S(2)}, u32[]{:S(2)}) collective-permute-start(f32[48,2048]{1,0:T(8,128)S(1)} %copy-done.38), channel_id=1, source_target_pairs={{0,16},{2,18},{4,20},{6,22},{8,24},{10,26},{12,28},{14,30},{16,0},... | collective-permute-start | bytes 1179656 | tf_op jit(solution)/shard_map/ppermute | solution.py:470
  218.3 64.4 %collective-permute-start.25 = (f32[192,1536]{1,0:T(8,128)}, f32[192,1536]{1,0:T(8,128)}, u32[]{:S(2)}, u32[]{:S(2)}) collective-permute-start(f32[192,1536]{1,0:T(8,128)} %copy-done.27), channel_id=1, source_target_pairs={{0,8},{2,10},{4,12},{6,14},{8,0},{10,2},{12,4},{14,6},{16,24},{18,... | collective-permute-start | bytes 3538952 | tf_op jit(solution)/shard_map/ppermute | solution.py:470
  258.5 28.3 %collective-permute-start.23 = (f32[192,1536]{1,0:T(8,128)S(1)}, f32[192,1536]{1,0:T(8,128)S(1)}, u32[]{:S(2)}, u32[]{:S(2)}) collective-permute-start(f32[192,1536]{1,0:T(8,128)S(1)} %get-tuple-element.168.refs_2_), channel_id=1, source_target_pairs={{0,4},{2,6},{4,0},{6,2},{8,12},{10,14},{12,8},{14,10},{16,20},{18,... | collective-permute-start | bytes 3538952 | tf_op jit(solution)/shard_map/ppermute | solution.py:470
  262.3 14.5 %collective-permute-start.38 = (f32[48,1536]{1,0:T(8,128)S(1)}, f32[48,1536]{1,0:T(8,128)S(1)}, u32[]{:S(2)}, u32[]{:S(2)}) collective-permute-start(f32[48,1536]{1,0:T(8,128)S(1)} %copy-done.42), channel_id=1, source_target_pairs={{0,16},{2,18},{4,20},{6,22},{8,24},{10,26},{12,28},{14,30},{16,0},... | collective-permute-start | bytes 884744 | tf_op jit(solution)/shard_map/ppermute | solution.py:470
  265.3 21.5 %collective-permute-start.24 = (f32[96,1024]{1,0:T(8,128)S(1)}, f32[96,1024]{1,0:T(8,128)S(1)}, u32[]{:S(2)}, u32[]{:S(2)}) collective-permute-start(f32[96,1024]{1,0:T(8,128)S(1)} %copy-done.40), channel_id=1, source_target_pairs={{0,8},{2,10},{4,12},{6,14},{8,0},{10,2},{12,4},{14,6},{16,24},{18,... | collective-permute-start | bytes 1179656 | tf_op jit(solution)/shard_map/ppermute | solution.py:470
  276.8 18.3 %collective-permute-start.20 = (f32[128,768]{1,0:T(8,128)S(1)}, f32[128,768]{1,0:T(8,128)}, u32[]{:S(2)}, u32[]{:S(2)}) collective-permute-start(f32[128,768]{1,0:T(8,128)S(1)} %dec_out_part.1.refs_10_), channel_id=1, source_target_pairs={{0,1},{1,0},{2,3},{3,2},{4,5},{5,4},{6,7},{7,6},{8,9},{9,8},{10,11... | collective-permute-start | bytes 1179656 | tf_op jit(solution)/shard_map/ppermute | solution.py:465
  282.5 32.3 %collective-permute-start.29 = (f32[96,2048]{1,0:T(8,128)}, f32[96,2048]{1,0:T(8,128)S(1)}, u32[]{:S(2)}, u32[]{:S(2)}) collective-permute-start(f32[96,2048]{1,0:T(8,128)} %get-tuple-element.181.refs_2_), channel_id=1, source_target_pairs={{0,8},{2,10},{4,12},{6,14},{8,0},{10,2},{12,4},{14,6},{16,24},{18,... | collective-permute-start | bytes 2359304 | tf_op jit(solution)/shard_map/ppermute | solution.py:470
  285.8 29.2 %collective-permute-start.28 = (f32[96,1536]{1,0:T(8,128)}, f32[96,1536]{1,0:T(8,128)S(1)}, u32[]{:S(2)}, u32[]{:S(2)}) collective-permute-start(f32[96,1536]{1,0:T(8,128)} %get-tuple-element.182.refs_2_), channel_id=1, source_target_pairs={{0,4},{2,6},{4,0},{6,2},{8,12},{10,14},{12,8},{14,10},{16,20},{18,... | collective-permute-start | bytes 1769480 | tf_op jit(solution)/shard_map/ppermute | solution.py:470
  289.1 35.9 %collective-permute-start.27 = (f32[96,1536]{1,0:T(8,128)S(1)}, f32[96,1536]{1,0:T(8,128)S(1)}, u32[]{:S(2)}, u32[]{:S(2)}) collective-permute-start(f32[96,1536]{1,0:T(8,128)S(1)} %get-tuple-element.185.refs_2_), channel_id=1, source_target_pairs={{0,8},{2,10},{4,12},{6,14},{8,0},{10,2},{12,4},{14,6},{16,24},{18,... | collective-permute-start | bytes 1769480 | tf_op jit(solution)/shard_map/ppermute | solution.py:470
  296.8 28.3 %collective-permute-start.32 = (f32[48,1024]{1,0:T(8,128)S(1)}, f32[48,1024]{1,0:T(8,128)S(1)}, u32[]{:S(2)}, u32[]{:S(2)}) collective-permute-start(f32[48,1024]{1,0:T(8,128)S(1)} %copy-done.49), channel_id=1, source_target_pairs={{0,16},{2,18},{4,20},{6,22},{8,24},{10,26},{12,28},{14,30},{16,0},... | collective-permute-start | bytes 589832 | tf_op jit(solution)/shard_map/ppermute | solution.py:470
  314.9 33.0 %collective-permute-start.31 = (f32[48,2048]{1,0:T(8,128)S(1)}, f32[48,2048]{1,0:T(8,128)S(1)}, u32[]{:S(2)}, u32[]{:S(2)}) collective-permute-start(f32[48,2048]{1,0:T(8,128)S(1)} %get-tuple-element.188.refs_2_), channel_id=1, source_target_pairs={{0,16},{2,18},{4,20},{6,22},{8,24},{10,26},{12,28},{14,30},{16,0},... | collective-permute-start | bytes 1179656 | tf_op jit(solution)/shard_map/ppermute | solution.py:470
  315.9 35.2 %collective-permute-start.37 = (f32[48,1536]{1,0:T(8,128)S(1)}, f32[48,1536]{1,0:T(8,128)S(1)}, u32[]{:S(2)}, u32[]{:S(2)}) collective-permute-start(f32[48,1536]{1,0:T(8,128)S(1)} %get-tuple-element.189.refs_2_), channel_id=1, source_target_pairs={{0,16},{2,18},{4,20},{6,22},{8,24},{10,26},{12,28},{14,30},{16,0},... | collective-permute-start | bytes 884744 | tf_op jit(solution)/shard_map/ppermute | solution.py:470
  325.1 29.2 %collective-permute-start.30 = (f32[48,1536]{1,0:T(8,128)S(1)}, f32[48,1536]{1,0:T(8,128)S(1)}, u32[]{:S(2)}, u32[]{:S(2)}) collective-permute-start(f32[48,1536]{1,0:T(8,128)S(1)} %get-tuple-element.191), channel_id=1, source_target_pairs={{0,16},{2,18},{4,20},{6,22},{8,24},{10,26},{12,28},{14,30},{16,0},... | collective-permute-start | bytes 884744 | tf_op jit(solution)/shard_map/ppermute | solution.py:470
  (111 other events, 679.6 us)

commit v4 on v3

--- a/solution.py
+++ b/solution.py
@@ -234,6 +234,10 @@
     part.flush()
     put_cut(send, keep, 0, normed, order)
     put_cut(send, keep, half + 2 * width, low, order_outer)
+
+
+def sum_kernel(state, own, other, out):
+    out[...] = (state[...] + own[...] + other[...]).astype(BF)
 
 
 def out_part_kernel(keep, outer, part):
@@ -344,22 +348,38 @@
     part.flush()
     put_cut(send, keep, 0, normed[...], order)
     at = put_cut(send, keep, half + 2 * width, low, order_outer)
-    put_both(send, keep, at, hidden[...])
+    for col in range(0, width, step):
+        at = put_both(send, keep, at, hidden[:, col : col + step])
 
 
 def last_kernel(
-    enc_own, enc_other, enc_state, enc_gain, enc_grad, dec_own, dec_other, dec_state, dec_gain, dec_grad,
-    enc_ref, enc_gain_ref, dec_ref, dec_gain_ref,
+    enc_own, enc_other, enc_state, enc_gain, enc_grad, dec_own, dec_other, dec_state, dec_gain, dec_grad, order,
+    e1, e2, d1, d2, enc_ref, dec_ref, send, keep,
 ):
-    grad_in, enc_gain_ref[...] = norm_back(
-        enc_own[...] + enc_other[...], enc_state[...].astype(F32), enc_gain[0:1, :]
-    )
+    grad_in, e0 = norm_back(enc_own[...] + enc_other[...], enc_state[...].astype(F32), enc_gain[0:1, :])
     enc_ref[...] = (enc_grad[...] + grad_in).astype(BF)
-    flush(enc_ref, enc_gain_ref)
-    grad_in, dec_gain_ref[...] = norm_back(
-        dec_own[...] + dec_other[...], dec_state[...].astype(F32), dec_gain[0:1, :]
-    )
+    grad_in, d0 = norm_back(dec_own[...] + dec_other[...], dec_state[...].astype(F32), dec_gain[0:1, :])
     dec_ref[...] = (dec_grad[...] + grad_in).astype(BF)
+    rest = jnp.concatenate(
+        [e0, e1[...], e2[...], d0, d1[...], d2[...], jnp.zeros((122, e0.shape[1]), F32)], 0
+    )
+    total = None
+    for _ in range(3):
+        low = rest.astype(BF)
+        rest = rest - low.astype(F32)
+        moved = lax.dot_general(order[...], low, (((0,), (1,)), ((), ())), preferred_element_type=F32)
+        total = moved if total is None else total + moved
+    half = total.shape[0] // 2
+    send[...] = total[:half]
+    keep[...] = total[half:]
+
+
+def gains_weight_kernel(segments, keep, recv, gains, other_gains, send_out, keep_out):
+    weight_kernel(segments, keep, recv, send_out, keep_out)
+    total = gains[...] + other_gains[...]
+    half, first = send_out.shape[0], send_out.shape[1] - total.shape[1]
+    send_out[:, first:] = total[:half]
+    keep_out[:, first:] = total[half:]
 
 
 def weight_kernel(segments, keep, recv, *outs):
@@ -397,13 +417,7 @@
 ANY = pl.BlockSpec(memory_space=pl.ANY)
 
 
-COST = {
-    "enc_attn_fwd": 2.3, "dec_self_fwd": 2.5, "enc_mlp_fwd": 1.7, "cross_fwd": 4.2, "dec_mlp": 2.7,
-    "dec_mlp_weights": 0.8, "cross_back": 4.6, "enc_mlp_back": 3.0, "cross_weights": 0.8, "enc_attn_back": 6.8,
-    "query_part": 0.3, "enc_mlp_weights": 2.4, "dec_self_back": 4.8, "dec_self_weights": 0.6,
-    "enc_attn_weights": 2.8, "dec_out_part": 0.4, "input_grads": 3.0, "halve": 1.0,
-}
-COST_SCALE = 1.0
+COST = {"enc_attn_fwd": 2.3, "dec_self_fwd": 2.5, "enc_mlp_fwd": 1.7, "cross_fwd": 4.2, "dec_mlp": 2.7}
 VMEM_LIMIT = 8
 
 
@@ -422,6 +436,41 @@
         pass
 
 
+class Columns:
+    def __init__(self, refs):
+        self.refs = refs
+        self.shape = (refs[0].shape[0], sum(ref.shape[1] for ref in refs))
+        self.dtype = refs[0].dtype
+
+    def part(self, at):
+        rows, cols = at
+        first = cols.start or 0
+        last = self.shape[1] if cols.stop is None else cols.stop
+        for ref in self.refs:
+            if last <= ref.shape[1]:
+                return ref, (rows, slice(first, last))
+            first, last = first - ref.shape[1], last - ref.shape[1]
+        raise ValueError(at)
+
+    def __getitem__(self, at):
+        rows, cols = at
+        first, last = cols.start or 0, self.shape[1] if cols.stop is None else cols.stop
+        pieces, start = [], 0
+        for ref in self.refs:
+            low, high = max(first - start, 0), min(last - start, ref.shape[1])
+            if low < high:
+                pieces.append(ref[rows, low:high])
+            start += ref.shape[1]
+        return pieces[0] if len(pieces) == 1 else jnp.concatenate(pieces, 1)
+
+    def __setitem__(self, at, value):
+        ref, inside = self.part(at)
+        ref[inside] = value
+
+    def flush(self, first=0, last=None):
+        pass
+
+
 def flush(*refs):
     for ref in refs:
         ref.flush()
@@ -431,21 +480,30 @@
     def __init__(self):
         self.last = None
 
-    def call(self, kernel, outs, args, name, scratch=()):
-        shapes = [jax.ShapeDtypeStruct(*out) for out in outs]
-        count, made = len(args), len(outs)
-        in_specs = [VMEM if a.ndim > 1 else SMEM for a in args]
+    def call(self, kernel, outs, args, name, scratch=(), cost=None):
+        flat_args, args_tree = jax.tree.flatten(list(args))
+        widths = [out if isinstance(out, list) else [out] for out in outs]
+        shapes = [jax.ShapeDtypeStruct(*out) for group in widths for out in group]
+        in_specs = [VMEM if a.ndim > 1 else SMEM for a in flat_args]
+        count, made = len(flat_args), len(shapes)
+        operands = list(flat_args)
         if self.last is not None:
-            args = list(args) + [self.last]
+            operands.append(self.last)
             in_specs.append(ANY)
-        total = len(args)
+        total = len(operands)
 
         def run(*refs):
-            stored = [Stored(ref) for ref in refs[total : total + made]]
-            kernel(*refs[:count], *stored, *refs[total + made :])
-
-        cost = COST[name] * COST_SCALE
-        results = pl.pallas_call(
+            ins = jax.tree.unflatten(args_tree, refs[:count])
+            ins = [Columns(i) if isinstance(i, list) else i for i in ins]
+            left = list(refs[total : total + made])
+            results = []
+            for group, out in zip(widths, outs):
+                taken, left = [Stored(ref) for ref in left[: len(group)]], left[len(group) :]
+                results.append(Columns(taken) if isinstance(out, list) else taken[0])
+            kernel(*ins, *results, *refs[total + made :])
+
+        cost = COST.get(name, 0.3) if cost is None else cost
+        flat = pl.pallas_call(
             run,
             out_shape=shapes,
             in_specs=in_specs,
@@ -456,18 +514,40 @@
                 flops=int(cost * 1.15e9), bytes_accessed=int(cost * 3.69e6), transcendentals=0
             ),
             name=name,
-        )(*args)
-        self.last = min(results, key=lambda r: r.size)
+        )(*operands)
+        self.last = min(flat, key=lambda r: r.size)
+        results, left = [], list(flat)
+        for group, out in zip(widths, outs):
+            results.append(left[: len(group)] if isinstance(out, list) else left[0])
+            left = left[len(group) :]
         return results
 
 
-def pair_other(part):
-    return lax.ppermute(part, "mp", [(0, 1), (1, 0)])
-
-
-def swap(value, bit):
+def finish_kernel(pieces, kept, recv, *outs):
+    for out, (first, count) in zip(outs, pieces):
+        width = out.shape[-1]
+        for i in range(count):
+            cols = slice(first + i * width, first + (i + 1) * width)
+            total = kept[:, cols] + recv[:, cols]
+            if count > 1:
+                out[i] = total
+            else:
+                out[...] = total
+
+
+def tick_kernel(source, target):
+    target[...] = source[0:1, 0:128]
+
+
+def pair_other(part, name):
+    with jax.named_scope("pair_" + name):
+        return lax.ppermute(part, "mp", [(0, 1), (1, 0)])
+
+
+def swap(value, bit, name):
     shards = lax.axis_size("dp")
-    return lax.ppermute(value, "dp", [(i, i ^ (1 << bit)) for i in range(shards)])
+    with jax.named_scope("swap_%s_bit%d" % (name, bit)):
+        return lax.ppermute(value, "dp", [(i, i ^ (1 << bit)) for i in range(shards)])
 
 
 def feature_order(features, bits_order):
@@ -486,25 +566,31 @@
 
 
 class Halving:
-    def __init__(self, sent, kept, bits_order):
+    def __init__(self, sent, kept, bits_order, name):
         self.bits = list(bits_order[1:])
         self.kept = kept
-        self.flying = swap(sent, self.bits[0])
+        self.name = name
+        self.flying = swap(sent, self.bits[0], name)
         self.steps = 1
 
     def step(self, line):
         rows, columns = self.kept.shape[0] // 2, self.kept.shape[1]
         shape = ((rows, columns), F32)
         sent, self.kept = line.call(halve_kernel, [shape, shape], [self.kept, self.flying], "halve")
-        self.flying = swap(sent, self.bits[self.steps])
+        self.flying = swap(sent, self.bits[self.steps], self.name)
         self.steps += 1
 
-    def finish(self):
-        total = self.kept + self.flying
+    def finish(self, line, *pieces):
         for bit in self.bits[self.steps :]:
-            rows = total.shape[0] // 2
-            total = total[rows:] + swap(total[:rows], bit)
-        return total
+            rows = self.kept.shape[0] // 2
+            total = self.kept + self.flying
+            self.kept, self.flying = total[rows:], swap(total[:rows], bit, self.name)
+        rows = self.kept.shape[0]
+        outs = [(((count, rows, width) if count > 1 else (rows, width)), F32) for _, count, width in pieces]
+        return line.call(
+            functools.partial(finish_kernel, [(first, count) for first, count, _ in pieces]),
+            outs, [self.kept, self.flying], "finish",
+        )
 
 
 def body(
@@ -531,6 +617,12 @@
     quarter = half // 2
     line = Line()
 
+    def tick(cost=2.0):
+        line.call(tick_kernel, [((1, 128), F32)], [enc_gains], "tick", cost=cost)
+
+    def wide(rows, *columns):
+        return [((rows, c), F32) for c in columns]
+
     def group(columns):
         return [((quarter, columns), F32)] * 2
 
@@ -557,29 +649,31 @@
     attn_wide = 2 * half + 4 * heads
     cross_wide = base + folds * fold_width
     order_m, order_mo, order_f, order_fo, order_c, order_s, order_a = (
-        order, order_turned, order, order, order, order_turned, order
-    )
-    bits_m, bits_mo, bits_f, bits_fo, bits_c, bits_s, bits_a = plain, turned, plain, plain, plain, turned, plain
-
+        order, order_turned, order, order_turned, order_turned, order, order_turned
+    )
+    bits_m, bits_mo, bits_f, bits_fo, bits_c, bits_s, bits_a = plain, turned, plain, turned, turned, plain, turned
+
+    tick(6.0)
     part_e1, u_e0, qkv_e, mixed_e = line.call(
         functools.partial(self_fwd_kernel, False, enc_len),
         [enc_wide, enc_low, ((enc_rows, 3 * heads), BF), ((enc_rows, heads), BF)],
         [patch_counts, x0, enc_gains, enc_qkv, enc_attn_out], "enc_attn_fwd",
     )
-    other_e1 = pair_other(part_e1)
+    other_e1 = pair_other(part_e1, "e1")
     part_d1, u_d0, qkv_d, mixed_d = line.call(
         functools.partial(self_fwd_kernel, True, dec_len),
         [dec_wide, dec_low, ((dec_rows, 3 * heads), BF), ((dec_rows, heads), BF)],
         [table_lengths, y0, dec_gains, dec_self_qkv, dec_self_out], "dec_self_fwd",
     )
-    other_d1 = pair_other(part_d1)
+    other_d1 = pair_other(part_d1, "d1")
     part_e2, x1, u_e1, gate, up, hidden = line.call(
         enc_mlp_fwd_kernel,
         [enc_wide, enc_wide, enc_low, ((enc_rows, units), F32), ((enc_rows, units), F32),
          ((enc_rows, units), BF)],
         [x0, part_e1, other_e1, enc_gains, enc_mlp_in, enc_mlp_out], "enc_mlp_fwd",
     )
-    other_e2 = pair_other(part_e2)
+    other_e2 = pair_other(part_e2, "e2")
+    tick(6.0)
     part_d2, x2, memory, y1, u_d1, query, kv, mixed_c = line.call(
         functools.partial(cross_fwd_kernel, enc_len),
         [dec_wide, enc_wide, enc_low, dec_wide, dec_low, ((dec_rows, heads), BF),
@@ -587,117 +681,117 @@
         [patch_counts, x1, part_e2, other_e2, enc_gains, y0, part_d1, other_d1, dec_gains, dec_cross_qkv, dec_cross_out],
         "cross_fwd",
     )
-    other_d2 = pair_other(part_d2)
+    other_d2 = pair_other(part_d2, "d2")
+    tick(6.0)
     part_g3, y2, send_m, keep_m = line.call(
         dec_mlp_kernel,
         [dec_wide, dec_wide, ((dec_rows, mlp_wide), F32), ((dec_rows, mlp_wide), BF)],
         [y1, part_d2, other_d2, dec_gains, top, dec_mlp_in, dec_mlp_out, order_m, order_mo], "dec_mlp",
     )
-    other_g3 = pair_other(part_g3)
-    recv_m = swap(send_m, 0)
+    other_g3 = pair_other(part_g3, "g3")
+    recv_m = swap(send_m, 0, "m")
+    tick()
     products = line.call(
         functools.partial(weight_kernel, mlp_segments), mlp_groups, [keep_m, recv_m], "dec_mlp_weights"
     )
-    sum_mo = Halving(products[2], products[3], bits_mo)
-    sum_m = Halving(products[0], products[1], bits_m)
+    sum_mo = Halving(products[2], products[3], bits_mo, "mo")
+    sum_m = Halving(products[0], products[1], bits_m, "m")
     part_m, g2, gain_d2, send_c, keep_c = line.call(
         functools.partial(cross_back_kernel, enc_len),
-        [enc_wide, dec_wide, gain_row, ((dec_rows, cross_wide), F32), ((dec_rows, cross_wide), BF)],
+        [enc_wide, dec_wide, gain_row, wide(dec_rows, half + heads, half + heads, *[half, 2 * heads] * folds), ((dec_rows, cross_wide), BF)],
         [patch_counts, part_g3, other_g3, y2, dec_gains, top, dec_cross_out, query, kv, dec_cross_qkv, order_c, u_d1,
          memory, mixed_c],
         "cross_back", scratch=[pltpu.VMEM((enc_rows, 2 * heads), BF)],
     )
-    other_m = pair_other(part_m)
-    recv_c = swap(send_c, 0)
+    other_m = pair_other(part_m, "m")
+    recv_c = [swap(part, 0, "c") for part in send_c]
+    tick()
     sum_mo.step(line)
+    products = line.call(
+        functools.partial(weight_kernel, cross_segments), attn_group, [keep_c, recv_c], "cross_weights"
+    )
+    sum_c = Halving(products[0], products[1], bits_c, "c")
     sum_m.step(line)
     part_g1, back2, gain_e2, send_f, keep_f = line.call(
         enc_mlp_back_kernel,
-        [enc_wide, enc_wide, gain_row, ((enc_rows, mlp_wide), F32), ((enc_rows, mlp_wide), BF)],
+        [enc_wide, enc_wide, gain_row, wide(enc_rows, half + units // 4, *[units // 2] * 3, half + units // 4, *[units // 2] * 2),
+         ((enc_rows, mlp_wide), BF)],
         [part_m, other_m, x2, enc_gains, enc_mlp_out, gate, up, enc_mlp_in, order_f, order_fo, u_e1, hidden],
         "enc_mlp_back",
     )
-    other_g1 = pair_other(part_g1)
-    recv_f = swap(send_f, 0)
+    other_g1 = pair_other(part_g1, "g1")
+    recv_f = [swap(part, 0, "f") for part in send_f]
+    tick()
     products = line.call(
-        functools.partial(weight_kernel, cross_segments), attn_group, [keep_c, recv_c], "cross_weights"
-    )
-    sum_c = Halving(products[0], products[1], bits_c)
+        functools.partial(weight_kernel, mlp_segments), mlp_groups, [keep_f, recv_f], "enc_mlp_weights"
+    )
+    sum_fo = Halving(products[2], products[3], bits_fo, "fo")
+    sum_f = Halving(products[0], products[1], bits_f, "f")
     sum_mo.step(line)
+    sum_c.step(line)
     part_ge, back1, gain_e1, send_a, keep_a = line.call(
         functools.partial(self_back_kernel, False, enc_len),
-        [enc_wide, enc_wide, gain_row, ((enc_rows, attn_wide), F32), ((enc_rows, attn_wide), BF)],
+        [enc_wide, enc_wide, gain_row, wide(enc_rows, half, heads, heads, heads, half, heads), ((enc_rows, attn_wide), BF)],
         [patch_counts, part_g1, other_g1, x1, enc_gains, back2, enc_attn_out, qkv_e, enc_qkv, order_a, u_e0, mixed_e],
         "enc_attn_back",
     )
-    recv_a = swap(send_a, 0)
     (part_q,) = line.call(query_part_kernel, [dec_wide], [keep_c, dec_cross_qkv], "query_part")
-    other_q = pair_other(part_q)
-    other_ge = pair_other(part_ge)
+    other_q = pair_other(part_q, "q")
+    other_ge = pair_other(part_ge, "ge")
+    recv_a = [swap(part, 0, "a") for part in send_a]
+    tick()
+    sum_m.step(line)
     products = line.call(
-        functools.partial(weight_kernel, mlp_segments), mlp_groups, [keep_f, recv_f], "enc_mlp_weights"
-    )
-    sum_fo = Halving(products[2], products[3], bits_fo)
-    sum_f = Halving(products[0], products[1], bits_f)
-    sum_m.step(line)
+        functools.partial(weight_kernel, attn_segments), attn_group, [keep_a, recv_a], "enc_attn_weights"
+    )
+    sum_a = Halving(products[0], products[1], bits_a, "a")
     sum_c.step(line)
     part_g0, g1, gain_d1, send_s, keep_s = line.call(
         functools.partial(self_back_kernel, True, dec_len),
-        [dec_wide, dec_wide, gain_row, ((dec_rows, attn_wide), F32), ((dec_rows, attn_wide), BF)],
+        [dec_wide, dec_wide, gain_row, wide(dec_rows, half + heads, 2 * heads, half + heads),
+         ((dec_rows, attn_wide), BF)],
         [table_lengths, part_q, other_q, y1, dec_gains, g2, dec_self_out, qkv_d, dec_self_qkv, order_s, u_d0, mixed_d],
         "dec_self_back",
     )
-    other_g0 = pair_other(part_g0)
-    recv_s = swap(send_s, 0)
+    other_g0 = pair_other(part_g0, "g0")
+    recv_s = [swap(part, 0, "s") for part in send_s]
+    tick()
+    (grad_mo,) = sum_mo.finish(line, (0, 1, units))
+    sum_fo.step(line)
+    (grad_m,) = sum_m.finish(line, (0, 2, units))
+    enc_out, dec_out_grad, send_g, keep_g = line.call(
+        last_kernel,
+        [enc_low, dec_low, ((half, 128), F32), ((half, 128), F32)],
+        [part_ge, other_ge, x0, enc_gains, back1, part_g0, other_g0, y0, dec_gains, g1, order_s, gain_e1, gain_e2,
+         gain_d1, gain_d2],
+        "input_grads",
+    )
+    recv_g = swap(send_g, 0, "g")
+    sum_f.step(line)
     products = line.call(
-        functools.partial(weight_kernel, attn_segments), attn_group, [keep_s, recv_s], "dec_self_weights"
-    )
-    sum_s = Halving(products[0], products[1], bits_s)
-    sum_c.step(line)
-    sum_fo.step(line)
-    products = line.call(
-        functools.partial(weight_kernel, attn_segments), attn_group, [keep_a, recv_a], "enc_attn_weights"
-    )
-    sum_a = Halving(products[0], products[1], bits_a)
+        functools.partial(gains_weight_kernel, attn_segments), group(4 * heads + 128),
+        [keep_s, recv_s, keep_g, recv_g], "dec_self_weights",
+    )
+    sum_s = Halving(products[0], products[1], bits_s, "s")
+    grad_cq, grad_co, grad_ckv = sum_c.finish(line, (0, 1, heads), (heads, 1, heads), (2 * heads, 2, heads))
     (part_out,) = line.call(out_part_kernel, [dec_wide], [keep_m, dec_mlp_out], "dec_out_part")
-    other_out = pair_other(part_out)
-    enc_out, gain_e0, dec_out_grad, gain_d0 = line.call(
-        last_kernel,
-        [enc_low, gain_row, dec_low, gain_row],
-        [part_ge, other_ge, x0, enc_gains, back1, part_g0, other_g0, y0, dec_gains, g1], "input_grads",
-    )
-    dec_out = (y2 + part_out + other_out).astype(BF)
-    sum_f.step(line)
-    sum_s.step(line)
+    other_out = pair_other(part_out, "out")
     sum_fo.step(line)
     sum_a.step(line)
     sum_f.step(line)
+    (grad_fo,) = sum_fo.finish(line, (0, 1, units))
+    sum_a.step(line)
     sum_s.step(line)
-    sum_a.step(line)
-    total_m, total_mo, total_c, total_s, total_f, total_fo, total_a = [
-        group.finish() for group in (sum_m, sum_mo, sum_c, sum_s, sum_f, sum_fo, sum_a)
-    ]
-
-    gains = jnp.concatenate([gain_e0, gain_e1, gain_e2, gain_d0, gain_d1, gain_d2], 0)
-    gains = gains.reshape((gains.shape[0],) + (2,) * bits + (-1,))
-    me = lax.axis_index("dp")
-    for bit in range(bits):
-        axis = bits - bit
-        mine = (me >> bit) & 1
-        sent = lax.dynamic_index_in_dim(gains, 1 - mine, axis, keepdims=False)
-        gains = lax.dynamic_index_in_dim(gains, mine, axis, keepdims=False) + swap(sent, bit)
-
-    def stacked_of(total, count):
-        return jnp.moveaxis(total.reshape(total.shape[0], count, -1), 1, 0)
-
-    def attn_grads(total):
-        return [stacked_of(total[:, : 3 * heads], 3), total[:, 3 * heads :].T]
-
-    cross_in = jnp.concatenate([total_c[:, :heads], total_c[:, 2 * heads :]], 1)
-    cross = [stacked_of(cross_in, 3), total_c[:, heads : 2 * heads].T]
+    (dec_out,) = line.call(sum_kernel, [dec_low], [y2, part_out, other_out], "dec_out")
+    (grad_f,) = sum_f.finish(line, (0, 2, units))
+    grad_a, grad_ao = sum_a.finish(line, (0, 3, heads), (3 * heads, 1, heads))
+    sum_s.step(line)
+    grad_s, grad_so, gains = sum_s.finish(line, (0, 3, heads), (3 * heads, 1, heads), (4 * heads, 1, 128))
+    gains = gains[:, :6].T
+    grad_c = jnp.concatenate([grad_cq[None], grad_ckv], 0)
     grads = (
-        attn_grads(total_a) + [stacked_of(total_f, 2), total_fo.T] + [gains[:3]]
-        + attn_grads(total_s) + cross + [stacked_of(total_m, 2), total_mo.T] + [gains[3:]]
+        grad_a, grad_ao.T, grad_f, grad_fo.T, gains[:3],
+        grad_s, grad_so.T, grad_c, grad_co.T, grad_m, grad_mo.T, gains[3:],
     )
     return (
         dec_out.reshape(cotangent.shape),

time: 358 us -> 312 us (0.87)
  local copies, waits for them, and re-layouts: 41 us -> 16.3 us
  waiting for transfers between devices: 212 us -> 195 us
  starting transfers between devices: 42.4 us -> 51.2 us
  Pallas kernels: 53.4 us -> 46.6 us
  other arithmetic: 6.05 us -> 1.55 us
    unnamed x206 -> x92, local copies, waits for them, and re-layouts: 34.7 us -> 16.2 us
    ppermute x11, waiting for transfers between devices: 67 us -> 52.9 us  [pair_other(): return lax.ppermute(part, 'mp', [(0, 1), (1, 0)])]
    ppermute x30 -> x45, starting transfers between devices: 27 us -> 36.6 us  [swap(): return lax.ppermute(value, 'dp', [(i, i ^ 1 << bit) for i in range(shards)])]
    pallas_call x31 -> x47, Pallas kernels: 53.4 us -> 46.6 us  [call(): pl.pallas_call(run, out_shape=shapes, in_specs=in_specs, out_specs=[VMEM]...]
    reshape x6 -> x0, local copies, waits for them, and re-layouts: 3.59 us -> none  [the longest x5 3.46 us: stacked_of(): return jnp.moveaxis(total.reshape(total.shape[0], count, -1), 1, 0)]
    ppermute x30 -> x45, waiting for transfers between devices: 145 us -> 142 us  [swap(): return lax.ppermute(value, 'dp', [(i, i ^ 1 << bit) for i in range(shards)])]
  transfers between devices with their start and end apart: 41 -> 56, of which waited for: 23 -> 31; matrix products, arithmetic and copies ran while one was open for 4% -> 0% of each run, Pallas kernels for 10% -> 10%
where the time goes in v4:
time: 312 us
  waiting for transfers between devices  195 us (62%)
  starting transfers between devices  51.2 us (16%)
  Pallas kernels  46.6 us (15%)
  local copies, waits for them, and re-layouts  16.3 us (5%)
    ppermute x45, waiting for transfers between devices, swap(): return lax.ppermute(value, 'dp', [(i, i ^ 1 << bit) for i in range(shards)])  142 us
    ppermute x11, waiting for transfers between devices, pair_other(): return lax.ppermute(part, 'mp', [(0, 1), (1, 0)])  52.9 us
    pallas_call x47, Pallas kernels, call(): pl.pallas_call(run, out_shape=shapes, in_specs=in_specs, out_specs=[VMEM]...  46.6 us
    ppermute x45, starting transfers between devices, swap(): return lax.ppermute(value, 'dp', [(i, i ^ 1 << bit) for i in range(shards)])  36.6 us
    unnamed x92, local copies, waits for them, and re-layouts  16.2 us
    ppermute x11, starting transfers between devices, pair_other(): return lax.ppermute(part, 'mp', [(0, 1), (1, 0)])  14.6 us
  transfers between devices with their start and end apart: 56, of which 31 were waited for; matrix products, arithmetic and copies ran while one was open for 0% of the time, Pallas kernels for 10%

profile of v4, /device:TPU:0, one launch (start us, length us, event | category | flops | bytes accessed | tf_op | source)
XLA Modules:
  0.0 311.8 jit_solution(16217960398284675240)
XLA Ops:
  2.4 3.2 %enc_attn_fwd.1 = (f32[256,768]{1,0:T(8,128)}, bf16[256,768]{1,0:T(8,128)(2,1)S(1)}, bf16[256,1152]{1,0:T(8,128)(2,1)S(1)}, bf16[256,384]{1,0:T(8,128)(2,1)S(1)}) custom-call(s32[2]{0:T(128)S(1)} %copy-done.41, bf16[256,768]{1,0:T(8,128)(2,1)S(1)} %bitcast.15, f32[3,768]{1,0:T(4,128)S(1)} %copy-done.34, bf16[3,768,384]{2,1,0:T(8,128)(2,1)S(1)} %copy-done.2, ...), custom_call_target="tpu_custom_call" | custom-call | flops 2644999936 | bytes 8487000 | tf_op jit(solution)/shard_map/enc_attn_fwd/pallas_call | solution.py:506
  5.6 3.0 collective-permute-start
  13.7 13.6 %collective-permute-done.refs_2_ = f32[256,768]{1,0:T(8,128)} collective-permute-done((f32[256,768]{1,0:T(8,128)}, f32[256,768]{1,0:T(8,128)}, u32[]{:S(2)}, u32[]{:S(2)}) %collective-permute-start) | collective-permute-done | bytes 786464 | tf_op jit(solution)/shard_map/pair_e1/ppermute | solution.py:544
  31.3 3.1 enc_mlp_fwd.1
  37.0 15.3 %collective-permute-done.1.refs_3_ = f32[256,768]{1,0:T(8,128)S(1)} collective-permute-done((f32[256,768]{1,0:T(8,128)S(1)}, f32[256,768]{1,0:T(8,128)S(1)}, u32[]{:S(2)}, u32[]{:S(2)}) %collective-permute-start.1) | collective-permute-done | bytes 786464 | tf_op jit(solution)/shard_map/pair_e2/ppermute | solution.py:544
  52.3 3.8 %cross_fwd.1 = (f32[128,768]{1,0:T(8,128)S(1)}, f32[256,768]{1,0:T(8,128)S(1)}, bf16[256,768]{1,0:T(8,128)(2,1)S(1)}, f32[128,768]{1,0:T(8,128)S(1)}, bf16[128,7...) custom-call(s32[2]{0:T(128)S(1)} %copy-done.41, ...), custom_call_target="tpu_custom_call" | custom-call | flops 4830000128 | bytes 15498000 | tf_op jit(solution)/shard_map/cross_fwd/pallas_call | solution.py:506
  57.7 7.1 %collective-permute-done.3.refs_2_ = f32[128,768]{1,0:T(8,128)S(1)} collective-permute-done((f32[128,768]{1,0:T(8,128)S(1)}, f32[128,768]{1,0:T(8,128)S(1)}, u32[]{:S(2)}, u32[]{:S(2)}) %collective-permute-start.3) | collective-permute-done | bytes 393248 | tf_op jit(solution)/shard_map/pair_d2/ppermute | solution.py:544
  67.2 3.9 %collective-permute-done.5.refs_1_ = f32[128,3840]{1,0:T(8,128)S(1)} collective-permute-done((f32[128,3840]{1,0:T(8,128)S(1)}, f32[128,3840]{1,0:T(8,128)S(1)}, u32[]{:S(2)}, u32[]{:S(2)}) %collective-permute-start.5) | collective-permute-done | bytes 1966112 | tf_op jit(solution)/shard_map/swap_m_bit0/ppermute | solution.py:550
  76.0 7.8 %collective-permute-done.4.refs_2_ = f32[128,768]{1,0:T(8,128)S(1)} collective-permute-done((f32[128,768]{1,0:T(8,128)S(1)}, f32[128,768]{1,0:T(8,128)S(1)}, u32[]{:S(2)}, u32[]{:S(2)}) %collective-permute-start.4) | collective-permute-done | bytes 393248 | tf_op jit(solution)/shard_map/pair_g3/ppermute | solution.py:544
  83.8 4.7 %cross_back.1 = (f32[256,768]{1,0:T(8,128)S(1)}, f32[128,768]{1,0:T(8,128)S(1)}, f32[1,768]{1,0:T(1,128)S(1)}, f32[128,768]{1,0:T(8,128)S(1)}, f32[128,768]{1,0:...) custom-call(s32[2]{0:T(128)S(1)} %copy-done.41, ...), custom_call_target="tpu_custom_call" | custom-call | flops 345000000 | bytes 1107000 | tf_op jit(solution)/shard_map/cross_back/pallas_call | solution.py:506
  96.0 12.6 %collective-permute-done.16.refs_1_ = f32[192,2048]{1,0:T(8,128)S(1)} collective-permute-done((f32[192,2048]{1,0:T(8,128)S(1)}, f32[192,2048]{1,0:T(8,128)S(1)}, u32[]{:S(2)}, u32[]{:S(2)}) %collective-permute-start.16) | collective-permute-done | bytes 1572896 | tf_op jit(solution)/shard_map/swap_m_bit1/ppermute | solution.py:550
  109.9 2.9 enc_mlp_back.1
  122.6 7.3 %collective-permute-done.14.refs_1_ = f32[96,1024]{1,0:T(8,128)S(1)} collective-permute-done((f32[96,1024]{1,0:T(8,128)S(1)}, f32[96,1024]{1,0:T(8,128)S(1)}, u32[]{:S(2)}, u32[]{:S(2)}) %collective-permute-start.14) | collective-permute-done | bytes 393248 | tf_op jit(solution)/shard_map/swap_mo_bit1/ppermute | solution.py:550
  130.0 12.7 %collective-permute-done.13.refs_1_ = f32[192,1536]{1,0:T(8,128)S(1)} collective-permute-done((f32[192,1536]{1,0:T(8,128)S(1)}, f32[192,1536]{1,0:T(8,128)S(1)}, u32[]{:S(2)}, u32[]{:S(2)}) %collective-permute-start.13) | collective-permute-done | bytes 1179680 | tf_op jit(solution)/shard_map/swap_c_bit2/ppermute | solution.py:550
  143.0 5.4 %enc_attn_back.1 = (f32[256,768]{1,0:T(8,128)S(1)}, f32[256,768]{1,0:T(8,128)S(1)}, f32[1,768]{1,0:T(1,128)S(1)}, f32[256,384]{1,0:T(8,128)S(1)}, f32[256,384]{1...) custom-call(s32[2]{0:T(128)S(1)} %copy-done.41, ...), custom_call_target="tpu_custom_call" | custom-call | flops 345000000 | bytes 1107000 | tf_op jit(solution)/shard_map/enc_attn_back/pallas_call | solution.py:506
  149.9 8.9 %collective-permute-done.32.refs_1_ = f32[96,2048]{1,0:T(8,128)S(1)} collective-permute-done((f32[96,2048]{1,0:T(8,128)S(1)}, f32[96,2048]{1,0:T(8,128)S(1)}, u32[]{:S(2)}, u32[]{:S(2)}) %collective-permute-start.32) | collective-permute-done | bytes 786464 | tf_op jit(solution)/shard_map/swap_m_bit2/ppermute | solution.py:550
  169.0 4.2 %collective-permute-done.34.refs_2_ = f32[128,768]{1,0:T(8,128)S(1)} collective-permute-done((f32[128,768]{1,0:T(8,128)S(1)}, f32[128,768]{1,0:T(8,128)S(1)}, u32[]{:S(2)}, u32[]{:S(2)}) %collective-permute-start.34) | collective-permute-done | bytes 393248 | tf_op jit(solution)/shard_map/pair_q/ppermute | solution.py:544
  173.2 2.6 collective-permute-start.40
  175.9 3.5 %dec_self_back.1 = (f32[128,768]{1,0:T(8,128)S(1)}, f32[128,768]{1,0:T(8,128)S(1)}, f32[1,768]{1,0:T(1,128)S(1)}, f32[128,768]{1,0:T(8,128)S(1)}, f32[128,768]{1...) custom-call(s32[2]{0:T(128)S(1)} %copy-done.43, f32[128,768]{1,0:T(8,128)S(1)} %query_part.1.refs_1_, ...), custom_call_target="tpu_custom_call" | custom-call | flops 345000000 | bytes 1107000 | tf_op jit(solution)/shard_map/dec_self_back/pallas_call | solution.py:506
  179.4 7.2 %collective-permute-done.42.refs_1_ = f32[48,1024]{1,0:T(8,128)S(1)} collective-permute-done((f32[48,1024]{1,0:T(8,128)S(1)}, f32[48,1024]{1,0:T(8,128)S(1)}, u32[]{:S(2)}, u32[]{:S(2)}) %collective-permute-start.42) | collective-permute-done | bytes 196640 | tf_op jit(solution)/shard_map/swap_mo_bit3/ppermute | solution.py:550
  187.1 6.8 %collective-permute-done.40.refs_1_ = f32[48,2048]{1,0:T(8,128)S(1)} collective-permute-done((f32[48,2048]{1,0:T(8,128)S(1)}, f32[48,2048]{1,0:T(8,128)S(1)}, u32[]{:S(2)}, u32[]{:S(2)}) %collective-permute-start.40) | collective-permute-done | bytes 393248 | tf_op jit(solution)/shard_map/swap_m_bit3/ppermute | solution.py:550
  193.9 3.5 %collective-permute-start.47 = (f32[192,1536]{1,0:T(8,128)S(1)}, f32[192,1536]{1,0:T(8,128)S(1)}, u32[]{:S(2)}, u32[]{:S(2)}) collective-permute-start(f32[192,1536]{1,0:T(8,128)S(1)} %get-tuple-element.200.refs_2_), channel_id=1, source_target_pairs={{0,8},{2,10},{4,12},{6,14},{8,0},{10,2},{12,4},{14,6},{16,24},{18,... | collective-permute-start | bytes 3538952 | tf_op jit(solution)/shard_map/swap_a_bit2/ppermute | solution.py:550
  207.9 3.3 %collective-permute-start.33 = (f32[48,1536]{1,0:T(8,128)S(1)}, f32[48,1536]{1,0:T(8,128)S(1)}, u32[]{:S(2)}, u32[]{:S(2)}) collective-permute-start(f32[48,1536]{1,0:T(8,128)S(1)} %get-tuple-element.202.refs_12_), channel_id=1, source_target_pairs={{0,16},{2,18},{4,20},{6,22},{8,24},{10,26},{12,28},{14,30},{16,0},... | collective-permute-start | bytes 884744 | tf_op jit(solution)/shard_map/swap_c_bit3/ppermute | solution.py:550
  211.9 18.2 %collective-permute-done.33.refs_1_ = f32[48,1536]{1,0:T(8,128)S(1)} collective-permute-done((f32[48,1536]{1,0:T(8,128)S(1)}, f32[48,1536]{1,0:T(8,128)S(1)}, u32[]{:S(2)}, u32[]{:S(2)}) %collective-permute-start.33) | collective-permute-done | bytes 294944 | tf_op jit(solution)/shard_map/swap_c_bit3/ppermute | solution.py:550
  231.1 13.5 %collective-permute-done.48.refs_1_ = f32[96,1024]{1,0:T(8,128)S(1)} collective-permute-done((f32[96,1024]{1,0:T(8,128)S(1)}, f32[96,1024]{1,0:T(8,128)S(1)}, u32[]{:S(2)}, u32[]{:S(2)}) %collective-permute-start.48) | collective-permute-done | bytes 393248 | tf_op jit(solution)/shard_map/swap_fo_bit1/ppermute | solution.py:550
  246.0 2.7 collective-permute-start.50
  248.8 8.5 %collective-permute-done.50.refs_1_ = f32[48,1024]{1,0:T(8,128)S(1)} collective-permute-done((f32[48,1024]{1,0:T(8,128)S(1)}, f32[48,1024]{1,0:T(8,128)S(1)}, u32[]{:S(2)}, u32[]{:S(2)}) %collective-permute-start.50) | collective-permute-done | bytes 196640 | tf_op jit(solution)/shard_map/swap_fo_bit3/ppermute | solution.py:550
  263.8 2.6 collective-permute-start.53
  266.8 4.9 %collective-permute-done.45.refs_2_ = f32[128,768]{1,0:T(8,128)S(1)} collective-permute-done((f32[128,768]{1,0:T(8,128)S(1)}, f32[128,768]{1,0:T(8,128)S(1)}, u32[]{:S(2)}, u32[]{:S(2)}) %collective-permute-start.45) | collective-permute-done | bytes 393248 | tf_op jit(solution)/shard_map/pair_out/ppermute | solution.py:544
  272.4 13.2 %collective-permute-done.53.refs_1_ = f32[48,2048]{1,0:T(8,128)S(1)} collective-permute-done((f32[48,2048]{1,0:T(8,128)S(1)}, f32[48,2048]{1,0:T(8,128)S(1)}, u32[]{:S(2)}, u32[]{:S(2)}) %collective-permute-start.53) | collective-permute-done | bytes 393248 | tf_op jit(solution)/shard_map/swap_f_bit3/ppermute | solution.py:550
  287.3 8.2 %collective-permute-done.52.refs_1_ = f32[48,1536]{1,0:T(8,128)S(1)} collective-permute-done((f32[48,1536]{1,0:T(8,128)S(1)}, f32[48,1536]{1,0:T(8,128)S(1)}, u32[]{:S(2)}, u32[]{:S(2)}) %collective-permute-start.52) | collective-permute-done | bytes 294944 | tf_op jit(solution)/shard_map/swap_a_bit3/ppermute | solution.py:550
  299.0 10.6 %collective-permute-done.55.refs_1_ = f32[48,1664]{1,0:T(8,128)S(1)} collective-permute-done((f32[48,1664]{1,0:T(8,128)S(1)}, f32[48,1664]{1,0:T(8,128)S(1)}, u32[]{:S(2)}, u32[]{:S(2)}) %collective-permute-start.55) | collective-permute-done | bytes 319520 | tf_op jit(solution)/shard_map/swap_s_bit3/ppermute | solution.py:550
  (225 shorter events, 81.7 us)
Async XLA Ops:
  5.6 21.7 %collective-permute-start = (f32[256,768]{1,0:T(8,128)}, f32[256,768]{1,0:T(8,128)}, u32[]{:S(2)}, u32[]{:S(2)}) collective-permute-start(f32[256,768]{1,0:T(8,128)} %get-tuple-element.133.refs_1_), channel_id=1, source_target_pairs={{0,1},{1,0},{2,3},{3,2},{4,5},{5,4},{6,7},{7,6},{8,9},{9,8},{10,11... | collective-permute-start | bytes 2359304 | tf_op jit(solution)/shard_map/pair_e1/ppermute | solution.py:544
  13.2 23.8 %collective-permute-start.2 = (f32[128,768]{1,0:T(8,128)}, f32[128,768]{1,0:T(8,128)}, u32[]{:S(2)}, u32[]{:S(2)}) collective-permute-start(f32[128,768]{1,0:T(8,128)} %get-tuple-element.138.refs_6_), channel_id=1, source_target_pairs={{0,1},{1,0},{2,3},{3,2},{4,5},{5,4},{6,7},{7,6},{8,9},{9,8},{10,11... | collective-permute-start | bytes 1179656 | tf_op jit(solution)/shard_map/pair_d1/ppermute | solution.py:544
  34.4 18.0 %collective-permute-start.1 = (f32[256,768]{1,0:T(8,128)S(1)}, f32[256,768]{1,0:T(8,128)S(1)}, u32[]{:S(2)}, u32[]{:S(2)}) collective-permute-start(f32[256,768]{1,0:T(8,128)S(1)} %get-tuple-element.137.refs_1_.refs_2_), channel_id=1, source_target_pairs={{0,1},{1,0},{2,3},{3,2},{4,5},{5,4},{6,7},{7,6},{8,9},{9,8},{10,11... | collective-permute-start | bytes 2359304 | tf_op jit(solution)/shard_map/pair_e2/ppermute | solution.py:544
  72.0 36.5 %collective-permute-start.16 = (f32[192,2048]{1,0:T(8,128)S(1)}, f32[192,2048]{1,0:T(8,128)S(1)}, u32[]{:S(2)}, u32[]{:S(2)}) collective-permute-start(f32[192,2048]{1,0:T(8,128)S(1)} %get-tuple-element.171), channel_id=1, source_target_pairs={{0,4},{2,6},{4,0},{6,2},{8,12},{10,14},{12,8},{14,10},{16,20},{18,... | collective-permute-start | bytes 4718600 | tf_op jit(solution)/shard_map/swap_m_bit1/ppermute | solution.py:550
  74.4 19.0 %collective-permute-start.12 = (f32[192,1024]{1,0:T(8,128)S(1)}, f32[192,1024]{1,0:T(8,128)S(1)}, u32[]{:S(2)}, u32[]{:S(2)}) collective-permute-start(f32[192,1024]{1,0:T(8,128)S(1)} %get-tuple-element.150.refs_14_), channel_id=1, source_target_pairs={{0,8},{2,10},{4,12},{6,14},{8,0},{10,2},{12,4},{14,6},{16,24},{18,... | collective-permute-start | bytes 2359304 | tf_op jit(solution)/shard_map/swap_mo_bit2/ppermute | solution.py:550
  89.1 19.6 %collective-permute-start.15 = (f32[256,768]{1,0:T(8,128)S(1)}, f32[256,768]{1,0:T(8,128)S(1)}, u32[]{:S(2)}, u32[]{:S(2)}) collective-permute-start(f32[256,768]{1,0:T(8,128)S(1)} %get-tuple-element.164.refs_0_), channel_id=1, source_target_pairs={{0,1},{1,0},{2,3},{3,2},{4,5},{5,4},{6,7},{7,6},{8,9},{9,8},{10,11... | collective-permute-start | bytes 2359304 | tf_op jit(solution)/shard_map/pair_m/ppermute | solution.py:544
  113.9 28.8 %collective-permute-start.13 = (f32[192,1536]{1,0:T(8,128)S(1)}, f32[192,1536]{1,0:T(8,128)S(1)}, u32[]{:S(2)}, u32[]{:S(2)}) collective-permute-start(f32[192,1536]{1,0:T(8,128)S(1)} %get-tuple-element.162.refs_2_), channel_id=1, source_target_pairs={{0,8},{2,10},{4,12},{6,14},{8,0},{10,2},{12,4},{14,6},{16,24},{18,... | collective-permute-start | bytes 3538952 | tf_op jit(solution)/shard_map/swap_c_bit2/ppermute | solution.py:550
  116.3 26.6 %collective-permute-start.25 = (f32[256,768]{1,0:T(8,128)S(1)}, f32[256,768]{1,0:T(8,128)S(1)}, u32[]{:S(2)}, u32[]{:S(2)}) collective-permute-start(f32[256,768]{1,0:T(8,128)S(1)} %get-tuple-element.186.refs_1_), channel_id=1, source_target_pairs={{0,1},{1,0},{2,3},{3,2},{4,5},{5,4},{6,7},{7,6},{8,9},{9,8},{10,11... | collective-permute-start | bytes 2359304 | tf_op jit(solution)/shard_map/pair_g1/ppermute | solution.py:544
  118.8 11.2 %collective-permute-start.14 = (f32[96,1024]{1,0:T(8,128)S(1)}, f32[96,1024]{1,0:T(8,128)S(1)}, u32[]{:S(2)}, u32[]{:S(2)}) collective-permute-start(f32[96,1024]{1,0:T(8,128)S(1)} %get-tuple-element.160.refs_7_), channel_id=1, source_target_pairs={{0,4},{2,6},{4,0},{6,2},{8,12},{10,14},{12,8},{14,10},{16,20},{18,... | collective-permute-start | bytes 1179656 | tf_op jit(solution)/shard_map/swap_mo_bit1/ppermute | solution.py:550
  119.6 39.2 %collective-permute-start.32 = (f32[96,2048]{1,0:T(8,128)S(1)}, f32[96,2048]{1,0:T(8,128)S(1)}, u32[]{:S(2)}, u32[]{:S(2)}) collective-permute-start(f32[96,2048]{1,0:T(8,128)S(1)} %get-tuple-element.172.refs_12_), channel_id=1, source_target_pairs={{0,8},{2,10},{4,12},{6,14},{8,0},{10,2},{12,4},{14,6},{16,24},{18,... | collective-permute-start | bytes 2359304 | tf_op jit(solution)/shard_map/swap_m_bit2/ppermute | solution.py:550
  148.4 11.1 %collective-permute-start.26 = (f32[256,384]{1,0:T(8,128)S(1)}, f32[256,384]{1,0:T(8,128)S(1)}, u32[]{:S(2)}, u32[]{:S(2)}) collective-permute-start(f32[256,384]{1,0:T(8,128)S(1)} %get-tuple-element.191), channel_id=1, source_target_pairs={{0,2},{2,0},{4,6},{6,4},{8,10},{10,8},{12,14},{14,12},{16,18},{18,... | collective-permute-start | bytes 1179656 | tf_op jit(solution)/shard_map/swap_a_bit0/ppermute | solution.py:550
  148.5 11.1 %collective-permute-start.27 = (f32[256,384]{1,0:T(8,128)S(1)}, f32[256,384]{1,0:T(8,128)S(1)}, u32[]{:S(2)}, u32[]{:S(2)}) collective-permute-start(f32[256,384]{1,0:T(8,128)S(1)} %get-tuple-element.192), channel_id=1, source_target_pairs={{0,2},{2,0},{4,6},{6,4},{8,10},{10,8},{12,14},{14,12},{16,18},{18,... | collective-permute-start | bytes 1179656 | tf_op jit(solution)/shard_map/swap_a_bit0/ppermute | solution.py:550
  149.0 11.1 %collective-permute-start.28 = (f32[256,384]{1,0:T(8,128)S(1)}, f32[256,384]{1,0:T(8,128)S(1)}, u32[]{:S(2)}, u32[]{:S(2)}) collective-permute-start(f32[256,384]{1,0:T(8,128)S(1)} %get-tuple-element.193), channel_id=1, source_target_pairs={{0,2},{2,0},{4,6},{6,4},{8,10},{10,8},{12,14},{14,12},{16,18},{18,... | collective-permute-start | bytes 1179656 | tf_op jit(solution)/shard_map/swap_a_bit0/ppermute | solution.py:550
  149.1 16.1 %collective-permute-start.24 = (f32[96,1536]{1,0:T(8,128)S(1)}, f32[96,1536]{1,0:T(8,128)S(1)}, u32[]{:S(2)}, u32[]{:S(2)}) collective-permute-start(f32[96,1536]{1,0:T(8,128)S(1)} %get-tuple-element.185.refs_12_), channel_id=1, source_target_pairs={{0,4},{2,6},{4,0},{6,2},{8,12},{10,14},{12,8},{14,10},{16,20},{18,... | collective-permute-start | bytes 1769480 | tf_op jit(solution)/shard_map/swap_c_bit1/ppermute | solution.py:550
  158.8 44.9 %collective-permute-start.44 = (f32[192,2048]{1,0:T(8,128)S(1)}, f32[192,2048]{1,0:T(8,128)S(1)}, u32[]{:S(2)}, u32[]{:S(2)}) collective-permute-start(f32[192,2048]{1,0:T(8,128)S(1)} %get-tuple-element.222), channel_id=1, source_target_pairs={{0,4},{2,6},{4,0},{6,2},{8,12},{10,14},{12,8},{14,10},{16,20},{18,... | collective-permute-start | bytes 4718600 | tf_op jit(solution)/shard_map/swap_f_bit1/ppermute | solution.py:550
  161.3 12.0 %collective-permute-start.34 = (f32[128,768]{1,0:T(8,128)S(1)}, f32[128,768]{1,0:T(8,128)S(1)}, u32[]{:S(2)}, u32[]{:S(2)}) collective-permute-start(f32[128,768]{1,0:T(8,128)S(1)} %query_part.1.refs_1_), channel_id=1, source_target_pairs={{0,1},{1,0},{2,3},{3,2},{4,5},{5,4},{6,7},{7,6},{8,9},{9,8},{10,11... | collective-permute-start | bytes 1179656 | tf_op jit(solution)/shard_map/pair_q/ppermute | solution.py:544
  162.8 34.5 %collective-permute-start.41 = (f32[192,1024]{1,0:T(8,128)S(1)}, f32[192,1024]{1,0:T(8,128)S(1)}, u32[]{:S(2)}, u32[]{:S(2)}) collective-permute-start(f32[192,1024]{1,0:T(8,128)S(1)} %get-tuple-element.182.refs_2_), channel_id=1, source_target_pairs={{0,8},{2,10},{4,12},{6,14},{8,0},{10,2},{12,4},{14,6},{16,24},{18,... | collective-permute-start | bytes 2359304 | tf_op jit(solution)/shard_map/swap_fo_bit2/ppermute | solution.py:550
  164.4 33.0 %collective-permute-start.38 = (f32[256,768]{1,0:T(8,128)S(1)}, f32[256,768]{1,0:T(8,128)S(1)}, u32[]{:S(2)}, u32[]{:S(2)}) collective-permute-start(f32[256,768]{1,0:T(8,128)S(1)} %get-tuple-element.210.refs_0_), channel_id=1, source_target_pairs={{0,1},{1,0},{2,3},{3,2},{4,5},{5,4},{6,7},{7,6},{8,9},{9,8},{10,11... | collective-permute-start | bytes 2359304 | tf_op jit(solution)/shard_map/pair_ge/ppermute | solution.py:544
  165.2 21.4 %collective-permute-start.42 = (f32[48,1024]{1,0:T(8,128)S(1)}, f32[48,1024]{1,0:T(8,128)S(1)}, u32[]{:S(2)}, u32[]{:S(2)}) collective-permute-start(f32[48,1024]{1,0:T(8,128)S(1)} %get-tuple-element.183.refs_2_), channel_id=1, source_target_pairs={{0,16},{2,18},{4,20},{6,22},{8,24},{10,26},{12,28},{14,30},{16,0},... | collective-permute-start | bytes 589832 | tf_op jit(solution)/shard_map/swap_mo_bit3/ppermute | solution.py:550
  173.2 20.6 %collective-permute-start.40 = (f32[48,2048]{1,0:T(8,128)S(1)}, f32[48,2048]{1,0:T(8,128)S(1)}, u32[]{:S(2)}, u32[]{:S(2)}) collective-permute-start(f32[48,2048]{1,0:T(8,128)S(1)} %get-tuple-element.199.refs_7_), channel_id=1, source_target_pairs={{0,16},{2,18},{4,20},{6,22},{8,24},{10,26},{12,28},{14,30},{16,0},... | collective-permute-start | bytes 1179656 | tf_op jit(solution)/shard_map/swap_m_bit3/ppermute | solution.py:550
  186.6 11.3 %collective-permute-start.39 = (f32[128,768]{1,0:T(8,128)S(1)}, f32[128,768]{1,0:T(8,128)S(1)}, u32[]{:S(2)}, u32[]{:S(2)}) collective-permute-start(f32[128,768]{1,0:T(8,128)S(1)} %get-tuple-element.212.refs_5_), channel_id=1, source_target_pairs={{0,1},{1,0},{2,3},{3,2},{4,5},{5,4},{6,7},{7,6},{8,9},{9,8},{10,11... | collective-permute-start | bytes 1179656 | tf_op jit(solution)/shard_map/pair_g0/ppermute | solution.py:544
  193.9 50.8 %collective-permute-start.47 = (f32[192,1536]{1,0:T(8,128)S(1)}, f32[192,1536]{1,0:T(8,128)S(1)}, u32[]{:S(2)}, u32[]{:S(2)}) collective-permute-start(f32[192,1536]{1,0:T(8,128)S(1)} %get-tuple-element.200.refs_2_), channel_id=1, source_target_pairs={{0,8},{2,10},{4,12},{6,14},{8,0},{10,2},{12,4},{14,6},{16,24},{18,... | collective-permute-start | bytes 3538952 | tf_op jit(solution)/shard_map/swap_a_bit2/ppermute | solution.py:550
  205.8 54.9 %collective-permute-start.46 = (f32[192,1664]{1,0:T(8,128)S(1)}, f32[192,1664]{1,0:T(8,128)S(1)}, u32[]{:S(2)}, u32[]{:S(2)}) collective-permute-start(f32[192,1664]{1,0:T(8,128)S(1)} %get-tuple-element.224.refs_2_), channel_id=1, source_target_pairs={{0,4},{2,6},{4,0},{6,2},{8,12},{10,14},{12,8},{14,10},{16,20},{18,... | collective-permute-start | bytes 3833864 | tf_op jit(solution)/shard_map/swap_s_bit1/ppermute | solution.py:550
  206.9 37.7 %collective-permute-start.48 = (f32[96,1024]{1,0:T(8,128)S(1)}, f32[96,1024]{1,0:T(8,128)S(1)}, u32[]{:S(2)}, u32[]{:S(2)}) collective-permute-start(f32[96,1024]{1,0:T(8,128)S(1)} %get-tuple-element.218.refs_2_), channel_id=1, source_target_pairs={{0,4},{2,6},{4,0},{6,2},{8,12},{10,14},{12,8},{14,10},{16,20},{18,... | collective-permute-start | bytes 1179656 | tf_op jit(solution)/shard_map/swap_fo_bit1/ppermute | solution.py:550
  207.9 22.2 %collective-permute-start.33 = (f32[48,1536]{1,0:T(8,128)S(1)}, f32[48,1536]{1,0:T(8,128)S(1)}, u32[]{:S(2)}, u32[]{:S(2)}) collective-permute-start(f32[48,1536]{1,0:T(8,128)S(1)} %get-tuple-element.202.refs_12_), channel_id=1, source_target_pairs={{0,16},{2,18},{4,20},{6,22},{8,24},{10,26},{12,28},{14,30},{16,0},... | collective-permute-start | bytes 884744 | tf_op jit(solution)/shard_map/swap_c_bit3/ppermute | solution.py:550
  211.2 37.5 %collective-permute-start.51 = (f32[96,2048]{1,0:T(8,128)S(1)}, f32[96,2048]{1,0:T(8,128)S(1)}, u32[]{:S(2)}, u32[]{:S(2)}) collective-permute-start(f32[96,2048]{1,0:T(8,128)S(1)} %get-tuple-element.223.refs_6_), channel_id=1, source_target_pairs={{0,8},{2,10},{4,12},{6,14},{8,0},{10,2},{12,4},{14,6},{16,24},{18,... | collective-permute-start | bytes 2359304 | tf_op jit(solution)/shard_map/swap_f_bit2/ppermute | solution.py:550
  244.8 14.9 %collective-permute-start.49 = (f32[96,1536]{1,0:T(8,128)S(1)}, f32[96,1536]{1,0:T(8,128)S(1)}, u32[]{:S(2)}, u32[]{:S(2)}) collective-permute-start(f32[96,1536]{1,0:T(8,128)S(1)} %get-tuple-element.231.refs_2_), channel_id=1, source_target_pairs={{0,4},{2,6},{4,0},{6,2},{8,12},{10,14},{12,8},{14,10},{16,20},{18,... | collective-permute-start | bytes 1769480 | tf_op jit(solution)/shard_map/swap_a_bit1/ppermute | solution.py:550
  246.0 11.3 %collective-permute-start.50 = (f32[48,1024]{1,0:T(8,128)S(1)}, f32[48,1024]{1,0:T(8,128)S(1)}, u32[]{:S(2)}, u32[]{:S(2)}) collective-permute-start(f32[48,1024]{1,0:T(8,128)S(1)} %get-tuple-element.229.refs_2_), channel_id=1, source_target_pairs={{0,16},{2,18},{4,20},{6,22},{8,24},{10,26},{12,28},{14,30},{16,0},... | collective-permute-start | bytes 589832 | tf_op jit(solution)/shard_map/swap_fo_bit3/ppermute | solution.py:550
  260.8 36.5 %collective-permute-start.54 = (f32[96,1664]{1,0:T(8,128)S(1)}, f32[96,1664]{1,0:T(8,128)S(1)}, u32[]{:S(2)}, u32[]{:S(2)}) collective-permute-start(f32[96,1664]{1,0:T(8,128)S(1)} %get-tuple-element.236.refs_3_), channel_id=1, source_target_pairs={{0,8},{2,10},{4,12},{6,14},{8,0},{10,2},{12,4},{14,6},{16,24},{18,... | collective-permute-start | bytes 1916936 | tf_op jit(solution)/shard_map/swap_s_bit2/ppermute | solution.py:550
  263.8 21.8 %collective-permute-start.53 = (f32[48,2048]{1,0:T(8,128)S(1)}, f32[48,2048]{1,0:T(8,128)S(1)}, u32[]{:S(2)}, u32[]{:S(2)}) collective-permute-start(f32[48,2048]{1,0:T(8,128)S(1)} %get-tuple-element.234.refs_2_), channel_id=1, source_target_pairs={{0,16},{2,18},{4,20},{6,22},{8,24},{10,26},{12,28},{14,30},{16,0},... | collective-permute-start | bytes 1179656 | tf_op jit(solution)/shard_map/swap_f_bit3/ppermute | solution.py:550
  266.4 29.1 %collective-permute-start.52 = (f32[48,1536]{1,0:T(8,128)S(1)}, f32[48,1536]{1,0:T(8,128)S(1)}, u32[]{:S(2)}, u32[]{:S(2)}) collective-permute-start(f32[48,1536]{1,0:T(8,128)S(1)} %get-tuple-element.235.refs_2_), channel_id=1, source_target_pairs={{0,16},{2,18},{4,20},{6,22},{8,24},{10,26},{12,28},{14,30},{16,0},... | collective-permute-start | bytes 884744 | tf_op jit(solution)/shard_map/swap_a_bit3/ppermute | solution.py:550
  298.3 11.4 %collective-permute-start.55 = (f32[48,1664]{1,0:T(8,128)S(1)}, f32[48,1664]{1,0:T(8,128)S(1)}, u32[]{:S(2)}, u32[]{:S(2)}) collective-permute-start(f32[48,1664]{1,0:T(8,128)S(1)} %get-tuple-element.245.refs_2_), channel_id=1, source_target_pairs={{0,16},{2,18},{4,20},{6,22},{8,24},{10,26},{12,28},{14,30},{16,0},... | collective-permute-start | bytes 958472 | tf_op jit(solution)/shard_map/swap_s_bit3/ppermute | solution.py:550
  (69 other events, 351.1 us)

commit v5 on v4

--- a/solution.py
+++ b/solution.py
@@ -132,81 +132,71 @@
     return put(keep, at, ordered[:, half:])
 
 
-def keys_of(causal, length, rows, counts):
+def keys_of(causal, length, rows, counts, first=0):
     plots = rows // length
     if causal:
         return [(slice(0, rows), causal_bias(counts, plots, length))]
-    return [(slice(p * length, (p + 1) * length), length_bias(counts[p], length, length)) for p in range(plots)]
-
-
-def self_fwd_kernel(causal, length, counts, state, gain, stacked, outer, part, normed_ref, qkv, mixed):
-    rows, width = state.shape[0], outer.shape[0]
-    normed = norm(state[...].astype(F32), gain[0:1, :])
-    normed_ref[...] = normed
-    normed_ref.flush()
+    return [
+        (slice(p * length, (p + 1) * length), length_bias(counts[first + p], length, length)) for p in range(plots)
+    ]
+
+
+def self_fwd_kernel(causal, length, first, counts, state, gain, stacked, outer, part, saved):
+    rows, width = part.shape[0], outer.shape[0]
+    normed = norm(state[first * length : first * length + rows, :].astype(F32), gain[0:1, :])
     for which in range(3):
-        put(qkv, which * width, mm(normed, stacked[which]))
-    for span, bias in keys_of(causal, length, rows, counts):
+        put(saved, which * width, mm(normed, stacked[which]))
+    for span, bias in keys_of(causal, length, rows, counts, first):
         for cols in pairs_of(width):
-            mixed[span, cols] = pair_fwd(
-                qkv[span, cols],
-                qkv[span, width + cols.start : width + cols.stop],
-                qkv[span, 2 * width + cols.start : 2 * width + cols.stop],
+            mixed = slice(3 * width + cols.start, 3 * width + cols.stop)
+            saved[span, mixed] = pair_fwd(
+                saved[span, cols],
+                saved[span, width + cols.start : width + cols.stop],
+                saved[span, 2 * width + cols.start : 2 * width + cols.stop],
                 bias,
             )
-    mixed.flush()
-    part[...] = mm(mixed[...], outer[...])
-
-
-def enc_mlp_fwd_kernel(state, own, other, gain, inner, outer, part, state_ref, normed, gate_ref, up_ref, hidden):
-    full = state[...].astype(F32) + own[...] + other[...]
+    part[...] = mm(saved[:, 3 * width :], outer[...])
+
+
+def enc_mlp_fwd_kernel(first, state, own, other, gain, inner, outer, part, state_ref, pre):
+    rows, width = part.shape[0], outer.shape[0]
+    full = state[first * rows : (first + 1) * rows, :].astype(F32) + own[...] + other[...]
     state_ref[...] = full
-    normed[...] = norm(full, gain[1:2, :])
-    flush(state_ref, normed)
-    width = outer.shape[0]
+    normed = norm(full, gain[1:2, :])
     step = 256
+    total = None
     for at in range(0, width, step):
         cols = slice(at, at + step)
-        gate = mm(normed[...], inner[0, :, cols])
-        up = mm(normed[...], inner[1, :, cols])
+        gate = mm(normed, inner[0, :, cols])
+        up = mm(normed, inner[1, :, cols])
         value, _ = gelu_parts(gate)
-        put(gate_ref, at, gate)
-        put(up_ref, at, up)
-        put(hidden, at, value * up)
-    part[...] = mm(hidden[...], outer[...])
+        pre[:, cols] = gate
+        pre[:, width + at : width + at + step] = up
+        add = mm((value * up).astype(BF), outer[cols, :])
+        total = add if total is None else total + add
+    part[...] = total
 
 
 def cross_fwd_kernel(
-    length, counts, enc_state, enc_own, enc_other, enc_gain, dec_state, dec_own, dec_other, dec_gain, stacked, outer,
-    part, enc_ref, memory, dec_ref, normed, query, kv, mixed,
+    length, first, counts, enc_state, enc_own, enc_other, enc_gain, dec_state, dec_own, dec_other, dec_gain, stacked,
+    outer, part, states, saved,
 ):
-    width = outer.shape[0]
-    dec_full = dec_state[...].astype(F32) + dec_own[...] + dec_other[...]
-    dec_ref[...] = dec_full
-    normed[...] = norm(dec_full, dec_gain[1:2, :])
-    flush(dec_ref, normed)
-    put(query, 0, mm(normed[...], stacked[0]))
+    rows, width = part.shape[0], outer.shape[0]
+    span = slice(first * rows, (first + 1) * rows)
+    dec_full = dec_state[span, :].astype(F32) + dec_own[span, :] + dec_other[span, :]
+    states[length:, :] = dec_full
+    normed = norm(dec_full, dec_gain[1:2, :])
+    saved[length:, :width] = mm(normed, stacked[0]).astype(BF)
     enc_full = enc_state[...] + enc_own[...] + enc_other[...]
-    enc_ref[...] = enc_full
-    memory[...] = norm(enc_full, enc_gain[2:3, :])
-    flush(enc_ref, memory)
-    put(kv, 0, mm(memory[...], stacked[1]))
-    put(kv, width, mm(memory[...], stacked[2]))
-    plots = enc_state.shape[0] // length
-    rows = dec_state.shape[0] // plots
-    for plot in range(plots):
-        bias = length_bias(counts[plot], rows, length)
-        q_span = slice(plot * rows, (plot + 1) * rows)
-        k_span = slice(plot * length, (plot + 1) * length)
-        for cols in pairs_of(width):
-            mixed[q_span, cols] = pair_fwd(
-                query[q_span, cols],
-                kv[k_span, cols],
-                kv[k_span, width + cols.start : width + cols.stop],
-                bias,
-            )
-    mixed.flush()
-    part[...] = mm(mixed[...], outer[...])
+    states[:length, :] = enc_full
+    memory = norm(enc_full, enc_gain[2:3, :])
+    saved[:length, :width] = mm(memory, stacked[1]).astype(BF)
+    saved[:length, width:] = mm(memory, stacked[2]).astype(BF)
+    bias = length_bias(counts[first], rows, length)
+    for cols in pairs_of(width):
+        beside = slice(width + cols.start, width + cols.stop)
+        saved[length:, beside] = pair_fwd(saved[length:, cols], saved[:length, cols], saved[:length, beside], bias)
+    part[...] = mm(saved[length:, width:], outer[...])
 
 
 def dec_mlp_kernel(
@@ -250,7 +240,7 @@
 
 
 def cross_back_kernel(
-    length, counts, own, other, state, gain, grad, outer, query, kv, stacked, order, normed, memory, mixed,
+    length, counts, own, other, state, gain, grad, outer, query, kv, stacked, order, dec_state, enc_state, enc_gain,
     part, grad_ref, gain_ref, send, keep, key_grads,
 ):
     grad_in, gain_ref[...] = norm_back(own[...] + other[...], state[...], gain[2:3, :])
@@ -279,10 +269,10 @@
     keep.flush(half, half + width)
     part[...] = mm_nt(key_grads[:, :width], stacked[1]) + mm_nt(key_grads[:, width:], stacked[2])
     part.flush()
-    put_cut(send, keep, 0, normed[...], order)
+    put_cut(send, keep, 0, norm(dec_state[...], gain[1:2, :]), order)
     at = put_cut(send, keep, half + width, low, order)
-    base = put_both(send, keep, at, mixed[...])
-    ordered = mm(memory[...], order[...])
+    base = put_both(send, keep, at, query[:, width : 2 * width])
+    ordered = mm(norm(enc_state[...], enc_gain[2:3, :]), order[...])
     for fold in range(kv.shape[0] // low.shape[0]):
         span = slice(fold * low.shape[0], (fold + 1) * low.shape[0])
         put(send, base, ordered[span, :half])
@@ -291,7 +281,7 @@
 
 
 def self_back_kernel(
-    causal, length, counts, own, other, state, gain, grad, outer, qkv, stacked, order, normed, mixed,
+    causal, length, counts, own, other, state, gain, grad, outer, qkv, stacked, order, inputs,
     part, grad_ref, gain_ref, send, keep,
 ):
     grad_in, gain_ref[...] = norm_back(own[...] + other[...], state[...], gain[1:2, :])
@@ -321,13 +311,13 @@
     total += mm_nt(keep[:, half + 2 * width : half + 3 * width], stacked[2])
     part[...] = total
     part.flush()
-    put_cut(send, keep, 0, normed[...], order)
+    put_cut(send, keep, 0, norm(inputs[...].astype(F32), gain[0:1, :]), order)
     at = put_cut(send, keep, half + 3 * width, low, order)
-    put_both(send, keep, at, mixed[...])
+    put_both(send, keep, at, qkv[:, 3 * width : 4 * width])
 
 
 def enc_mlp_back_kernel(
-    own, other, state, gain, outer, gate, up, inner, order, order_outer, normed, hidden,
+    own, other, state, gain, outer, pre, inner, order, order_outer, middle,
     part, grad_ref, gain_ref, send, keep,
 ):
     full, gain_ref[...] = norm_back(own[...] + other[...], state[...], gain[2:3, :])
@@ -338,18 +328,18 @@
     step = 256
     for col in range(0, width, step):
         cols = slice(col, col + step)
-        value, rise = gelu_parts(gate[:, cols])
+        value, rise = gelu_parts(pre[:, cols])
+        up = pre[:, width + col : width + col + step]
         grad_hidden = mm_nt(low, outer[cols, :])
-        put_both(send, keep, half + col, (grad_hidden * up[:, cols] * rise).astype(BF))
+        put_both(send, keep, half + col, (grad_hidden * up * rise).astype(BF))
         put_both(send, keep, half + width + col, (grad_hidden * value).astype(BF))
+        put_both(send, keep, 2 * half + 2 * width + col, (value * up).astype(BF))
     part[...] = mm_nt(keep[:, half : half + width], inner[0]) + mm_nt(
         keep[:, half + width : half + 2 * width], inner[1]
     )
     part.flush()
-    put_cut(send, keep, 0, normed[...], order)
-    at = put_cut(send, keep, half + 2 * width, low, order_outer)
-    for col in range(0, width, step):
-        at = put_both(send, keep, at, hidden[:, col : col + step])
+    put_cut(send, keep, 0, norm(middle[...], gain[1:2, :]), order)
+    put_cut(send, keep, half + 2 * width, low, order_outer)
 
 
 def last_kernel(
@@ -417,8 +407,27 @@
 ANY = pl.BlockSpec(memory_space=pl.ANY)
 
 
-COST = {"enc_attn_fwd": 2.3, "dec_self_fwd": 2.5, "enc_mlp_fwd": 1.7, "cross_fwd": 4.2, "dec_mlp": 2.7}
+COST = {
+    "enc_attn_fwd": 2.3, "dec_self_fwd": 2.5, "enc_mlp_fwd": 1.7, "cross_fwd": 4.2, "dec_mlp": 2.7,
+    "dec_out_part": 3, "finish_f": 0.3, "query_part": 3, "weights_f": 0.1, "cross_back": 3,
+    "dec_self_back": 1, "halve_s": 3, "weights_m": 8, "weights_a": 0.3, "halve_m": 20,
+    "halve_f": 0.3,
+}
 VMEM_LIMIT = 8
+
+LINE = (
+    "pause", "enc_attn_0", "enc_attn_1", "dec_self", "pause", "enc_mlp_0", "enc_mlp_1", "pause",
+    "cross_0", "cross_1", "pause", "dec_mlp", "tick", "w_m", "tick", "cross_back",
+    "h_mo", "h_m", "tick", "enc_mlp_back", "h_mo", "w_c", "w_f", "h_c",
+    "tick", "query_part", "enc_attn_back", "e_mo", "h_m", "w_a", "e_m", "h_c",
+    "dec_self_back", "h_f", "h_a", "input_grads", "e_c", "w_s", "h_f", "out_part",
+    "h_s", "h_a", "e_f", "dec_out", "h_s", "e_a", "e_s",
+)
+ACROSS, NEAR, FAR = 1, 2, 3
+HALVINGS = {"m": (ACROSS, NEAR, FAR), "mo": (NEAR, ACROSS, FAR), "c": (ACROSS, NEAR, FAR), "f": (ACROSS, NEAR, FAR), "a": (NEAR, ACROSS, FAR), "s": (ACROSS, NEAR, FAR)}
+PARTS = {"m": 1, "c": 1, "f": 3, "a": 1, "s": 1}
+TICK = 4
+GAINS_WITH = "s"
 
 
 class Stored:
@@ -441,16 +450,6 @@
         self.refs = refs
         self.shape = (refs[0].shape[0], sum(ref.shape[1] for ref in refs))
         self.dtype = refs[0].dtype
-
-    def part(self, at):
-        rows, cols = at
-        first = cols.start or 0
-        last = self.shape[1] if cols.stop is None else cols.stop
-        for ref in self.refs:
-            if last <= ref.shape[1]:
-                return ref, (rows, slice(first, last))
-            first, last = first - ref.shape[1], last - ref.shape[1]
-        raise ValueError(at)
 
     def __getitem__(self, at):
         rows, cols = at
@@ -464,11 +463,42 @@
         return pieces[0] if len(pieces) == 1 else jnp.concatenate(pieces, 1)
 
     def __setitem__(self, at, value):
-        ref, inside = self.part(at)
-        ref[inside] = value
+        rows, cols = at
+        first, last = cols.start or 0, self.shape[1] if cols.stop is None else cols.stop
+        start = 0
+        for ref in self.refs:
+            low, high = max(first - start, 0), min(last - start, ref.shape[1])
+            if low < high:
+                ref[rows, low:high] = value[:, low + start - first : high + start - first]
+            start += ref.shape[1]
 
     def flush(self, first=0, last=None):
         pass
+
+
+class Stack:
+    def __init__(self, *parts):
+        self.parts = parts
+
+
+class Rows:
+    def __init__(self, refs, spans):
+        self.refs = [ref.at[first:last] if (first, last) != (0, ref.shape[0]) else ref
+                     for ref, (first, last) in zip(refs, spans)]
+        self.heights = [last - first for first, last in spans]
+        self.shape = (sum(self.heights),) + tuple(refs[0].shape[1:])
+        self.dtype = refs[0].dtype
+
+    def __getitem__(self, at):
+        rows, cols = (slice(None), slice(None)) if at is Ellipsis else at
+        first, last, _ = rows.indices(self.shape[0])
+        pieces, start = [], 0
+        for ref, height in zip(self.refs, self.heights):
+            low, high = max(first - start, 0), min(last - start, height)
+            if low < high:
+                pieces.append(ref[low:high, cols])
+            start += height
+        return pieces[0] if len(pieces) == 1 else jnp.concatenate(pieces, 0)
 
 
 def flush(*refs):
@@ -481,6 +511,8 @@
         self.last = None
 
     def call(self, kernel, outs, args, name, scratch=(), cost=None):
+        spans = [[part[1:] for part in a.parts] if isinstance(a, Stack) else None for a in args]
+        args = [[part[0] for part in a.parts] if isinstance(a, Stack) else a for a in args]
         flat_args, args_tree = jax.tree.flatten(list(args))
         widths = [out if isinstance(out, list) else [out] for out in outs]
         shapes = [jax.ShapeDtypeStruct(*out) for group in widths for out in group]
@@ -494,7 +526,7 @@
 
         def run(*refs):
             ins = jax.tree.unflatten(args_tree, refs[:count])
-            ins = [Columns(i) if isinstance(i, list) else i for i in ins]
+            ins = [Rows(i, span) if span else Columns(i) if isinstance(i, list) else i for i, span in zip(ins, spans)]
             left = list(refs[total : total + made])
             results = []
             for group, out in zip(widths, outs):
@@ -576,7 +608,7 @@
     def step(self, line):
         rows, columns = self.kept.shape[0] // 2, self.kept.shape[1]
         shape = ((rows, columns), F32)
-        sent, self.kept = line.call(halve_kernel, [shape, shape], [self.kept, self.flying], "halve")
+        sent, self.kept = line.call(halve_kernel, [shape, shape], [self.kept, self.flying], "halve_" + self.name)
         self.flying = swap(sent, self.bits[self.steps], self.name)
         self.steps += 1
 
@@ -589,7 +621,7 @@
         outs = [(((count, rows, width) if count > 1 else (rows, width)), F32) for _, count, width in pieces]
         return line.call(
             functools.partial(finish_kernel, [(first, count) for first, count, _ in pieces]),
-            outs, [self.kept, self.flying], "finish",
+            outs, [self.kept, self.flying], "finish_" + self.name,
         )
 
 
@@ -604,10 +636,18 @@
     units = enc_mlp_out.shape[0]
     half = features // 2
     bits = lax.axis_size("dp").bit_length() - 1
-    plain = tuple(range(bits))
-    turned = (0, 2, 1) + tuple(range(3, bits))
-    order = feature_order(features, plain)
-    order_turned = feature_order(features, turned)
+    orders = {}
+
+    def halving(*first):
+        chosen = [0] + [bit for bit in first if bit < bits]
+        chosen = tuple(chosen + [bit for bit in range(bits) if bit not in chosen])
+        if chosen not in orders:
+            orders[chosen] = feature_order(features, chosen)
+        return chosen, orders[chosen]
+
+    halvings = {name: halving(*first) for name, first in HALVINGS.items()}
+    bits_of = {name: pair[0] for name, pair in halvings.items()}
+    order_of = {name: pair[1] for name, pair in halvings.items()}
     x0 = enc_in.reshape(enc_rows, features)
     y0 = dec_in.reshape(dec_rows, features)
     top = cotangent.reshape(dec_rows, features)
@@ -617,21 +657,29 @@
     quarter = half // 2
     line = Line()
 
-    def tick(cost=2.0):
+    def tick(cost=TICK):
         line.call(tick_kernel, [((1, 128), F32)], [enc_gains], "tick", cost=cost)
 
-    def wide(rows, *columns):
-        return [((rows, c), F32) for c in columns]
+    def parts_of(name, rows, width):
+        count, tiles = PARTS[name], width // 128
+        edges = [128 * (tiles * i // count) for i in range(count + 1)]
+        return [((rows, high - low), F32) for low, high in zip(edges, edges[1:])]
+
+    def swap_cores(name, parts):
+        return [swap(part, 0, name) for part in parts]
 
     def group(columns):
         return [((quarter, columns), F32)] * 2
 
-    mlp_groups = group(2 * units) + group(units)
-
-    mlp_segments = (
-        (0, half, half, 2 * units, 0, 0),
-        (half + 2 * units, half, 2 * half + 2 * units, units, 1, 0),
-    )
+    def mlp_of(name):
+        apart = name + "o" in HALVINGS
+        target = (1, 0) if apart else (0, 2 * units)
+        segments = (
+            (0, half, half, 2 * units, 0, 0),
+            (half + 2 * units, half, 2 * half + 2 * units, units) + target,
+        )
+        return segments, group(2 * units) + group(units) if apart else group(3 * units)
+
     attn_segments = (
         (0, half, half, 3 * heads, 0, 0),
         (half + 3 * heads, half, 2 * half + 3 * heads, heads, 0, 3 * heads),
@@ -648,156 +696,208 @@
     mlp_wide = 2 * half + 3 * units
     attn_wide = 2 * half + 4 * heads
     cross_wide = base + folds * fold_width
-    order_m, order_mo, order_f, order_fo, order_c, order_s, order_a = (
-        order, order_turned, order, order_turned, order_turned, order, order_turned
-    )
-    bits_m, bits_mo, bits_f, bits_fo, bits_c, bits_s, bits_a = plain, turned, plain, turned, turned, plain, turned
-
-    tick(6.0)
-    part_e1, u_e0, qkv_e, mixed_e = line.call(
-        functools.partial(self_fwd_kernel, False, enc_len),
-        [enc_wide, enc_low, ((enc_rows, 3 * heads), BF), ((enc_rows, heads), BF)],
-        [patch_counts, x0, enc_gains, enc_qkv, enc_attn_out], "enc_attn_fwd",
-    )
-    other_e1 = pair_other(part_e1, "e1")
-    part_d1, u_d0, qkv_d, mixed_d = line.call(
-        functools.partial(self_fwd_kernel, True, dec_len),
-        [dec_wide, dec_low, ((dec_rows, 3 * heads), BF), ((dec_rows, heads), BF)],
-        [table_lengths, y0, dec_gains, dec_self_qkv, dec_self_out], "dec_self_fwd",
-    )
-    other_d1 = pair_other(part_d1, "d1")
-    part_e2, x1, u_e1, gate, up, hidden = line.call(
-        enc_mlp_fwd_kernel,
-        [enc_wide, enc_wide, enc_low, ((enc_rows, units), F32), ((enc_rows, units), F32),
-         ((enc_rows, units), BF)],
-        [x0, part_e1, other_e1, enc_gains, enc_mlp_in, enc_mlp_out], "enc_mlp_fwd",
-    )
-    other_e2 = pair_other(part_e2, "e2")
-    tick(6.0)
-    part_d2, x2, memory, y1, u_d1, query, kv, mixed_c = line.call(
-        functools.partial(cross_fwd_kernel, enc_len),
-        [dec_wide, enc_wide, enc_low, dec_wide, dec_low, ((dec_rows, heads), BF),
-         ((enc_rows, 2 * heads), BF), ((dec_rows, heads), BF)],
-        [patch_counts, x1, part_e2, other_e2, enc_gains, y0, part_d1, other_d1, dec_gains, dec_cross_qkv, dec_cross_out],
-        "cross_fwd",
-    )
-    other_d2 = pair_other(part_d2, "d2")
-    tick(6.0)
-    part_g3, y2, send_m, keep_m = line.call(
-        dec_mlp_kernel,
-        [dec_wide, dec_wide, ((dec_rows, mlp_wide), F32), ((dec_rows, mlp_wide), BF)],
-        [y1, part_d2, other_d2, dec_gains, top, dec_mlp_in, dec_mlp_out, order_m, order_mo], "dec_mlp",
-    )
-    other_g3 = pair_other(part_g3, "g3")
-    recv_m = swap(send_m, 0, "m")
-    tick()
-    products = line.call(
-        functools.partial(weight_kernel, mlp_segments), mlp_groups, [keep_m, recv_m], "dec_mlp_weights"
-    )
-    sum_mo = Halving(products[2], products[3], bits_mo, "mo")
-    sum_m = Halving(products[0], products[1], bits_m, "m")
-    part_m, g2, gain_d2, send_c, keep_c = line.call(
-        functools.partial(cross_back_kernel, enc_len),
-        [enc_wide, dec_wide, gain_row, wide(dec_rows, half + heads, half + heads, *[half, 2 * heads] * folds), ((dec_rows, cross_wide), BF)],
-        [patch_counts, part_g3, other_g3, y2, dec_gains, top, dec_cross_out, query, kv, dec_cross_qkv, order_c, u_d1,
-         memory, mixed_c],
-        "cross_back", scratch=[pltpu.VMEM((enc_rows, 2 * heads), BF)],
-    )
-    other_m = pair_other(part_m, "m")
-    recv_c = [swap(part, 0, "c") for part in send_c]
-    tick()
-    sum_mo.step(line)
-    products = line.call(
-        functools.partial(weight_kernel, cross_segments), attn_group, [keep_c, recv_c], "cross_weights"
-    )
-    sum_c = Halving(products[0], products[1], bits_c, "c")
-    sum_m.step(line)
-    part_g1, back2, gain_e2, send_f, keep_f = line.call(
-        enc_mlp_back_kernel,
-        [enc_wide, enc_wide, gain_row, wide(enc_rows, half + units // 4, *[units // 2] * 3, half + units // 4, *[units // 2] * 2),
-         ((enc_rows, mlp_wide), BF)],
-        [part_m, other_m, x2, enc_gains, enc_mlp_out, gate, up, enc_mlp_in, order_f, order_fo, u_e1, hidden],
-        "enc_mlp_back",
-    )
-    other_g1 = pair_other(part_g1, "g1")
-    recv_f = [swap(part, 0, "f") for part in send_f]
-    tick()
-    products = line.call(
-        functools.partial(weight_kernel, mlp_segments), mlp_groups, [keep_f, recv_f], "enc_mlp_weights"
-    )
-    sum_fo = Halving(products[2], products[3], bits_fo, "fo")
-    sum_f = Halving(products[0], products[1], bits_f, "f")
-    sum_mo.step(line)
-    sum_c.step(line)
-    part_ge, back1, gain_e1, send_a, keep_a = line.call(
-        functools.partial(self_back_kernel, False, enc_len),
-        [enc_wide, enc_wide, gain_row, wide(enc_rows, half, heads, heads, heads, half, heads), ((enc_rows, attn_wide), BF)],
-        [patch_counts, part_g1, other_g1, x1, enc_gains, back2, enc_attn_out, qkv_e, enc_qkv, order_a, u_e0, mixed_e],
-        "enc_attn_back",
-    )
-    (part_q,) = line.call(query_part_kernel, [dec_wide], [keep_c, dec_cross_qkv], "query_part")
-    other_q = pair_other(part_q, "q")
-    other_ge = pair_other(part_ge, "ge")
-    recv_a = [swap(part, 0, "a") for part in send_a]
-    tick()
-    sum_m.step(line)
-    products = line.call(
-        functools.partial(weight_kernel, attn_segments), attn_group, [keep_a, recv_a], "enc_attn_weights"
-    )
-    sum_a = Halving(products[0], products[1], bits_a, "a")
-    sum_c.step(line)
-    part_g0, g1, gain_d1, send_s, keep_s = line.call(
-        functools.partial(self_back_kernel, True, dec_len),
-        [dec_wide, dec_wide, gain_row, wide(dec_rows, half + heads, 2 * heads, half + heads),
-         ((dec_rows, attn_wide), BF)],
-        [table_lengths, part_q, other_q, y1, dec_gains, g2, dec_self_out, qkv_d, dec_self_qkv, order_s, u_d0, mixed_d],
-        "dec_self_back",
-    )
-    other_g0 = pair_other(part_g0, "g0")
-    recv_s = [swap(part, 0, "s") for part in send_s]
-    tick()
-    (grad_mo,) = sum_mo.finish(line, (0, 1, units))
-    sum_fo.step(line)
-    (grad_m,) = sum_m.finish(line, (0, 2, units))
-    enc_out, dec_out_grad, send_g, keep_g = line.call(
-        last_kernel,
-        [enc_low, dec_low, ((half, 128), F32), ((half, 128), F32)],
-        [part_ge, other_ge, x0, enc_gains, back1, part_g0, other_g0, y0, dec_gains, g1, order_s, gain_e1, gain_e2,
-         gain_d1, gain_d2],
-        "input_grads",
-    )
-    recv_g = swap(send_g, 0, "g")
-    sum_f.step(line)
-    products = line.call(
-        functools.partial(gains_weight_kernel, attn_segments), group(4 * heads + 128),
-        [keep_s, recv_s, keep_g, recv_g], "dec_self_weights",
-    )
-    sum_s = Halving(products[0], products[1], bits_s, "s")
-    grad_cq, grad_co, grad_ckv = sum_c.finish(line, (0, 1, heads), (heads, 1, heads), (2 * heads, 2, heads))
-    (part_out,) = line.call(out_part_kernel, [dec_wide], [keep_m, dec_mlp_out], "dec_out_part")
-    other_out = pair_other(part_out, "out")
-    sum_fo.step(line)
-    sum_a.step(line)
-    sum_f.step(line)
-    (grad_fo,) = sum_fo.finish(line, (0, 1, units))
-    sum_a.step(line)
-    sum_s.step(line)
-    (dec_out,) = line.call(sum_kernel, [dec_low], [y2, part_out, other_out], "dec_out")
-    (grad_f,) = sum_f.finish(line, (0, 2, units))
-    grad_a, grad_ao = sum_a.finish(line, (0, 3, heads), (3 * heads, 1, heads))
-    sum_s.step(line)
-    grad_s, grad_so, gains = sum_s.finish(line, (0, 3, heads), (3 * heads, 1, heads), (4 * heads, 1, 128))
+    v, sums, grad_of = {}, {}, {}
+
+    def pause():
+        tick(6.0)
+
+    def enc_attn(p):
+        v["part_e1", p], v["enc_saved", p] = line.call(
+            functools.partial(self_fwd_kernel, False, enc_len, p),
+            [((enc_len, features), F32), ((enc_len, 4 * heads), BF)],
+            [patch_counts, x0, enc_gains, enc_qkv, enc_attn_out], "enc_attn_fwd",
+        )
+        v["other_e1", p] = pair_other(v["part_e1", p], "e1")
+
+    def dec_self():
+        v["part_d1"], v["dec_saved"] = line.call(
+            functools.partial(self_fwd_kernel, True, dec_len, 0),
+            [dec_wide, ((dec_rows, 4 * heads), BF)],
+            [table_lengths, y0, dec_gains, dec_self_qkv, dec_self_out], "dec_self_fwd",
+        )
+        v["other_d1"] = pair_other(v["part_d1"], "d1")
+
+    def enc_mlp(p):
+        v["part_e2", p], v["x1", p], v["pre", p] = line.call(
+            functools.partial(enc_mlp_fwd_kernel, p),
+            [((enc_len, features), F32), ((enc_len, features), F32), ((enc_len, 2 * units), F32)],
+            [x0, v["part_e1", p], v["other_e1", p], enc_gains, enc_mlp_in, enc_mlp_out], "enc_mlp_fwd",
+        )
+        v["other_e2", p] = pair_other(v["part_e2", p], "e2")
+
+    def cross(p):
+        v["part_d2", p], v["states", p], v["saved", p] = line.call(
+            functools.partial(cross_fwd_kernel, enc_len, p),
+            [((dec_len, features), F32), ((enc_len + dec_len, features), F32), ((enc_len + dec_len, 2 * heads), BF)],
+            [patch_counts, v["x1", p], v["part_e2", p], v["other_e2", p], enc_gains, y0, v["part_d1"], v["other_d1"],
+             dec_gains, dec_cross_qkv, dec_cross_out],
+            "cross_fwd",
+        )
+        v["other_d2", p] = pair_other(v["part_d2", p], "d2")
+
+    def stack(name, first, last):
+        return Stack(*[(v[name, p], first, last) for p in range(plots)])
+
+    def enc_part(name):
+        return stack(name, 0, enc_len)
+
+    def dec_part(name):
+        return stack(name, enc_len, enc_len + dec_len)
+
+    def dec_mlp():
+        v["part_g3"], v["y2"], send, v["keep_m"] = line.call(
+            dec_mlp_kernel,
+            [dec_wide, dec_wide, parts_of("m", dec_rows, mlp_wide), ((dec_rows, mlp_wide), BF)],
+            [dec_part("states"), stack("part_d2", 0, dec_len), stack("other_d2", 0, dec_len), dec_gains, top,
+             dec_mlp_in, dec_mlp_out, order_of["m"], order_of.get("mo", order_of["m"])],
+            "dec_mlp",
+        )
+        v["other_g3"] = pair_other(v["part_g3"], "g3")
+        v["recv_m"] = swap_cores("m", send)
+
+
+    def start_sums(name, products):
+        for group_name, pair in zip((name, name + "o"), zip(products[::2], products[1::2])):
+            sums[group_name] = Halving(pair[0], pair[1], bits_of[group_name], group_name)
+
+    def mlp_weights(name, keep, recv):
+        segments, groups = mlp_of(name)
+        start_sums(
+            name, line.call(functools.partial(weight_kernel, segments), groups, [keep, recv], "weights_" + name)
+        )
+
+    def dec_mlp_weights():
+        mlp_weights("m", v["keep_m"], v["recv_m"])
+
+    def cross_back():
+        v["part_m"], v["g2"], v["gain_d2"], send, v["keep_c"] = line.call(
+            functools.partial(cross_back_kernel, enc_len),
+            [enc_wide, dec_wide, gain_row, parts_of("c", dec_rows, cross_wide), ((dec_rows, cross_wide), BF)],
+            [patch_counts, v["part_g3"], v["other_g3"], v["y2"], dec_gains, top, dec_cross_out, dec_part("saved"),
+             enc_part("saved"), dec_cross_qkv, order_of["c"], dec_part("states"), enc_part("states"), enc_gains],
+            "cross_back", scratch=[pltpu.VMEM((enc_rows, 2 * heads), BF)],
+        )
+        v["other_m"] = pair_other(v["part_m"], "m")
+        v["recv_c"] = swap_cores("c", send)
+
+    def cross_weights():
+        start_sums("c", line.call(
+            functools.partial(weight_kernel, cross_segments), attn_group, [v["keep_c"], v["recv_c"]], "weights_c"
+        ))
+
+    def enc_mlp_back():
+        v["part_g1"], v["back2"], v["gain_e2"], send, v["keep_f"] = line.call(
+            enc_mlp_back_kernel,
+            [enc_wide, enc_wide, gain_row, parts_of("f", enc_rows, mlp_wide), ((enc_rows, mlp_wide), BF)],
+            [v["part_m"], v["other_m"], enc_part("states"), enc_gains, enc_mlp_out, enc_part("pre"), enc_mlp_in,
+             order_of["f"], order_of.get("fo", order_of["f"]), enc_part("x1")],
+            "enc_mlp_back",
+        )
+        v["other_g1"] = pair_other(v["part_g1"], "g1")
+        v["recv_f"] = swap_cores("f", send)
+
+    def enc_mlp_weights():
+        mlp_weights("f", v["keep_f"], v["recv_f"])
+
+    def enc_attn_back():
+        v["part_ge"], v["back1"], v["gain_e1"], send, v["keep_a"] = line.call(
+            functools.partial(self_back_kernel, False, enc_len),
+            [enc_wide, enc_wide, gain_row, parts_of("a", enc_rows, attn_wide), ((enc_rows, attn_wide), BF)],
+            [patch_counts, v["part_g1"], v["other_g1"], enc_part("x1"), enc_gains, v["back2"], enc_attn_out,
+             enc_part("enc_saved"), enc_qkv, order_of["a"], x0],
+            "enc_attn_back",
+        )
+        v["other_ge"] = pair_other(v["part_ge"], "ge")
+        v["recv_a"] = swap_cores("a", send)
+
+    def query_part():
+        (v["part_q"],) = line.call(query_part_kernel, [dec_wide], [v["keep_c"], dec_cross_qkv], "query_part")
+        v["other_q"] = pair_other(v["part_q"], "q")
+
+    def dec_self_back():
+        v["part_g0"], v["g1"], v["gain_d1"], send, v["keep_s"] = line.call(
+            functools.partial(self_back_kernel, True, dec_len),
+            [dec_wide, dec_wide, gain_row, parts_of("s", dec_rows, attn_wide), ((dec_rows, attn_wide), BF)],
+            [table_lengths, v["part_q"], v["other_q"], dec_part("states"), dec_gains, v["g2"], dec_self_out,
+             v["dec_saved"], dec_self_qkv, order_of["s"], y0],
+            "dec_self_back",
+        )
+        v["other_g0"] = pair_other(v["part_g0"], "g0")
+        v["recv_s"] = swap_cores("s", send)
+
+    def input_grads():
+        v["enc_out"], v["dec_out_grad"], send, v["keep_g"] = line.call(
+            last_kernel,
+            [enc_low, dec_low, ((half, 128), F32), ((half, 128), F32)],
+            [v["part_ge"], v["other_ge"], x0, enc_gains, v["back1"], v["part_g0"], v["other_g0"], y0, dec_gains,
+             v["g1"], order_of[GAINS_WITH], v["gain_e1"], v["gain_e2"], v["gain_d1"], v["gain_d2"]],
+            "input_grads",
+        )
+        v["recv_g"] = swap(send, 0, "g")
+
+    def attn_weights(name):
+        if name == GAINS_WITH:
+            products = line.call(
+                functools.partial(gains_weight_kernel, attn_segments), group(4 * heads + 128),
+                [v["keep_" + name], v["recv_" + name], v["keep_g"], v["recv_g"]], "weights_" + name,
+            )
+        else:
+            products = line.call(
+                functools.partial(weight_kernel, attn_segments), attn_group,
+                [v["keep_" + name], v["recv_" + name]], "weights_" + name,
+            )
+        start_sums(name, products)
+
+    def out_part():
+        (v["part_out"],) = line.call(out_part_kernel, [dec_wide], [v["keep_m"], dec_mlp_out], "dec_out_part")
+        v["other_out"] = pair_other(v["part_out"], "out")
+
+    def dec_out_sum():
+        (v["dec_out"],) = line.call(sum_kernel, [dec_low], [v["y2"], v["part_out"], v["other_out"]], "dec_out")
+
+    attn_pieces = ((0, 3, heads), (3 * heads, 1, heads))
+    ends = {
+        "m": ((0, 2, units),), "f": ((0, 2, units),), "mo": ((0, 1, units),), "fo": ((0, 1, units),),
+        "c": ((0, 1, heads), (heads, 1, heads), (2 * heads, 2, heads)), "a": attn_pieces, "s": attn_pieces,
+    }
+    for name in ("m", "f"):
+        if name + "o" not in HALVINGS:
+            ends[name] += ((2 * units, 1, units),)
+    ends[GAINS_WITH] += ((4 * heads, 1, 128),)
+    stages = {
+        "tick": tick, "pause": pause, "dec_self": dec_self, "dec_mlp": dec_mlp, "w_m": dec_mlp_weights,
+        "cross_back": cross_back, "w_c": cross_weights, "enc_mlp_back": enc_mlp_back,
+        "w_f": enc_mlp_weights, "enc_attn_back": enc_attn_back, "query_part": query_part,
+        "w_a": functools.partial(attn_weights, "a"), "dec_self_back": dec_self_back, "input_grads": input_grads,
+        "w_s": functools.partial(attn_weights, "s"), "out_part": out_part, "dec_out": dec_out_sum,
+    }
+    for name, stage in (("enc_attn", enc_attn), ("enc_mlp", enc_mlp), ("cross", cross)):
+        for p in range(plots):
+            stages["%s_%d" % (name, p)] = functools.partial(stage, p)
+    for stage in LINE:
+        kind, _, name = stage.partition("_")
+        if stage in stages:
+            stages[stage]()
+        elif kind == "h":
+            sums[name].step(line)
+        else:
+            grad_of[name] = sums[name].finish(line, *ends[name])
+    mlp_grads = {
+        name: grad_of[name] if name + "o" not in HALVINGS else grad_of[name] + grad_of[name + "o"] for name in ("m", "f")
+    }
+    gains = grad_of[GAINS_WITH][2]
     gains = gains[:, :6].T
-    grad_c = jnp.concatenate([grad_cq[None], grad_ckv], 0)
+    grad_c = jnp.concatenate([grad_of["c"][0][None], grad_of["c"][2]], 0)
     grads = (
-        grad_a, grad_ao.T, grad_f, grad_fo.T, gains[:3],
-        grad_s, grad_so.T, grad_c, grad_co.T, grad_m, grad_mo.T, gains[3:],
+        grad_of["a"][0], grad_of["a"][1].T, mlp_grads["f"][0], mlp_grads["f"][1].T, gains[:3],
+        grad_of["s"][0], grad_of["s"][1].T, grad_c, grad_of["c"][1].T, mlp_grads["m"][0], mlp_grads["m"][1].T,
+        gains[3:],
     )
     return (
-        dec_out.reshape(cotangent.shape),
-        enc_out.reshape(enc_in.shape),
-        dec_out_grad.reshape(dec_in.shape),
-    ) + tuple(grads)
+        v["dec_out"].reshape(cotangent.shape),
+        v["enc_out"].reshape(enc_in.shape),
+        v["dec_out_grad"].reshape(dec_in.shape),
+    ) + grads
 
 
 def solution(mesh):

time: 312 us -> 297 us (0.952)
  waiting for transfers between devices: 195 us -> 185 us
  starting transfers between devices: 51.2 us -> 44.8 us
  Pallas kernels: 46.6 us -> 51 us
  local copies, waits for them, and re-layouts: 16.3 us -> 12.4 us
    ppermute x45 -> x26, starting transfers between devices: 36.6 us -> 21.5 us  [swap(): return lax.ppermute(value, 'dp', [(i, i ^ 1 << bit) for i in range(shards)])]
    ppermute x11 -> x14, starting transfers between devices: 14.6 us -> 23.3 us  [pair_other(): return lax.ppermute(part, 'mp', [(0, 1), (1, 0)])]
    ppermute x11 -> x14, waiting for transfers between devices: 52.9 us -> 46.8 us  [pair_other(): return lax.ppermute(part, 'mp', [(0, 1), (1, 0)])]
    pallas_call x47, Pallas kernels: 46.6 us -> 51 us  [call(): pl.pallas_call(run, out_shape=shapes, in_specs=in_specs, out_specs=[VMEM]...]
    unnamed x92 -> x78, local copies, waits for them, and re-layouts: 16.2 us -> 12.3 us
    ppermute x45 -> x26, waiting for transfers between devices: 142 us -> 138 us  [swap(): return lax.ppermute(value, 'dp', [(i, i ^ 1 << bit) for i in range(shards)])]
  transfers between devices with their start and end apart: 56 -> 40, of which waited for: 31 -> 23; matrix products, arithmetic and copies ran while one was open for 0% -> 1% of each run, Pallas kernels for 10% -> 15%
where the time goes in v5:
time: 297 us; the launch traced here: 296 us
  waiting for transfers between devices  185 us (62%)
  Pallas kernels  51 us (17%)
  starting transfers between devices  44.8 us (15%)
  local copies, waits for them, and re-layouts  12.4 us (4%)
    ppermute x26, waiting for transfers between devices, swap(): return lax.ppermute(value, 'dp', [(i, i ^ 1 << bit) for i in range(shards)])  138 us
    pallas_call x47, Pallas kernels, call(): pl.pallas_call(run, out_shape=shapes, in_specs=in_specs, out_specs=[VMEM]...  51 us
    ppermute x14, waiting for transfers between devices, pair_other(): return lax.ppermute(part, 'mp', [(0, 1), (1, 0)])  46.8 us
    ppermute x14, starting transfers between devices, pair_other(): return lax.ppermute(part, 'mp', [(0, 1), (1, 0)])  23.3 us
    ppermute x26, starting transfers between devices, swap(): return lax.ppermute(value, 'dp', [(i, i ^ 1 << bit) for i in range(shards)])  21.5 us
    unnamed x78, local copies, waits for them, and re-layouts  12.3 us
  transfers between devices with their start and end apart: 40, of which 23 were waited for; matrix products, arithmetic and copies ran while one was open for 1% of the time, Pallas kernels for 15%

profile of v5, /device:TPU:0, one launch (start us, length us, event | category | flops | bytes accessed | tf_op | source)
XLA Modules:
  0.0 296.1 jit_solution(6152056760492260507)
XLA Ops:
  2.4 2.5 enc_attn_fwd.2
  5.7 3.0 %collective-permute-start = (f32[128,768]{1,0:T(8,128)}, f32[128,768]{1,0:T(8,128)}, u32[]{:S(2)}, u32[]{:S(2)}) collective-permute-start(f32[128,768]{1,0:T(8,128)} %get-tuple-element.109.refs_5_.refs_1_), channel_id=1, source_target_pairs={{0,1},{1,0},{2,3},{3,2},{4,5},{5,4},{6,7},{7,6},{8,9},{9,8},{10,11... | collective-permute-start | bytes 1179656 | tf_op jit(solution)/shard_map/pair_e1/ppermute | solution.py:576
  8.7 2.5 enc_attn_fwd.3
  12.1 2.5 dec_self_fwd.1
  23.6 3.8 %collective-permute-done.3.refs_2_ = f32[128,768]{1,0:T(8,128)} collective-permute-done((f32[128,768]{1,0:T(8,128)}, f32[128,768]{1,0:T(8,128)}, u32[]{:S(2)}, u32[]{:S(2)}) %collective-permute-start.3) | collective-permute-done | bytes 393248 | tf_op jit(solution)/shard_map/pair_e1/ppermute | solution.py:576
  27.4 2.4 enc_mlp_fwd.3
  32.0 3.8 %collective-permute-done.2.refs_7_ = f32[128,768]{1,0:T(8,128)} collective-permute-done((f32[128,768]{1,0:T(8,128)}, f32[128,768]{1,0:T(8,128)}, u32[]{:S(2)}, u32[]{:S(2)}) %collective-permute-start.2) | collective-permute-done | bytes 393248 | tf_op jit(solution)/shard_map/pair_d1/ppermute | solution.py:576
  35.8 8.3 %collective-permute-done.1.refs_3_ = f32[128,768]{1,0:T(8,128)S(1)} collective-permute-done((f32[128,768]{1,0:T(8,128)S(1)}, f32[128,768]{1,0:T(8,128)S(1)}, u32[]{:S(2)}, u32[]{:S(2)}) %collective-permute-start.1) | collective-permute-done | bytes 393248 | tf_op jit(solution)/shard_map/pair_e2/ppermute | solution.py:576
  48.6 4.0 %collective-permute-done.4.refs_3_ = f32[128,768]{1,0:T(8,128)S(1)} collective-permute-done((f32[128,768]{1,0:T(8,128)S(1)}, f32[128,768]{1,0:T(8,128)S(1)}, u32[]{:S(2)}, u32[]{:S(2)}) %collective-permute-start.4) | collective-permute-done | bytes 393248 | tf_op jit(solution)/shard_map/pair_e2/ppermute | solution.py:576
  57.1 3.6 %collective-permute-done.6.refs_5_ = f32[64,768]{1,0:T(8,128)S(1)} collective-permute-done((f32[64,768]{1,0:T(8,128)S(1)}, f32[64,768]{1,0:T(8,128)S(1)}, u32[]{:S(2)}, u32[]{:S(2)}) %collective-permute-start.6) | collective-permute-done | bytes 196640 | tf_op jit(solution)/shard_map/pair_d2/ppermute | solution.py:576
  60.7 2.5 dec_mlp.1
  63.3 3.9 %collective-permute-done.8.refs_1_ = f32[128,3840]{1,0:T(8,128)S(1)} collective-permute-done((f32[128,3840]{1,0:T(8,128)S(1)}, f32[128,3840]{1,0:T(8,128)S(1)}, u32[]{:S(2)}, u32[]{:S(2)}) %collective-permute-start.8) | collective-permute-done | bytes 1966112 | tf_op jit(solution)/shard_map/swap_m_bit0/ppermute | solution.py:582
  73.2 9.1 %collective-permute-done.7.refs_2_ = f32[128,768]{1,0:T(8,128)S(1)} collective-permute-done((f32[128,768]{1,0:T(8,128)S(1)}, f32[128,768]{1,0:T(8,128)S(1)}, u32[]{:S(2)}, u32[]{:S(2)}) %collective-permute-start.7) | collective-permute-done | bytes 393248 | tf_op jit(solution)/shard_map/pair_g3/ppermute | solution.py:576
  82.3 4.8 %cross_back.1 = (f32[256,768]{1,0:T(8,128)S(1)}, f32[128,768]{1,0:T(8,128)S(1)}, f32[1,768]{1,0:T(1,128)S(1)}, f32[128,3840]{1,0:T(8,128)S(1)}, bf16[128,3840]{1,0:T(8,128)(2,1)S(1)}) custom-call(s32[2]{0:T(128)S(1)} %copy-done.26, f32[128,768]{1,0:T(8,128)S(1)} %get-tuple-element.122.refs_1_, f32[128,768]{1,0:T(8,128)S(1)} %collective-permute-done.7.refs_2_, ...), custom_call_target="tpu_custom_call" | custom-call | flops 3449999872 | bytes 11070000 | tf_op jit(solution)/shard_map/cross_back/pallas_call | solution.py:538
  89.9 15.4 %collective-permute-done.10.refs_1_ = f32[192,2048]{1,0:T(8,128)S(1)} collective-permute-done((f32[192,2048]{1,0:T(8,128)S(1)}, f32[192,2048]{1,0:T(8,128)S(1)}, u32[]{:S(2)}, u32[]{:S(2)}) %collective-permute-start.10) | collective-permute-done | bytes 1572896 | tf_op jit(solution)/shard_map/swap_m_bit1/ppermute | solution.py:582
  105.5 3.1 %enc_mlp_back.1 = (f32[256,768]{1,0:T(8,128)S(1)}, f32[256,768]{1,0:T(8,128)S(1)}, f32[1,768]{1,0:T(1,128)S(1)}, f32[256,1280]{1,0:T(8,128)S(1)}, f32[256,1280]{...) custom-call(f32[256,768]{1,0:T(8,128)S(1)} %get-tuple-element.127.refs_0_, ...), custom_call_target="tpu_custom_call" | custom-call | flops 345000000 | bytes 1107000 | tf_op jit(solution)/shard_map/enc_mlp_back/pallas_call | solution.py:538
  109.3 3.9 %collective-permute-done.16.refs_1_ = f32[96,1024]{1,0:T(8,128)S(1)} collective-permute-done((f32[96,1024]{1,0:T(8,128)S(1)}, f32[96,1024]{1,0:T(8,128)S(1)}, u32[]{:S(2)}, u32[]{:S(2)}) %collective-permute-start.16) | collective-permute-done | bytes 393248 | tf_op jit(solution)/shard_map/swap_mo_bit1/ppermute | solution.py:582
  115.9 2.6 collective-permute-start.22
  123.7 19.4 %collective-permute-done.18.refs_1_ = f32[192,1536]{1,0:T(8,128)S(1)} collective-permute-done((f32[192,1536]{1,0:T(8,128)S(1)}, f32[192,1536]{1,0:T(8,128)S(1)}, u32[]{:S(2)}, u32[]{:S(2)}) %collective-permute-start.18) | collective-permute-done | bytes 1179680 | tf_op jit(solution)/shard_map/swap_c_bit1/ppermute | solution.py:582
  146.9 5.5 %enc_attn_back.1 = (f32[256,768]{1,0:T(8,128)S(1)}, f32[256,768]{1,0:T(8,128)S(1)}, f32[1,768]{1,0:T(1,128)S(1)}, f32[256,2304]{1,0:T(8,128)S(1)}, bf16[256,2304]{1,0:T(8,128)(2,1)S(1)}) custom-call(s32[2]{0:T(128)S(1)} %copy-done.26, f32[256,768]{1,0:T(8,128)S(1)} %get-tuple-element.155.refs_1_, f32[256,768]{1,0:T(8,128)S(1)} %collective-permute-done.23.refs_2_, ...), custom_call_target="tpu_custom_call" | custom-call | flops 345000000 | bytes 1107000 | tf_op jit(solution)/shard_map/enc_attn_back/pallas_call | solution.py:538
  154.2 2.7 collective-permute-start.24
  160.2 14.9 %collective-permute-done.24.refs_1_ = f32[48,2048]{1,0:T(8,128)S(1)} collective-permute-done((f32[48,2048]{1,0:T(8,128)S(1)}, f32[48,2048]{1,0:T(8,128)S(1)}, u32[]{:S(2)}, u32[]{:S(2)}) %collective-permute-start.24) | collective-permute-done | bytes 393248 | tf_op jit(solution)/shard_map/swap_m_bit3/ppermute | solution.py:582
  177.9 3.5 %dec_self_back.1 = (f32[128,768]{1,0:T(8,128)S(1)}, f32[128,768]{1,0:T(8,128)S(1)}, f32[1,768]{1,0:T(1,128)S(1)}, f32[128,2304]{1,0:T(8,128)S(1)}, bf16[128,2304]{1,0:T(8,128)(2,1)S(1)}) custom-call(s32[2]{0:T(128)S(1)} %copy-done.28, f32[128,768]{1,0:T(8,128)S(1)} %query_part.1.refs_13_.refs_1_, f32[128,768]{1,0:T(8,128)S(1)} %collective-permute-done.19.refs_2_, ...), custom_call_target="tpu_custom_call" | custom-call | flops 1150000000 | bytes 3690000 | tf_op jit(solution)/shard_map/dec_self_back/pallas_call | solution.py:538
  183.6 8.6 %collective-permute-done.17.refs_1_ = f32[192,3072]{1,0:T(8,128)S(1)} collective-permute-done((f32[192,3072]{1,0:T(8,128)S(1)}, f32[192,3072]{1,0:T(8,128)S(1)}, u32[]{:S(2)}, u32[]{:S(2)}) %collective-permute-start.17) | collective-permute-done | bytes 2359328 | tf_op jit(solution)/shard_map/swap_f_bit1/ppermute | solution.py:582
  192.2 2.6 collective-permute-start.32
  196.8 5.1 %collective-permute-done.28.refs_1_ = f32[256,768]{1,0:T(8,128)S(1)} collective-permute-done((f32[256,768]{1,0:T(8,128)S(1)}, f32[256,768]{1,0:T(8,128)S(1)}, u32[]{:S(2)}, u32[]{:S(2)}) %collective-permute-start.28) | collective-permute-done | bytes 786464 | tf_op jit(solution)/shard_map/pair_ge/ppermute | solution.py:576
  202.0 8.0 %collective-permute-done.29.refs_6_ = f32[128,768]{1,0:T(8,128)S(1)} collective-permute-done((f32[128,768]{1,0:T(8,128)S(1)}, f32[128,768]{1,0:T(8,128)S(1)}, u32[]{:S(2)}, u32[]{:S(2)}) %collective-permute-start.29) | collective-permute-done | bytes 393248 | tf_op jit(solution)/shard_map/pair_g0/ppermute | solution.py:576
  216.3 12.8 %collective-permute-done.26.refs_1_ = f32[96,3072]{1,0:T(8,128)S(1)} collective-permute-done((f32[96,3072]{1,0:T(8,128)S(1)}, f32[96,3072]{1,0:T(8,128)S(1)}, u32[]{:S(2)}, u32[]{:S(2)}) %collective-permute-start.26) | collective-permute-done | bytes 1179680 | tf_op jit(solution)/shard_map/swap_f_bit2/ppermute | solution.py:582
  229.7 15.5 %collective-permute-done.36.refs_1_ = f32[192,1664]{1,0:T(8,128)S(1)} collective-permute-done((f32[192,1664]{1,0:T(8,128)S(1)}, f32[192,1664]{1,0:T(8,128)S(1)}, u32[]{:S(2)}, u32[]{:S(2)}) %collective-permute-start.36) | collective-permute-done | bytes 1277984 | tf_op jit(solution)/shard_map/swap_s_bit1/ppermute | solution.py:582
  247.0 10.0 %collective-permute-done.35.refs_1_ = f32[96,1536]{1,0:T(8,128)S(1)} collective-permute-done((f32[96,1536]{1,0:T(8,128)S(1)}, f32[96,1536]{1,0:T(8,128)S(1)}, u32[]{:S(2)}, u32[]{:S(2)}) %collective-permute-start.35) | collective-permute-done | bytes 589856 | tf_op jit(solution)/shard_map/swap_a_bit1/ppermute | solution.py:582
  259.8 16.1 %collective-permute-done.38.refs_1_ = f32[96,1664]{1,0:T(8,128)S(1)} collective-permute-done((f32[96,1664]{1,0:T(8,128)S(1)}, f32[96,1664]{1,0:T(8,128)S(1)}, u32[]{:S(2)}, u32[]{:S(2)}) %collective-permute-start.38) | collective-permute-done | bytes 639008 | tf_op jit(solution)/shard_map/swap_s_bit2/ppermute | solution.py:582
  278.4 14.7 %collective-permute-done.39.refs_1_ = f32[48,1664]{1,0:T(8,128)S(1)} collective-permute-done((f32[48,1664]{1,0:T(8,128)S(1)}, f32[48,1664]{1,0:T(8,128)S(1)}, u32[]{:S(2)}, u32[]{:S(2)}) %collective-permute-start.39) | collective-permute-done | bytes 319520 | tf_op jit(solution)/shard_map/swap_s_bit3/ppermute | solution.py:582
  (179 shorter events, 73.7 us)
Async XLA Ops:
  5.7 13.3 %collective-permute-start = (f32[128,768]{1,0:T(8,128)}, f32[128,768]{1,0:T(8,128)}, u32[]{:S(2)}, u32[]{:S(2)}) collective-permute-start(f32[128,768]{1,0:T(8,128)} %get-tuple-element.109.refs_5_.refs_1_), channel_id=1, source_target_pairs={{0,1},{1,0},{2,3},{3,2},{4,5},{5,4},{6,7},{7,6},{8,9},{9,8},{10,11... | collective-permute-start | bytes 1179656 | tf_op jit(solution)/shard_map/pair_e1/ppermute | solution.py:576
  12.0 15.4 %collective-permute-start.3 = (f32[128,768]{1,0:T(8,128)}, f32[128,768]{1,0:T(8,128)}, u32[]{:S(2)}, u32[]{:S(2)}) collective-permute-start(f32[128,768]{1,0:T(8,128)} %get-tuple-element.110.refs_5_.refs_1_), channel_id=1, source_target_pairs={{0,1},{1,0},{2,3},{3,2},{4,5},{5,4},{6,7},{7,6},{8,9},{9,8},{10,11... | collective-permute-start | bytes 1179656 | tf_op jit(solution)/shard_map/pair_e1/ppermute | solution.py:576
  14.6 21.2 %collective-permute-start.2 = (f32[128,768]{1,0:T(8,128)}, f32[128,768]{1,0:T(8,128)}, u32[]{:S(2)}, u32[]{:S(2)}) collective-permute-start(f32[128,768]{1,0:T(8,128)} %get-tuple-element.111.refs_1_.refs_6_), channel_id=1, source_target_pairs={{0,1},{1,0},{2,3},{3,2},{4,5},{5,4},{6,7},{7,6},{8,9},{9,8},{10,11... | collective-permute-start | bytes 1179656 | tf_op jit(solution)/shard_map/pair_d1/ppermute | solution.py:576
  21.5 22.6 %collective-permute-start.1 = (f32[128,768]{1,0:T(8,128)S(1)}, f32[128,768]{1,0:T(8,128)S(1)}, u32[]{:S(2)}, u32[]{:S(2)}) collective-permute-start(f32[128,768]{1,0:T(8,128)S(1)} %get-tuple-element.113.refs_6_.refs_2_), channel_id=1, source_target_pairs={{0,1},{1,0},{2,3},{3,2},{4,5},{5,4},{6,7},{7,6},{8,9},{9,8},{10,11... | collective-permute-start | bytes 1179656 | tf_op jit(solution)/shard_map/pair_e2/ppermute | solution.py:576
  29.9 22.7 %collective-permute-start.4 = (f32[128,768]{1,0:T(8,128)S(1)}, f32[128,768]{1,0:T(8,128)S(1)}, u32[]{:S(2)}, u32[]{:S(2)}) collective-permute-start(f32[128,768]{1,0:T(8,128)S(1)} %get-tuple-element.114.refs_1_.refs_2_), channel_id=1, source_target_pairs={{0,1},{1,0},{2,3},{3,2},{4,5},{5,4},{6,7},{7,6},{8,9},{9,8},{10,11... | collective-permute-start | bytes 1179656 | tf_op jit(solution)/shard_map/pair_e2/ppermute | solution.py:576
  46.5 14.2 %collective-permute-start.5 = (f32[64,768]{1,0:T(8,128)S(1)}, f32[64,768]{1,0:T(8,128)S(1)}, u32[]{:S(2)}, u32[]{:S(2)}) collective-permute-start(f32[64,768]{1,0:T(8,128)S(1)} %get-tuple-element.117.refs_11_.refs_2_), channel_id=1, source_target_pairs={{0,1},{1,0},{2,3},{3,2},{4,5},{5,4},{6,7},{7,6},{8,9},{9,8},{10,11... | collective-permute-start | bytes 589832 | tf_op jit(solution)/shard_map/pair_d2/ppermute | solution.py:576
  68.1 37.3 %collective-permute-start.10 = (f32[192,2048]{1,0:T(8,128)S(1)}, f32[192,2048]{1,0:T(8,128)S(1)}, u32[]{:S(2)}, u32[]{:S(2)}) collective-permute-start(f32[192,2048]{1,0:T(8,128)S(1)} %get-tuple-element.131), channel_id=1, source_target_pairs={{0,4},{2,6},{4,0},{6,2},{8,12},{10,14},{12,8},{14,10},{16,20},{18,... | collective-permute-start | bytes 4718600 | tf_op jit(solution)/shard_map/swap_m_bit1/ppermute | solution.py:582
  70.1 19.3 %collective-permute-start.11 = (f32[192,1024]{1,0:T(8,128)S(1)}, f32[192,1024]{1,0:T(8,128)S(1)}, u32[]{:S(2)}, u32[]{:S(2)}) collective-permute-start(f32[192,1024]{1,0:T(8,128)S(1)} %get-tuple-element.126.refs_1_), channel_id=1, source_target_pairs={{0,8},{2,10},{4,12},{6,14},{8,0},{10,2},{12,4},{14,6},{16,24},{18,... | collective-permute-start | bytes 2359304 | tf_op jit(solution)/shard_map/swap_mo_bit2/ppermute | solution.py:582
  87.1 18.5 %collective-permute-start.9 = (f32[256,768]{1,0:T(8,128)S(1)}, f32[256,768]{1,0:T(8,128)S(1)}, u32[]{:S(2)}, u32[]{:S(2)}) collective-permute-start(f32[256,768]{1,0:T(8,128)S(1)} %get-tuple-element.127.refs_0_), channel_id=1, source_target_pairs={{0,1},{1,0},{2,3},{3,2},{4,5},{5,4},{6,7},{7,6},{8,9},{9,8},{10,11... | collective-permute-start | bytes 2359304 | tf_op jit(solution)/shard_map/pair_m/ppermute | solution.py:576
  88.7 24.6 %collective-permute-start.15 = (f32[128,3840]{1,0:T(8,128)S(1)}, f32[128,3840]{1,0:T(8,128)S(1)}, u32[]{:S(2)}, u32[]{:S(2)}) collective-permute-start(f32[128,3840]{1,0:T(8,128)S(1)} %get-tuple-element.141), channel_id=1, source_target_pairs={{0,2},{2,0},{4,6},{6,4},{8,10},{10,8},{12,14},{14,12},{16,18},{18,... | collective-permute-start | bytes 5898248 | tf_op jit(solution)/shard_map/swap_c_bit0/ppermute | solution.py:582
  89.5 23.7 %collective-permute-start.16 = (f32[96,1024]{1,0:T(8,128)S(1)}, f32[96,1024]{1,0:T(8,128)S(1)}, u32[]{:S(2)}, u32[]{:S(2)}) collective-permute-start(f32[96,1024]{1,0:T(8,128)S(1)} %get-tuple-element.134.refs_2_), channel_id=1, source_target_pairs={{0,4},{2,6},{4,0},{6,2},{8,12},{10,14},{12,8},{14,10},{16,20},{18,... | collective-permute-start | bytes 1179656 | tf_op jit(solution)/shard_map/swap_mo_bit1/ppermute | solution.py:582
  114.1 29.0 %collective-permute-start.18 = (f32[192,1536]{1,0:T(8,128)S(1)}, f32[192,1536]{1,0:T(8,128)S(1)}, u32[]{:S(2)}, u32[]{:S(2)}) collective-permute-start(f32[192,1536]{1,0:T(8,128)S(1)} %get-tuple-element.145.refs_4_), channel_id=1, source_target_pairs={{0,4},{2,6},{4,0},{6,2},{8,12},{10,14},{12,8},{14,10},{16,20},{18,... | collective-permute-start | bytes 3538952 | tf_op jit(solution)/shard_map/swap_c_bit1/ppermute | solution.py:582
  115.9 36.6 %collective-permute-start.22 = (f32[48,1024]{1,0:T(8,128)S(1)}, f32[48,1024]{1,0:T(8,128)S(1)}, u32[]{:S(2)}, u32[]{:S(2)}) collective-permute-start(f32[48,1024]{1,0:T(8,128)S(1)} %get-tuple-element.144.refs_2_), channel_id=1, source_target_pairs={{0,16},{2,18},{4,20},{6,22},{8,24},{10,26},{12,28},{14,30},{16,0},... | collective-permute-start | bytes 589832 | tf_op jit(solution)/shard_map/swap_mo_bit3/ppermute | solution.py:582
  118.5 34.7 %collective-permute-start.21 = (f32[96,2048]{1,0:T(8,128)S(1)}, f32[96,2048]{1,0:T(8,128)S(1)}, u32[]{:S(2)}, u32[]{:S(2)}) collective-permute-start(f32[96,2048]{1,0:T(8,128)S(1)} %get-tuple-element.135.refs_1_), channel_id=1, source_target_pairs={{0,8},{2,10},{4,12},{6,14},{8,0},{10,2},{12,4},{14,6},{16,24},{18,... | collective-permute-start | bytes 2359304 | tf_op jit(solution)/shard_map/swap_m_bit2/ppermute | solution.py:582
  120.1 25.4 %collective-permute-start.23 = (f32[256,768]{1,0:T(8,128)S(1)}, f32[256,768]{1,0:T(8,128)S(1)}, u32[]{:S(2)}, u32[]{:S(2)}) collective-permute-start(f32[256,768]{1,0:T(8,128)S(1)} %get-tuple-element.155.refs_1_), channel_id=1, source_target_pairs={{0,1},{1,0},{2,3},{3,2},{4,5},{5,4},{6,7},{7,6},{8,9},{9,8},{10,11... | collective-permute-start | bytes 2359304 | tf_op jit(solution)/shard_map/pair_g1/ppermute | solution.py:576
  123.1 69.1 %collective-permute-start.17 = (f32[192,3072]{1,0:T(8,128)S(1)}, f32[192,3072]{1,0:T(8,128)S(1)}, u32[]{:S(2)}, u32[]{:S(2)}) collective-permute-start(f32[192,3072]{1,0:T(8,128)S(1)} %get-tuple-element.147.refs_2_), channel_id=1, source_target_pairs={{0,4},{2,6},{4,0},{6,2},{8,12},{10,14},{12,8},{14,10},{16,20},{18,... | collective-permute-start | bytes 7077896 | tf_op jit(solution)/shard_map/swap_f_bit1/ppermute | solution.py:582
  143.2 32.7 %collective-permute-start.20 = (f32[96,1536]{1,0:T(8,128)S(1)}, f32[96,1536]{1,0:T(8,128)S(1)}, u32[]{:S(2)}, u32[]{:S(2)}) collective-permute-start(f32[96,1536]{1,0:T(8,128)S(1)} %get-tuple-element.149.refs_1_), channel_id=1, source_target_pairs={{0,8},{2,10},{4,12},{6,14},{8,0},{10,2},{12,4},{14,6},{16,24},{18,... | collective-permute-start | bytes 1769480 | tf_op jit(solution)/shard_map/swap_c_bit2/ppermute | solution.py:582
  154.2 20.8 %collective-permute-start.24 = (f32[48,2048]{1,0:T(8,128)S(1)}, f32[48,2048]{1,0:T(8,128)S(1)}, u32[]{:S(2)}, u32[]{:S(2)}) collective-permute-start(f32[48,2048]{1,0:T(8,128)S(1)} %get-tuple-element.161.refs_2_), channel_id=1, source_target_pairs={{0,16},{2,18},{4,20},{6,22},{8,24},{10,26},{12,28},{14,30},{16,0},... | collective-permute-start | bytes 1179656 | tf_op jit(solution)/shard_map/swap_m_bit3/ppermute | solution.py:582
  156.9 20.1 %collective-permute-start.19 = (f32[128,768]{1,0:T(8,128)S(1)}, f32[128,768]{1,0:T(8,128)S(1)}, u32[]{:S(2)}, u32[]{:S(2)}) collective-permute-start(f32[128,768]{1,0:T(8,128)S(1)} %query_part.1.refs_13_.refs_1_), channel_id=1, source_target_pairs={{0,1},{1,0},{2,3},{3,2},{4,5},{5,4},{6,7},{7,6},{8,9},{9,8},{10,11... | collective-permute-start | bytes 1179656 | tf_op jit(solution)/shard_map/pair_q/ppermute | solution.py:576
  159.7 37.0 %collective-permute-start.30 = (f32[192,1536]{1,0:T(8,128)S(1)}, f32[192,1536]{1,0:T(8,128)S(1)}, u32[]{:S(2)}, u32[]{:S(2)}) collective-permute-start(f32[192,1536]{1,0:T(8,128)S(1)} %get-tuple-element.164.refs_2_), channel_id=1, source_target_pairs={{0,8},{2,10},{4,12},{6,14},{8,0},{10,2},{12,4},{14,6},{16,24},{18,... | collective-permute-start | bytes 3538952 | tf_op jit(solution)/shard_map/swap_a_bit2/ppermute | solution.py:582
  181.5 31.4 %collective-permute-start.27 = (f32[128,2304]{1,0:T(8,128)S(1)}, f32[128,2304]{1,0:T(8,128)S(1)}, u32[]{:S(2)}, u32[]{:S(2)}) collective-permute-start(f32[128,2304]{1,0:T(8,128)S(1)} %get-tuple-element.170), channel_id=1, source_target_pairs={{0,2},{2,0},{4,6},{6,4},{8,10},{10,8},{12,14},{14,12},{16,18},{18,... | collective-permute-start | bytes 3538952 | tf_op jit(solution)/shard_map/swap_s_bit0/ppermute | solution.py:582
  181.5 20.4 %collective-permute-start.28 = (f32[256,768]{1,0:T(8,128)S(1)}, f32[256,768]{1,0:T(8,128)S(1)}, u32[]{:S(2)}, u32[]{:S(2)}) collective-permute-start(f32[256,768]{1,0:T(8,128)S(1)} %get-tuple-element.171.refs_0_), channel_id=1, source_target_pairs={{0,1},{1,0},{2,3},{3,2},{4,5},{5,4},{6,7},{7,6},{8,9},{9,8},{10,11... | collective-permute-start | bytes 2359304 | tf_op jit(solution)/shard_map/pair_ge/ppermute | solution.py:576
  183.2 26.7 %collective-permute-start.29 = (f32[128,768]{1,0:T(8,128)S(1)}, f32[128,768]{1,0:T(8,128)S(1)}, u32[]{:S(2)}, u32[]{:S(2)}) collective-permute-start(f32[128,768]{1,0:T(8,128)S(1)} %get-tuple-element.173.refs_5_), channel_id=1, source_target_pairs={{0,1},{1,0},{2,3},{3,2},{4,5},{5,4},{6,7},{7,6},{8,9},{9,8},{10,11... | collective-permute-start | bytes 1179656 | tf_op jit(solution)/shard_map/pair_g0/ppermute | solution.py:576
  192.2 19.9 %collective-permute-start.32 = (f32[48,1536]{1,0:T(8,128)S(1)}, f32[48,1536]{1,0:T(8,128)S(1)}, u32[]{:S(2)}, u32[]{:S(2)}) collective-permute-start(f32[48,1536]{1,0:T(8,128)S(1)} %get-tuple-element.165.refs_12_), channel_id=1, source_target_pairs={{0,16},{2,18},{4,20},{6,22},{8,24},{10,26},{12,28},{14,30},{16,0},... | collective-permute-start | bytes 884744 | tf_op jit(solution)/shard_map/swap_c_bit3/ppermute | solution.py:582
  196.6 32.5 %collective-permute-start.26 = (f32[96,3072]{1,0:T(8,128)S(1)}, f32[96,3072]{1,0:T(8,128)S(1)}, u32[]{:S(2)}, u32[]{:S(2)}) collective-permute-start(f32[96,3072]{1,0:T(8,128)S(1)} %get-tuple-element.168.refs_2_), channel_id=1, source_target_pairs={{0,8},{2,10},{4,12},{6,14},{8,0},{10,2},{12,4},{14,6},{16,24},{18,... | collective-permute-start | bytes 3538952 | tf_op jit(solution)/shard_map/swap_f_bit2/ppermute | solution.py:582
  214.2 31.0 %collective-permute-start.36 = (f32[192,1664]{1,0:T(8,128)S(1)}, f32[192,1664]{1,0:T(8,128)S(1)}, u32[]{:S(2)}, u32[]{:S(2)}) collective-permute-start(f32[192,1664]{1,0:T(8,128)S(1)} %get-tuple-element.181.refs_2_), channel_id=1, source_target_pairs={{0,4},{2,6},{4,0},{6,2},{8,12},{10,14},{12,8},{14,10},{16,20},{18,... | collective-permute-start | bytes 3833864 | tf_op jit(solution)/shard_map/swap_s_bit1/ppermute | solution.py:582
  215.8 41.2 %collective-permute-start.35 = (f32[96,1536]{1,0:T(8,128)S(1)}, f32[96,1536]{1,0:T(8,128)S(1)}, u32[]{:S(2)}, u32[]{:S(2)}) collective-permute-start(f32[96,1536]{1,0:T(8,128)S(1)} %get-tuple-element.176.refs_15_), channel_id=1, source_target_pairs={{0,4},{2,6},{4,0},{6,2},{8,12},{10,14},{12,8},{14,10},{16,20},{18,... | collective-permute-start | bytes 1769480 | tf_op jit(solution)/shard_map/swap_a_bit1/ppermute | solution.py:582
  229.2 27.9 %collective-permute-start.34 = (f32[48,3072]{1,0:T(8,128)S(1)}, f32[48,3072]{1,0:T(8,128)S(1)}, u32[]{:S(2)}, u32[]{:S(2)}) collective-permute-start(f32[48,3072]{1,0:T(8,128)S(1)} %get-tuple-element.182.refs_2_), channel_id=1, source_target_pairs={{0,16},{2,18},{4,20},{6,22},{8,24},{10,26},{12,28},{14,30},{16,0},... | collective-permute-start | bytes 1769480 | tf_op jit(solution)/shard_map/swap_f_bit3/ppermute | solution.py:582
  245.3 30.6 %collective-permute-start.38 = (f32[96,1664]{1,0:T(8,128)S(1)}, f32[96,1664]{1,0:T(8,128)S(1)}, u32[]{:S(2)}, u32[]{:S(2)}) collective-permute-start(f32[96,1664]{1,0:T(8,128)S(1)} %get-tuple-element.186.refs_2_), channel_id=1, source_target_pairs={{0,8},{2,10},{4,12},{6,14},{8,0},{10,2},{12,4},{14,6},{16,24},{18,... | collective-permute-start | bytes 1916936 | tf_op jit(solution)/shard_map/swap_s_bit2/ppermute | solution.py:582
  245.4 12.7 %collective-permute-start.33 = (f32[128,768]{1,0:T(8,128)S(1)}, f32[128,768]{1,0:T(8,128)S(1)}, u32[]{:S(2)}, u32[]{:S(2)}) collective-permute-start(f32[128,768]{1,0:T(8,128)S(1)} %dec_out_part.1.refs_2_.refs_1_), channel_id=1, source_target_pairs={{0,1},{1,0},{2,3},{3,2},{4,5},{5,4},{6,7},{7,6},{8,9},{9,8},{10,11... | collective-permute-start | bytes 1179656 | tf_op jit(solution)/shard_map/pair_out/ppermute | solution.py:576
  257.1 20.6 %collective-permute-start.37 = (f32[48,1536]{1,0:T(8,128)S(1)}, f32[48,1536]{1,0:T(8,128)S(1)}, u32[]{:S(2)}, u32[]{:S(2)}) collective-permute-start(f32[48,1536]{1,0:T(8,128)S(1)} %get-tuple-element.187.refs_2_), channel_id=1, source_target_pairs={{0,16},{2,18},{4,20},{6,22},{8,24},{10,26},{12,28},{14,30},{16,0},... | collective-permute-start | bytes 884744 | tf_op jit(solution)/shard_map/swap_a_bit3/ppermute | solution.py:582
  276.9 16.2 %collective-permute-start.39 = (f32[48,1664]{1,0:T(8,128)S(1)}, f32[48,1664]{1,0:T(8,128)S(1)}, u32[]{:S(2)}, u32[]{:S(2)}) collective-permute-start(f32[48,1664]{1,0:T(8,128)S(1)} %get-tuple-element.193.refs_2_), channel_id=1, source_target_pairs={{0,16},{2,18},{4,20},{6,22},{8,24},{10,26},{12,28},{14,30},{16,0},... | collective-permute-start | bytes 958472 | tf_op jit(solution)/shard_map/swap_s_bit3/ppermute | solution.py:582
  (46 other events, 206.0 us)

commit v6 on v5

--- a/solution.py
+++ b/solution.py
@@ -29,17 +29,23 @@
     return lax.dot_general(left, right, (((0,), (0,)), ((), ())), preferred_element_type=F32)
 
 
+def scaled(hidden):
+    return hidden * lax.rsqrt(jnp.mean(hidden * hidden, -1, keepdims=True) + EPSILON)
+
+
 def norm(hidden, gain):
-    scaling = lax.rsqrt(jnp.mean(hidden * hidden, -1, keepdims=True) + EPSILON)
-    return (hidden * scaling * gain).astype(BF)
+    return (scaled(hidden) * gain).astype(BF)
 
 
 def norm_back(grad, hidden, gain):
     scaling = lax.rsqrt(jnp.mean(hidden * hidden, -1, keepdims=True) + EPSILON)
     normed = hidden * scaling
     grad_hat = grad * gain
-    grad_in = scaling * (grad_hat - normed * jnp.mean(grad_hat * normed, -1, keepdims=True))
-    return grad_in, jnp.sum(grad * normed, 0, keepdims=True)
+    return scaling * (grad_hat - normed * jnp.mean(grad_hat * normed, -1, keepdims=True)), normed
+
+
+def gain_part(part, normed):
+    return jnp.sum(part * normed, 0, keepdims=True)
 
 
 def gelu_parts(gate):
@@ -226,12 +232,23 @@
     put_cut(send, keep, half + 2 * width, low, order_outer)
 
 
-def sum_kernel(state, own, other, out):
-    out[...] = (state[...] + own[...] + other[...]).astype(BF)
-
-
-def out_part_kernel(keep, outer, part):
-    part[...] = mm(keep[:, keep.shape[1] - outer.shape[0] :], outer[...])
+def tail_parts_kernel(enc_part, dec_part, keep, outer, part):
+    enc_rows, dec_rows = enc_part.shape[0], dec_part.shape[0]
+    part[:enc_rows, :] = enc_part[...]
+    part[enc_rows : enc_rows + dec_rows, :] = dec_part[...]
+    part[enc_rows + dec_rows :, :] = mm(keep[:, keep.shape[1] - outer.shape[0] :], outer[...])
+
+
+def tail_kernel(own, other, enc_state, enc_gain, enc_grad, dec_state, dec_gain, dec_grad, state, enc_out, dec_out, out):
+    enc_rows, dec_rows = enc_out.shape[0], dec_out.shape[0]
+    span = slice(0, enc_rows)
+    grad_in, _ = norm_back(own[span, :] + other[span, :], enc_state[...].astype(F32), enc_gain[0:1, :])
+    enc_out[...] = (enc_grad[...] + grad_in).astype(BF)
+    span = slice(enc_rows, enc_rows + dec_rows)
+    grad_in, _ = norm_back(own[span, :] + other[span, :], dec_state[...].astype(F32), dec_gain[0:1, :])
+    dec_out[...] = (dec_grad[...] + grad_in).astype(BF)
+    span = slice(enc_rows + dec_rows, enc_rows + 2 * dec_rows)
+    out[...] = (state[...] + own[span, :] + other[span, :]).astype(BF)
 
 
 def query_part_kernel(keep, stacked, part):
@@ -243,7 +260,8 @@
     length, counts, own, other, state, gain, grad, outer, query, kv, stacked, order, dec_state, enc_state, enc_gain,
     part, grad_ref, gain_ref, send, keep, key_grads,
 ):
-    grad_in, gain_ref[...] = norm_back(own[...] + other[...], state[...], gain[2:3, :])
+    grad_in, normed = norm_back(own[...] + other[...], state[...], gain[2:3, :])
+    gain_ref[...] = gain_part(own[...], normed)
     full = grad[...].astype(F32) + grad_in
     grad_ref[...] = full
     flush(gain_ref, grad_ref)
@@ -284,7 +302,8 @@
     causal, length, counts, own, other, state, gain, grad, outer, qkv, stacked, order, inputs,
     part, grad_ref, gain_ref, send, keep,
 ):
-    grad_in, gain_ref[...] = norm_back(own[...] + other[...], state[...], gain[1:2, :])
+    grad_in, normed = norm_back(own[...] + other[...], state[...], gain[1:2, :])
+    gain_ref[0:1, :] = gain_part(own[...], normed)
     full = grad[...] + grad_in
     grad_ref[...] = full
     flush(gain_ref, grad_ref)
@@ -310,8 +329,9 @@
     total += mm_nt(keep[:, half + width : half + 2 * width], stacked[1])
     total += mm_nt(keep[:, half + 2 * width : half + 3 * width], stacked[2])
     part[...] = total
-    part.flush()
-    put_cut(send, keep, 0, norm(inputs[...].astype(F32), gain[0:1, :]), order)
+    normed = scaled(inputs[...].astype(F32))
+    gain_ref[1:2, :] = gain_part(total, normed)
+    put_cut(send, keep, 0, (normed * gain[0:1, :]).astype(BF), order)
     at = put_cut(send, keep, half + 3 * width, low, order)
     put_both(send, keep, at, qkv[:, 3 * width : 4 * width])
 
@@ -320,7 +340,8 @@
     own, other, state, gain, outer, pre, inner, order, order_outer, middle,
     part, grad_ref, gain_ref, send, keep,
 ):
-    full, gain_ref[...] = norm_back(own[...] + other[...], state[...], gain[2:3, :])
+    full, normed = norm_back(own[...] + other[...], state[...], gain[2:3, :])
+    gain_ref[...] = gain_part(own[...], normed)
     grad_ref[...] = full
     flush(gain_ref, grad_ref)
     low = full.astype(BF)
@@ -342,17 +363,9 @@
     put_cut(send, keep, half + 2 * width, low, order_outer)
 
 
-def last_kernel(
-    enc_own, enc_other, enc_state, enc_gain, enc_grad, dec_own, dec_other, dec_state, dec_gain, dec_grad, order,
-    e1, e2, d1, d2, enc_ref, dec_ref, send, keep,
-):
-    grad_in, e0 = norm_back(enc_own[...] + enc_other[...], enc_state[...].astype(F32), enc_gain[0:1, :])
-    enc_ref[...] = (enc_grad[...] + grad_in).astype(BF)
-    grad_in, d0 = norm_back(dec_own[...] + dec_other[...], dec_state[...].astype(F32), dec_gain[0:1, :])
-    dec_ref[...] = (dec_grad[...] + grad_in).astype(BF)
-    rest = jnp.concatenate(
-        [e0, e1[...], e2[...], d0, d1[...], d2[...], jnp.zeros((122, e0.shape[1]), F32)], 0
-    )
+def gains_kernel(enc_attn, enc_mlp, dec_self, dec_cross, order, send, keep):
+    rows = [enc_attn[1:2, :], enc_attn[0:1, :], enc_mlp[...], dec_self[1:2, :], dec_self[0:1, :], dec_cross[...]]
+    rest = jnp.concatenate(rows + [jnp.zeros((128 - len(rows), order.shape[0]), F32)], 0)
     total = None
     for _ in range(3):
         low = rest.astype(BF)
@@ -362,6 +375,14 @@
     half = total.shape[0] // 2
     send[...] = total[:half]
     keep[...] = total[half:]
+
+
+def gains_out_kernel(own, other, enc_out, dec_out):
+    total = own[...] + other[...]
+    rows, columns = total.shape
+    total = jnp.concatenate([total, jnp.zeros((columns - rows, columns), F32)], 0).T
+    enc_out[...] = total[0:3, :rows]
+    dec_out[...] = total[3:6, :rows]
 
 
 def gains_weight_kernel(segments, keep, recv, gains, other_gains, send_out, keep_out):
@@ -409,24 +430,33 @@
 
 COST = {
     "enc_attn_fwd": 2.3, "dec_self_fwd": 2.5, "enc_mlp_fwd": 1.7, "cross_fwd": 4.2, "dec_mlp": 2.7,
-    "dec_out_part": 3, "finish_f": 0.3, "query_part": 3, "weights_f": 0.1, "cross_back": 3,
-    "dec_self_back": 1, "halve_s": 3, "weights_m": 8, "weights_a": 0.3, "halve_m": 20,
-    "halve_f": 0.3,
+    "cross_back": 0.1, "dec_self_back": 0.3, "enc_attn_back": 0.1, "enc_mlp_back": 8, "finish_a": 20,
+    "finish_c": 3, "finish_f": 20, "finish_fo": 20, "finish_m": 0.1, "finish_mo": 3,
+    "finish_s": 0.3, "gains": 20, "gains_out": 8, "halve_a": 3, "halve_c": 3,
+    "halve_f": 0.3, "halve_fo": 0.3, "halve_m": 1, "halve_mo": 0.3, "halve_s": 0.3,
+    "query_part": 8, "tail": 3, "tail_parts": 0.1, "weights_a": 8, "weights_c": 3,
+    "weights_f": 3, "weights_m": 0.3, "weights_s": 0.1,
 }
 VMEM_LIMIT = 8
 
 LINE = (
     "pause", "enc_attn_0", "enc_attn_1", "dec_self", "pause", "enc_mlp_0", "enc_mlp_1", "pause",
-    "cross_0", "cross_1", "pause", "dec_mlp", "tick", "w_m", "tick", "cross_back",
-    "h_mo", "h_m", "tick", "enc_mlp_back", "h_mo", "w_c", "w_f", "h_c",
-    "tick", "query_part", "enc_attn_back", "e_mo", "h_m", "w_a", "e_m", "h_c",
-    "dec_self_back", "h_f", "h_a", "input_grads", "e_c", "w_s", "h_f", "out_part",
-    "h_s", "h_a", "e_f", "dec_out", "h_s", "e_a", "e_s",
+    "cross_0", "cross_1", "pause", "dec_mlp", "tick", "w_m", "cross_back", "tick",
+    "tick", "tick", "tick", "tick", "tick", "tick", "tick", "tick",
+    "tick", "tick", "tick", "tick", "tick", "tick", "tick", "tick",
+    "tick", "tick", "w_c", "tick", "tick", "tick", "enc_mlp_back", "tick",
+    "tick", "tick", "tick", "tick", "tick", "tick", "tick", "tick",
+    "tick", "tick", "tick", "tick", "tick", "query_part", "tick", "tick",
+    "w_f", "tick", "tick", "tick", "h_c", "h_m", "enc_attn_back", "h_fo",
+    "tick", "h_f", "tick", "dec_self_back", "h_c", "tick", "gains", "w_a",
+    "w_s", "h_f", "h_c", "h_m", "tick", "tick", "tail_parts", "h_f",
+    "h_s", "h_a", "h_s", "h_m", "tail", "e_c", "h_a", "h_s",
+    "e_m", "h_fo", "h_a", "e_s", "h_fo", "e_f", "gains_out", "e_a",
+    "e_fo",
 )
-ACROSS, NEAR, FAR = 1, 2, 3
-HALVINGS = {"m": (ACROSS, NEAR, FAR), "mo": (NEAR, ACROSS, FAR), "c": (ACROSS, NEAR, FAR), "f": (ACROSS, NEAR, FAR), "a": (NEAR, ACROSS, FAR), "s": (ACROSS, NEAR, FAR)}
-PARTS = {"m": 1, "c": 1, "f": 3, "a": 1, "s": 1}
-TICK = 4
+HALVINGS = {"a": "xpme", "c": "xpme", "f": "xpme", "m": "pxme", "s": "pxme", "fo": "pxme"}
+PARTS = {"a": 1, "c": 1, "f": 1, "m": 1, "s": 1}
+TICK = 2
 GAINS_WITH = "s"
 
 
@@ -555,6 +585,18 @@
         return results
 
 
+def join_kernel(kept, recv, out):
+    out[...] = kept[...] + recv[...]
+
+
+def middle_kernel(kept, recv, send_out, keep_out):
+    rows = send_out.shape[0]
+    me = lax.axis_index("dp")
+    inner = ((me >> 2) ^ (me >> 3)) & 1
+    send_out[...] = jnp.where(inner == 1, recv[rows:], kept[:rows])
+    keep_out[...] = jnp.where(inner == 1, recv[:rows], kept[rows:])
+
+
 def finish_kernel(pieces, kept, recv, *outs):
     for out, (first, count) in zip(outs, pieces):
         width = out.shape[-1]
@@ -576,44 +618,58 @@
         return lax.ppermute(part, "mp", [(0, 1), (1, 0)])
 
 
-def swap(value, bit, name):
+def swap(value, step, name):
     shards = lax.axis_size("dp")
-    with jax.named_scope("swap_%s_bit%d" % (name, bit)):
-        return lax.ppermute(value, "dp", [(i, i ^ (1 << bit)) for i in range(shards)])
-
-
-def feature_order(features, bits_order):
+    bit = {"x": 1, "p": 2, "e": 2}.get(step, step)
+    if step == "m":
+        pairs = [(i, i ^ 12) for i in range(shards) if (i >> 2 ^ i >> 3) & 1]
+    else:
+        pairs = [(i, i ^ (1 << bit)) for i in range(shards)]
+    with jax.named_scope("swap_%s_%s" % (name, step)):
+        return lax.ppermute(value, "dp", pairs)
+
+
+def feature_order(features, steps):
     shards = lax.axis_size("dp")
     me = lax.axis_index("dp")
     block = features // shards
     column = jnp.arange(features, dtype=jnp.int32)
     place = column // block
     owner = jnp.zeros_like(column)
-    count = len(bits_order)
-    for at, bit in enumerate(bits_order):
-        own = (place >> (count - 1 - at)) & 1
-        owner = owner | ((((me >> bit) & 1) ^ (1 - own)) << bit)
+    other = {step: 1 - ((place >> (len(steps) - 1 - at)) & 1) for at, step in enumerate(steps)}
+    near = (me >> 2) & 1
+    for step in steps:
+        if step == "p":
+            owner = owner | ((near ^ other["p"]) << 3)
+        elif step == "e":
+            owner = owner | ((near ^ other["e"] ^ other["p"]) << 2)
+        else:
+            bit = 1 if step == "x" else step
+            owner = owner | ((((me >> bit) & 1) ^ other[step]) << bit)
     source = owner * block + column % block
     return (jnp.arange(features, dtype=jnp.int32)[:, None] == source[None, :]).astype(BF)
 
 
 class Halving:
-    def __init__(self, sent, kept, bits_order, name):
-        self.bits = list(bits_order[1:])
+    def __init__(self, sent, kept, steps, name):
+        self.steps, self.name, self.at = steps, name, 0
         self.kept = kept
-        self.name = name
-        self.flying = swap(sent, self.bits[0], name)
-        self.steps = 1
+        self.flying = swap(sent, steps[0], name)
 
     def step(self, line):
-        rows, columns = self.kept.shape[0] // 2, self.kept.shape[1]
-        shape = ((rows, columns), F32)
-        sent, self.kept = line.call(halve_kernel, [shape, shape], [self.kept, self.flying], "halve_" + self.name)
-        self.flying = swap(sent, self.bits[self.steps], self.name)
-        self.steps += 1
+        came, self.at = self.steps[self.at], self.at + 1
+        rows, columns = self.kept.shape
+        args, name = [self.kept, self.flying], "halve_" + self.name
+        if self.steps[self.at] == "m":
+            (self.kept,) = line.call(join_kernel, [((rows, columns), F32)], args, name)
+            sent = self.kept
+        else:
+            shape = ((rows // 2, columns), F32)
+            sent, self.kept = line.call(middle_kernel if came == "m" else halve_kernel, [shape, shape], args, name)
+        self.flying = swap(sent, self.steps[self.at], self.name)
 
     def finish(self, line, *pieces):
-        for bit in self.bits[self.steps :]:
+        for bit in range(4, lax.axis_size("dp").bit_length() - 1):
             rows = self.kept.shape[0] // 2
             total = self.kept + self.flying
             self.kept, self.flying = total[rows:], swap(total[:rows], bit, self.name)
@@ -638,22 +694,19 @@
     bits = lax.axis_size("dp").bit_length() - 1
     orders = {}
 
-    def halving(*first):
-        chosen = [0] + [bit for bit in first if bit < bits]
-        chosen = tuple(chosen + [bit for bit in range(bits) if bit not in chosen])
-        if chosen not in orders:
-            orders[chosen] = feature_order(features, chosen)
-        return chosen, orders[chosen]
-
-    halvings = {name: halving(*first) for name, first in HALVINGS.items()}
-    bits_of = {name: pair[0] for name, pair in halvings.items()}
-    order_of = {name: pair[1] for name, pair in halvings.items()}
+    def order_by(steps):
+        cuts = (0,) + tuple(step for step in steps if step != "m") + tuple(range(4, bits))
+        if cuts not in orders:
+            orders[cuts] = feature_order(features, cuts)
+        return orders[cuts]
+
+    order_of = {name: order_by(steps) for name, steps in HALVINGS.items()}
     x0 = enc_in.reshape(enc_rows, features)
     y0 = dec_in.reshape(dec_rows, features)
     top = cotangent.reshape(dec_rows, features)
     enc_wide, dec_wide = ((enc_rows, features), F32), ((dec_rows, features), F32)
     enc_low, dec_low = ((enc_rows, features), BF), ((dec_rows, features), BF)
-    gain_row = ((1, features), F32)
+    gain_row, gain_rows = ((1, features), F32), ((2, features), F32)
     quarter = half // 2
     line = Line()
 
@@ -755,10 +808,9 @@
         v["other_g3"] = pair_other(v["part_g3"], "g3")
         v["recv_m"] = swap_cores("m", send)
 
-
     def start_sums(name, products):
         for group_name, pair in zip((name, name + "o"), zip(products[::2], products[1::2])):
-            sums[group_name] = Halving(pair[0], pair[1], bits_of[group_name], group_name)
+            sums[group_name] = Halving(pair[0], pair[1], HALVINGS[group_name], group_name)
 
     def mlp_weights(name, keep, recv):
         segments, groups = mlp_of(name)
@@ -770,7 +822,7 @@
         mlp_weights("m", v["keep_m"], v["recv_m"])
 
     def cross_back():
-        v["part_m"], v["g2"], v["gain_d2"], send, v["keep_c"] = line.call(
+        v["part_m"], v["g2"], v["gain_dec_cross"], send, v["keep_c"] = line.call(
             functools.partial(cross_back_kernel, enc_len),
             [enc_wide, dec_wide, gain_row, parts_of("c", dec_rows, cross_wide), ((dec_rows, cross_wide), BF)],
             [patch_counts, v["part_g3"], v["other_g3"], v["y2"], dec_gains, top, dec_cross_out, dec_part("saved"),
@@ -786,7 +838,7 @@
         ))
 
     def enc_mlp_back():
-        v["part_g1"], v["back2"], v["gain_e2"], send, v["keep_f"] = line.call(
+        v["part_g1"], v["back2"], v["gain_enc_mlp"], send, v["keep_f"] = line.call(
             enc_mlp_back_kernel,
             [enc_wide, enc_wide, gain_row, parts_of("f", enc_rows, mlp_wide), ((enc_rows, mlp_wide), BF)],
             [v["part_m"], v["other_m"], enc_part("states"), enc_gains, enc_mlp_out, enc_part("pre"), enc_mlp_in,
@@ -800,14 +852,13 @@
         mlp_weights("f", v["keep_f"], v["recv_f"])
 
     def enc_attn_back():
-        v["part_ge"], v["back1"], v["gain_e1"], send, v["keep_a"] = line.call(
+        v["part_ge"], v["back1"], v["gain_enc_attn"], send, v["keep_a"] = line.call(
             functools.partial(self_back_kernel, False, enc_len),
-            [enc_wide, enc_wide, gain_row, parts_of("a", enc_rows, attn_wide), ((enc_rows, attn_wide), BF)],
+            [enc_wide, enc_wide, gain_rows, parts_of("a", enc_rows, attn_wide), ((enc_rows, attn_wide), BF)],
             [patch_counts, v["part_g1"], v["other_g1"], enc_part("x1"), enc_gains, v["back2"], enc_attn_out,
              enc_part("enc_saved"), enc_qkv, order_of["a"], x0],
             "enc_attn_back",
         )
-        v["other_ge"] = pair_other(v["part_ge"], "ge")
         v["recv_a"] = swap_cores("a", send)
 
     def query_part():
@@ -815,25 +866,43 @@
         v["other_q"] = pair_other(v["part_q"], "q")
 
     def dec_self_back():
-        v["part_g0"], v["g1"], v["gain_d1"], send, v["keep_s"] = line.call(
+        v["part_g0"], v["g1"], v["gain_dec_self"], send, v["keep_s"] = line.call(
             functools.partial(self_back_kernel, True, dec_len),
-            [dec_wide, dec_wide, gain_row, parts_of("s", dec_rows, attn_wide), ((dec_rows, attn_wide), BF)],
+            [dec_wide, dec_wide, gain_rows, parts_of("s", dec_rows, attn_wide), ((dec_rows, attn_wide), BF)],
             [table_lengths, v["part_q"], v["other_q"], dec_part("states"), dec_gains, v["g2"], dec_self_out,
              v["dec_saved"], dec_self_qkv, order_of["s"], y0],
             "dec_self_back",
         )
-        v["other_g0"] = pair_other(v["part_g0"], "g0")
         v["recv_s"] = swap_cores("s", send)
 
-    def input_grads():
-        v["enc_out"], v["dec_out_grad"], send, v["keep_g"] = line.call(
-            last_kernel,
-            [enc_low, dec_low, ((half, 128), F32), ((half, 128), F32)],
-            [v["part_ge"], v["other_ge"], x0, enc_gains, v["back1"], v["part_g0"], v["other_g0"], y0, dec_gains,
-             v["g1"], order_of[GAINS_WITH], v["gain_e1"], v["gain_e2"], v["gain_d1"], v["gain_d2"]],
-            "input_grads",
+    def tail_parts():
+        (v["part_tail"],) = line.call(
+            tail_parts_kernel, [((enc_rows + 2 * dec_rows, features), F32)],
+            [v["part_ge"], v["part_g0"], v["keep_m"], dec_mlp_out], "tail_parts",
+        )
+        v["other_tail"] = pair_other(v["part_tail"], "tail")
+
+    def tail():
+        v["enc_out"], v["dec_out_grad"], v["dec_out"] = line.call(
+            tail_kernel, [enc_low, dec_low, dec_low],
+            [v["part_tail"], v["other_tail"], x0, enc_gains, v["back1"], y0, dec_gains, v["g1"], v["y2"]], "tail",
+        )
+
+    def gains():
+        send, v["keep_g"] = line.call(
+            gains_kernel, [((half, 128), F32), ((half, 128), F32)],
+            [v["gain_enc_attn"], v["gain_enc_mlp"], v["gain_dec_self"], v["gain_dec_cross"], order_of[GAINS_WITH]],
+            "gains",
         )
         v["recv_g"] = swap(send, 0, "g")
+
+    def gains_sum():
+        v["other_gains"] = pair_other(grad_of[GAINS_WITH][2], "gains")
+
+    def gains_out():
+        own = grad_of[GAINS_WITH][2]
+        shape = ((3, own.shape[0]), F32)
+        v["gains_out"] = line.call(gains_out_kernel, [shape, shape], [own, v["other_gains"]], "gains_out")
 
     def attn_weights(name):
         if name == GAINS_WITH:
@@ -848,13 +917,6 @@
             )
         start_sums(name, products)
 
-    def out_part():
-        (v["part_out"],) = line.call(out_part_kernel, [dec_wide], [v["keep_m"], dec_mlp_out], "dec_out_part")
-        v["other_out"] = pair_other(v["part_out"], "out")
-
-    def dec_out_sum():
-        (v["dec_out"],) = line.call(sum_kernel, [dec_low], [v["y2"], v["part_out"], v["other_out"]], "dec_out")
-
     attn_pieces = ((0, 3, heads), (3 * heads, 1, heads))
     ends = {
         "m": ((0, 2, units),), "f": ((0, 2, units),), "mo": ((0, 1, units),), "fo": ((0, 1, units),),
@@ -867,9 +929,10 @@
     stages = {
         "tick": tick, "pause": pause, "dec_self": dec_self, "dec_mlp": dec_mlp, "w_m": dec_mlp_weights,
         "cross_back": cross_back, "w_c": cross_weights, "enc_mlp_back": enc_mlp_back,
-        "w_f": enc_mlp_weights, "enc_attn_back": enc_attn_back, "query_part": query_part,
-        "w_a": functools.partial(attn_weights, "a"), "dec_self_back": dec_self_back, "input_grads": input_grads,
-        "w_s": functools.partial(attn_weights, "s"), "out_part": out_part, "dec_out": dec_out_sum,
+        "w_f": enc_mlp_weights, "enc_attn_back": enc_attn_back, "query_part": query_part, "gains": gains,
+        "tail_parts": tail_parts, "tail": tail, "gains_out": gains_out,
+        "w_a": functools.partial(attn_weights, "a"), "dec_self_back": dec_self_back,
+        "w_s": functools.partial(attn_weights, "s"),
     }
     for name, stage in (("enc_attn", enc_attn), ("enc_mlp", enc_mlp), ("cross", cross)):
         for p in range(plots):
@@ -882,16 +945,16 @@
             sums[name].step(line)
         else:
             grad_of[name] = sums[name].finish(line, *ends[name])
+            if name == GAINS_WITH:
+                gains_sum()
     mlp_grads = {
         name: grad_of[name] if name + "o" not in HALVINGS else grad_of[name] + grad_of[name + "o"] for name in ("m", "f")
     }
-    gains = grad_of[GAINS_WITH][2]
-    gains = gains[:, :6].T
     grad_c = jnp.concatenate([grad_of["c"][0][None], grad_of["c"][2]], 0)
     grads = (
-        grad_of["a"][0], grad_of["a"][1].T, mlp_grads["f"][0], mlp_grads["f"][1].T, gains[:3],
+        grad_of["a"][0], grad_of["a"][1].T, mlp_grads["f"][0], mlp_grads["f"][1].T, v["gains_out"][0],
         grad_of["s"][0], grad_of["s"][1].T, grad_c, grad_of["c"][1].T, mlp_grads["m"][0], mlp_grads["m"][1].T,
-        gains[3:],
+        v["gains_out"][1],
     )
     return (
         v["dec_out"].reshape(cotangent.shape),

time: 297 us -> 258 us (0.87)
  waiting for transfers between devices: 185 us -> 121 us
  starting transfers between devices: 44.8 us -> 72.2 us
    ppermute x26 -> x30, waiting for transfers between devices: 138 us -> 68.6 us  [swap(): return lax.ppermute(value, 'dp', pairs)]
    ppermute x26 -> x30, starting transfers between devices: 21.5 us -> 49.3 us  [swap(): return lax.ppermute(value, 'dp', pairs)]
    ppermute x14 -> x13, waiting for transfers between devices: 46.8 us -> 51.9 us  [pair_other(): return lax.ppermute(part, 'mp', [(0, 1), (1, 0)])]
    unnamed x78 -> x68, local copies, waits for them, and re-layouts: 12.3 us -> 9.81 us
    pallas_call x47 -> x97, Pallas kernels: 51 us -> 52 us  [call(): pl.pallas_call(run, out_shape=shapes, in_specs=in_specs, out_specs=[VMEM]...]
    ppermute x14 -> x13, starting transfers between devices: 23.3 us -> 22.9 us  [pair_other(): return lax.ppermute(part, 'mp', [(0, 1), (1, 0)])]
  transfers between devices with their start and end apart: 40 -> 43, of which waited for: 23 -> 22; matrix products, arithmetic and copies ran while one was open for 1% -> 1% of each run, Pallas kernels for 15% -> 18%
where the time goes in v6:
time: 258 us
  waiting for transfers between devices  121 us (47%)
  starting transfers between devices  72.2 us (28%)
  Pallas kernels  52 us (20%)
  local copies, waits for them, and re-layouts  9.81 us (4%)
    ppermute x30, waiting for transfers between devices, swap(): return lax.ppermute(value, 'dp', pairs)  68.6 us
    pallas_call x97, Pallas kernels, call(): pl.pallas_call(run, out_shape=shapes, in_specs=in_specs, out_specs=[VMEM]...  52 us
    ppermute x13, waiting for transfers between devices, pair_other(): return lax.ppermute(part, 'mp', [(0, 1), (1, 0)])  51.9 us
    ppermute x30, starting transfers between devices, swap(): return lax.ppermute(value, 'dp', pairs)  49.3 us
    ppermute x13, starting transfers between devices, pair_other(): return lax.ppermute(part, 'mp', [(0, 1), (1, 0)])  22.9 us
    unnamed x68, local copies, waits for them, and re-layouts  9.81 us
  transfers between devices with their start and end apart: 43, of which 22 were waited for; matrix products, arithmetic and copies ran while one was open for 1% of the time, Pallas kernels for 18%

profile of v6, /device:TPU:0, one launch (start us, length us, event | category | flops | bytes accessed | tf_op | source)
XLA Modules:
  0.0 257.6 jit_solution(1220452404651777956)
XLA Ops:
  2.4 2.5 enc_attn_fwd.2
  4.9 3.0 %collective-permute-start = (f32[128,768]{1,0:T(8,128)}, f32[128,768]{1,0:T(8,128)}, u32[]{:S(2)}, u32[]{:S(2)}) collective-permute-start(f32[128,768]{1,0:T(8,128)} %get-tuple-element.110.refs_5_.refs_1_), channel_id=1, source_target_pairs={{0,1},{1,0},{2,3},{3,2},{4,5},{5,4},{6,7},{7,6},{8,9},{9,8},{10,11... | collective-permute-start | bytes 1179656 | tf_op jit(solution)/shard_map/pair_e1/ppermute | solution.py:618
  8.0 2.5 enc_attn_fwd.3
  10.6 2.5 dec_self_fwd.1
  15.6 2.7 %collective-permute-done.refs_2_ = f32[128,768]{1,0:T(8,128)} collective-permute-done((f32[128,768]{1,0:T(8,128)}, f32[128,768]{1,0:T(8,128)}, u32[]{:S(2)}, u32[]{:S(2)}) %collective-permute-start) | collective-permute-done | bytes 393248 | tf_op jit(solution)/shard_map/pair_e1/ppermute | solution.py:618
  20.1 2.6 %enc_mlp_fwd.2 = (f32[128,768]{1,0:T(8,128)S(1)}, f32[128,768]{1,0:T(8,128)S(1)}, f32[128,2048]{1,0:T(8,128)S(1)}) custom-call(bf16[256,768]{1,0:T(8,128)(2,1)S(1)} %bitcast.14, f32[128,768]{1,0:T(8,128)} %get-tuple-element.110.refs_5_.refs_1_, f32[128,768]{1,0:T(8,128)} %collective-permute-done.refs_2_, f32[3,768]{1,0:T(4,128)S(1)} %copy-done.21, ...), custom_call_target="tpu_custom_call" | custom-call | flops 1955000064 | bytes 6273000 | tf_op jit(solution)/shard_map/enc_mlp_fwd/pallas_call | solution.py:568
  26.7 2.5 enc_mlp_fwd.3
  31.3 3.8 %collective-permute-done.2.refs_7_ = f32[128,768]{1,0:T(8,128)} collective-permute-done((f32[128,768]{1,0:T(8,128)}, f32[128,768]{1,0:T(8,128)}, u32[]{:S(2)}, u32[]{:S(2)}) %collective-permute-start.2) | collective-permute-done | bytes 393248 | tf_op jit(solution)/shard_map/pair_d1/ppermute | solution.py:618
  35.1 8.3 %collective-permute-done.1.refs_3_ = f32[128,768]{1,0:T(8,128)S(1)} collective-permute-done((f32[128,768]{1,0:T(8,128)S(1)}, f32[128,768]{1,0:T(8,128)S(1)}, u32[]{:S(2)}, u32[]{:S(2)}) %collective-permute-start.1) | collective-permute-done | bytes 393248 | tf_op jit(solution)/shard_map/pair_e2/ppermute | solution.py:618
  47.8 4.0 %collective-permute-done.4.refs_3_ = f32[128,768]{1,0:T(8,128)S(1)} collective-permute-done((f32[128,768]{1,0:T(8,128)S(1)}, f32[128,768]{1,0:T(8,128)S(1)}, u32[]{:S(2)}, u32[]{:S(2)}) %collective-permute-start.4) | collective-permute-done | bytes 393248 | tf_op jit(solution)/shard_map/pair_e2/ppermute | solution.py:618
  56.3 3.6 %collective-permute-done.6.refs_5_ = f32[64,768]{1,0:T(8,128)S(1)} collective-permute-done((f32[64,768]{1,0:T(8,128)S(1)}, f32[64,768]{1,0:T(8,128)S(1)}, u32[]{:S(2)}, u32[]{:S(2)}) %collective-permute-start.6) | collective-permute-done | bytes 196640 | tf_op jit(solution)/shard_map/pair_d2/ppermute | solution.py:618
  60.0 2.4 dec_mlp.1
  69.4 5.0 %collective-permute-done.7.refs_2_ = f32[128,768]{1,0:T(8,128)S(1)} collective-permute-done((f32[128,768]{1,0:T(8,128)S(1)}, f32[128,768]{1,0:T(8,128)S(1)}, u32[]{:S(2)}, u32[]{:S(2)}) %collective-permute-start.7) | collective-permute-done | bytes 393248 | tf_op jit(solution)/shard_map/pair_g3/ppermute | solution.py:618
  74.3 4.8 %cross_back.1 = (f32[256,768]{1,0:T(8,128)S(1)}, f32[128,768]{1,0:T(8,128)S(1)}, f32[1,768]{1,0:T(1,128)S(1)}, f32[128,3840]{1,0:T(8,128)S(1)}, bf16[128,3840]{1,0:T(8,128)(2,1)S(1)}) custom-call(s32[2]{0:T(128)S(1)} %copy-done.23, f32[128,768]{1,0:T(8,128)S(1)} %get-tuple-element.121.refs_1_, f32[128,768]{1,0:T(8,128)S(1)} %collective-permute-done.7.refs_2_, ...), custom_call_target="tpu_custom_call" | custom-call | flops 115000000 | bytes 369000 | tf_op jit(solution)/shard_map/cross_back/pallas_call | solution.py:568
  85.7 13.5 %collective-permute-done.9.refs_1_ = f32[256,768]{1,0:T(8,128)S(1)} collective-permute-done((f32[256,768]{1,0:T(8,128)S(1)}, f32[256,768]{1,0:T(8,128)S(1)}, u32[]{:S(2)}, u32[]{:S(2)}) %collective-permute-start.9) | collective-permute-done | bytes 786464 | tf_op jit(solution)/shard_map/pair_m/ppermute | solution.py:618
  99.3 3.1 %enc_mlp_back.1 = (f32[256,768]{1,0:T(8,128)S(1)}, f32[256,768]{1,0:T(8,128)S(1)}, f32[1,768]{1,0:T(1,128)S(1)}, f32[256,3840]{1,0:T(8,128)S(1)}, bf16[256,3840]{1,0:T(8,128)(2,1)S(1)}) custom-call(f32[256,768]{1,0:T(8,128)S(1)} %get-tuple-element.128.refs_0_, f32[256,768]{1,0:T(8,128)S(1)} %collective-permute-done.9.refs_1_, ...), custom_call_target="tpu_custom_call" | custom-call | flops 9200000000 | bytes 29520000 | tf_op jit(solution)/shard_map/enc_mlp_back/pallas_call | solution.py:568
  103.0 6.3 %collective-permute-done.14.refs_1_ = f32[256,3840]{1,0:T(8,128)S(1)} collective-permute-done((f32[256,3840]{1,0:T(8,128)S(1)}, f32[256,3840]{1,0:T(8,128)S(1)}, u32[]{:S(2)}, u32[]{:S(2)}) %collective-permute-start.14) | collective-permute-done | bytes 3932192 | tf_op jit(solution)/shard_map/swap_f_0/ppermute | solution.py:629
  116.3 5.1 %collective-permute-done.12.refs_1_ = f32[192,3072]{1,0:T(8,128)S(1)} collective-permute-done((f32[192,3072]{1,0:T(8,128)S(1)}, f32[192,3072]{1,0:T(8,128)S(1)}, u32[]{:S(2)}, u32[]{:S(2)}) %collective-permute-start.12) | collective-permute-done | bytes 2359328 | tf_op jit(solution)/shard_map/swap_m_p/ppermute | solution.py:629
  123.7 9.2 %collective-permute-done.11.refs_2_ = f32[256,768]{1,0:T(8,128)S(1)} collective-permute-done((f32[256,768]{1,0:T(8,128)S(1)}, f32[256,768]{1,0:T(8,128)S(1)}, u32[]{:S(2)}, u32[]{:S(2)}) %collective-permute-start.11) | collective-permute-done | bytes 786464 | tf_op jit(solution)/shard_map/pair_g1/ppermute | solution.py:618
  133.2 5.5 %enc_attn_back.1 = (f32[256,768]{1,0:T(8,128)S(1)}, f32[256,768]{1,0:T(8,128)S(1)}, f32[2,768]{1,0:T(2,128)S(1)}, f32[256,2304]{1,0:T(8,128)S(1)}, bf16[256,2304]{1,0:T(8,128)(2,1)S(1)}) custom-call(s32[2]{0:T(128)S(1)} %copy-done.23, f32[256,768]{1,0:T(8,128)S(1)} %get-tuple-element.135.refs_1_, f32[256,768]{1,0:T(8,128)S(1)} %collective-permute-done.11.refs_2_, ...), custom_call_target="tpu_custom_call" | custom-call | flops 115000000 | bytes 369000 | tf_op jit(solution)/shard_map/enc_attn_back/pallas_call | solution.py:568
  138.9 9.1 %collective-permute-done.16.refs_1_ = f32[192,2048]{1,0:T(8,128)S(1)} collective-permute-done((f32[192,2048]{1,0:T(8,128)S(1)}, f32[192,2048]{1,0:T(8,128)S(1)}, u32[]{:S(2)}, u32[]{:S(2)}) %collective-permute-start.16) | collective-permute-done | bytes 1572896 | tf_op jit(solution)/shard_map/swap_f_x/ppermute | solution.py:629
  150.1 3.8 %dec_self_back.1 = (f32[128,768]{1,0:T(8,128)S(1)}, f32[128,768]{1,0:T(8,128)S(1)}, f32[2,768]{1,0:T(2,128)S(1)}, f32[128,2304]{1,0:T(8,128)S(1)}, bf16[128,2304]{1,0:T(8,128)(2,1)S(1)}) custom-call(s32[2]{0:T(128)S(1)} %copy-done.25, f32[128,768]{1,0:T(8,128)S(1)} %query_part.1.refs_1_, f32[128,768]{1,0:T(8,128)S(1)} %collective-permute-done.15.refs_2_, ...), custom_call_target="tpu_custom_call" | custom-call | flops 345000000 | bytes 1107000 | tf_op jit(solution)/shard_map/dec_self_back/pallas_call | solution.py:568
  159.6 4.3 %collective-permute-start.27 = (f32[192,1664]{1,0:T(8,128)S(1)}, f32[192,1664]{1,0:T(8,128)S(1)}, u32[]{:S(2)}, u32[]{:S(2)}) collective-permute-start(f32[192,1664]{1,0:T(8,128)S(1)} %get-tuple-element.168.refs_2_), channel_id=1, source_target_pairs={{0,8},{2,10},{4,12},{6,14},{8,0},{10,2},{12,4},{14,6},{16,24},{18,... | collective-permute-start | bytes 3833864 | tf_op jit(solution)/shard_map/swap_s_p/ppermute | solution.py:629
  163.9 4.8 %collective-permute-done.21.refs_1_ = f32[96,2048]{1,0:T(8,128)S(1)} collective-permute-done((f32[96,2048]{1,0:T(8,128)S(1)}, f32[96,2048]{1,0:T(8,128)S(1)}, u32[]{:S(2)}, u32[]{:S(2)}) %collective-permute-start.21) | collective-permute-done | bytes 786464 | tf_op jit(solution)/shard_map/swap_f_p/ppermute | solution.py:629
  169.6 3.6 %collective-permute-done.18.refs_1_ = f32[96,3072]{1,0:T(8,128)S(1)} collective-permute-done((f32[96,3072]{1,0:T(8,128)S(1)}, f32[96,3072]{1,0:T(8,128)S(1)}, u32[]{:S(2)}, u32[]{:S(2)}) %collective-permute-start.18) | collective-permute-done | bytes 1179680 | tf_op jit(solution)/shard_map/swap_m_x/ppermute | solution.py:629
  178.3 16.4 %collective-permute-done.27.refs_1_ = f32[192,1664]{1,0:T(8,128)S(1)} collective-permute-done((f32[192,1664]{1,0:T(8,128)S(1)}, f32[192,1664]{1,0:T(8,128)S(1)}, u32[]{:S(2)}, u32[]{:S(2)}) %collective-permute-start.27) | collective-permute-done | bytes 1277984 | tf_op jit(solution)/shard_map/swap_s_p/ppermute | solution.py:629
  200.6 10.9 %collective-permute-done.29.refs_1_ = f32[96,1664]{1,0:T(8,128)S(1)} collective-permute-done((f32[96,1664]{1,0:T(8,128)S(1)}, f32[96,1664]{1,0:T(8,128)S(1)}, u32[]{:S(2)}, u32[]{:S(2)}) %collective-permute-start.29) | collective-permute-done | bytes 639008 | tf_op jit(solution)/shard_map/swap_s_x/ppermute | solution.py:629
  212.5 4.6 %collective-permute-start.35 = (f32[48,3072]{1,0:T(8,128)S(1)}, f32[48,3072]{1,0:T(8,128)S(1)}, u32[]{:S(2)}, u32[]{:S(2)}) collective-permute-start(f32[48,3072]{1,0:T(8,128)S(1)} %get-tuple-element.178.refs_9_), channel_id=1, source_target_pairs={{0,8},{2,10},{4,12},{6,14},{8,0},{10,2},{12,4},{14,6},{16,24},{18,... | collective-permute-start | bytes 1769480 | tf_op jit(solution)/shard_map/swap_m_e/ppermute | solution.py:629
  224.3 7.1 %collective-permute-done.35.refs_1_ = f32[48,3072]{1,0:T(8,128)S(1)} collective-permute-done((f32[48,3072]{1,0:T(8,128)S(1)}, f32[48,3072]{1,0:T(8,128)S(1)}, u32[]{:S(2)}, u32[]{:S(2)}) %collective-permute-start.35) | collective-permute-done | bytes 589856 | tf_op jit(solution)/shard_map/swap_m_e/ppermute | solution.py:629
  234.6 4.1 %collective-permute-start.38 = (f32[48,1664]{1,0:T(8,128)S(1)}, f32[48,1664]{1,0:T(8,128)S(1)}, u32[]{:S(2)}, u32[]{:S(2)}) collective-permute-start(f32[48,1664]{1,0:T(8,128)S(1)} %get-tuple-element.187.refs_2_), channel_id=1, source_target_pairs={{0,8},{2,10},{4,12},{6,14},{8,0},{10,2},{12,4},{14,6},{16,24},{18,... | collective-permute-start | bytes 958472 | tf_op jit(solution)/shard_map/swap_s_e/ppermute | solution.py:629
  238.9 6.6 %collective-permute-start.37 = (f32[48,1536]{1,0:T(8,128)S(1)}, f32[48,1536]{1,0:T(8,128)S(1)}, u32[]{:S(2)}, u32[]{:S(2)}) collective-permute-start(f32[48,1536]{1,0:T(8,128)S(1)} %get-tuple-element.190.refs_2_), channel_id=1, source_target_pairs={{0,8},{2,10},{4,12},{6,14},{8,0},{10,2},{12,4},{14,6},{16,24},{18,... | collective-permute-start | bytes 884744 | tf_op jit(solution)/shard_map/swap_a_e/ppermute | solution.py:629
  249.2 3.0 %collective-permute-start.42 = (f32[48,1024]{1,0:T(8,128)S(1)}, f32[48,1024]{1,0:T(8,128)S(1)}, u32[]{:S(2)}, u32[]{:S(2)}) collective-permute-start(f32[48,1024]{1,0:T(8,128)S(1)} %get-tuple-element.194.refs_2_), channel_id=1, source_target_pairs={{0,8},{2,10},{4,12},{6,14},{8,0},{10,2},{12,4},{14,6},{16,24},{18,... | collective-permute-start | bytes 589832 | tf_op jit(solution)/shard_map/swap_fo_e/ppermute | solution.py:629
  (224 shorter events, 84.8 us)
Async XLA Ops:
  4.9 13.3 %collective-permute-start = (f32[128,768]{1,0:T(8,128)}, f32[128,768]{1,0:T(8,128)}, u32[]{:S(2)}, u32[]{:S(2)}) collective-permute-start(f32[128,768]{1,0:T(8,128)} %get-tuple-element.110.refs_5_.refs_1_), channel_id=1, source_target_pairs={{0,1},{1,0},{2,3},{3,2},{4,5},{5,4},{6,7},{7,6},{8,9},{9,8},{10,11... | collective-permute-start | bytes 1179656 | tf_op jit(solution)/shard_map/pair_e1/ppermute | solution.py:618
  10.5 16.2 %collective-permute-start.3 = (f32[128,768]{1,0:T(8,128)}, f32[128,768]{1,0:T(8,128)}, u32[]{:S(2)}, u32[]{:S(2)}) collective-permute-start(f32[128,768]{1,0:T(8,128)} %get-tuple-element.111.refs_5_.refs_1_), channel_id=1, source_target_pairs={{0,1},{1,0},{2,3},{3,2},{4,5},{5,4},{6,7},{7,6},{8,9},{9,8},{10,11... | collective-permute-start | bytes 1179656 | tf_op jit(solution)/shard_map/pair_e1/ppermute | solution.py:618
  13.1 22.0 %collective-permute-start.2 = (f32[128,768]{1,0:T(8,128)}, f32[128,768]{1,0:T(8,128)}, u32[]{:S(2)}, u32[]{:S(2)}) collective-permute-start(f32[128,768]{1,0:T(8,128)} %get-tuple-element.112.refs_1_.refs_6_), channel_id=1, source_target_pairs={{0,1},{1,0},{2,3},{3,2},{4,5},{5,4},{6,7},{7,6},{8,9},{9,8},{10,11... | collective-permute-start | bytes 1179656 | tf_op jit(solution)/shard_map/pair_d1/ppermute | solution.py:618
  22.7 20.7 %collective-permute-start.1 = (f32[128,768]{1,0:T(8,128)S(1)}, f32[128,768]{1,0:T(8,128)S(1)}, u32[]{:S(2)}, u32[]{:S(2)}) collective-permute-start(f32[128,768]{1,0:T(8,128)S(1)} %get-tuple-element.114.refs_6_.refs_2_), channel_id=1, source_target_pairs={{0,1},{1,0},{2,3},{3,2},{4,5},{5,4},{6,7},{7,6},{8,9},{9,8},{10,11... | collective-permute-start | bytes 1179656 | tf_op jit(solution)/shard_map/pair_e2/ppermute | solution.py:618
  29.2 22.7 %collective-permute-start.4 = (f32[128,768]{1,0:T(8,128)S(1)}, f32[128,768]{1,0:T(8,128)S(1)}, u32[]{:S(2)}, u32[]{:S(2)}) collective-permute-start(f32[128,768]{1,0:T(8,128)S(1)} %get-tuple-element.115.refs_1_.refs_2_), channel_id=1, source_target_pairs={{0,1},{1,0},{2,3},{3,2},{4,5},{5,4},{6,7},{7,6},{8,9},{9,8},{10,11... | collective-permute-start | bytes 1179656 | tf_op jit(solution)/shard_map/pair_e2/ppermute | solution.py:618
  45.7 14.2 %collective-permute-start.5 = (f32[64,768]{1,0:T(8,128)S(1)}, f32[64,768]{1,0:T(8,128)S(1)}, u32[]{:S(2)}, u32[]{:S(2)}) collective-permute-start(f32[64,768]{1,0:T(8,128)S(1)} %get-tuple-element.118.refs_11_.refs_2_), channel_id=1, source_target_pairs={{0,1},{1,0},{2,3},{3,2},{4,5},{5,4},{6,7},{7,6},{8,9},{9,8},{10,11... | collective-permute-start | bytes 589832 | tf_op jit(solution)/shard_map/pair_d2/ppermute | solution.py:618
  67.2 54.2 %collective-permute-start.12 = (f32[192,3072]{1,0:T(8,128)S(1)}, f32[192,3072]{1,0:T(8,128)S(1)}, u32[]{:S(2)}, u32[]{:S(2)}) collective-permute-start(f32[192,3072]{1,0:T(8,128)S(1)} %get-tuple-element.127.refs_18_), channel_id=1, source_target_pairs={{0,8},{2,10},{4,12},{6,14},{8,0},{10,2},{12,4},{14,6},{16,24},{18,... | collective-permute-start | bytes 7077896 | tf_op jit(solution)/shard_map/swap_m_p/ppermute | solution.py:629
  79.3 20.0 %collective-permute-start.9 = (f32[256,768]{1,0:T(8,128)S(1)}, f32[256,768]{1,0:T(8,128)S(1)}, u32[]{:S(2)}, u32[]{:S(2)}) collective-permute-start(f32[256,768]{1,0:T(8,128)S(1)} %get-tuple-element.128.refs_0_), channel_id=1, source_target_pairs={{0,1},{1,0},{2,3},{3,2},{4,5},{5,4},{6,7},{7,6},{8,9},{9,8},{10,11... | collective-permute-start | bytes 2359304 | tf_op jit(solution)/shard_map/pair_m/ppermute | solution.py:618
  84.0 31.6 %collective-permute-start.13 = (f32[192,1536]{1,0:T(8,128)S(1)}, f32[192,1536]{1,0:T(8,128)S(1)}, u32[]{:S(2)}, u32[]{:S(2)}) collective-permute-start(f32[192,1536]{1,0:T(8,128)S(1)} %get-tuple-element.134.refs_1_), channel_id=1, source_target_pairs={{0,4},{2,6},{4,0},{6,2},{8,12},{10,14},{12,8},{14,10},{16,20},{18,... | collective-permute-start | bytes 3538952 | tf_op jit(solution)/shard_map/swap_c_x/ppermute | solution.py:629
  110.7 37.3 %collective-permute-start.16 = (f32[192,2048]{1,0:T(8,128)S(1)}, f32[192,2048]{1,0:T(8,128)S(1)}, u32[]{:S(2)}, u32[]{:S(2)}) collective-permute-start(f32[192,2048]{1,0:T(8,128)S(1)} %get-tuple-element.151), channel_id=1, source_target_pairs={{0,4},{2,6},{4,0},{6,2},{8,12},{10,14},{12,8},{14,10},{16,20},{18,... | collective-permute-start | bytes 4718600 | tf_op jit(solution)/shard_map/swap_f_x/ppermute | solution.py:629
  112.5 20.4 %collective-permute-start.11 = (f32[256,768]{1,0:T(8,128)S(1)}, f32[256,768]{1,0:T(8,128)S(1)}, u32[]{:S(2)}, u32[]{:S(2)}) collective-permute-start(f32[256,768]{1,0:T(8,128)S(1)} %get-tuple-element.135.refs_1_), channel_id=1, source_target_pairs={{0,1},{1,0},{2,3},{3,2},{4,5},{5,4},{6,7},{7,6},{8,9},{9,8},{10,11... | collective-permute-start | bytes 2359304 | tf_op jit(solution)/shard_map/pair_g1/ppermute | solution.py:618
  114.0 24.7 %collective-permute-start.17 = (f32[192,1024]{1,0:T(8,128)S(1)}, f32[192,1024]{1,0:T(8,128)S(1)}, u32[]{:S(2)}, u32[]{:S(2)}) collective-permute-start(f32[192,1024]{1,0:T(8,128)S(1)} %get-tuple-element.144.refs_1_), channel_id=1, source_target_pairs={{0,8},{2,10},{4,12},{6,14},{8,0},{10,2},{12,4},{14,6},{16,24},{18,... | collective-permute-start | bytes 2359304 | tf_op jit(solution)/shard_map/swap_fo_p/ppermute | solution.py:629
  115.6 34.5 %collective-permute-start.15 = (f32[128,768]{1,0:T(8,128)S(1)}, f32[128,768]{1,0:T(8,128)S(1)}, u32[]{:S(2)}, u32[]{:S(2)}) collective-permute-start(f32[128,768]{1,0:T(8,128)S(1)} %query_part.1.refs_1_), channel_id=1, source_target_pairs={{0,1},{1,0},{2,3},{3,2},{4,5},{5,4},{6,7},{7,6},{8,9},{9,8},{10,11... | collective-permute-start | bytes 1179656 | tf_op jit(solution)/shard_map/pair_q/ppermute | solution.py:618
  121.4 32.5 %collective-permute-start.19 = (f32[96,1536]{1,0:T(8,128)S(1)}, f32[96,1536]{1,0:T(8,128)S(1)}, u32[]{:S(2)}, u32[]{:S(2)}) collective-permute-start(f32[96,1536]{1,0:T(8,128)S(1)} %get-tuple-element.145.refs_2_), channel_id=1, source_target_pairs={{0,8},{2,10},{4,12},{6,14},{8,0},{10,2},{12,4},{14,6},{16,24},{18,... | collective-permute-start | bytes 1769480 | tf_op jit(solution)/shard_map/swap_c_p/ppermute | solution.py:629
  132.9 40.4 %collective-permute-start.18 = (f32[96,3072]{1,0:T(8,128)S(1)}, f32[96,3072]{1,0:T(8,128)S(1)}, u32[]{:S(2)}, u32[]{:S(2)}) collective-permute-start(f32[96,3072]{1,0:T(8,128)S(1)} %get-tuple-element.146.refs_13_), channel_id=1, source_target_pairs={{0,4},{2,6},{4,0},{6,2},{8,12},{10,14},{12,8},{14,10},{16,20},{18,... | collective-permute-start | bytes 3538952 | tf_op jit(solution)/shard_map/swap_m_x/ppermute | solution.py:629
  138.7 17.1 %collective-permute-start.24 = (f32[256,2304]{1,0:T(8,128)S(1)}, f32[256,2304]{1,0:T(8,128)S(1)}, u32[]{:S(2)}, u32[]{:S(2)}) collective-permute-start(f32[256,2304]{1,0:T(8,128)S(1)} %get-tuple-element.166), channel_id=1, source_target_pairs={{0,2},{2,0},{4,6},{6,4},{8,10},{10,8},{12,14},{14,12},{16,18},{18,... | collective-permute-start | bytes 7077896 | tf_op jit(solution)/shard_map/swap_a_0/ppermute | solution.py:629
  148.2 20.5 %collective-permute-start.21 = (f32[96,2048]{1,0:T(8,128)S(1)}, f32[96,2048]{1,0:T(8,128)S(1)}, u32[]{:S(2)}, u32[]{:S(2)}) collective-permute-start(f32[96,2048]{1,0:T(8,128)S(1)} %get-tuple-element.155.refs_1_), channel_id=1, source_target_pairs={{0,8},{2,10},{4,12},{6,14},{8,0},{10,2},{12,4},{14,6},{16,24},{18,... | collective-permute-start | bytes 2359304 | tf_op jit(solution)/shard_map/swap_f_p/ppermute | solution.py:629
  154.0 15.5 %collective-permute-start.20 = (f32[96,1536]{1,0:T(8,128)S(1)}, f32[96,1536]{1,0:T(8,128)S(1)}, u32[]{:S(2)}, u32[]{:S(2)}) collective-permute-start(f32[96,1536]{1,0:T(8,128)S(1)} %halve_c.4.refs_1_.refs_0_), channel_id=1, source_target_pairs={{8,16},{10,18},{12,20},{14,22},{16,8},{18,10},{20,12},{22,14},{9,1... | collective-permute-start | bytes 1769480 | tf_op jit(solution)/shard_map/swap_c_m/ppermute | solution.py:629
  157.5 41.1 %collective-permute-start.30 = (f32[192,1536]{1,0:T(8,128)S(1)}, f32[192,1536]{1,0:T(8,128)S(1)}, u32[]{:S(2)}, u32[]{:S(2)}) collective-permute-start(f32[192,1536]{1,0:T(8,128)S(1)} %get-tuple-element.167.refs_4_), channel_id=1, source_target_pairs={{0,4},{2,6},{4,0},{6,2},{8,12},{10,14},{12,8},{14,10},{16,20},{18,... | collective-permute-start | bytes 3538952 | tf_op jit(solution)/shard_map/swap_a_x/ppermute | solution.py:629
  159.6 35.0 %collective-permute-start.27 = (f32[192,1664]{1,0:T(8,128)S(1)}, f32[192,1664]{1,0:T(8,128)S(1)}, u32[]{:S(2)}, u32[]{:S(2)}) collective-permute-start(f32[192,1664]{1,0:T(8,128)S(1)} %get-tuple-element.168.refs_2_), channel_id=1, source_target_pairs={{0,8},{2,10},{4,12},{6,14},{8,0},{10,2},{12,4},{14,6},{16,24},{18,... | collective-permute-start | bytes 3833864 | tf_op jit(solution)/shard_map/swap_s_p/ppermute | solution.py:629
  175.6 41.5 %collective-permute-start.25 = (f32[512,768]{1,0:T(8,128)S(1)}, f32[512,768]{1,0:T(8,128)S(1)}, u32[]{:S(2)}, u32[]{:S(2)}) collective-permute-start(f32[512,768]{1,0:T(8,128)S(1)} %tail_parts.1.refs_2_.refs_0_), channel_id=1, source_target_pairs={{0,1},{1,0},{2,3},{3,2},{4,5},{5,4},{6,7},{7,6},{8,9},{9,8},{10,11... | collective-permute-start | bytes 4718600 | tf_op jit(solution)/shard_map/pair_tail/ppermute | solution.py:618
  177.5 34.9 %collective-permute-start.26 = (f32[96,3072]{1,0:T(8,128)S(1)}, f32[96,3072]{1,0:T(8,128)S(1)}, u32[]{:S(2)}, u32[]{:S(2)}) collective-permute-start(f32[96,3072]{1,0:T(8,128)S(1)} %halve_m.4.refs_1_.refs_0_), channel_id=1, source_target_pairs={{8,16},{10,18},{12,20},{14,22},{16,8},{18,10},{20,12},{22,14},{9,1... | collective-permute-start | bytes 3538952 | tf_op jit(solution)/shard_map/swap_m_m/ppermute | solution.py:629
  194.8 16.6 %collective-permute-start.29 = (f32[96,1664]{1,0:T(8,128)S(1)}, f32[96,1664]{1,0:T(8,128)S(1)}, u32[]{:S(2)}, u32[]{:S(2)}) collective-permute-start(f32[96,1664]{1,0:T(8,128)S(1)} %get-tuple-element.175.refs_2_), channel_id=1, source_target_pairs={{0,4},{2,6},{4,0},{6,2},{8,12},{10,14},{12,8},{14,10},{16,20},{18,... | collective-permute-start | bytes 1916936 | tf_op jit(solution)/shard_map/swap_s_x/ppermute | solution.py:629
  196.5 22.1 %collective-permute-start.32 = (f32[48,1536]{1,0:T(8,128)S(1)}, f32[48,1536]{1,0:T(8,128)S(1)}, u32[]{:S(2)}, u32[]{:S(2)}) collective-permute-start(f32[48,1536]{1,0:T(8,128)S(1)} %get-tuple-element.169.refs_2_), channel_id=1, source_target_pairs={{0,8},{2,10},{4,12},{6,14},{8,0},{10,2},{12,4},{14,6},{16,24},{18,... | collective-permute-start | bytes 884744 | tf_op jit(solution)/shard_map/swap_c_e/ppermute | solution.py:629
  198.7 21.5 %collective-permute-start.31 = (f32[96,1536]{1,0:T(8,128)S(1)}, f32[96,1536]{1,0:T(8,128)S(1)}, u32[]{:S(2)}, u32[]{:S(2)}) collective-permute-start(f32[96,1536]{1,0:T(8,128)S(1)} %get-tuple-element.177.refs_2_), channel_id=1, source_target_pairs={{0,8},{2,10},{4,12},{6,14},{8,0},{10,2},{12,4},{14,6},{16,24},{18,... | collective-permute-start | bytes 1769480 | tf_op jit(solution)/shard_map/swap_a_p/ppermute | solution.py:629
  211.5 12.7 %collective-permute-start.36 = (f32[96,1664]{1,0:T(8,128)S(1)}, f32[96,1664]{1,0:T(8,128)S(1)}, u32[]{:S(2)}, u32[]{:S(2)}) collective-permute-start(f32[96,1664]{1,0:T(8,128)S(1)} %halve_s.4.refs_2_.refs_0_), channel_id=1, source_target_pairs={{8,16},{10,18},{12,20},{14,22},{16,8},{18,10},{20,12},{22,14},{9,1... | collective-permute-start | bytes 1916936 | tf_op jit(solution)/shard_map/swap_s_m/ppermute | solution.py:629
  212.5 18.9 %collective-permute-start.35 = (f32[48,3072]{1,0:T(8,128)S(1)}, f32[48,3072]{1,0:T(8,128)S(1)}, u32[]{:S(2)}, u32[]{:S(2)}) collective-permute-start(f32[48,3072]{1,0:T(8,128)S(1)} %get-tuple-element.178.refs_9_), channel_id=1, source_target_pairs={{0,8},{2,10},{4,12},{6,14},{8,0},{10,2},{12,4},{14,6},{16,24},{18,... | collective-permute-start | bytes 1769480 | tf_op jit(solution)/shard_map/swap_m_e/ppermute | solution.py:629
  220.3 18.5 %collective-permute-start.33 = (f32[96,1536]{1,0:T(8,128)S(1)}, f32[96,1536]{1,0:T(8,128)S(1)}, u32[]{:S(2)}, u32[]{:S(2)}) collective-permute-start(f32[96,1536]{1,0:T(8,128)S(1)} %halve_a.4.refs_2_.refs_0_), channel_id=1, source_target_pairs={{8,16},{10,18},{12,20},{14,22},{16,8},{18,10},{20,12},{22,14},{9,1... | collective-permute-start | bytes 1769480 | tf_op jit(solution)/shard_map/swap_a_m/ppermute | solution.py:629
  222.5 29.6 %collective-permute-start.40 = (f32[48,2048]{1,0:T(8,128)S(1)}, f32[48,2048]{1,0:T(8,128)S(1)}, u32[]{:S(2)}, u32[]{:S(2)}) collective-permute-start(f32[48,2048]{1,0:T(8,128)S(1)} %get-tuple-element.173.refs_2_), channel_id=1, source_target_pairs={{0,8},{2,10},{4,12},{6,14},{8,0},{10,2},{12,4},{14,6},{16,24},{18,... | collective-permute-start | bytes 1179656 | tf_op jit(solution)/shard_map/swap_f_e/ppermute | solution.py:629
  233.2 15.9 %collective-permute-start.41 = (f32[96,1024]{1,0:T(8,128)S(1)}, f32[96,1024]{1,0:T(8,128)S(1)}, u32[]{:S(2)}, u32[]{:S(2)}) collective-permute-start(f32[96,1024]{1,0:T(8,128)S(1)} %halve_fo.4.refs_2_.refs_0_), channel_id=1, source_target_pairs={{8,16},{10,18},{12,20},{14,22},{16,8},{18,10},{20,12},{22,14},{9,1... | collective-permute-start | bytes 1179656 | tf_op jit(solution)/shard_map/swap_fo_m/ppermute | solution.py:629
  234.6 12.2 %collective-permute-start.38 = (f32[48,1664]{1,0:T(8,128)S(1)}, f32[48,1664]{1,0:T(8,128)S(1)}, u32[]{:S(2)}, u32[]{:S(2)}) collective-permute-start(f32[48,1664]{1,0:T(8,128)S(1)} %get-tuple-element.187.refs_2_), channel_id=1, source_target_pairs={{0,8},{2,10},{4,12},{6,14},{8,0},{10,2},{12,4},{14,6},{16,24},{18,... | collective-permute-start | bytes 958472 | tf_op jit(solution)/shard_map/swap_s_e/ppermute | solution.py:629
  238.9 15.7 %collective-permute-start.37 = (f32[48,1536]{1,0:T(8,128)S(1)}, f32[48,1536]{1,0:T(8,128)S(1)}, u32[]{:S(2)}, u32[]{:S(2)}) collective-permute-start(f32[48,1536]{1,0:T(8,128)S(1)} %get-tuple-element.190.refs_2_), channel_id=1, source_target_pairs={{0,8},{2,10},{4,12},{6,14},{8,0},{10,2},{12,4},{14,6},{16,24},{18,... | collective-permute-start | bytes 884744 | tf_op jit(solution)/shard_map/swap_a_e/ppermute | solution.py:629
  (45 other events, 224.5 us)

commit v7 on v6

--- a/solution.py
+++ b/solution.py
@@ -430,34 +430,29 @@
 
 COST = {
     "enc_attn_fwd": 2.3, "dec_self_fwd": 2.5, "enc_mlp_fwd": 1.7, "cross_fwd": 4.2, "dec_mlp": 2.7,
-    "cross_back": 0.1, "dec_self_back": 0.3, "enc_attn_back": 0.1, "enc_mlp_back": 8, "finish_a": 20,
-    "finish_c": 3, "finish_f": 20, "finish_fo": 20, "finish_m": 0.1, "finish_mo": 3,
-    "finish_s": 0.3, "gains": 20, "gains_out": 8, "halve_a": 3, "halve_c": 3,
-    "halve_f": 0.3, "halve_fo": 0.3, "halve_m": 1, "halve_mo": 0.3, "halve_s": 0.3,
-    "query_part": 8, "tail": 3, "tail_parts": 0.1, "weights_a": 8, "weights_c": 3,
-    "weights_f": 3, "weights_m": 0.3, "weights_s": 0.1,
+    "cross_back": 3.0, "weights_c": 0.3, "enc_mlp_back": 3.0, "enc_attn_back": 1.0, "query_part": 20.0,
+    "weights_f": 8.0, "weights_a": 0.1, "dec_self_back": 3.0, "weights_s": 3.0, "tail_parts": 0.1,
+    "tail": 8.0, "gains": 8.0, "gains_out": 0.1, "halve_m": 20.0, "halve_mo": 1.0,
+    "halve_c": 0.1, "halve_f": 3.0, "halve_fo": 3.0, "halve_s": 0.1, "halve_a": 1.0,
+    "finish_m": 3.0, "finish_mo": 1.0, "finish_c": 8.0, "finish_f": 1.0, "finish_fo": 3.0,
+    "finish_s": 1.0, "finish_a": 1.0, "weights_m": 1.0,
 }
 VMEM_LIMIT = 8
 
 LINE = (
     "pause", "enc_attn_0", "enc_attn_1", "dec_self", "pause", "enc_mlp_0", "enc_mlp_1", "pause",
-    "cross_0", "cross_1", "pause", "dec_mlp", "tick", "w_m", "cross_back", "tick",
-    "tick", "tick", "tick", "tick", "tick", "tick", "tick", "tick",
-    "tick", "tick", "tick", "tick", "tick", "tick", "tick", "tick",
-    "tick", "tick", "w_c", "tick", "tick", "tick", "enc_mlp_back", "tick",
-    "tick", "tick", "tick", "tick", "tick", "tick", "tick", "tick",
-    "tick", "tick", "tick", "tick", "tick", "query_part", "tick", "tick",
-    "w_f", "tick", "tick", "tick", "h_c", "h_m", "enc_attn_back", "h_fo",
-    "tick", "h_f", "tick", "dec_self_back", "h_c", "tick", "gains", "w_a",
-    "w_s", "h_f", "h_c", "h_m", "tick", "tick", "tail_parts", "h_f",
-    "h_s", "h_a", "h_s", "h_m", "tail", "e_c", "h_a", "h_s",
-    "e_m", "h_fo", "h_a", "e_s", "h_fo", "e_f", "gains_out", "e_a",
-    "e_fo",
+    "cross_0", "cross_1", "pause", "dec_mlp", "tick", "w_m", "cross_back", "h_mo",
+    "w_c", "enc_mlp_back", "tick", "h_m", "query_part", "w_f", "h_mo", "dec_self_back",
+    "h_c", "h_fo", "enc_attn_back", "h_mo", "h_f", "w_s", "gains", "h_m",
+    "w_a", "h_c", "h_f", "h_m", "h_c", "h_s", "h_a", "tail_parts",
+    "h_fo", "h_f", "e_c", "h_s", "tick", "h_a", "e_f", "h_fo",
+    "h_a", "tail", "e_m", "e_mo", "h_s", "e_a", "e_fo", "gains_out",
+    "e_s",
 )
-HALVINGS = {"a": "xpme", "c": "xpme", "f": "xpme", "m": "pxme", "s": "pxme", "fo": "pxme"}
-PARTS = {"a": 1, "c": 1, "f": 1, "m": 1, "s": 1}
-TICK = 2
-GAINS_WITH = "s"
+HALVINGS = {"m": "pxme", "mo": "xpme", "c": "xpme", "f": "pxme", "fo": "xpme", "s": "pxme", "a": "xpme"}
+PARTS = {"m": 1, "c": 3, "f": 1, "a": 1, "s": 1}
+TICK = 0.1
+GAINS_WITH = "a"
 
 
 class Stored:

time: 258 us -> 256 us (level)
  waiting for transfers between devices: 121 us -> 92.8 us
  starting transfers between devices: 72.2 us -> 97.2 us
    ppermute x30 -> x36, starting transfers between devices: 49.3 us -> 74.5 us  [swap(): return lax.ppermute(value, 'dp', pairs)]
    ppermute x30 -> x36, waiting for transfers between devices: 68.6 us -> 48.4 us  [swap(): return lax.ppermute(value, 'dp', pairs)]
    ppermute x13, waiting for transfers between devices: 51.9 us -> 44.4 us  [pair_other(): return lax.ppermute(part, 'mp', [(0, 1), (1, 0)])]
    unnamed x68 -> x88, local copies, waits for them, and re-layouts: 9.81 us -> 10.2 us
    pallas_call x97 -> x57, Pallas kernels: 52 us -> 51.8 us  [call(): pl.pallas_call(run, out_shape=shapes, in_specs=in_specs, out_specs=[VMEM]...]
  transfers between devices with their start and end apart: 43 -> 49, of which waited for: 22 -> 26; matrix products, arithmetic and copies ran while one was open for 1% -> 1% of each run, Pallas kernels for 18% -> 18%
where the time goes in v7:
time: 256 us; the launch traced here: 255 us
  starting transfers between devices  97.2 us (38%)
  waiting for transfers between devices  92.8 us (36%)
  Pallas kernels  51.8 us (20%)
  local copies, waits for them, and re-layouts  10.2 us (4%)
    ppermute x36, starting transfers between devices, swap(): return lax.ppermute(value, 'dp', pairs)  74.5 us
    pallas_call x57, Pallas kernels, call(): pl.pallas_call(run, out_shape=shapes, in_specs=in_specs, out_specs=[VMEM]...  51.8 us
    ppermute x36, waiting for transfers between devices, swap(): return lax.ppermute(value, 'dp', pairs)  48.4 us
    ppermute x13, waiting for transfers between devices, pair_other(): return lax.ppermute(part, 'mp', [(0, 1), (1, 0)])  44.4 us
    ppermute x13, starting transfers between devices, pair_other(): return lax.ppermute(part, 'mp', [(0, 1), (1, 0)])  22.7 us
    unnamed x88, local copies, waits for them, and re-layouts  10.2 us
  transfers between devices with their start and end apart: 49, of which 26 were waited for; matrix products, arithmetic and copies ran while one was open for 1% of the time, Pallas kernels for 18%

profile of v7, /device:TPU:0, one launch (start us, length us, event | category | flops | bytes accessed | tf_op | source)
XLA Modules:
  0.0 254.9 jit_solution(2132537873243623777)
XLA Ops:
  2.4 2.5 enc_attn_fwd.2
  5.0 3.0 %collective-permute-start = (f32[128,768]{1,0:T(8,128)}, f32[128,768]{1,0:T(8,128)}, u32[]{:S(2)}, u32[]{:S(2)}) collective-permute-start(f32[128,768]{1,0:T(8,128)} %get-tuple-element.116.refs_5_.refs_1_), channel_id=1, source_target_pairs={{0,1},{1,0},{2,3},{3,2},{4,5},{5,4},{6,7},{7,6},{8,9},{9,8},{10,11... | collective-permute-start | bytes 1179656 | tf_op jit(solution)/shard_map/pair_e1/ppermute | solution.py:613
  8.0 2.5 enc_attn_fwd.3
  11.3 2.5 dec_self_fwd.1
  19.1 2.5 enc_mlp_fwd.2
  22.8 3.8 %collective-permute-done.3.refs_2_ = f32[128,768]{1,0:T(8,128)} collective-permute-done((f32[128,768]{1,0:T(8,128)}, f32[128,768]{1,0:T(8,128)}, u32[]{:S(2)}, u32[]{:S(2)}) %collective-permute-start.3) | collective-permute-done | bytes 393248 | tf_op jit(solution)/shard_map/pair_e1/ppermute | solution.py:613
  26.7 2.5 enc_mlp_fwd.3
  31.3 3.8 %collective-permute-done.2.refs_7_ = f32[128,768]{1,0:T(8,128)} collective-permute-done((f32[128,768]{1,0:T(8,128)}, f32[128,768]{1,0:T(8,128)}, u32[]{:S(2)}, u32[]{:S(2)}) %collective-permute-start.2) | collective-permute-done | bytes 393248 | tf_op jit(solution)/shard_map/pair_d1/ppermute | solution.py:613
  35.1 8.3 %collective-permute-done.1.refs_3_ = f32[128,768]{1,0:T(8,128)S(1)} collective-permute-done((f32[128,768]{1,0:T(8,128)S(1)}, f32[128,768]{1,0:T(8,128)S(1)}, u32[]{:S(2)}, u32[]{:S(2)}) %collective-permute-start.1) | collective-permute-done | bytes 393248 | tf_op jit(solution)/shard_map/pair_e2/ppermute | solution.py:613
  47.9 4.0 %collective-permute-done.4.refs_3_ = f32[128,768]{1,0:T(8,128)S(1)} collective-permute-done((f32[128,768]{1,0:T(8,128)S(1)}, f32[128,768]{1,0:T(8,128)S(1)}, u32[]{:S(2)}, u32[]{:S(2)}) %collective-permute-start.4) | collective-permute-done | bytes 393248 | tf_op jit(solution)/shard_map/pair_e2/ppermute | solution.py:613
  56.3 3.6 %collective-permute-done.6.refs_5_ = f32[64,768]{1,0:T(8,128)S(1)} collective-permute-done((f32[64,768]{1,0:T(8,128)S(1)}, f32[64,768]{1,0:T(8,128)S(1)}, u32[]{:S(2)}, u32[]{:S(2)}) %collective-permute-start.6) | collective-permute-done | bytes 196640 | tf_op jit(solution)/shard_map/pair_d2/ppermute | solution.py:613
  70.9 3.4 %collective-permute-done.7.refs_2_ = f32[128,768]{1,0:T(8,128)S(1)} collective-permute-done((f32[128,768]{1,0:T(8,128)S(1)}, f32[128,768]{1,0:T(8,128)S(1)}, u32[]{:S(2)}, u32[]{:S(2)}) %collective-permute-start.7) | collective-permute-done | bytes 393248 | tf_op jit(solution)/shard_map/pair_g3/ppermute | solution.py:613
  74.3 4.8 %cross_back.1 = (f32[256,768]{1,0:T(8,128)S(1)}, f32[128,768]{1,0:T(8,128)S(1)}, f32[1,768]{1,0:T(1,128)S(1)}, f32[128,1280]{1,0:T(8,128)S(1)}, f32[128,1280]{1,...) custom-call(s32[2]{0:T(128)S(1)} %copy-done.18, f32[128,768]{1,0:T(8,128)S(1)} %get-tuple-element.127.refs_1_, ...), custom_call_target="tpu_custom_call" | custom-call | flops 3449999872 | bytes 11070000 | tf_op jit(solution)/shard_map/cross_back/pallas_call | solution.py:563
  81.4 5.8 %collective-permute-done.13.refs_1_ = f32[192,1024]{1,0:T(8,128)S(1)} collective-permute-done((f32[192,1024]{1,0:T(8,128)S(1)}, f32[192,1024]{1,0:T(8,128)S(1)}, u32[]{:S(2)}, u32[]{:S(2)}) %collective-permute-start.13) | collective-permute-done | bytes 786464 | tf_op jit(solution)/shard_map/swap_mo_x/ppermute | solution.py:624
  91.9 6.5 %collective-permute-done.9.refs_1_ = f32[256,768]{1,0:T(8,128)S(1)} collective-permute-done((f32[256,768]{1,0:T(8,128)S(1)}, f32[256,768]{1,0:T(8,128)S(1)}, u32[]{:S(2)}, u32[]{:S(2)}) %collective-permute-start.9) | collective-permute-done | bytes 786464 | tf_op jit(solution)/shard_map/pair_m/ppermute | solution.py:613
  98.4 3.0 %enc_mlp_back.1 = (f32[256,768]{1,0:T(8,128)S(1)}, f32[256,768]{1,0:T(8,128)S(1)}, f32[1,768]{1,0:T(1,128)S(1)}, f32[256,3840]{1,0:T(8,128)S(1)}, bf16[256,3840]{1,0:T(8,128)(2,1)S(1)}) custom-call(f32[256,768]{1,0:T(8,128)S(1)} %get-tuple-element.134.refs_0_, f32[256,768]{1,0:T(8,128)S(1)} %collective-permute-done.9.refs_1_, ...), custom_call_target="tpu_custom_call" | custom-call | flops 3449999872 | bytes 11070000 | tf_op jit(solution)/shard_map/enc_mlp_back/pallas_call | solution.py:563
  101.5 5.1 %collective-permute-done.16.refs_1_ = f32[192,2048]{1,0:T(8,128)S(1)} collective-permute-done((f32[192,2048]{1,0:T(8,128)S(1)}, f32[192,2048]{1,0:T(8,128)S(1)}, u32[]{:S(2)}, u32[]{:S(2)}) %collective-permute-start.16) | collective-permute-done | bytes 1572896 | tf_op jit(solution)/shard_map/swap_m_p/ppermute | solution.py:624
  116.6 6.8 %collective-permute-done.19.refs_2_ = f32[128,768]{1,0:T(8,128)S(1)} collective-permute-done((f32[128,768]{1,0:T(8,128)S(1)}, f32[128,768]{1,0:T(8,128)S(1)}, u32[]{:S(2)}, u32[]{:S(2)}) %collective-permute-start.19) | collective-permute-done | bytes 393248 | tf_op jit(solution)/shard_map/pair_q/ppermute | solution.py:613
  123.4 3.5 %dec_self_back.1 = (f32[128,768]{1,0:T(8,128)S(1)}, f32[128,768]{1,0:T(8,128)S(1)}, f32[2,768]{1,0:T(2,128)S(1)}, f32[128,2304]{1,0:T(8,128)S(1)}, bf16[128,2304]{1,0:T(8,128)(2,1)S(1)}) custom-call(s32[2]{0:T(128)S(1)} %copy-done.32, f32[128,768]{1,0:T(8,128)S(1)} %query_part.1.refs_2_.refs_1_, f32[128,768]{1,0:T(8,128)S(1)} %collective-permute-done.19.refs_2_, ...), custom_call_target="tpu_custom_call" | custom-call | flops 3449999872 | bytes 11070000 | tf_op jit(solution)/shard_map/dec_self_back/pallas_call | solution.py:563
  128.7 7.1 %collective-permute-done.17.refs_1_ = f32[192,1024]{1,0:T(8,128)S(1)} collective-permute-done((f32[192,1024]{1,0:T(8,128)S(1)}, f32[192,1024]{1,0:T(8,128)S(1)}, u32[]{:S(2)}, u32[]{:S(2)}) %collective-permute-start.17) | collective-permute-done | bytes 786464 | tf_op jit(solution)/shard_map/swap_fo_x/ppermute | solution.py:624
  139.1 2.4 collective-permute-start.29
  141.6 5.4 %enc_attn_back.1 = (f32[256,768]{1,0:T(8,128)S(1)}, f32[256,768]{1,0:T(8,128)S(1)}, f32[2,768]{1,0:T(2,128)S(1)}, f32[256,2304]{1,0:T(8,128)S(1)}, bf16[256,2304]{1,0:T(8,128)(2,1)S(1)}) custom-call(s32[2]{0:T(128)S(1)} %copy-done.18, f32[256,768]{1,0:T(8,128)S(1)} %get-tuple-element.145.refs_1_, f32[256,768]{1,0:T(8,128)S(1)} %collective-permute-done.14.refs_2_, ...), custom_call_target="tpu_custom_call" | custom-call | flops 1150000000 | bytes 3690000 | tf_op jit(solution)/shard_map/enc_attn_back/pallas_call | solution.py:563
  155.0 4.6 %collective-permute-start.38 = (f32[96,1024]{1,0:T(8,128)S(1)}, f32[96,1024]{1,0:T(8,128)S(1)}, u32[]{:S(2)}, u32[]{:S(2)}) collective-permute-start(f32[96,1024]{1,0:T(8,128)S(1)} %get-tuple-element.163.refs_13_), channel_id=1, source_target_pairs={{0,8},{2,10},{4,12},{6,14},{8,0},{10,2},{12,4},{14,6},{16,24},{18,... | collective-permute-start | bytes 1179656 | tf_op jit(solution)/shard_map/swap_fo_p/ppermute | solution.py:624
  162.3 7.2 %collective-permute-done.32.refs_1_ = f32[96,2048]{1,0:T(8,128)S(1)} collective-permute-done((f32[96,2048]{1,0:T(8,128)S(1)}, f32[96,2048]{1,0:T(8,128)S(1)}, u32[]{:S(2)}, u32[]{:S(2)}) %collective-permute-start.32) | collective-permute-done | bytes 786464 | tf_op jit(solution)/shard_map/swap_f_x/ppermute | solution.py:624
  171.2 18.4 %collective-permute-start.36 = (f32[48,1536]{1,0:T(8,128)S(1)}, f32[48,1536]{1,0:T(8,128)S(1)}, u32[]{:S(2)}, u32[]{:S(2)}) collective-permute-start(f32[48,1536]{1,0:T(8,128)S(1)} %get-tuple-element.185.refs_2_), channel_id=1, source_target_pairs={{0,8},{2,10},{4,12},{6,14},{8,0},{10,2},{12,4},{14,6},{16,24},{18,... | collective-permute-start | bytes 884744 | tf_op jit(solution)/shard_map/swap_c_e/ppermute | solution.py:624
  189.6 5.2 %collective-permute-done.28.refs_1_ = f32[192,1536]{1,0:T(8,128)S(1)} collective-permute-done((f32[192,1536]{1,0:T(8,128)S(1)}, f32[192,1536]{1,0:T(8,128)S(1)}, u32[]{:S(2)}, u32[]{:S(2)}) %collective-permute-start.28) | collective-permute-done | bytes 1179680 | tf_op jit(solution)/shard_map/swap_s_p/ppermute | solution.py:624
  201.8 5.8 %collective-permute-start.41 = (f32[48,2048]{1,0:T(8,128)S(1)}, f32[48,2048]{1,0:T(8,128)S(1)}, u32[]{:S(2)}, u32[]{:S(2)}) collective-permute-start(f32[48,2048]{1,0:T(8,128)S(1)} %get-tuple-element.194.refs_2_), channel_id=1, source_target_pairs={{0,8},{2,10},{4,12},{6,14},{8,0},{10,2},{12,4},{14,6},{16,24},{18,... | collective-permute-start | bytes 1179656 | tf_op jit(solution)/shard_map/swap_f_e/ppermute | solution.py:624
  209.4 5.4 %collective-permute-done.34.refs_1_ = f32[96,1664]{1,0:T(8,128)S(1)} collective-permute-done((f32[96,1664]{1,0:T(8,128)S(1)}, f32[96,1664]{1,0:T(8,128)S(1)}, u32[]{:S(2)}, u32[]{:S(2)}) %collective-permute-start.34) | collective-permute-done | bytes 639008 | tf_op jit(solution)/shard_map/swap_a_p/ppermute | solution.py:624
  215.6 4.2 %collective-permute-start.44 = (f32[48,1024]{1,0:T(8,128)S(1)}, f32[48,1024]{1,0:T(8,128)S(1)}, u32[]{:S(2)}, u32[]{:S(2)}) collective-permute-start(f32[48,1024]{1,0:T(8,128)S(1)} %get-tuple-element.173.refs_2_), channel_id=1, source_target_pairs={{0,8},{2,10},{4,12},{6,14},{8,0},{10,2},{12,4},{14,6},{16,24},{18,... | collective-permute-start | bytes 589832 | tf_op jit(solution)/shard_map/swap_mo_e/ppermute | solution.py:624
  220.4 2.8 %collective-permute-done.41.refs_1_ = f32[48,2048]{1,0:T(8,128)S(1)} collective-permute-done((f32[48,2048]{1,0:T(8,128)S(1)}, f32[48,2048]{1,0:T(8,128)S(1)}, u32[]{:S(2)}, u32[]{:S(2)}) %collective-permute-start.41) | collective-permute-done | bytes 393248 | tf_op jit(solution)/shard_map/swap_f_e/ppermute | solution.py:624
  227.8 8.3 %collective-permute-start.46 = (f32[48,1024]{1,0:T(8,128)S(1)}, f32[48,1024]{1,0:T(8,128)S(1)}, u32[]{:S(2)}, u32[]{:S(2)}) collective-permute-start(f32[48,1024]{1,0:T(8,128)S(1)} %get-tuple-element.197.refs_2_), channel_id=1, source_target_pairs={{0,8},{2,10},{4,12},{6,14},{8,0},{10,2},{12,4},{14,6},{16,24},{18,... | collective-permute-start | bytes 589832 | tf_op jit(solution)/shard_map/swap_fo_e/ppermute | solution.py:624
  242.1 5.2 %collective-permute-start.48 = (f32[48,1536]{1,0:T(8,128)S(1)}, f32[48,1536]{1,0:T(8,128)S(1)}, u32[]{:S(2)}, u32[]{:S(2)}) collective-permute-start(f32[48,1536]{1,0:T(8,128)S(1)} %get-tuple-element.205.refs_2_), channel_id=1, source_target_pairs={{0,8},{2,10},{4,12},{6,14},{8,0},{10,2},{12,4},{14,6},{16,24},{18,... | collective-permute-start | bytes 884744 | tf_op jit(solution)/shard_map/swap_s_e/ppermute | solution.py:624
  (215 shorter events, 93.6 us)
Async XLA Ops:
  11.3 15.4 %collective-permute-start.3 = (f32[128,768]{1,0:T(8,128)}, f32[128,768]{1,0:T(8,128)}, u32[]{:S(2)}, u32[]{:S(2)}) collective-permute-start(f32[128,768]{1,0:T(8,128)} %get-tuple-element.117.refs_5_.refs_1_), channel_id=1, source_target_pairs={{0,1},{1,0},{2,3},{3,2},{4,5},{5,4},{6,7},{7,6},{8,9},{9,8},{10,11... | collective-permute-start | bytes 1179656 | tf_op jit(solution)/shard_map/pair_e1/ppermute | solution.py:613
  14.6 20.5 %collective-permute-start.2 = (f32[128,768]{1,0:T(8,128)}, f32[128,768]{1,0:T(8,128)}, u32[]{:S(2)}, u32[]{:S(2)}) collective-permute-start(f32[128,768]{1,0:T(8,128)} %get-tuple-element.118.refs_1_.refs_6_), channel_id=1, source_target_pairs={{0,1},{1,0},{2,3},{3,2},{4,5},{5,4},{6,7},{7,6},{8,9},{9,8},{10,11... | collective-permute-start | bytes 1179656 | tf_op jit(solution)/shard_map/pair_d1/ppermute | solution.py:613
  21.6 21.9 %collective-permute-start.1 = (f32[128,768]{1,0:T(8,128)S(1)}, f32[128,768]{1,0:T(8,128)S(1)}, u32[]{:S(2)}, u32[]{:S(2)}) collective-permute-start(f32[128,768]{1,0:T(8,128)S(1)} %get-tuple-element.120.refs_6_.refs_2_), channel_id=1, source_target_pairs={{0,1},{1,0},{2,3},{3,2},{4,5},{5,4},{6,7},{7,6},{8,9},{9,8},{10,11... | collective-permute-start | bytes 1179656 | tf_op jit(solution)/shard_map/pair_e2/ppermute | solution.py:613
  29.2 22.7 %collective-permute-start.4 = (f32[128,768]{1,0:T(8,128)S(1)}, f32[128,768]{1,0:T(8,128)S(1)}, u32[]{:S(2)}, u32[]{:S(2)}) collective-permute-start(f32[128,768]{1,0:T(8,128)S(1)} %get-tuple-element.121.refs_1_.refs_2_), channel_id=1, source_target_pairs={{0,1},{1,0},{2,3},{3,2},{4,5},{5,4},{6,7},{7,6},{8,9},{9,8},{10,11... | collective-permute-start | bytes 1179656 | tf_op jit(solution)/shard_map/pair_e2/ppermute | solution.py:613
  45.8 14.2 %collective-permute-start.5 = (f32[64,768]{1,0:T(8,128)S(1)}, f32[64,768]{1,0:T(8,128)S(1)}, u32[]{:S(2)}, u32[]{:S(2)}) collective-permute-start(f32[64,768]{1,0:T(8,128)S(1)} %get-tuple-element.124.refs_11_.refs_2_), channel_id=1, source_target_pairs={{0,1},{1,0},{2,3},{3,2},{4,5},{5,4},{6,7},{7,6},{8,9},{9,8},{10,11... | collective-permute-start | bytes 589832 | tf_op jit(solution)/shard_map/pair_d2/ppermute | solution.py:613
  67.3 19.9 %collective-permute-start.13 = (f32[192,1024]{1,0:T(8,128)S(1)}, f32[192,1024]{1,0:T(8,128)S(1)}, u32[]{:S(2)}, u32[]{:S(2)}) collective-permute-start(f32[192,1024]{1,0:T(8,128)S(1)} %get-tuple-element.133.refs_18_), channel_id=1, source_target_pairs={{0,4},{2,6},{4,0},{6,2},{8,12},{10,14},{12,8},{14,10},{16,20},{18,... | collective-permute-start | bytes 2359304 | tf_op jit(solution)/shard_map/swap_mo_x/ppermute | solution.py:624
  69.3 37.3 %collective-permute-start.16 = (f32[192,2048]{1,0:T(8,128)S(1)}, f32[192,2048]{1,0:T(8,128)S(1)}, u32[]{:S(2)}, u32[]{:S(2)}) collective-permute-start(f32[192,2048]{1,0:T(8,128)S(1)} %get-tuple-element.152), channel_id=1, source_target_pairs={{0,8},{2,10},{4,12},{6,14},{8,0},{10,2},{12,4},{14,6},{16,24},{18,... | collective-permute-start | bytes 4718600 | tf_op jit(solution)/shard_map/swap_m_p/ppermute | solution.py:624
  79.1 19.4 %collective-permute-start.9 = (f32[256,768]{1,0:T(8,128)S(1)}, f32[256,768]{1,0:T(8,128)S(1)}, u32[]{:S(2)}, u32[]{:S(2)}) collective-permute-start(f32[256,768]{1,0:T(8,128)S(1)} %get-tuple-element.134.refs_0_), channel_id=1, source_target_pairs={{0,1},{1,0},{2,3},{3,2},{4,5},{5,4},{6,7},{7,6},{8,9},{9,8},{10,11... | collective-permute-start | bytes 2359304 | tf_op jit(solution)/shard_map/pair_m/ppermute | solution.py:613
  87.3 27.8 %collective-permute-start.20 = (f32[96,1024]{1,0:T(8,128)S(1)}, f32[96,1024]{1,0:T(8,128)S(1)}, u32[]{:S(2)}, u32[]{:S(2)}) collective-permute-start(f32[96,1024]{1,0:T(8,128)S(1)} %get-tuple-element.143.refs_4_), channel_id=1, source_target_pairs={{0,8},{2,10},{4,12},{6,14},{8,0},{10,2},{12,4},{14,6},{16,24},{18,... | collective-permute-start | bytes 1179656 | tf_op jit(solution)/shard_map/swap_mo_p/ppermute | solution.py:624
  90.1 36.9 %collective-permute-start.18 = (f32[192,1536]{1,0:T(8,128)S(1)}, f32[192,1536]{1,0:T(8,128)S(1)}, u32[]{:S(2)}, u32[]{:S(2)}) collective-permute-start(f32[192,1536]{1,0:T(8,128)S(1)} %get-tuple-element.144.refs_13_), channel_id=1, source_target_pairs={{0,4},{2,6},{4,0},{6,2},{8,12},{10,14},{12,8},{14,10},{16,20},{18,... | collective-permute-start | bytes 3538952 | tf_op jit(solution)/shard_map/swap_c_x/ppermute | solution.py:624
  109.7 39.0 %collective-permute-start.23 = (f32[192,2048]{1,0:T(8,128)S(1)}, f32[192,2048]{1,0:T(8,128)S(1)}, u32[]{:S(2)}, u32[]{:S(2)}) collective-permute-start(f32[192,2048]{1,0:T(8,128)S(1)} %get-tuple-element.172), channel_id=1, source_target_pairs={{0,8},{2,10},{4,12},{6,14},{8,0},{10,2},{12,4},{14,6},{16,24},{18,... | collective-permute-start | bytes 4718600 | tf_op jit(solution)/shard_map/swap_f_p/ppermute | solution.py:624
  112.9 22.9 %collective-permute-start.17 = (f32[192,1024]{1,0:T(8,128)S(1)}, f32[192,1024]{1,0:T(8,128)S(1)}, u32[]{:S(2)}, u32[]{:S(2)}) collective-permute-start(f32[192,1024]{1,0:T(8,128)S(1)} %get-tuple-element.156.refs_2_), channel_id=1, source_target_pairs={{0,4},{2,6},{4,0},{6,2},{8,12},{10,14},{12,8},{14,10},{16,20},{18,... | collective-permute-start | bytes 2359304 | tf_op jit(solution)/shard_map/swap_fo_x/ppermute | solution.py:624
  115.0 24.1 %collective-permute-start.14 = (f32[256,768]{1,0:T(8,128)S(1)}, f32[256,768]{1,0:T(8,128)S(1)}, u32[]{:S(2)}, u32[]{:S(2)}) collective-permute-start(f32[256,768]{1,0:T(8,128)S(1)} %get-tuple-element.145.refs_1_), channel_id=1, source_target_pairs={{0,1},{1,0},{2,3},{3,2},{4,5},{5,4},{6,7},{7,6},{8,9},{9,8},{10,11... | collective-permute-start | bytes 2359304 | tf_op jit(solution)/shard_map/pair_g1/ppermute | solution.py:613
  126.9 22.1 %collective-permute-start.22 = (f32[128,2304]{1,0:T(8,128)S(1)}, f32[128,2304]{1,0:T(8,128)S(1)}, u32[]{:S(2)}, u32[]{:S(2)}) collective-permute-start(f32[128,2304]{1,0:T(8,128)S(1)} %get-tuple-element.170), channel_id=1, source_target_pairs={{0,2},{2,0},{4,6},{6,4},{8,10},{10,8},{12,14},{14,12},{16,18},{18,... | collective-permute-start | bytes 3538952 | tf_op jit(solution)/shard_map/swap_s_0/ppermute | solution.py:624
  127.0 25.7 %collective-permute-start.26 = (f32[96,2048]{1,0:T(8,128)S(1)}, f32[96,2048]{1,0:T(8,128)S(1)}, u32[]{:S(2)}, u32[]{:S(2)}) collective-permute-start(f32[96,2048]{1,0:T(8,128)S(1)} %get-tuple-element.154.refs_2_), channel_id=1, source_target_pairs={{0,4},{2,6},{4,0},{6,2},{8,12},{10,14},{12,8},{14,10},{16,20},{18,... | collective-permute-start | bytes 2359304 | tf_op jit(solution)/shard_map/swap_m_x/ppermute | solution.py:624
  139.1 21.5 %collective-permute-start.29 = (f32[96,1536]{1,0:T(8,128)S(1)}, f32[96,1536]{1,0:T(8,128)S(1)}, u32[]{:S(2)}, u32[]{:S(2)}) collective-permute-start(f32[96,1536]{1,0:T(8,128)S(1)} %get-tuple-element.162.refs_2_), channel_id=1, source_target_pairs={{0,8},{2,10},{4,12},{6,14},{8,0},{10,2},{12,4},{14,6},{16,24},{18,... | collective-permute-start | bytes 1769480 | tf_op jit(solution)/shard_map/swap_c_p/ppermute | solution.py:624
  149.0 20.6 %collective-permute-start.32 = (f32[96,2048]{1,0:T(8,128)S(1)}, f32[96,2048]{1,0:T(8,128)S(1)}, u32[]{:S(2)}, u32[]{:S(2)}) collective-permute-start(f32[96,2048]{1,0:T(8,128)S(1)} %get-tuple-element.174.refs_2_), channel_id=1, source_target_pairs={{0,4},{2,6},{4,0},{6,2},{8,12},{10,14},{12,8},{14,10},{16,20},{18,... | collective-permute-start | bytes 2359304 | tf_op jit(solution)/shard_map/swap_f_x/ppermute | solution.py:624
  152.8 17.5 %collective-permute-start.31 = (f32[96,2048]{1,0:T(8,128)S(1)}, f32[96,2048]{1,0:T(8,128)S(1)}, u32[]{:S(2)}, u32[]{:S(2)}) collective-permute-start(f32[96,2048]{1,0:T(8,128)S(1)} %halve_m.4.refs_4_.refs_0_), channel_id=1, source_target_pairs={{8,16},{10,18},{12,20},{14,22},{16,8},{18,10},{20,12},{22,14},{9,1... | collective-permute-start | bytes 2359304 | tf_op jit(solution)/shard_map/swap_m_m/ppermute | solution.py:624
  155.0 44.3 %collective-permute-start.38 = (f32[96,1024]{1,0:T(8,128)S(1)}, f32[96,1024]{1,0:T(8,128)S(1)}, u32[]{:S(2)}, u32[]{:S(2)}) collective-permute-start(f32[96,1024]{1,0:T(8,128)S(1)} %get-tuple-element.163.refs_13_), channel_id=1, source_target_pairs={{0,8},{2,10},{4,12},{6,14},{8,0},{10,2},{12,4},{14,6},{16,24},{18,... | collective-permute-start | bytes 1179656 | tf_op jit(solution)/shard_map/swap_fo_p/ppermute | solution.py:624
  159.6 35.2 %collective-permute-start.28 = (f32[192,1536]{1,0:T(8,128)S(1)}, f32[192,1536]{1,0:T(8,128)S(1)}, u32[]{:S(2)}, u32[]{:S(2)}) collective-permute-start(f32[192,1536]{1,0:T(8,128)S(1)} %get-tuple-element.175.refs_5_), channel_id=1, source_target_pairs={{0,8},{2,10},{4,12},{6,14},{8,0},{10,2},{12,4},{14,6},{16,24},{18,... | collective-permute-start | bytes 3538952 | tf_op jit(solution)/shard_map/swap_s_p/ppermute | solution.py:624
  160.7 35.8 %collective-permute-start.27 = (f32[192,1664]{1,0:T(8,128)S(1)}, f32[192,1664]{1,0:T(8,128)S(1)}, u32[]{:S(2)}, u32[]{:S(2)}) collective-permute-start(f32[192,1664]{1,0:T(8,128)S(1)} %get-tuple-element.180.refs_2_), channel_id=1, source_target_pairs={{0,4},{2,6},{4,0},{6,2},{8,12},{10,14},{12,8},{14,10},{16,20},{18,... | collective-permute-start | bytes 3833864 | tf_op jit(solution)/shard_map/swap_a_x/ppermute | solution.py:624
  170.3 30.6 %collective-permute-start.37 = (f32[96,2048]{1,0:T(8,128)S(1)}, f32[96,2048]{1,0:T(8,128)S(1)}, u32[]{:S(2)}, u32[]{:S(2)}) collective-permute-start(f32[96,2048]{1,0:T(8,128)S(1)} %halve_f.4.refs_2_.refs_0_), channel_id=1, source_target_pairs={{8,16},{10,18},{12,20},{14,22},{16,8},{18,10},{20,12},{22,14},{9,1... | collective-permute-start | bytes 2359304 | tf_op jit(solution)/shard_map/swap_f_m/ppermute | solution.py:624
  171.2 30.5 %collective-permute-start.36 = (f32[48,1536]{1,0:T(8,128)S(1)}, f32[48,1536]{1,0:T(8,128)S(1)}, u32[]{:S(2)}, u32[]{:S(2)}) collective-permute-start(f32[48,1536]{1,0:T(8,128)S(1)} %get-tuple-element.185.refs_2_), channel_id=1, source_target_pairs={{0,8},{2,10},{4,12},{6,14},{8,0},{10,2},{12,4},{14,6},{16,24},{18,... | collective-permute-start | bytes 884744 | tf_op jit(solution)/shard_map/swap_c_e/ppermute | solution.py:624
  194.9 14.4 %collective-permute-start.35 = (f32[96,1536]{1,0:T(8,128)S(1)}, f32[96,1536]{1,0:T(8,128)S(1)}, u32[]{:S(2)}, u32[]{:S(2)}) collective-permute-start(f32[96,1536]{1,0:T(8,128)S(1)} %get-tuple-element.186.refs_2_), channel_id=1, source_target_pairs={{0,4},{2,6},{4,0},{6,2},{8,12},{10,14},{12,8},{14,10},{16,20},{18,... | collective-permute-start | bytes 1769480 | tf_op jit(solution)/shard_map/swap_s_x/ppermute | solution.py:624
  196.6 18.2 %collective-permute-start.34 = (f32[96,1664]{1,0:T(8,128)S(1)}, f32[96,1664]{1,0:T(8,128)S(1)}, u32[]{:S(2)}, u32[]{:S(2)}) collective-permute-start(f32[96,1664]{1,0:T(8,128)S(1)} %get-tuple-element.187.refs_4_), channel_id=1, source_target_pairs={{0,8},{2,10},{4,12},{6,14},{8,0},{10,2},{12,4},{14,6},{16,24},{18,... | collective-permute-start | bytes 1916936 | tf_op jit(solution)/shard_map/swap_a_p/ppermute | solution.py:624
  199.3 36.9 %collective-permute-start.33 = (f32[512,768]{1,0:T(8,128)S(1)}, f32[512,768]{1,0:T(8,128)S(1)}, u32[]{:S(2)}, u32[]{:S(2)}) collective-permute-start(f32[512,768]{1,0:T(8,128)S(1)} %tail_parts.1.refs_2_.refs_0_), channel_id=1, source_target_pairs={{0,1},{1,0},{2,3},{3,2},{4,5},{5,4},{6,7},{7,6},{8,9},{9,8},{10,11... | collective-permute-start | bytes 4718600 | tf_op jit(solution)/shard_map/pair_tail/ppermute | solution.py:613
  201.0 25.1 %collective-permute-start.40 = (f32[96,1024]{1,0:T(8,128)S(1)}, f32[96,1024]{1,0:T(8,128)S(1)}, u32[]{:S(2)}, u32[]{:S(2)}) collective-permute-start(f32[96,1024]{1,0:T(8,128)S(1)} %halve_fo.4.refs_2_.refs_0_), channel_id=1, source_target_pairs={{8,16},{10,18},{12,20},{14,22},{16,8},{18,10},{20,12},{22,14},{9,1... | collective-permute-start | bytes 1179656 | tf_op jit(solution)/shard_map/swap_fo_m/ppermute | solution.py:624
  201.8 21.5 %collective-permute-start.41 = (f32[48,2048]{1,0:T(8,128)S(1)}, f32[48,2048]{1,0:T(8,128)S(1)}, u32[]{:S(2)}, u32[]{:S(2)}) collective-permute-start(f32[48,2048]{1,0:T(8,128)S(1)} %get-tuple-element.194.refs_2_), channel_id=1, source_target_pairs={{0,8},{2,10},{4,12},{6,14},{8,0},{10,2},{12,4},{14,6},{16,24},{18,... | collective-permute-start | bytes 1179656 | tf_op jit(solution)/shard_map/swap_f_e/ppermute | solution.py:624
  215.6 23.8 %collective-permute-start.44 = (f32[48,1024]{1,0:T(8,128)S(1)}, f32[48,1024]{1,0:T(8,128)S(1)}, u32[]{:S(2)}, u32[]{:S(2)}) collective-permute-start(f32[48,1024]{1,0:T(8,128)S(1)} %get-tuple-element.173.refs_2_), channel_id=1, source_target_pairs={{0,8},{2,10},{4,12},{6,14},{8,0},{10,2},{12,4},{14,6},{16,24},{18,... | collective-permute-start | bytes 589832 | tf_op jit(solution)/shard_map/swap_mo_e/ppermute | solution.py:624
  223.2 14.4 %collective-permute-start.45 = (f32[48,2048]{1,0:T(8,128)S(1)}, f32[48,2048]{1,0:T(8,128)S(1)}, u32[]{:S(2)}, u32[]{:S(2)}) collective-permute-start(f32[48,2048]{1,0:T(8,128)S(1)} %get-tuple-element.184.refs_2_), channel_id=1, source_target_pairs={{0,8},{2,10},{4,12},{6,14},{8,0},{10,2},{12,4},{14,6},{16,24},{18,... | collective-permute-start | bytes 1179656 | tf_op jit(solution)/shard_map/swap_m_e/ppermute | solution.py:624
  226.1 15.0 %collective-permute-start.43 = (f32[96,1536]{1,0:T(8,128)S(1)}, f32[96,1536]{1,0:T(8,128)S(1)}, u32[]{:S(2)}, u32[]{:S(2)}) collective-permute-start(f32[96,1536]{1,0:T(8,128)S(1)} %halve_s.4.refs_1_.refs_0_), channel_id=1, source_target_pairs={{8,16},{10,18},{12,20},{14,22},{16,8},{18,10},{20,12},{22,14},{9,1... | collective-permute-start | bytes 1769480 | tf_op jit(solution)/shard_map/swap_s_m/ppermute | solution.py:624
  227.8 21.8 %collective-permute-start.46 = (f32[48,1024]{1,0:T(8,128)S(1)}, f32[48,1024]{1,0:T(8,128)S(1)}, u32[]{:S(2)}, u32[]{:S(2)}) collective-permute-start(f32[48,1024]{1,0:T(8,128)S(1)} %get-tuple-element.197.refs_2_), channel_id=1, source_target_pairs={{0,8},{2,10},{4,12},{6,14},{8,0},{10,2},{12,4},{14,6},{16,24},{18,... | collective-permute-start | bytes 589832 | tf_op jit(solution)/shard_map/swap_fo_e/ppermute | solution.py:624
  (61 other events, 349.9 us)

commit v8 on v7

--- a/solution.py
+++ b/solution.py
@@ -363,9 +363,16 @@
     put_cut(send, keep, half + 2 * width, low, order_outer)
 
 
-def gains_kernel(enc_attn, enc_mlp, dec_self, dec_cross, order, send, keep):
-    rows = [enc_attn[1:2, :], enc_attn[0:1, :], enc_mlp[...], dec_self[1:2, :], dec_self[0:1, :], dec_cross[...]]
-    rest = jnp.concatenate(rows + [jnp.zeros((128 - len(rows), order.shape[0]), F32)], 0)
+def gain_rows_kernel(enc_attn, enc_mlp, dec_self, dec_cross, out):
+    for at, row in enumerate((enc_attn[1:2, :], enc_attn[0:1, :], enc_mlp[...], dec_self[1:2, :], dec_self[0:1, :],
+                              dec_cross[...])):
+        out[at : at + 1, :] = row
+    out[6:8, :] = jnp.zeros((2, out.shape[1]), F32)
+
+
+def gains_kernel(own, other, order, send, keep):
+    rest = own[...] + other[...]
+    rest = jnp.concatenate([rest, jnp.zeros((128 - rest.shape[0], rest.shape[1]), F32)], 0)
     total = None
     for _ in range(3):
         low = rest.astype(BF)
@@ -375,14 +382,6 @@
     half = total.shape[0] // 2
     send[...] = total[:half]
     keep[...] = total[half:]
-
-
-def gains_out_kernel(own, other, enc_out, dec_out):
-    total = own[...] + other[...]
-    rows, columns = total.shape
-    total = jnp.concatenate([total, jnp.zeros((columns - rows, columns), F32)], 0).T
-    enc_out[...] = total[0:3, :rows]
-    dec_out[...] = total[3:6, :rows]
 
 
 def gains_weight_kernel(segments, keep, recv, gains, other_gains, send_out, keep_out):
@@ -430,27 +429,26 @@
 
 COST = {
     "enc_attn_fwd": 2.3, "dec_self_fwd": 2.5, "enc_mlp_fwd": 1.7, "cross_fwd": 4.2, "dec_mlp": 2.7,
-    "cross_back": 3.0, "weights_c": 0.3, "enc_mlp_back": 3.0, "enc_attn_back": 1.0, "query_part": 20.0,
-    "weights_f": 8.0, "weights_a": 0.1, "dec_self_back": 3.0, "weights_s": 3.0, "tail_parts": 0.1,
-    "tail": 8.0, "gains": 8.0, "gains_out": 0.1, "halve_m": 20.0, "halve_mo": 1.0,
-    "halve_c": 0.1, "halve_f": 3.0, "halve_fo": 3.0, "halve_s": 0.1, "halve_a": 1.0,
-    "finish_m": 3.0, "finish_mo": 1.0, "finish_c": 8.0, "finish_f": 1.0, "finish_fo": 3.0,
-    "finish_s": 1.0, "finish_a": 1.0, "weights_m": 1.0,
+    "cross_back": 20.0, "weights_c": 0.1, "enc_mlp_back": 3.0, "enc_attn_back": 0.3, "query_part": 20.0,
+    "weights_f": 3.0, "weights_a": 0.1, "dec_self_back": 0.3, "weights_s": 1.0, "tail_parts": 3.0,
+    "tail": 20.0, "gains": 1.0, "gain_rows": 1.0, "halve_m": 20.0, "halve_mo": 0.3,
+    "halve_c": 0.1, "halve_f": 0.1, "halve_fo": 3.0, "halve_s": 8.0, "halve_a": 0.1,
+    "finish_m": 0.3, "finish_mo": 3.0, "finish_c": 0.1, "finish_f": 0.1, "finish_fo": 1.0,
+    "finish_s": 0.1, "finish_a": 8.0, "weights_m": 0.1,
 }
 VMEM_LIMIT = 8
 
 LINE = (
     "pause", "enc_attn_0", "enc_attn_1", "dec_self", "pause", "enc_mlp_0", "enc_mlp_1", "pause",
     "cross_0", "cross_1", "pause", "dec_mlp", "tick", "w_m", "cross_back", "h_mo",
-    "w_c", "enc_mlp_back", "tick", "h_m", "query_part", "w_f", "h_mo", "dec_self_back",
-    "h_c", "h_fo", "enc_attn_back", "h_mo", "h_f", "w_s", "gains", "h_m",
-    "w_a", "h_c", "h_f", "h_m", "h_c", "h_s", "h_a", "tail_parts",
-    "h_fo", "h_f", "e_c", "h_s", "tick", "h_a", "e_f", "h_fo",
-    "h_a", "tail", "e_m", "e_mo", "h_s", "e_a", "e_fo", "gains_out",
-    "e_s",
+    "w_c", "enc_mlp_back", "h_m", "query_part", "tick", "w_f", "h_mo", "enc_attn_back",
+    "h_c", "dec_self_back", "h_fo", "w_s", "gain_rows", "gains", "h_f", "h_mo",
+    "h_m", "w_a", "h_c", "h_fo", "h_f", "h_m", "h_s", "h_c",
+    "h_a", "h_f", "e_m", "tick", "tail_parts", "h_s", "h_a", "h_fo",
+    "e_c", "h_s", "h_a", "e_f", "tail", "e_s", "e_a",
 )
 HALVINGS = {"m": "pxme", "mo": "xpme", "c": "xpme", "f": "pxme", "fo": "xpme", "s": "pxme", "a": "xpme"}
-PARTS = {"m": 1, "c": 3, "f": 1, "a": 1, "s": 1}
+PARTS = {"m": 1, "c": 3, "f": 1, "a": 1, "s": 2}
 TICK = 0.1
 GAINS_WITH = "a"
 
@@ -592,13 +590,26 @@
     keep_out[...] = jnp.where(inner == 1, recv[:rows], kept[rows:])
 
 
-def finish_kernel(pieces, kept, recv, *outs):
-    for out, (first, count) in zip(outs, pieces):
-        width = out.shape[-1]
-        for i in range(count):
-            cols = slice(first + i * width, first + (i + 1) * width)
+def finish_kernel(pieces, *refs):
+    groups = 1 + max(group for group, _ in pieces)
+    outs = refs[2 * groups :]
+    at = 0
+    for group, firsts in pieces:
+        kept, recv = refs[2 * group], refs[2 * group + 1]
+        if firsts is None:
+            total = kept[:, -128:] + recv[:, -128:]
+            rows = total.shape[0]
+            total = jnp.concatenate([total, jnp.zeros((128 - rows, 128), F32)], 0).T
+            outs[at][...] = total[0:3, :rows]
+            outs[at + 1][...] = total[3:6, :rows]
+            at += 2
+            continue
+        out = outs[at]
+        at += 1
+        for i, first in enumerate(firsts):
+            cols = slice(first, first + out.shape[-1])
             total = kept[:, cols] + recv[:, cols]
-            if count > 1:
+            if len(firsts) > 1:
                 out[i] = total
             else:
                 out[...] = total
@@ -663,17 +674,25 @@
             sent, self.kept = line.call(middle_kernel if came == "m" else halve_kernel, [shape, shape], args, name)
         self.flying = swap(sent, self.steps[self.at], self.name)
 
-    def finish(self, line, *pieces):
+    def last(self):
         for bit in range(4, lax.axis_size("dp").bit_length() - 1):
             rows = self.kept.shape[0] // 2
             total = self.kept + self.flying
             self.kept, self.flying = total[rows:], swap(total[:rows], bit, self.name)
-        rows = self.kept.shape[0]
-        outs = [(((count, rows, width) if count > 1 else (rows, width)), F32) for _, count, width in pieces]
-        return line.call(
-            functools.partial(finish_kernel, [(first, count) for first, count, _ in pieces]),
-            outs, [self.kept, self.flying], "finish_" + self.name,
-        )
+        return [self.kept, self.flying]
+
+
+def finish(line, groups, pieces, name):
+    args = [array for group in groups for array in group.last()]
+    rows = args[0].shape[0]
+    outs = []
+    for _, firsts, width in pieces:
+        if firsts is None:
+            outs += [((3, rows), F32)] * 2
+        else:
+            outs.append((((len(firsts), rows, width) if len(firsts) > 1 else (rows, width)), F32))
+    kernel = functools.partial(finish_kernel, [(group, firsts) for group, firsts, _ in pieces])
+    return line.call(kernel, outs, args, "finish_" + name)
 
 
 def body(
@@ -883,21 +902,19 @@
             [v["part_tail"], v["other_tail"], x0, enc_gains, v["back1"], y0, dec_gains, v["g1"], v["y2"]], "tail",
         )
 
+    def collect_gains():
+        (v["gain_rows"],) = line.call(
+            gain_rows_kernel, [((8, features), F32)],
+            [v["gain_enc_attn"], v["gain_enc_mlp"], v["gain_dec_self"], v["gain_dec_cross"]], "gain_rows",
+        )
+        v["other_rows"] = pair_other(v["gain_rows"], "gains")
+
     def gains():
         send, v["keep_g"] = line.call(
             gains_kernel, [((half, 128), F32), ((half, 128), F32)],
-            [v["gain_enc_attn"], v["gain_enc_mlp"], v["gain_dec_self"], v["gain_dec_cross"], order_of[GAINS_WITH]],
-            "gains",
+            [v["gain_rows"], v["other_rows"], order_of[GAINS_WITH]], "gains",
         )
         v["recv_g"] = swap(send, 0, "g")
-
-    def gains_sum():
-        v["other_gains"] = pair_other(grad_of[GAINS_WITH][2], "gains")
-
-    def gains_out():
-        own = grad_of[GAINS_WITH][2]
-        shape = ((3, own.shape[0]), F32)
-        v["gains_out"] = line.call(gains_out_kernel, [shape, shape], [own, v["other_gains"]], "gains_out")
 
     def attn_weights(name):
         if name == GAINS_WITH:
@@ -912,20 +929,17 @@
             )
         start_sums(name, products)
 
-    attn_pieces = ((0, 3, heads), (3 * heads, 1, heads))
-    ends = {
-        "m": ((0, 2, units),), "f": ((0, 2, units),), "mo": ((0, 1, units),), "fo": ((0, 1, units),),
-        "c": ((0, 1, heads), (heads, 1, heads), (2 * heads, 2, heads)), "a": attn_pieces, "s": attn_pieces,
-    }
+    attn_pieces = ((0, (0, heads, 2 * heads), heads), (0, (3 * heads,), heads))
+    ends = {"c": ((0, (0, 2 * heads, 3 * heads), heads), (0, (heads,), heads)), "a": attn_pieces, "s": attn_pieces}
     for name in ("m", "f"):
-        if name + "o" not in HALVINGS:
-            ends[name] += ((2 * units, 1, units),)
-    ends[GAINS_WITH] += ((4 * heads, 1, 128),)
+        outer = (1, (0,), units) if name + "o" in HALVINGS else (0, (2 * units,), units)
+        ends[name] = ((0, (0, units), units), outer)
+    ends[GAINS_WITH] += ((0, None, 0),)
     stages = {
         "tick": tick, "pause": pause, "dec_self": dec_self, "dec_mlp": dec_mlp, "w_m": dec_mlp_weights,
         "cross_back": cross_back, "w_c": cross_weights, "enc_mlp_back": enc_mlp_back,
-        "w_f": enc_mlp_weights, "enc_attn_back": enc_attn_back, "query_part": query_part, "gains": gains,
-        "tail_parts": tail_parts, "tail": tail, "gains_out": gains_out,
+        "w_f": enc_mlp_weights, "enc_attn_back": enc_attn_back, "query_part": query_part, "gains": gains, "gain_rows": collect_gains,
+        "tail_parts": tail_parts, "tail": tail,
         "w_a": functools.partial(attn_weights, "a"), "dec_self_back": dec_self_back,
         "w_s": functools.partial(attn_weights, "s"),
     }
@@ -939,17 +953,13 @@
         elif kind == "h":
             sums[name].step(line)
         else:
-            grad_of[name] = sums[name].finish(line, *ends[name])
-            if name == GAINS_WITH:
-                gains_sum()
-    mlp_grads = {
-        name: grad_of[name] if name + "o" not in HALVINGS else grad_of[name] + grad_of[name + "o"] for name in ("m", "f")
-    }
-    grad_c = jnp.concatenate([grad_of["c"][0][None], grad_of["c"][2]], 0)
+            groups = [sums[part] for part in (name, name + "o") if part in sums]
+            grad_of[name] = finish(line, groups, ends[name], name)
+    gains_out = grad_of[GAINS_WITH][2:]
     grads = (
-        grad_of["a"][0], grad_of["a"][1].T, mlp_grads["f"][0], mlp_grads["f"][1].T, v["gains_out"][0],
-        grad_of["s"][0], grad_of["s"][1].T, grad_c, grad_of["c"][1].T, mlp_grads["m"][0], mlp_grads["m"][1].T,
-        v["gains_out"][1],
+        grad_of["a"][0], grad_of["a"][1].T, grad_of["f"][0], grad_of["f"][1].T, gains_out[0],
+        grad_of["s"][0], grad_of["s"][1].T, grad_of["c"][0], grad_of["c"][1].T, grad_of["m"][0], grad_of["m"][1].T,
+        gains_out[1],
     )
     return (
         v["dec_out"].reshape(cotangent.shape),

time: 256 us -> 255 us (level)
  waiting for transfers between devices: 92.8 us -> 107 us
  starting transfers between devices: 97.2 us -> 87.2 us
    ppermute x36 -> x37, waiting for transfers between devices: 48.4 us -> 63.5 us  [swap(): return lax.ppermute(value, 'dp', pairs)]
    ppermute x36 -> x37, starting transfers between devices: 74.5 us -> 63.4 us  [swap(): return lax.ppermute(value, 'dp', pairs)]
    unnamed x88 -> x86, local copies, waits for them, and re-layouts: 10.2 us -> 7.74 us
    pallas_call x57 -> x55, Pallas kernels: 51.8 us -> 50.1 us  [call(): pl.pallas_call(run, out_shape=shapes, in_specs=in_specs, out_specs=[VMEM]...]
  transfers between devices with their start and end apart: 49 -> 50, of which waited for: 26 -> 27; matrix products, arithmetic and copies ran while one was open for 1% -> 0% of each run, Pallas kernels for 18% -> 17%
where the time goes in v8:
time: 255 us; the launch traced here: 254 us
  waiting for transfers between devices  107 us (42%)
  starting transfers between devices  87.2 us (34%)
  Pallas kernels  50.1 us (20%)
  local copies, waits for them, and re-layouts  7.74 us (3%)
    ppermute x37, waiting for transfers between devices, swap(): return lax.ppermute(value, 'dp', pairs)  63.5 us
    ppermute x37, starting transfers between devices, swap(): return lax.ppermute(value, 'dp', pairs)  63.4 us
    pallas_call x55, Pallas kernels, call(): pl.pallas_call(run, out_shape=shapes, in_specs=in_specs, out_specs=[VMEM]...  50.1 us
    ppermute x13, waiting for transfers between devices, pair_other(): return lax.ppermute(part, 'mp', [(0, 1), (1, 0)])  43.3 us
    ppermute x13, starting transfers between devices, pair_other(): return lax.ppermute(part, 'mp', [(0, 1), (1, 0)])  23.8 us
    unnamed x86, local copies, waits for them, and re-layouts  7.74 us
  transfers between devices with their start and end apart: 50, of which 27 were waited for; matrix products, arithmetic and copies ran while one was open for 0% of the time, Pallas kernels for 17%

profile of v8, /device:TPU:0, one launch (start us, length us, event | category | flops | bytes accessed | tf_op | source)
XLA Modules:
  0.0 254.0 jit_solution(2843484109354200456)
XLA Ops:
  2.4 2.5 enc_attn_fwd.2
  5.0 3.0 %collective-permute-start = (f32[128,768]{1,0:T(8,128)}, f32[128,768]{1,0:T(8,128)}, u32[]{:S(2)}, u32[]{:S(2)}) collective-permute-start(f32[128,768]{1,0:T(8,128)} %get-tuple-element.119.refs_5_.refs_1_), channel_id=1, source_target_pairs={{0,1},{1,0},{2,3},{3,2},{4,5},{5,4},{6,7},{7,6},{8,9},{9,8},{10,11... | collective-permute-start | bytes 1179656 | tf_op jit(solution)/shard_map/pair_e1/ppermute | solution.py:624
  8.0 2.5 enc_attn_fwd.3
  11.3 2.5 dec_self_fwd.1
  22.8 3.8 %collective-permute-done.3.refs_2_ = f32[128,768]{1,0:T(8,128)} collective-permute-done((f32[128,768]{1,0:T(8,128)}, f32[128,768]{1,0:T(8,128)}, u32[]{:S(2)}, u32[]{:S(2)}) %collective-permute-start.3) | collective-permute-done | bytes 393248 | tf_op jit(solution)/shard_map/pair_e1/ppermute | solution.py:624
  26.7 2.5 enc_mlp_fwd.3
  31.3 3.8 %collective-permute-done.2.refs_7_ = f32[128,768]{1,0:T(8,128)} collective-permute-done((f32[128,768]{1,0:T(8,128)}, f32[128,768]{1,0:T(8,128)}, u32[]{:S(2)}, u32[]{:S(2)}) %collective-permute-start.2) | collective-permute-done | bytes 393248 | tf_op jit(solution)/shard_map/pair_d1/ppermute | solution.py:624
  35.1 8.3 %collective-permute-done.1.refs_3_ = f32[128,768]{1,0:T(8,128)S(1)} collective-permute-done((f32[128,768]{1,0:T(8,128)S(1)}, f32[128,768]{1,0:T(8,128)S(1)}, u32[]{:S(2)}, u32[]{:S(2)}) %collective-permute-start.1) | collective-permute-done | bytes 393248 | tf_op jit(solution)/shard_map/pair_e2/ppermute | solution.py:624
  47.9 4.0 %collective-permute-done.4.refs_3_ = f32[128,768]{1,0:T(8,128)S(1)} collective-permute-done((f32[128,768]{1,0:T(8,128)S(1)}, f32[128,768]{1,0:T(8,128)S(1)}, u32[]{:S(2)}, u32[]{:S(2)}) %collective-permute-start.4) | collective-permute-done | bytes 393248 | tf_op jit(solution)/shard_map/pair_e2/ppermute | solution.py:624
  56.3 3.6 %collective-permute-done.6.refs_5_ = f32[64,768]{1,0:T(8,128)S(1)} collective-permute-done((f32[64,768]{1,0:T(8,128)S(1)}, f32[64,768]{1,0:T(8,128)S(1)}, u32[]{:S(2)}, u32[]{:S(2)}) %collective-permute-start.6) | collective-permute-done | bytes 196640 | tf_op jit(solution)/shard_map/pair_d2/ppermute | solution.py:624
  70.9 3.4 %collective-permute-done.7.refs_2_ = f32[128,768]{1,0:T(8,128)S(1)} collective-permute-done((f32[128,768]{1,0:T(8,128)S(1)}, f32[128,768]{1,0:T(8,128)S(1)}, u32[]{:S(2)}, u32[]{:S(2)}) %collective-permute-start.7) | collective-permute-done | bytes 393248 | tf_op jit(solution)/shard_map/pair_g3/ppermute | solution.py:624
  74.3 4.7 %cross_back.1 = (f32[256,768]{1,0:T(8,128)S(1)}, f32[128,768]{1,0:T(8,128)S(1)}, f32[1,768]{1,0:T(1,128)S(1)}, f32[128,1280]{1,0:T(8,128)S(1)}, f32[128,1280]{1,...) custom-call(s32[2]{0:T(128)S(1)} %copy-done.26, f32[128,768]{1,0:T(8,128)S(1)} %get-tuple-element.130.refs_1_, ...), custom_call_target="tpu_custom_call" | custom-call | flops 23000000512 | bytes 73800000 | tf_op jit(solution)/shard_map/cross_back/pallas_call | solution.py:561
  81.3 5.8 %collective-permute-done.13.refs_1_ = f32[192,1024]{1,0:T(8,128)S(1)} collective-permute-done((f32[192,1024]{1,0:T(8,128)S(1)}, f32[192,1024]{1,0:T(8,128)S(1)}, u32[]{:S(2)}, u32[]{:S(2)}) %collective-permute-start.13) | collective-permute-done | bytes 786464 | tf_op jit(solution)/shard_map/swap_mo_x/ppermute | solution.py:635
  91.9 6.5 %collective-permute-done.9.refs_1_ = f32[256,768]{1,0:T(8,128)S(1)} collective-permute-done((f32[256,768]{1,0:T(8,128)S(1)}, f32[256,768]{1,0:T(8,128)S(1)}, u32[]{:S(2)}, u32[]{:S(2)}) %collective-permute-start.9) | collective-permute-done | bytes 786464 | tf_op jit(solution)/shard_map/pair_m/ppermute | solution.py:624
  98.3 3.0 %enc_mlp_back.1 = (f32[256,768]{1,0:T(8,128)S(1)}, f32[256,768]{1,0:T(8,128)S(1)}, f32[1,768]{1,0:T(1,128)S(1)}, f32[256,3840]{1,0:T(8,128)S(1)}, bf16[256,3840]{1,0:T(8,128)(2,1)S(1)}) custom-call(f32[256,768]{1,0:T(8,128)S(1)} %get-tuple-element.137.refs_0_, f32[256,768]{1,0:T(8,128)S(1)} %collective-permute-done.9.refs_1_, ...), custom_call_target="tpu_custom_call" | custom-call | flops 3449999872 | bytes 11070000 | tf_op jit(solution)/shard_map/enc_mlp_back/pallas_call | solution.py:561
  103.1 3.5 %collective-permute-done.17.refs_1_ = f32[192,2048]{1,0:T(8,128)S(1)} collective-permute-done((f32[192,2048]{1,0:T(8,128)S(1)}, f32[192,2048]{1,0:T(8,128)S(1)}, u32[]{:S(2)}, u32[]{:S(2)}) %collective-permute-start.17) | collective-permute-done | bytes 1572896 | tf_op jit(solution)/shard_map/swap_m_p/ppermute | solution.py:635
  116.6 5.3 %collective-permute-done.14.refs_2_ = f32[256,768]{1,0:T(8,128)S(1)} collective-permute-done((f32[256,768]{1,0:T(8,128)S(1)}, f32[256,768]{1,0:T(8,128)S(1)}, u32[]{:S(2)}, u32[]{:S(2)}) %collective-permute-start.14) | collective-permute-done | bytes 786464 | tf_op jit(solution)/shard_map/pair_g1/ppermute | solution.py:624
  121.9 5.4 %enc_attn_back.1 = (f32[256,768]{1,0:T(8,128)S(1)}, f32[256,768]{1,0:T(8,128)S(1)}, f32[2,768]{1,0:T(2,128)S(1)}, f32[256,2304]{1,0:T(8,128)S(1)}, bf16[256,2304]{1,0:T(8,128)(2,1)S(1)}) custom-call(s32[2]{0:T(128)S(1)} %copy-done.26, f32[256,768]{1,0:T(8,128)S(1)} %get-tuple-element.148.refs_1_, f32[256,768]{1,0:T(8,128)S(1)} %collective-permute-done.14.refs_2_, ...), custom_call_target="tpu_custom_call" | custom-call | flops 345000000 | bytes 1107000 | tf_op jit(solution)/shard_map/enc_attn_back/pallas_call | solution.py:561
  129.8 3.7 %dec_self_back.1 = (f32[128,768]{1,0:T(8,128)S(1)}, f32[128,768]{1,0:T(8,128)S(1)}, f32[2,768]{1,0:T(2,128)S(1)}, f32[128,1152]{1,0:T(8,128)S(1)}, f32[128,1152]...) custom-call(s32[2]{0:T(128)S(1)} %copy-done.28, f32[128,768]{1,0:T(8,128)S(1)} %query_part.1.refs_1_, ...), custom_call_target="tpu_custom_call" | custom-call | flops 345000000 | bytes 1107000 | tf_op jit(solution)/shard_map/dec_self_back/pallas_call | solution.py:561
  138.7 4.3 %collective-permute-start.30 = (f32[96,1536]{1,0:T(8,128)S(1)}, f32[96,1536]{1,0:T(8,128)S(1)}, u32[]{:S(2)}, u32[]{:S(2)}) collective-permute-start(f32[96,1536]{1,0:T(8,128)S(1)} %get-tuple-element.165.refs_12_), channel_id=1, source_target_pairs={{0,8},{2,10},{4,12},{6,14},{8,0},{10,2},{12,4},{14,6},{16,24},{18,... | collective-permute-start | bytes 1769480 | tf_op jit(solution)/shard_map/swap_c_p/ppermute | solution.py:635
  144.2 4.5 %collective-permute-done.22.refs_1_ = f32[192,2048]{1,0:T(8,128)S(1)} collective-permute-done((f32[192,2048]{1,0:T(8,128)S(1)}, f32[192,2048]{1,0:T(8,128)S(1)}, u32[]{:S(2)}, u32[]{:S(2)}) %collective-permute-start.22) | collective-permute-done | bytes 1572896 | tf_op jit(solution)/shard_map/swap_f_p/ppermute | solution.py:635
  149.0 5.5 %collective-permute-done.20.refs_1_ = f32[96,2048]{1,0:T(8,128)S(1)} collective-permute-done((f32[96,2048]{1,0:T(8,128)S(1)}, f32[96,2048]{1,0:T(8,128)S(1)}, u32[]{:S(2)}, u32[]{:S(2)}) %collective-permute-start.20) | collective-permute-done | bytes 786464 | tf_op jit(solution)/shard_map/swap_m_x/ppermute | solution.py:635
  155.3 4.5 %collective-permute-start.29 = (f32[96,1024]{1,0:T(8,128)S(1)}, f32[96,1024]{1,0:T(8,128)S(1)}, u32[]{:S(2)}, u32[]{:S(2)}) collective-permute-start(f32[96,1024]{1,0:T(8,128)S(1)} %get-tuple-element.175.refs_3_), channel_id=1, source_target_pairs={{0,8},{2,10},{4,12},{6,14},{8,0},{10,2},{12,4},{14,6},{16,24},{18,... | collective-permute-start | bytes 1179656 | tf_op jit(solution)/shard_map/swap_fo_p/ppermute | solution.py:635
  162.6 7.2 %collective-permute-done.29.refs_1_ = f32[96,1024]{1,0:T(8,128)S(1)} collective-permute-done((f32[96,1024]{1,0:T(8,128)S(1)}, f32[96,1024]{1,0:T(8,128)S(1)}, u32[]{:S(2)}, u32[]{:S(2)}) %collective-permute-start.29) | collective-permute-done | bytes 393248 | tf_op jit(solution)/shard_map/swap_fo_p/ppermute | solution.py:635
  172.3 6.2 %collective-permute-start.33 = (f32[48,2048]{1,0:T(8,128)S(1)}, f32[48,2048]{1,0:T(8,128)S(1)}, u32[]{:S(2)}, u32[]{:S(2)}) collective-permute-start(f32[48,2048]{1,0:T(8,128)S(1)} %get-tuple-element.188.refs_2_), channel_id=1, source_target_pairs={{0,8},{2,10},{4,12},{6,14},{8,0},{10,2},{12,4},{14,6},{16,24},{18,... | collective-permute-start | bytes 1179656 | tf_op jit(solution)/shard_map/swap_m_e/ppermute | solution.py:635
  178.5 16.6 %collective-permute-done.38.refs_1_ = f32[192,1536]{1,0:T(8,128)S(1)} collective-permute-done((f32[192,1536]{1,0:T(8,128)S(1)}, f32[192,1536]{1,0:T(8,128)S(1)}, u32[]{:S(2)}, u32[]{:S(2)}) %collective-permute-start.38) | collective-permute-done | bytes 1179680 | tf_op jit(solution)/shard_map/swap_s_p/ppermute | solution.py:635
  199.8 7.8 %collective-permute-start.42 = (f32[96,1664]{1,0:T(8,128)S(1)}, f32[96,1664]{1,0:T(8,128)S(1)}, u32[]{:S(2)}, u32[]{:S(2)}) collective-permute-start(f32[96,1664]{1,0:T(8,128)S(1)} %get-tuple-element.194.refs_2_), channel_id=1, source_target_pairs={{0,8},{2,10},{4,12},{6,14},{8,0},{10,2},{12,4},{14,6},{16,24},{18,... | collective-permute-start | bytes 1916936 | tf_op jit(solution)/shard_map/swap_a_p/ppermute | solution.py:635
  212.5 4.4 %collective-permute-start.47 = (f32[48,1536]{1,0:T(8,128)S(1)}, f32[48,1536]{1,0:T(8,128)S(1)}, u32[]{:S(2)}, u32[]{:S(2)}) collective-permute-start(f32[48,1536]{1,0:T(8,128)S(1)} %get-tuple-element.193.refs_2_), channel_id=1, source_target_pairs={{0,8},{2,10},{4,12},{6,14},{8,0},{10,2},{12,4},{14,6},{16,24},{18,... | collective-permute-start | bytes 884744 | tf_op jit(solution)/shard_map/swap_c_e/ppermute | solution.py:635
  216.8 6.0 %collective-permute-done.42.refs_1_ = f32[96,1664]{1,0:T(8,128)S(1)} collective-permute-done((f32[96,1664]{1,0:T(8,128)S(1)}, f32[96,1664]{1,0:T(8,128)S(1)}, u32[]{:S(2)}, u32[]{:S(2)}) %collective-permute-start.42) | collective-permute-done | bytes 639008 | tf_op jit(solution)/shard_map/swap_a_p/ppermute | solution.py:635
  225.8 3.4 %collective-permute-done.47.refs_1_ = f32[48,1536]{1,0:T(8,128)S(1)} collective-permute-done((f32[48,1536]{1,0:T(8,128)S(1)}, f32[48,1536]{1,0:T(8,128)S(1)}, u32[]{:S(2)}, u32[]{:S(2)}) %collective-permute-start.47) | collective-permute-done | bytes 294944 | tf_op jit(solution)/shard_map/swap_c_e/ppermute | solution.py:635
  233.1 9.1 %collective-permute-start.48 = (f32[48,1664]{1,0:T(8,128)S(1)}, f32[48,1664]{1,0:T(8,128)S(1)}, u32[]{:S(2)}, u32[]{:S(2)}) collective-permute-start(f32[48,1664]{1,0:T(8,128)S(1)} %get-tuple-element.207.refs_4_), channel_id=1, source_target_pairs={{0,8},{2,10},{4,12},{6,14},{8,0},{10,2},{12,4},{14,6},{16,24},{18,... | collective-permute-start | bytes 958472 | tf_op jit(solution)/shard_map/swap_a_e/ppermute | solution.py:635
  249.8 2.6 %collective-permute-done.48.refs_1_ = f32[48,1664]{1,0:T(8,128)S(1)} collective-permute-done((f32[48,1664]{1,0:T(8,128)S(1)}, f32[48,1664]{1,0:T(8,128)S(1)}, u32[]{:S(2)}, u32[]{:S(2)}) %collective-permute-start.48) | collective-permute-done | bytes 319520 | tf_op jit(solution)/shard_map/swap_a_e/ppermute | solution.py:635
  (212 shorter events, 92.5 us)
Async XLA Ops:
  11.3 15.4 %collective-permute-start.3 = (f32[128,768]{1,0:T(8,128)}, f32[128,768]{1,0:T(8,128)}, u32[]{:S(2)}, u32[]{:S(2)}) collective-permute-start(f32[128,768]{1,0:T(8,128)} %get-tuple-element.120.refs_5_.refs_1_), channel_id=1, source_target_pairs={{0,1},{1,0},{2,3},{3,2},{4,5},{5,4},{6,7},{7,6},{8,9},{9,8},{10,11... | collective-permute-start | bytes 1179656 | tf_op jit(solution)/shard_map/pair_e1/ppermute | solution.py:624
  13.9 21.3 %collective-permute-start.2 = (f32[128,768]{1,0:T(8,128)}, f32[128,768]{1,0:T(8,128)}, u32[]{:S(2)}, u32[]{:S(2)}) collective-permute-start(f32[128,768]{1,0:T(8,128)} %get-tuple-element.121.refs_1_.refs_6_), channel_id=1, source_target_pairs={{0,1},{1,0},{2,3},{3,2},{4,5},{5,4},{6,7},{7,6},{8,9},{9,8},{10,11... | collective-permute-start | bytes 1179656 | tf_op jit(solution)/shard_map/pair_d1/ppermute | solution.py:624
  20.8 22.6 %collective-permute-start.1 = (f32[128,768]{1,0:T(8,128)S(1)}, f32[128,768]{1,0:T(8,128)S(1)}, u32[]{:S(2)}, u32[]{:S(2)}) collective-permute-start(f32[128,768]{1,0:T(8,128)S(1)} %get-tuple-element.123.refs_6_.refs_2_), channel_id=1, source_target_pairs={{0,1},{1,0},{2,3},{3,2},{4,5},{5,4},{6,7},{7,6},{8,9},{9,8},{10,11... | collective-permute-start | bytes 1179656 | tf_op jit(solution)/shard_map/pair_e2/ppermute | solution.py:624
  29.2 22.7 %collective-permute-start.4 = (f32[128,768]{1,0:T(8,128)S(1)}, f32[128,768]{1,0:T(8,128)S(1)}, u32[]{:S(2)}, u32[]{:S(2)}) collective-permute-start(f32[128,768]{1,0:T(8,128)S(1)} %get-tuple-element.124.refs_1_.refs_2_), channel_id=1, source_target_pairs={{0,1},{1,0},{2,3},{3,2},{4,5},{5,4},{6,7},{7,6},{8,9},{9,8},{10,11... | collective-permute-start | bytes 1179656 | tf_op jit(solution)/shard_map/pair_e2/ppermute | solution.py:624
  67.2 19.9 %collective-permute-start.13 = (f32[192,1024]{1,0:T(8,128)S(1)}, f32[192,1024]{1,0:T(8,128)S(1)}, u32[]{:S(2)}, u32[]{:S(2)}) collective-permute-start(f32[192,1024]{1,0:T(8,128)S(1)} %get-tuple-element.136.refs_18_), channel_id=1, source_target_pairs={{0,4},{2,6},{4,0},{6,2},{8,12},{10,14},{12,8},{14,10},{16,20},{18,... | collective-permute-start | bytes 2359304 | tf_op jit(solution)/shard_map/swap_mo_x/ppermute | solution.py:635
  69.3 37.3 %collective-permute-start.17 = (f32[192,2048]{1,0:T(8,128)S(1)}, f32[192,2048]{1,0:T(8,128)S(1)}, u32[]{:S(2)}, u32[]{:S(2)}) collective-permute-start(f32[192,2048]{1,0:T(8,128)S(1)} %get-tuple-element.156), channel_id=1, source_target_pairs={{0,8},{2,10},{4,12},{6,14},{8,0},{10,2},{12,4},{14,6},{16,24},{18,... | collective-permute-start | bytes 4718600 | tf_op jit(solution)/shard_map/swap_m_p/ppermute | solution.py:635
  79.0 19.4 %collective-permute-start.9 = (f32[256,768]{1,0:T(8,128)S(1)}, f32[256,768]{1,0:T(8,128)S(1)}, u32[]{:S(2)}, u32[]{:S(2)}) collective-permute-start(f32[256,768]{1,0:T(8,128)S(1)} %get-tuple-element.137.refs_0_), channel_id=1, source_target_pairs={{0,1},{1,0},{2,3},{3,2},{4,5},{5,4},{6,7},{7,6},{8,9},{9,8},{10,11... | collective-permute-start | bytes 2359304 | tf_op jit(solution)/shard_map/pair_m/ppermute | solution.py:624
  87.2 27.8 %collective-permute-start.15 = (f32[96,1024]{1,0:T(8,128)S(1)}, f32[96,1024]{1,0:T(8,128)S(1)}, u32[]{:S(2)}, u32[]{:S(2)}) collective-permute-start(f32[96,1024]{1,0:T(8,128)S(1)} %get-tuple-element.146.refs_4_), channel_id=1, source_target_pairs={{0,8},{2,10},{4,12},{6,14},{8,0},{10,2},{12,4},{14,6},{16,24},{18,... | collective-permute-start | bytes 1179656 | tf_op jit(solution)/shard_map/swap_mo_p/ppermute | solution.py:635
  90.1 37.3 %collective-permute-start.19 = (f32[192,1536]{1,0:T(8,128)S(1)}, f32[192,1536]{1,0:T(8,128)S(1)}, u32[]{:S(2)}, u32[]{:S(2)}) collective-permute-start(f32[192,1536]{1,0:T(8,128)S(1)} %get-tuple-element.147.refs_13_), channel_id=1, source_target_pairs={{0,4},{2,6},{4,0},{6,2},{8,12},{10,14},{12,8},{14,10},{16,20},{18,... | collective-permute-start | bytes 3538952 | tf_op jit(solution)/shard_map/swap_c_x/ppermute | solution.py:635
  101.4 20.4 %collective-permute-start.14 = (f32[256,768]{1,0:T(8,128)S(1)}, f32[256,768]{1,0:T(8,128)S(1)}, u32[]{:S(2)}, u32[]{:S(2)}) collective-permute-start(f32[256,768]{1,0:T(8,128)S(1)} %get-tuple-element.148.refs_1_), channel_id=1, source_target_pairs={{0,1},{1,0},{2,3},{3,2},{4,5},{5,4},{6,7},{7,6},{8,9},{9,8},{10,11... | collective-permute-start | bytes 2359304 | tf_op jit(solution)/shard_map/pair_g1/ppermute | solution.py:624
  109.6 39.1 %collective-permute-start.22 = (f32[192,2048]{1,0:T(8,128)S(1)}, f32[192,2048]{1,0:T(8,128)S(1)}, u32[]{:S(2)}, u32[]{:S(2)}) collective-permute-start(f32[192,2048]{1,0:T(8,128)S(1)} %get-tuple-element.169), channel_id=1, source_target_pairs={{0,8},{2,10},{4,12},{6,14},{8,0},{10,2},{12,4},{14,6},{16,24},{18,... | collective-permute-start | bytes 4718600 | tf_op jit(solution)/shard_map/swap_f_p/ppermute | solution.py:635
  111.4 24.3 %collective-permute-start.25 = (f32[192,1024]{1,0:T(8,128)S(1)}, f32[192,1024]{1,0:T(8,128)S(1)}, u32[]{:S(2)}, u32[]{:S(2)}) collective-permute-start(f32[192,1024]{1,0:T(8,128)S(1)} %get-tuple-element.159.refs_2_), channel_id=1, source_target_pairs={{0,4},{2,6},{4,0},{6,2},{8,12},{10,14},{12,8},{14,10},{16,20},{18,... | collective-permute-start | bytes 2359304 | tf_op jit(solution)/shard_map/swap_fo_x/ppermute | solution.py:635
  115.0 14.8 %collective-permute-start.18 = (f32[128,768]{1,0:T(8,128)S(1)}, f32[128,768]{1,0:T(8,128)S(1)}, u32[]{:S(2)}, u32[]{:S(2)}) collective-permute-start(f32[128,768]{1,0:T(8,128)S(1)} %query_part.1.refs_1_), channel_id=1, source_target_pairs={{0,1},{1,0},{2,3},{3,2},{4,5},{5,4},{6,7},{7,6},{8,9},{9,8},{10,11... | collective-permute-start | bytes 1179656 | tf_op jit(solution)/shard_map/pair_q/ppermute | solution.py:624
  134.1 20.4 %collective-permute-start.20 = (f32[96,2048]{1,0:T(8,128)S(1)}, f32[96,2048]{1,0:T(8,128)S(1)}, u32[]{:S(2)}, u32[]{:S(2)}) collective-permute-start(f32[96,2048]{1,0:T(8,128)S(1)} %get-tuple-element.158.refs_2_), channel_id=1, source_target_pairs={{0,4},{2,6},{4,0},{6,2},{8,12},{10,14},{12,8},{14,10},{16,20},{18,... | collective-permute-start | bytes 2359304 | tf_op jit(solution)/shard_map/swap_m_x/ppermute | solution.py:635
  138.7 22.6 %collective-permute-start.30 = (f32[96,1536]{1,0:T(8,128)S(1)}, f32[96,1536]{1,0:T(8,128)S(1)}, u32[]{:S(2)}, u32[]{:S(2)}) collective-permute-start(f32[96,1536]{1,0:T(8,128)S(1)} %get-tuple-element.165.refs_12_), channel_id=1, source_target_pairs={{0,8},{2,10},{4,12},{6,14},{8,0},{10,2},{12,4},{14,6},{16,24},{18,... | collective-permute-start | bytes 1769480 | tf_op jit(solution)/shard_map/swap_c_p/ppermute | solution.py:635
  143.1 16.7 %collective-permute-start.31 = (f32[256,2304]{1,0:T(8,128)S(1)}, f32[256,2304]{1,0:T(8,128)S(1)}, u32[]{:S(2)}, u32[]{:S(2)}) collective-permute-start(f32[256,2304]{1,0:T(8,128)S(1)} %get-tuple-element.184), channel_id=1, source_target_pairs={{0,2},{2,0},{4,6},{6,4},{8,10},{10,8},{12,14},{14,12},{16,18},{18,... | collective-permute-start | bytes 7077896 | tf_op jit(solution)/shard_map/swap_a_0/ppermute | solution.py:635
  148.9 22.5 %collective-permute-start.28 = (f32[96,2048]{1,0:T(8,128)S(1)}, f32[96,2048]{1,0:T(8,128)S(1)}, u32[]{:S(2)}, u32[]{:S(2)}) collective-permute-start(f32[96,2048]{1,0:T(8,128)S(1)} %get-tuple-element.178.refs_2_), channel_id=1, source_target_pairs={{0,4},{2,6},{4,0},{6,2},{8,12},{10,14},{12,8},{14,10},{16,20},{18,... | collective-permute-start | bytes 2359304 | tf_op jit(solution)/shard_map/swap_f_x/ppermute | solution.py:635
  154.6 17.6 %collective-permute-start.27 = (f32[96,2048]{1,0:T(8,128)S(1)}, f32[96,2048]{1,0:T(8,128)S(1)}, u32[]{:S(2)}, u32[]{:S(2)}) collective-permute-start(f32[96,2048]{1,0:T(8,128)S(1)} %halve_m.4.refs_4_.refs_0_), channel_id=1, source_target_pairs={{8,16},{10,18},{12,20},{14,22},{16,8},{18,10},{20,12},{22,14},{9,1... | collective-permute-start | bytes 2359304 | tf_op jit(solution)/shard_map/swap_m_m/ppermute | solution.py:635
  159.8 35.3 %collective-permute-start.38 = (f32[192,1536]{1,0:T(8,128)S(1)}, f32[192,1536]{1,0:T(8,128)S(1)}, u32[]{:S(2)}, u32[]{:S(2)}) collective-permute-start(f32[192,1536]{1,0:T(8,128)S(1)} %get-tuple-element.176.refs_4_), channel_id=1, source_target_pairs={{0,8},{2,10},{4,12},{6,14},{8,0},{10,2},{12,4},{14,6},{16,24},{18,... | collective-permute-start | bytes 3538952 | tf_op jit(solution)/shard_map/swap_s_p/ppermute | solution.py:635
  161.4 37.6 %collective-permute-start.36 = (f32[192,1664]{1,0:T(8,128)S(1)}, f32[192,1664]{1,0:T(8,128)S(1)}, u32[]{:S(2)}, u32[]{:S(2)}) collective-permute-start(f32[192,1664]{1,0:T(8,128)S(1)} %get-tuple-element.186.refs_2_), channel_id=1, source_target_pairs={{0,4},{2,6},{4,0},{6,2},{8,12},{10,14},{12,8},{14,10},{16,20},{18,... | collective-permute-start | bytes 3833864 | tf_op jit(solution)/shard_map/swap_a_x/ppermute | solution.py:635
  169.8 27.0 %collective-permute-start.37 = (f32[96,1536]{1,0:T(8,128)S(1)}, f32[96,1536]{1,0:T(8,128)S(1)}, u32[]{:S(2)}, u32[]{:S(2)}) collective-permute-start(f32[96,1536]{1,0:T(8,128)S(1)} %halve_c.4.refs_2_.refs_0_), channel_id=1, source_target_pairs={{8,16},{10,18},{12,20},{14,22},{16,8},{18,10},{20,12},{22,14},{9,1... | collective-permute-start | bytes 1769480 | tf_op jit(solution)/shard_map/swap_c_m/ppermute | solution.py:635
  171.5 28.3 %collective-permute-start.35 = (f32[96,2048]{1,0:T(8,128)S(1)}, f32[96,2048]{1,0:T(8,128)S(1)}, u32[]{:S(2)}, u32[]{:S(2)}) collective-permute-start(f32[96,2048]{1,0:T(8,128)S(1)} %halve_f.4.refs_2_.refs_0_), channel_id=1, source_target_pairs={{8,16},{10,18},{12,20},{14,22},{16,8},{18,10},{20,12},{22,14},{9,1... | collective-permute-start | bytes 2359304 | tf_op jit(solution)/shard_map/swap_f_m/ppermute | solution.py:635
  172.3 35.4 %collective-permute-start.33 = (f32[48,2048]{1,0:T(8,128)S(1)}, f32[48,2048]{1,0:T(8,128)S(1)}, u32[]{:S(2)}, u32[]{:S(2)}) collective-permute-start(f32[48,2048]{1,0:T(8,128)S(1)} %get-tuple-element.188.refs_2_), channel_id=1, source_target_pairs={{0,8},{2,10},{4,12},{6,14},{8,0},{10,2},{12,4},{14,6},{16,24},{18,... | collective-permute-start | bytes 1179656 | tf_op jit(solution)/shard_map/swap_m_e/ppermute | solution.py:635
  195.2 16.5 %collective-permute-start.43 = (f32[96,1536]{1,0:T(8,128)S(1)}, f32[96,1536]{1,0:T(8,128)S(1)}, u32[]{:S(2)}, u32[]{:S(2)}) collective-permute-start(f32[96,1536]{1,0:T(8,128)S(1)} %get-tuple-element.192.refs_2_), channel_id=1, source_target_pairs={{0,4},{2,6},{4,0},{6,2},{8,12},{10,14},{12,8},{14,10},{16,20},{18,... | collective-permute-start | bytes 1769480 | tf_op jit(solution)/shard_map/swap_s_x/ppermute | solution.py:635
  198.9 26.1 %collective-permute-start.41 = (f32[96,1024]{1,0:T(8,128)S(1)}, f32[96,1024]{1,0:T(8,128)S(1)}, u32[]{:S(2)}, u32[]{:S(2)}) collective-permute-start(f32[96,1024]{1,0:T(8,128)S(1)} %halve_fo.4.refs_2_.refs_0_), channel_id=1, source_target_pairs={{8,16},{10,18},{12,20},{14,22},{16,8},{18,10},{20,12},{22,14},{9,1... | collective-permute-start | bytes 1179656 | tf_op jit(solution)/shard_map/swap_fo_m/ppermute | solution.py:635
  199.8 23.1 %collective-permute-start.42 = (f32[96,1664]{1,0:T(8,128)S(1)}, f32[96,1664]{1,0:T(8,128)S(1)}, u32[]{:S(2)}, u32[]{:S(2)}) collective-permute-start(f32[96,1664]{1,0:T(8,128)S(1)} %get-tuple-element.194.refs_2_), channel_id=1, source_target_pairs={{0,8},{2,10},{4,12},{6,14},{8,0},{10,2},{12,4},{14,6},{16,24},{18,... | collective-permute-start | bytes 1916936 | tf_op jit(solution)/shard_map/swap_a_p/ppermute | solution.py:635
  210.0 34.2 %collective-permute-start.39 = (f32[512,768]{1,0:T(8,128)S(1)}, f32[512,768]{1,0:T(8,128)S(1)}, u32[]{:S(2)}, u32[]{:S(2)}) collective-permute-start(f32[512,768]{1,0:T(8,128)S(1)} %tail_parts.1.refs_2_.refs_0_), channel_id=1, source_target_pairs={{0,1},{1,0},{2,3},{3,2},{4,5},{5,4},{6,7},{7,6},{8,9},{9,8},{10,11... | collective-permute-start | bytes 4718600 | tf_op jit(solution)/shard_map/pair_tail/ppermute | solution.py:624
  211.8 20.2 %collective-permute-start.46 = (f32[96,1536]{1,0:T(8,128)S(1)}, f32[96,1536]{1,0:T(8,128)S(1)}, u32[]{:S(2)}, u32[]{:S(2)}) collective-permute-start(f32[96,1536]{1,0:T(8,128)S(1)} %halve_s.4.refs_2_.refs_0_), channel_id=1, source_target_pairs={{8,16},{10,18},{12,20},{14,22},{16,8},{18,10},{20,12},{22,14},{9,1... | collective-permute-start | bytes 1769480 | tf_op jit(solution)/shard_map/swap_s_m/ppermute | solution.py:635
  212.5 16.7 %collective-permute-start.47 = (f32[48,1536]{1,0:T(8,128)S(1)}, f32[48,1536]{1,0:T(8,128)S(1)}, u32[]{:S(2)}, u32[]{:S(2)}) collective-permute-start(f32[48,1536]{1,0:T(8,128)S(1)} %get-tuple-element.193.refs_2_), channel_id=1, source_target_pairs={{0,8},{2,10},{4,12},{6,14},{8,0},{10,2},{12,4},{14,6},{16,24},{18,... | collective-permute-start | bytes 884744 | tf_op jit(solution)/shard_map/swap_c_e/ppermute | solution.py:635
  222.9 19.3 %collective-permute-start.40 = (f32[48,2048]{1,0:T(8,128)S(1)}, f32[48,2048]{1,0:T(8,128)S(1)}, u32[]{:S(2)}, u32[]{:S(2)}) collective-permute-start(f32[48,2048]{1,0:T(8,128)S(1)} %get-tuple-element.195.refs_4_), channel_id=1, source_target_pairs={{0,8},{2,10},{4,12},{6,14},{8,0},{10,2},{12,4},{14,6},{16,24},{18,... | collective-permute-start | bytes 1179656 | tf_op jit(solution)/shard_map/swap_f_e/ppermute | solution.py:635
  232.9 15.2 %collective-permute-start.49 = (f32[48,1536]{1,0:T(8,128)S(1)}, f32[48,1536]{1,0:T(8,128)S(1)}, u32[]{:S(2)}, u32[]{:S(2)}) collective-permute-start(f32[48,1536]{1,0:T(8,128)S(1)} %get-tuple-element.206.refs_2_), channel_id=1, source_target_pairs={{0,8},{2,10},{4,12},{6,14},{8,0},{10,2},{12,4},{14,6},{16,24},{18,... | collective-permute-start | bytes 884744 | tf_op jit(solution)/shard_map/swap_s_e/ppermute | solution.py:635
  233.1 19.3 %collective-permute-start.48 = (f32[48,1664]{1,0:T(8,128)S(1)}, f32[48,1664]{1,0:T(8,128)S(1)}, u32[]{:S(2)}, u32[]{:S(2)}) collective-permute-start(f32[48,1664]{1,0:T(8,128)S(1)} %get-tuple-element.207.refs_4_), channel_id=1, source_target_pairs={{0,8},{2,10},{4,12},{6,14},{8,0},{10,2},{12,4},{14,6},{16,24},{18,... | collective-permute-start | bytes 958472 | tf_op jit(solution)/shard_map/swap_a_e/ppermute | solution.py:635
  (61 other events, 403.5 us)

commit v9 on v8

--- a/solution.py
+++ b/solution.py
@@ -445,7 +445,7 @@
     "h_c", "dec_self_back", "h_fo", "w_s", "gain_rows", "gains", "h_f", "h_mo",
     "h_m", "w_a", "h_c", "h_fo", "h_f", "h_m", "h_s", "h_c",
     "h_a", "h_f", "e_m", "tick", "tail_parts", "h_s", "h_a", "h_fo",
-    "e_c", "h_s", "h_a", "e_f", "tail", "e_s", "e_a",
+    "e_c", "h_s", "h_a", "e_f", "tail", "e_s", "pause", "e_a",
 )
 HALVINGS = {"m": "pxme", "mo": "xpme", "c": "xpme", "f": "pxme", "fo": "xpme", "s": "pxme", "a": "xpme"}
 PARTS = {"m": 1, "c": 3, "f": 1, "a": 1, "s": 2}

time: 255 us -> 254 us (level)
    pallas_call x55 -> x56, Pallas kernels: 50.1 us -> 50.1 us  [call(): pl.pallas_call(run, out_shape=shapes, in_specs=in_specs, out_specs=[VMEM]...]
  transfers between devices with their start and end apart: 50 -> 50, of which waited for: 27 -> 27; matrix products, arithmetic and copies ran while one was open for 0% -> 0% of each run, Pallas kernels for 17% -> 18%
where the time goes in v9:
time: 254 us; the launch traced here: 253 us
  waiting for transfers between devices  106 us (42%)
  starting transfers between devices  87.2 us (34%)
  Pallas kernels  50.1 us (20%)
  local copies, waits for them, and re-layouts  7.74 us (3%)
    ppermute x37, starting transfers between devices, swap(): return lax.ppermute(value, 'dp', pairs)  63.4 us
    ppermute x37, waiting for transfers between devices, swap(): return lax.ppermute(value, 'dp', pairs)  62.6 us
    pallas_call x56, Pallas kernels, call(): pl.pallas_call(run, out_shape=shapes, in_specs=in_specs, out_specs=[VMEM]...  50.1 us
    ppermute x13, waiting for transfers between devices, pair_other(): return lax.ppermute(part, 'mp', [(0, 1), (1, 0)])  43.3 us
    ppermute x13, starting transfers between devices, pair_other(): return lax.ppermute(part, 'mp', [(0, 1), (1, 0)])  23.8 us
    unnamed x86, local copies, waits for them, and re-layouts  7.74 us
  transfers between devices with their start and end apart: 50, of which 27 were waited for; matrix products, arithmetic and copies ran while one was open for 0% of the time, Pallas kernels for 18%

profile of v9, /device:TPU:0, one launch (start us, length us, event | category | flops | bytes accessed | tf_op | source)
XLA Modules:
  0.0 253.1 jit_solution(485496008593345119)
XLA Ops:
  2.4 2.5 %enc_attn_fwd.2 = (f32[128,768]{1,0:T(8,128)}, bf16[128,1536]{1,0:T(8,128)(2,1)S(1)}) custom-call(s32[2]{0:T(128)S(1)} %copy-done.26, bf16[256,768]{1,0:T(8,128)(2,1)S(1)} %bitcast.11, f32[3,768]{1,0:T(4,128)S(1)} %copy-done.22, bf16[3,768,384]{2,1,0:T(8,128)(2,1)S(1)} %copy-done.1, bf16[384,768]{1,0:T(8,128)(2,1)S(1)} %copy-done.8, f32[1,128]{1,0:T(1,128)S(1)} %tick.8.refs_5_), custom_call_target="tpu_custom_call" | custom-call | flops 2644999936 | bytes 8487000 | tf_op jit(solution)/shard_map/enc_attn_fwd/pallas_call | solution.py:561
  5.0 3.0 %collective-permute-start = (f32[128,768]{1,0:T(8,128)}, f32[128,768]{1,0:T(8,128)}, u32[]{:S(2)}, u32[]{:S(2)}) collective-permute-start(f32[128,768]{1,0:T(8,128)} %get-tuple-element.119.refs_5_.refs_1_), channel_id=1, source_target_pairs={{0,1},{1,0},{2,3},{3,2},{4,5},{5,4},{6,7},{7,6},{8,9},{9,8},{10,11... | collective-permute-start | bytes 1179656 | tf_op jit(solution)/shard_map/pair_e1/ppermute | solution.py:624
  8.0 2.5 enc_attn_fwd.3
  11.3 2.5 dec_self_fwd.1
  18.3 2.4 enc_mlp_fwd.2
  22.8 3.8 %collective-permute-done.3.refs_2_ = f32[128,768]{1,0:T(8,128)} collective-permute-done((f32[128,768]{1,0:T(8,128)}, f32[128,768]{1,0:T(8,128)}, u32[]{:S(2)}, u32[]{:S(2)}) %collective-permute-start.3) | collective-permute-done | bytes 393248 | tf_op jit(solution)/shard_map/pair_e1/ppermute | solution.py:624
  26.7 2.5 enc_mlp_fwd.3
  31.3 3.8 %collective-permute-done.2.refs_7_ = f32[128,768]{1,0:T(8,128)} collective-permute-done((f32[128,768]{1,0:T(8,128)}, f32[128,768]{1,0:T(8,128)}, u32[]{:S(2)}, u32[]{:S(2)}) %collective-permute-start.2) | collective-permute-done | bytes 393248 | tf_op jit(solution)/shard_map/pair_d1/ppermute | solution.py:624
  35.1 8.3 %collective-permute-done.1.refs_3_ = f32[128,768]{1,0:T(8,128)S(1)} collective-permute-done((f32[128,768]{1,0:T(8,128)S(1)}, f32[128,768]{1,0:T(8,128)S(1)}, u32[]{:S(2)}, u32[]{:S(2)}) %collective-permute-start.1) | collective-permute-done | bytes 393248 | tf_op jit(solution)/shard_map/pair_e2/ppermute | solution.py:624
  47.9 4.0 %collective-permute-done.4.refs_3_ = f32[128,768]{1,0:T(8,128)S(1)} collective-permute-done((f32[128,768]{1,0:T(8,128)S(1)}, f32[128,768]{1,0:T(8,128)S(1)}, u32[]{:S(2)}, u32[]{:S(2)}) %collective-permute-start.4) | collective-permute-done | bytes 393248 | tf_op jit(solution)/shard_map/pair_e2/ppermute | solution.py:624
  56.3 3.6 %collective-permute-done.6.refs_5_ = f32[64,768]{1,0:T(8,128)S(1)} collective-permute-done((f32[64,768]{1,0:T(8,128)S(1)}, f32[64,768]{1,0:T(8,128)S(1)}, u32[]{:S(2)}, u32[]{:S(2)}) %collective-permute-start.6) | collective-permute-done | bytes 196640 | tf_op jit(solution)/shard_map/pair_d2/ppermute | solution.py:624
  70.9 3.4 %collective-permute-done.7.refs_2_ = f32[128,768]{1,0:T(8,128)S(1)} collective-permute-done((f32[128,768]{1,0:T(8,128)S(1)}, f32[128,768]{1,0:T(8,128)S(1)}, u32[]{:S(2)}, u32[]{:S(2)}) %collective-permute-start.7) | collective-permute-done | bytes 393248 | tf_op jit(solution)/shard_map/pair_g3/ppermute | solution.py:624
  74.3 4.7 %cross_back.1 = (f32[256,768]{1,0:T(8,128)S(1)}, f32[128,768]{1,0:T(8,128)S(1)}, f32[1,768]{1,0:T(1,128)S(1)}, f32[128,1280]{1,0:T(8,128)S(1)}, f32[128,1280]{1,...) custom-call(s32[2]{0:T(128)S(1)} %copy-done.26, f32[128,768]{1,0:T(8,128)S(1)} %get-tuple-element.130.refs_1_, ...), custom_call_target="tpu_custom_call" | custom-call | flops 23000000512 | bytes 73800000 | tf_op jit(solution)/shard_map/cross_back/pallas_call | solution.py:561
  81.3 5.8 %collective-permute-done.13.refs_1_ = f32[192,1024]{1,0:T(8,128)S(1)} collective-permute-done((f32[192,1024]{1,0:T(8,128)S(1)}, f32[192,1024]{1,0:T(8,128)S(1)}, u32[]{:S(2)}, u32[]{:S(2)}) %collective-permute-start.13) | collective-permute-done | bytes 786464 | tf_op jit(solution)/shard_map/swap_mo_x/ppermute | solution.py:635
  91.9 6.5 %collective-permute-done.9.refs_1_ = f32[256,768]{1,0:T(8,128)S(1)} collective-permute-done((f32[256,768]{1,0:T(8,128)S(1)}, f32[256,768]{1,0:T(8,128)S(1)}, u32[]{:S(2)}, u32[]{:S(2)}) %collective-permute-start.9) | collective-permute-done | bytes 786464 | tf_op jit(solution)/shard_map/pair_m/ppermute | solution.py:624
  98.3 3.0 %enc_mlp_back.1 = (f32[256,768]{1,0:T(8,128)S(1)}, f32[256,768]{1,0:T(8,128)S(1)}, f32[1,768]{1,0:T(1,128)S(1)}, f32[256,3840]{1,0:T(8,128)S(1)}, bf16[256,3840]{1,0:T(8,128)(2,1)S(1)}) custom-call(f32[256,768]{1,0:T(8,128)S(1)} %get-tuple-element.137.refs_0_, f32[256,768]{1,0:T(8,128)S(1)} %collective-permute-done.9.refs_1_, ...), custom_call_target="tpu_custom_call" | custom-call | flops 3449999872 | bytes 11070000 | tf_op jit(solution)/shard_map/enc_mlp_back/pallas_call | solution.py:561
  103.1 3.5 %collective-permute-done.17.refs_1_ = f32[192,2048]{1,0:T(8,128)S(1)} collective-permute-done((f32[192,2048]{1,0:T(8,128)S(1)}, f32[192,2048]{1,0:T(8,128)S(1)}, u32[]{:S(2)}, u32[]{:S(2)}) %collective-permute-start.17) | collective-permute-done | bytes 1572896 | tf_op jit(solution)/shard_map/swap_m_p/ppermute | solution.py:635
  116.6 5.3 %collective-permute-done.14.refs_2_ = f32[256,768]{1,0:T(8,128)S(1)} collective-permute-done((f32[256,768]{1,0:T(8,128)S(1)}, f32[256,768]{1,0:T(8,128)S(1)}, u32[]{:S(2)}, u32[]{:S(2)}) %collective-permute-start.14) | collective-permute-done | bytes 786464 | tf_op jit(solution)/shard_map/pair_g1/ppermute | solution.py:624
  121.9 5.4 %enc_attn_back.1 = (f32[256,768]{1,0:T(8,128)S(1)}, f32[256,768]{1,0:T(8,128)S(1)}, f32[2,768]{1,0:T(2,128)S(1)}, f32[256,2304]{1,0:T(8,128)S(1)}, bf16[256,2304]{1,0:T(8,128)(2,1)S(1)}) custom-call(s32[2]{0:T(128)S(1)} %copy-done.26, f32[256,768]{1,0:T(8,128)S(1)} %get-tuple-element.148.refs_1_, f32[256,768]{1,0:T(8,128)S(1)} %collective-permute-done.14.refs_2_, ...), custom_call_target="tpu_custom_call" | custom-call | flops 345000000 | bytes 1107000 | tf_op jit(solution)/shard_map/enc_attn_back/pallas_call | solution.py:561
  129.8 3.7 %dec_self_back.1 = (f32[128,768]{1,0:T(8,128)S(1)}, f32[128,768]{1,0:T(8,128)S(1)}, f32[2,768]{1,0:T(2,128)S(1)}, f32[128,1152]{1,0:T(8,128)S(1)}, f32[128,1152]...) custom-call(s32[2]{0:T(128)S(1)} %copy-done.28, f32[128,768]{1,0:T(8,128)S(1)} %query_part.1.refs_1_, ...), custom_call_target="tpu_custom_call" | custom-call | flops 345000000 | bytes 1107000 | tf_op jit(solution)/shard_map/dec_self_back/pallas_call | solution.py:561
  138.7 4.3 %collective-permute-start.30 = (f32[96,1536]{1,0:T(8,128)S(1)}, f32[96,1536]{1,0:T(8,128)S(1)}, u32[]{:S(2)}, u32[]{:S(2)}) collective-permute-start(f32[96,1536]{1,0:T(8,128)S(1)} %get-tuple-element.165.refs_12_), channel_id=1, source_target_pairs={{0,8},{2,10},{4,12},{6,14},{8,0},{10,2},{12,4},{14,6},{16,24},{18,... | collective-permute-start | bytes 1769480 | tf_op jit(solution)/shard_map/swap_c_p/ppermute | solution.py:635
  144.2 4.5 %collective-permute-done.22.refs_1_ = f32[192,2048]{1,0:T(8,128)S(1)} collective-permute-done((f32[192,2048]{1,0:T(8,128)S(1)}, f32[192,2048]{1,0:T(8,128)S(1)}, u32[]{:S(2)}, u32[]{:S(2)}) %collective-permute-start.22) | collective-permute-done | bytes 1572896 | tf_op jit(solution)/shard_map/swap_f_p/ppermute | solution.py:635
  149.0 5.5 %collective-permute-done.20.refs_1_ = f32[96,2048]{1,0:T(8,128)S(1)} collective-permute-done((f32[96,2048]{1,0:T(8,128)S(1)}, f32[96,2048]{1,0:T(8,128)S(1)}, u32[]{:S(2)}, u32[]{:S(2)}) %collective-permute-start.20) | collective-permute-done | bytes 786464 | tf_op jit(solution)/shard_map/swap_m_x/ppermute | solution.py:635
  155.3 4.5 %collective-permute-start.29 = (f32[96,1024]{1,0:T(8,128)S(1)}, f32[96,1024]{1,0:T(8,128)S(1)}, u32[]{:S(2)}, u32[]{:S(2)}) collective-permute-start(f32[96,1024]{1,0:T(8,128)S(1)} %get-tuple-element.175.refs_3_), channel_id=1, source_target_pairs={{0,8},{2,10},{4,12},{6,14},{8,0},{10,2},{12,4},{14,6},{16,24},{18,... | collective-permute-start | bytes 1179656 | tf_op jit(solution)/shard_map/swap_fo_p/ppermute | solution.py:635
  162.6 7.2 %collective-permute-done.29.refs_1_ = f32[96,1024]{1,0:T(8,128)S(1)} collective-permute-done((f32[96,1024]{1,0:T(8,128)S(1)}, f32[96,1024]{1,0:T(8,128)S(1)}, u32[]{:S(2)}, u32[]{:S(2)}) %collective-permute-start.29) | collective-permute-done | bytes 393248 | tf_op jit(solution)/shard_map/swap_fo_p/ppermute | solution.py:635
  172.3 6.2 %collective-permute-start.33 = (f32[48,2048]{1,0:T(8,128)S(1)}, f32[48,2048]{1,0:T(8,128)S(1)}, u32[]{:S(2)}, u32[]{:S(2)}) collective-permute-start(f32[48,2048]{1,0:T(8,128)S(1)} %get-tuple-element.188.refs_2_), channel_id=1, source_target_pairs={{0,8},{2,10},{4,12},{6,14},{8,0},{10,2},{12,4},{14,6},{16,24},{18,... | collective-permute-start | bytes 1179656 | tf_op jit(solution)/shard_map/swap_m_e/ppermute | solution.py:635
  178.5 16.6 %collective-permute-done.38.refs_1_ = f32[192,1536]{1,0:T(8,128)S(1)} collective-permute-done((f32[192,1536]{1,0:T(8,128)S(1)}, f32[192,1536]{1,0:T(8,128)S(1)}, u32[]{:S(2)}, u32[]{:S(2)}) %collective-permute-start.38) | collective-permute-done | bytes 1179680 | tf_op jit(solution)/shard_map/swap_s_p/ppermute | solution.py:635
  199.8 7.8 %collective-permute-start.42 = (f32[96,1664]{1,0:T(8,128)S(1)}, f32[96,1664]{1,0:T(8,128)S(1)}, u32[]{:S(2)}, u32[]{:S(2)}) collective-permute-start(f32[96,1664]{1,0:T(8,128)S(1)} %get-tuple-element.194.refs_2_), channel_id=1, source_target_pairs={{0,8},{2,10},{4,12},{6,14},{8,0},{10,2},{12,4},{14,6},{16,24},{18,... | collective-permute-start | bytes 1916936 | tf_op jit(solution)/shard_map/swap_a_p/ppermute | solution.py:635
  212.5 4.4 %collective-permute-start.47 = (f32[48,1536]{1,0:T(8,128)S(1)}, f32[48,1536]{1,0:T(8,128)S(1)}, u32[]{:S(2)}, u32[]{:S(2)}) collective-permute-start(f32[48,1536]{1,0:T(8,128)S(1)} %get-tuple-element.193.refs_2_), channel_id=1, source_target_pairs={{0,8},{2,10},{4,12},{6,14},{8,0},{10,2},{12,4},{14,6},{16,24},{18,... | collective-permute-start | bytes 884744 | tf_op jit(solution)/shard_map/swap_c_e/ppermute | solution.py:635
  216.8 6.0 %collective-permute-done.42.refs_1_ = f32[96,1664]{1,0:T(8,128)S(1)} collective-permute-done((f32[96,1664]{1,0:T(8,128)S(1)}, f32[96,1664]{1,0:T(8,128)S(1)}, u32[]{:S(2)}, u32[]{:S(2)}) %collective-permute-start.42) | collective-permute-done | bytes 639008 | tf_op jit(solution)/shard_map/swap_a_p/ppermute | solution.py:635
  225.8 3.4 %collective-permute-done.47.refs_1_ = f32[48,1536]{1,0:T(8,128)S(1)} collective-permute-done((f32[48,1536]{1,0:T(8,128)S(1)}, f32[48,1536]{1,0:T(8,128)S(1)}, u32[]{:S(2)}, u32[]{:S(2)}) %collective-permute-start.47) | collective-permute-done | bytes 294944 | tf_op jit(solution)/shard_map/swap_c_e/ppermute | solution.py:635
  233.1 9.1 %collective-permute-start.48 = (f32[48,1664]{1,0:T(8,128)S(1)}, f32[48,1664]{1,0:T(8,128)S(1)}, u32[]{:S(2)}, u32[]{:S(2)}) collective-permute-start(f32[48,1664]{1,0:T(8,128)S(1)} %get-tuple-element.207.refs_4_), channel_id=1, source_target_pairs={{0,8},{2,10},{4,12},{6,14},{8,0},{10,2},{12,4},{14,6},{16,24},{18,... | collective-permute-start | bytes 958472 | tf_op jit(solution)/shard_map/swap_a_e/ppermute | solution.py:635
  (213 shorter events, 91.8 us)
Async XLA Ops:
  11.3 15.4 %collective-permute-start.3 = (f32[128,768]{1,0:T(8,128)}, f32[128,768]{1,0:T(8,128)}, u32[]{:S(2)}, u32[]{:S(2)}) collective-permute-start(f32[128,768]{1,0:T(8,128)} %get-tuple-element.120.refs_5_.refs_1_), channel_id=1, source_target_pairs={{0,1},{1,0},{2,3},{3,2},{4,5},{5,4},{6,7},{7,6},{8,9},{9,8},{10,11... | collective-permute-start | bytes 1179656 | tf_op jit(solution)/shard_map/pair_e1/ppermute | solution.py:624
  13.9 21.3 %collective-permute-start.2 = (f32[128,768]{1,0:T(8,128)}, f32[128,768]{1,0:T(8,128)}, u32[]{:S(2)}, u32[]{:S(2)}) collective-permute-start(f32[128,768]{1,0:T(8,128)} %get-tuple-element.121.refs_1_.refs_6_), channel_id=1, source_target_pairs={{0,1},{1,0},{2,3},{3,2},{4,5},{5,4},{6,7},{7,6},{8,9},{9,8},{10,11... | collective-permute-start | bytes 1179656 | tf_op jit(solution)/shard_map/pair_d1/ppermute | solution.py:624
  20.8 22.6 %collective-permute-start.1 = (f32[128,768]{1,0:T(8,128)S(1)}, f32[128,768]{1,0:T(8,128)S(1)}, u32[]{:S(2)}, u32[]{:S(2)}) collective-permute-start(f32[128,768]{1,0:T(8,128)S(1)} %get-tuple-element.123.refs_6_.refs_2_), channel_id=1, source_target_pairs={{0,1},{1,0},{2,3},{3,2},{4,5},{5,4},{6,7},{7,6},{8,9},{9,8},{10,11... | collective-permute-start | bytes 1179656 | tf_op jit(solution)/shard_map/pair_e2/ppermute | solution.py:624
  29.2 22.7 %collective-permute-start.4 = (f32[128,768]{1,0:T(8,128)S(1)}, f32[128,768]{1,0:T(8,128)S(1)}, u32[]{:S(2)}, u32[]{:S(2)}) collective-permute-start(f32[128,768]{1,0:T(8,128)S(1)} %get-tuple-element.124.refs_1_.refs_2_), channel_id=1, source_target_pairs={{0,1},{1,0},{2,3},{3,2},{4,5},{5,4},{6,7},{7,6},{8,9},{9,8},{10,11... | collective-permute-start | bytes 1179656 | tf_op jit(solution)/shard_map/pair_e2/ppermute | solution.py:624
  67.2 19.9 %collective-permute-start.13 = (f32[192,1024]{1,0:T(8,128)S(1)}, f32[192,1024]{1,0:T(8,128)S(1)}, u32[]{:S(2)}, u32[]{:S(2)}) collective-permute-start(f32[192,1024]{1,0:T(8,128)S(1)} %get-tuple-element.136.refs_18_), channel_id=1, source_target_pairs={{0,4},{2,6},{4,0},{6,2},{8,12},{10,14},{12,8},{14,10},{16,20},{18,... | collective-permute-start | bytes 2359304 | tf_op jit(solution)/shard_map/swap_mo_x/ppermute | solution.py:635
  69.3 37.3 %collective-permute-start.17 = (f32[192,2048]{1,0:T(8,128)S(1)}, f32[192,2048]{1,0:T(8,128)S(1)}, u32[]{:S(2)}, u32[]{:S(2)}) collective-permute-start(f32[192,2048]{1,0:T(8,128)S(1)} %get-tuple-element.156), channel_id=1, source_target_pairs={{0,8},{2,10},{4,12},{6,14},{8,0},{10,2},{12,4},{14,6},{16,24},{18,... | collective-permute-start | bytes 4718600 | tf_op jit(solution)/shard_map/swap_m_p/ppermute | solution.py:635
  79.0 19.4 %collective-permute-start.9 = (f32[256,768]{1,0:T(8,128)S(1)}, f32[256,768]{1,0:T(8,128)S(1)}, u32[]{:S(2)}, u32[]{:S(2)}) collective-permute-start(f32[256,768]{1,0:T(8,128)S(1)} %get-tuple-element.137.refs_0_), channel_id=1, source_target_pairs={{0,1},{1,0},{2,3},{3,2},{4,5},{5,4},{6,7},{7,6},{8,9},{9,8},{10,11... | collective-permute-start | bytes 2359304 | tf_op jit(solution)/shard_map/pair_m/ppermute | solution.py:624
  87.2 27.8 %collective-permute-start.15 = (f32[96,1024]{1,0:T(8,128)S(1)}, f32[96,1024]{1,0:T(8,128)S(1)}, u32[]{:S(2)}, u32[]{:S(2)}) collective-permute-start(f32[96,1024]{1,0:T(8,128)S(1)} %get-tuple-element.146.refs_4_), channel_id=1, source_target_pairs={{0,8},{2,10},{4,12},{6,14},{8,0},{10,2},{12,4},{14,6},{16,24},{18,... | collective-permute-start | bytes 1179656 | tf_op jit(solution)/shard_map/swap_mo_p/ppermute | solution.py:635
  90.1 37.3 %collective-permute-start.19 = (f32[192,1536]{1,0:T(8,128)S(1)}, f32[192,1536]{1,0:T(8,128)S(1)}, u32[]{:S(2)}, u32[]{:S(2)}) collective-permute-start(f32[192,1536]{1,0:T(8,128)S(1)} %get-tuple-element.147.refs_13_), channel_id=1, source_target_pairs={{0,4},{2,6},{4,0},{6,2},{8,12},{10,14},{12,8},{14,10},{16,20},{18,... | collective-permute-start | bytes 3538952 | tf_op jit(solution)/shard_map/swap_c_x/ppermute | solution.py:635
  101.4 20.4 %collective-permute-start.14 = (f32[256,768]{1,0:T(8,128)S(1)}, f32[256,768]{1,0:T(8,128)S(1)}, u32[]{:S(2)}, u32[]{:S(2)}) collective-permute-start(f32[256,768]{1,0:T(8,128)S(1)} %get-tuple-element.148.refs_1_), channel_id=1, source_target_pairs={{0,1},{1,0},{2,3},{3,2},{4,5},{5,4},{6,7},{7,6},{8,9},{9,8},{10,11... | collective-permute-start | bytes 2359304 | tf_op jit(solution)/shard_map/pair_g1/ppermute | solution.py:624
  109.6 39.1 %collective-permute-start.22 = (f32[192,2048]{1,0:T(8,128)S(1)}, f32[192,2048]{1,0:T(8,128)S(1)}, u32[]{:S(2)}, u32[]{:S(2)}) collective-permute-start(f32[192,2048]{1,0:T(8,128)S(1)} %get-tuple-element.169), channel_id=1, source_target_pairs={{0,8},{2,10},{4,12},{6,14},{8,0},{10,2},{12,4},{14,6},{16,24},{18,... | collective-permute-start | bytes 4718600 | tf_op jit(solution)/shard_map/swap_f_p/ppermute | solution.py:635
  111.4 24.3 %collective-permute-start.25 = (f32[192,1024]{1,0:T(8,128)S(1)}, f32[192,1024]{1,0:T(8,128)S(1)}, u32[]{:S(2)}, u32[]{:S(2)}) collective-permute-start(f32[192,1024]{1,0:T(8,128)S(1)} %get-tuple-element.159.refs_2_), channel_id=1, source_target_pairs={{0,4},{2,6},{4,0},{6,2},{8,12},{10,14},{12,8},{14,10},{16,20},{18,... | collective-permute-start | bytes 2359304 | tf_op jit(solution)/shard_map/swap_fo_x/ppermute | solution.py:635
  115.0 14.8 %collective-permute-start.18 = (f32[128,768]{1,0:T(8,128)S(1)}, f32[128,768]{1,0:T(8,128)S(1)}, u32[]{:S(2)}, u32[]{:S(2)}) collective-permute-start(f32[128,768]{1,0:T(8,128)S(1)} %query_part.1.refs_1_), channel_id=1, source_target_pairs={{0,1},{1,0},{2,3},{3,2},{4,5},{5,4},{6,7},{7,6},{8,9},{9,8},{10,11... | collective-permute-start | bytes 1179656 | tf_op jit(solution)/shard_map/pair_q/ppermute | solution.py:624
  134.1 20.4 %collective-permute-start.20 = (f32[96,2048]{1,0:T(8,128)S(1)}, f32[96,2048]{1,0:T(8,128)S(1)}, u32[]{:S(2)}, u32[]{:S(2)}) collective-permute-start(f32[96,2048]{1,0:T(8,128)S(1)} %get-tuple-element.158.refs_2_), channel_id=1, source_target_pairs={{0,4},{2,6},{4,0},{6,2},{8,12},{10,14},{12,8},{14,10},{16,20},{18,... | collective-permute-start | bytes 2359304 | tf_op jit(solution)/shard_map/swap_m_x/ppermute | solution.py:635
  138.7 22.6 %collective-permute-start.30 = (f32[96,1536]{1,0:T(8,128)S(1)}, f32[96,1536]{1,0:T(8,128)S(1)}, u32[]{:S(2)}, u32[]{:S(2)}) collective-permute-start(f32[96,1536]{1,0:T(8,128)S(1)} %get-tuple-element.165.refs_12_), channel_id=1, source_target_pairs={{0,8},{2,10},{4,12},{6,14},{8,0},{10,2},{12,4},{14,6},{16,24},{18,... | collective-permute-start | bytes 1769480 | tf_op jit(solution)/shard_map/swap_c_p/ppermute | solution.py:635
  143.1 16.7 %collective-permute-start.31 = (f32[256,2304]{1,0:T(8,128)S(1)}, f32[256,2304]{1,0:T(8,128)S(1)}, u32[]{:S(2)}, u32[]{:S(2)}) collective-permute-start(f32[256,2304]{1,0:T(8,128)S(1)} %get-tuple-element.184), channel_id=1, source_target_pairs={{0,2},{2,0},{4,6},{6,4},{8,10},{10,8},{12,14},{14,12},{16,18},{18,... | collective-permute-start | bytes 7077896 | tf_op jit(solution)/shard_map/swap_a_0/ppermute | solution.py:635
  148.9 22.5 %collective-permute-start.28 = (f32[96,2048]{1,0:T(8,128)S(1)}, f32[96,2048]{1,0:T(8,128)S(1)}, u32[]{:S(2)}, u32[]{:S(2)}) collective-permute-start(f32[96,2048]{1,0:T(8,128)S(1)} %get-tuple-element.178.refs_2_), channel_id=1, source_target_pairs={{0,4},{2,6},{4,0},{6,2},{8,12},{10,14},{12,8},{14,10},{16,20},{18,... | collective-permute-start | bytes 2359304 | tf_op jit(solution)/shard_map/swap_f_x/ppermute | solution.py:635
  154.6 17.6 %collective-permute-start.27 = (f32[96,2048]{1,0:T(8,128)S(1)}, f32[96,2048]{1,0:T(8,128)S(1)}, u32[]{:S(2)}, u32[]{:S(2)}) collective-permute-start(f32[96,2048]{1,0:T(8,128)S(1)} %halve_m.4.refs_4_.refs_0_), channel_id=1, source_target_pairs={{8,16},{10,18},{12,20},{14,22},{16,8},{18,10},{20,12},{22,14},{9,1... | collective-permute-start | bytes 2359304 | tf_op jit(solution)/shard_map/swap_m_m/ppermute | solution.py:635
  159.8 35.3 %collective-permute-start.38 = (f32[192,1536]{1,0:T(8,128)S(1)}, f32[192,1536]{1,0:T(8,128)S(1)}, u32[]{:S(2)}, u32[]{:S(2)}) collective-permute-start(f32[192,1536]{1,0:T(8,128)S(1)} %get-tuple-element.176.refs_4_), channel_id=1, source_target_pairs={{0,8},{2,10},{4,12},{6,14},{8,0},{10,2},{12,4},{14,6},{16,24},{18,... | collective-permute-start | bytes 3538952 | tf_op jit(solution)/shard_map/swap_s_p/ppermute | solution.py:635
  161.4 37.6 %collective-permute-start.36 = (f32[192,1664]{1,0:T(8,128)S(1)}, f32[192,1664]{1,0:T(8,128)S(1)}, u32[]{:S(2)}, u32[]{:S(2)}) collective-permute-start(f32[192,1664]{1,0:T(8,128)S(1)} %get-tuple-element.186.refs_2_), channel_id=1, source_target_pairs={{0,4},{2,6},{4,0},{6,2},{8,12},{10,14},{12,8},{14,10},{16,20},{18,... | collective-permute-start | bytes 3833864 | tf_op jit(solution)/shard_map/swap_a_x/ppermute | solution.py:635
  169.8 27.0 %collective-permute-start.37 = (f32[96,1536]{1,0:T(8,128)S(1)}, f32[96,1536]{1,0:T(8,128)S(1)}, u32[]{:S(2)}, u32[]{:S(2)}) collective-permute-start(f32[96,1536]{1,0:T(8,128)S(1)} %halve_c.4.refs_2_.refs_0_), channel_id=1, source_target_pairs={{8,16},{10,18},{12,20},{14,22},{16,8},{18,10},{20,12},{22,14},{9,1... | collective-permute-start | bytes 1769480 | tf_op jit(solution)/shard_map/swap_c_m/ppermute | solution.py:635
  171.5 28.3 %collective-permute-start.35 = (f32[96,2048]{1,0:T(8,128)S(1)}, f32[96,2048]{1,0:T(8,128)S(1)}, u32[]{:S(2)}, u32[]{:S(2)}) collective-permute-start(f32[96,2048]{1,0:T(8,128)S(1)} %halve_f.4.refs_2_.refs_0_), channel_id=1, source_target_pairs={{8,16},{10,18},{12,20},{14,22},{16,8},{18,10},{20,12},{22,14},{9,1... | collective-permute-start | bytes 2359304 | tf_op jit(solution)/shard_map/swap_f_m/ppermute | solution.py:635
  172.3 35.4 %collective-permute-start.33 = (f32[48,2048]{1,0:T(8,128)S(1)}, f32[48,2048]{1,0:T(8,128)S(1)}, u32[]{:S(2)}, u32[]{:S(2)}) collective-permute-start(f32[48,2048]{1,0:T(8,128)S(1)} %get-tuple-element.188.refs_2_), channel_id=1, source_target_pairs={{0,8},{2,10},{4,12},{6,14},{8,0},{10,2},{12,4},{14,6},{16,24},{18,... | collective-permute-start | bytes 1179656 | tf_op jit(solution)/shard_map/swap_m_e/ppermute | solution.py:635
  195.2 16.5 %collective-permute-start.43 = (f32[96,1536]{1,0:T(8,128)S(1)}, f32[96,1536]{1,0:T(8,128)S(1)}, u32[]{:S(2)}, u32[]{:S(2)}) collective-permute-start(f32[96,1536]{1,0:T(8,128)S(1)} %get-tuple-element.192.refs_2_), channel_id=1, source_target_pairs={{0,4},{2,6},{4,0},{6,2},{8,12},{10,14},{12,8},{14,10},{16,20},{18,... | collective-permute-start | bytes 1769480 | tf_op jit(solution)/shard_map/swap_s_x/ppermute | solution.py:635
  198.9 26.1 %collective-permute-start.41 = (f32[96,1024]{1,0:T(8,128)S(1)}, f32[96,1024]{1,0:T(8,128)S(1)}, u32[]{:S(2)}, u32[]{:S(2)}) collective-permute-start(f32[96,1024]{1,0:T(8,128)S(1)} %halve_fo.4.refs_2_.refs_0_), channel_id=1, source_target_pairs={{8,16},{10,18},{12,20},{14,22},{16,8},{18,10},{20,12},{22,14},{9,1... | collective-permute-start | bytes 1179656 | tf_op jit(solution)/shard_map/swap_fo_m/ppermute | solution.py:635
  199.8 23.1 %collective-permute-start.42 = (f32[96,1664]{1,0:T(8,128)S(1)}, f32[96,1664]{1,0:T(8,128)S(1)}, u32[]{:S(2)}, u32[]{:S(2)}) collective-permute-start(f32[96,1664]{1,0:T(8,128)S(1)} %get-tuple-element.194.refs_2_), channel_id=1, source_target_pairs={{0,8},{2,10},{4,12},{6,14},{8,0},{10,2},{12,4},{14,6},{16,24},{18,... | collective-permute-start | bytes 1916936 | tf_op jit(solution)/shard_map/swap_a_p/ppermute | solution.py:635
  210.0 34.2 %collective-permute-start.39 = (f32[512,768]{1,0:T(8,128)S(1)}, f32[512,768]{1,0:T(8,128)S(1)}, u32[]{:S(2)}, u32[]{:S(2)}) collective-permute-start(f32[512,768]{1,0:T(8,128)S(1)} %tail_parts.1.refs_2_.refs_0_), channel_id=1, source_target_pairs={{0,1},{1,0},{2,3},{3,2},{4,5},{5,4},{6,7},{7,6},{8,9},{9,8},{10,11... | collective-permute-start | bytes 4718600 | tf_op jit(solution)/shard_map/pair_tail/ppermute | solution.py:624
  211.8 20.2 %collective-permute-start.46 = (f32[96,1536]{1,0:T(8,128)S(1)}, f32[96,1536]{1,0:T(8,128)S(1)}, u32[]{:S(2)}, u32[]{:S(2)}) collective-permute-start(f32[96,1536]{1,0:T(8,128)S(1)} %halve_s.4.refs_2_.refs_0_), channel_id=1, source_target_pairs={{8,16},{10,18},{12,20},{14,22},{16,8},{18,10},{20,12},{22,14},{9,1... | collective-permute-start | bytes 1769480 | tf_op jit(solution)/shard_map/swap_s_m/ppermute | solution.py:635
  212.5 16.7 %collective-permute-start.47 = (f32[48,1536]{1,0:T(8,128)S(1)}, f32[48,1536]{1,0:T(8,128)S(1)}, u32[]{:S(2)}, u32[]{:S(2)}) collective-permute-start(f32[48,1536]{1,0:T(8,128)S(1)} %get-tuple-element.193.refs_2_), channel_id=1, source_target_pairs={{0,8},{2,10},{4,12},{6,14},{8,0},{10,2},{12,4},{14,6},{16,24},{18,... | collective-permute-start | bytes 884744 | tf_op jit(solution)/shard_map/swap_c_e/ppermute | solution.py:635
  222.9 19.3 %collective-permute-start.40 = (f32[48,2048]{1,0:T(8,128)S(1)}, f32[48,2048]{1,0:T(8,128)S(1)}, u32[]{:S(2)}, u32[]{:S(2)}) collective-permute-start(f32[48,2048]{1,0:T(8,128)S(1)} %get-tuple-element.195.refs_4_), channel_id=1, source_target_pairs={{0,8},{2,10},{4,12},{6,14},{8,0},{10,2},{12,4},{14,6},{16,24},{18,... | collective-permute-start | bytes 1179656 | tf_op jit(solution)/shard_map/swap_f_e/ppermute | solution.py:635
  232.9 15.2 %collective-permute-start.49 = (f32[48,1536]{1,0:T(8,128)S(1)}, f32[48,1536]{1,0:T(8,128)S(1)}, u32[]{:S(2)}, u32[]{:S(2)}) collective-permute-start(f32[48,1536]{1,0:T(8,128)S(1)} %get-tuple-element.206.refs_2_), channel_id=1, source_target_pairs={{0,8},{2,10},{4,12},{6,14},{8,0},{10,2},{12,4},{14,6},{16,24},{18,... | collective-permute-start | bytes 884744 | tf_op jit(solution)/shard_map/swap_s_e/ppermute | solution.py:635
  233.1 19.3 %collective-permute-start.48 = (f32[48,1664]{1,0:T(8,128)S(1)}, f32[48,1664]{1,0:T(8,128)S(1)}, u32[]{:S(2)}, u32[]{:S(2)}) collective-permute-start(f32[48,1664]{1,0:T(8,128)S(1)} %get-tuple-element.207.refs_4_), channel_id=1, source_target_pairs={{0,8},{2,10},{4,12},{6,14},{8,0},{10,2},{12,4},{14,6},{16,24},{18,... | collective-permute-start | bytes 958472 | tf_op jit(solution)/shard_map/swap_a_e/ppermute | solution.py:635
  (61 other events, 403.5 us)

commit v10 on v9

--- a/solution.py
+++ b/solution.py
@@ -429,26 +429,26 @@
 
 COST = {
     "enc_attn_fwd": 2.3, "dec_self_fwd": 2.5, "enc_mlp_fwd": 1.7, "cross_fwd": 4.2, "dec_mlp": 2.7,
-    "cross_back": 20.0, "weights_c": 0.1, "enc_mlp_back": 3.0, "enc_attn_back": 0.3, "query_part": 20.0,
-    "weights_f": 3.0, "weights_a": 0.1, "dec_self_back": 0.3, "weights_s": 1.0, "tail_parts": 3.0,
-    "tail": 20.0, "gains": 1.0, "gain_rows": 1.0, "halve_m": 20.0, "halve_mo": 0.3,
-    "halve_c": 0.1, "halve_f": 0.1, "halve_fo": 3.0, "halve_s": 8.0, "halve_a": 0.1,
-    "finish_m": 0.3, "finish_mo": 3.0, "finish_c": 0.1, "finish_f": 0.1, "finish_fo": 1.0,
-    "finish_s": 0.1, "finish_a": 8.0, "weights_m": 0.1,
+    "cross_back": 20.0, "weights_c": 1.0, "enc_mlp_back": 0.1, "enc_attn_back": 0.3, "query_part": 20.0,
+    "weights_f": 1.0, "weights_a": 0.3, "dec_self_back": 3.0, "weights_s": 1.0, "tail_parts": 0.1,
+    "tail": 1.0, "gains": 20.0, "gain_rows": 1.0, "halve_m": 20.0, "halve_mo": 0.3,
+    "halve_c": 0.3, "halve_f": 3.0, "halve_fo": 0.3, "halve_s": 3.0, "halve_a": 8.0,
+    "finish_m": 3.0, "finish_mo": 0.3, "finish_c": 3.0, "finish_f": 1.0, "finish_fo": 3.0,
+    "finish_s": 1.0, "finish_a": 8.0, "weights_m": 0.1,
 }
 VMEM_LIMIT = 8
 
 LINE = (
     "pause", "enc_attn_0", "enc_attn_1", "dec_self", "pause", "enc_mlp_0", "enc_mlp_1", "pause",
     "cross_0", "cross_1", "pause", "dec_mlp", "tick", "w_m", "cross_back", "h_mo",
-    "w_c", "enc_mlp_back", "h_m", "query_part", "tick", "w_f", "h_mo", "enc_attn_back",
-    "h_c", "dec_self_back", "h_fo", "w_s", "gain_rows", "gains", "h_f", "h_mo",
-    "h_m", "w_a", "h_c", "h_fo", "h_f", "h_m", "h_s", "h_c",
-    "h_a", "h_f", "e_m", "tick", "tail_parts", "h_s", "h_a", "h_fo",
-    "e_c", "h_s", "h_a", "e_f", "tail", "e_s", "pause", "e_a",
+    "w_c", "enc_mlp_back", "h_m", "query_part", "w_f", "h_mo", "h_mo", "h_c",
+    "enc_attn_back", "dec_self_back", "h_fo", "gain_rows", "h_f", "gains", "w_s", "h_m",
+    "h_c", "w_a", "h_fo", "h_f", "h_m", "tick", "tick", "h_c",
+    "h_s", "h_fo", "h_a", "tail_parts", "e_c", "h_s", "h_f", "h_a",
+    "e_f", "h_s", "tail", "h_a", "e_m", "e_s", "pause", "e_a",
 )
 HALVINGS = {"m": "pxme", "mo": "xpme", "c": "xpme", "f": "pxme", "fo": "xpme", "s": "pxme", "a": "xpme"}
-PARTS = {"m": 1, "c": 3, "f": 1, "a": 1, "s": 2}
+PARTS = {"m": 1, "c": 3, "f": 1, "a": 1, "s": 1}
 TICK = 0.1
 GAINS_WITH = "a"
 

time: 254 us -> 254 us (level)
  waiting for transfers between devices: 106 us -> 101 us
  starting transfers between devices: 87.2 us -> 91.7 us
    ppermute x37 -> x36, waiting for transfers between devices: 62.6 us -> 49.9 us  [swap(): return lax.ppermute(value, 'dp', pairs)]
    ppermute x13, waiting for transfers between devices: 43.3 us -> 51.5 us  [pair_other(): return lax.ppermute(part, 'mp', [(0, 1), (1, 0)])]
    ppermute x37 -> x36, starting transfers between devices: 63.4 us -> 68.2 us  [swap(): return lax.ppermute(value, 'dp', pairs)]
  transfers between devices with their start and end apart: 50 -> 49, of which waited for: 27 -> 29; matrix products, arithmetic and copies ran while one was open for 0% -> 0% of each run, Pallas kernels for 18% -> 17%
where the time goes in v10:
time: 254 us
  waiting for transfers between devices  101 us (40%)
  starting transfers between devices  91.7 us (36%)
  Pallas kernels  50 us (20%)
  local copies, waits for them, and re-layouts  8.52 us (3%)
    ppermute x36, starting transfers between devices, swap(): return lax.ppermute(value, 'dp', pairs)  68.2 us
    ppermute x13, waiting for transfers between devices, pair_other(): return lax.ppermute(part, 'mp', [(0, 1), (1, 0)])  51.5 us
    pallas_call x56, Pallas kernels, call(): pl.pallas_call(run, out_shape=shapes, in_specs=in_specs, out_specs=[VMEM]...  50 us
    ppermute x36, waiting for transfers between devices, swap(): return lax.ppermute(value, 'dp', pairs)  49.9 us
    ppermute x13, starting transfers between devices, pair_other(): return lax.ppermute(part, 'mp', [(0, 1), (1, 0)])  23.5 us
    unnamed x86, local copies, waits for them, and re-layouts  8.52 us
  transfers between devices with their start and end apart: 49, of which 29 were waited for; matrix products, arithmetic and copies ran while one was open for 0% of the time, Pallas kernels for 17%

profile of v10, /device:TPU:0, one launch (start us, length us, event | category | flops | bytes accessed | tf_op | source)
XLA Modules:
  0.0 253.9 jit_solution(18410459879115558817)
XLA Ops:
  2.4 2.5 enc_attn_fwd.2
  5.7 3.0 %collective-permute-start = (f32[128,768]{1,0:T(8,128)}, f32[128,768]{1,0:T(8,128)}, u32[]{:S(2)}, u32[]{:S(2)}) collective-permute-start(f32[128,768]{1,0:T(8,128)} %get-tuple-element.118.refs_5_.refs_1_), channel_id=1, source_target_pairs={{0,1},{1,0},{2,3},{3,2},{4,5},{5,4},{6,7},{7,6},{8,9},{9,8},{10,11... | collective-permute-start | bytes 1179656 | tf_op jit(solution)/shard_map/pair_e1/ppermute | solution.py:624
  12.1 2.5 %dec_self_fwd.1 = (f32[128,768]{1,0:T(8,128)}, bf16[128,1536]{1,0:T(8,128)(2,1)S(1)}) custom-call(s32[2]{0:T(128)S(1)} %copy-done.33, bf16[128,768]{1,0:T(8,128)(2,1)S(1)} %bitcast.17, f32[3,768]{1,0:T(4,128)S(1)} %copy-done.21, bf16[3,768,384]{2,1,0:T(8,128)(2,1)S(1)} %copy-done.26, bf16[384,768]{1,0:T(8,128)(2,1)S(1)} %copy-done.29, ...), custom_call_target="tpu_custom_call" | custom-call | flops 2875000064 | bytes 9225000 | tf_op jit(solution)/shard_map/dec_self_fwd/pallas_call | solution.py:561
  23.6 3.8 %collective-permute-done.3.refs_2_ = f32[128,768]{1,0:T(8,128)} collective-permute-done((f32[128,768]{1,0:T(8,128)}, f32[128,768]{1,0:T(8,128)}, u32[]{:S(2)}, u32[]{:S(2)}) %collective-permute-start.3) | collective-permute-done | bytes 393248 | tf_op jit(solution)/shard_map/pair_e1/ppermute | solution.py:624
  32.0 3.8 %collective-permute-done.2.refs_7_ = f32[128,768]{1,0:T(8,128)} collective-permute-done((f32[128,768]{1,0:T(8,128)}, f32[128,768]{1,0:T(8,128)}, u32[]{:S(2)}, u32[]{:S(2)}) %collective-permute-start.2) | collective-permute-done | bytes 393248 | tf_op jit(solution)/shard_map/pair_d1/ppermute | solution.py:624
  35.8 8.3 %collective-permute-done.1.refs_3_ = f32[128,768]{1,0:T(8,128)S(1)} collective-permute-done((f32[128,768]{1,0:T(8,128)S(1)}, f32[128,768]{1,0:T(8,128)S(1)}, u32[]{:S(2)}, u32[]{:S(2)}) %collective-permute-start.1) | collective-permute-done | bytes 393248 | tf_op jit(solution)/shard_map/pair_e2/ppermute | solution.py:624
  48.6 4.0 %collective-permute-done.4.refs_3_ = f32[128,768]{1,0:T(8,128)S(1)} collective-permute-done((f32[128,768]{1,0:T(8,128)S(1)}, f32[128,768]{1,0:T(8,128)S(1)}, u32[]{:S(2)}, u32[]{:S(2)}) %collective-permute-start.4) | collective-permute-done | bytes 393248 | tf_op jit(solution)/shard_map/pair_e2/ppermute | solution.py:624
  57.0 3.6 %collective-permute-done.6.refs_5_ = f32[64,768]{1,0:T(8,128)S(1)} collective-permute-done((f32[64,768]{1,0:T(8,128)S(1)}, f32[64,768]{1,0:T(8,128)S(1)}, u32[]{:S(2)}, u32[]{:S(2)}) %collective-permute-start.6) | collective-permute-done | bytes 196640 | tf_op jit(solution)/shard_map/pair_d2/ppermute | solution.py:624
  71.6 3.4 %collective-permute-done.7.refs_2_ = f32[128,768]{1,0:T(8,128)S(1)} collective-permute-done((f32[128,768]{1,0:T(8,128)S(1)}, f32[128,768]{1,0:T(8,128)S(1)}, u32[]{:S(2)}, u32[]{:S(2)}) %collective-permute-start.7) | collective-permute-done | bytes 393248 | tf_op jit(solution)/shard_map/pair_g3/ppermute | solution.py:624
  75.0 4.7 %cross_back.1 = (f32[256,768]{1,0:T(8,128)S(1)}, f32[128,768]{1,0:T(8,128)S(1)}, f32[1,768]{1,0:T(1,128)S(1)}, f32[128,1280]{1,0:T(8,128)S(1)}, f32[128,1280]{1,...) custom-call(s32[2]{0:T(128)S(1)} %copy-done.23, f32[128,768]{1,0:T(8,128)S(1)} %get-tuple-element.129.refs_1_, ...), custom_call_target="tpu_custom_call" | custom-call | flops 23000000512 | bytes 73800000 | tf_op jit(solution)/shard_map/cross_back/pallas_call | solution.py:561
  82.1 5.8 %collective-permute-done.13.refs_1_ = f32[192,1024]{1,0:T(8,128)S(1)} collective-permute-done((f32[192,1024]{1,0:T(8,128)S(1)}, f32[192,1024]{1,0:T(8,128)S(1)}, u32[]{:S(2)}, u32[]{:S(2)}) %collective-permute-start.13) | collective-permute-done | bytes 786464 | tf_op jit(solution)/shard_map/swap_mo_x/ppermute | solution.py:635
  92.6 6.5 %collective-permute-done.9.refs_1_ = f32[256,768]{1,0:T(8,128)S(1)} collective-permute-done((f32[256,768]{1,0:T(8,128)S(1)}, f32[256,768]{1,0:T(8,128)S(1)}, u32[]{:S(2)}, u32[]{:S(2)}) %collective-permute-start.9) | collective-permute-done | bytes 786464 | tf_op jit(solution)/shard_map/pair_m/ppermute | solution.py:624
  99.1 3.0 %enc_mlp_back.1 = (f32[256,768]{1,0:T(8,128)S(1)}, f32[256,768]{1,0:T(8,128)S(1)}, f32[1,768]{1,0:T(1,128)S(1)}, f32[256,3840]{1,0:T(8,128)S(1)}, bf16[256,3840]{1,0:T(8,128)(2,1)S(1)}) custom-call(f32[256,768]{1,0:T(8,128)S(1)} %get-tuple-element.136.refs_0_, f32[256,768]{1,0:T(8,128)S(1)} %collective-permute-done.9.refs_1_, ...), custom_call_target="tpu_custom_call" | custom-call | flops 115000000 | bytes 369000 | tf_op jit(solution)/shard_map/enc_mlp_back/pallas_call | solution.py:561
  102.2 5.1 %collective-permute-done.18.refs_1_ = f32[192,2048]{1,0:T(8,128)S(1)} collective-permute-done((f32[192,2048]{1,0:T(8,128)S(1)}, f32[192,2048]{1,0:T(8,128)S(1)}, u32[]{:S(2)}, u32[]{:S(2)}) %collective-permute-start.18) | collective-permute-done | bytes 1572896 | tf_op jit(solution)/shard_map/swap_m_p/ppermute | solution.py:635
  121.6 11.0 %collective-permute-done.14.refs_2_ = f32[256,768]{1,0:T(8,128)S(1)} collective-permute-done((f32[256,768]{1,0:T(8,128)S(1)}, f32[256,768]{1,0:T(8,128)S(1)}, u32[]{:S(2)}, u32[]{:S(2)}) %collective-permute-start.14) | collective-permute-done | bytes 786464 | tf_op jit(solution)/shard_map/pair_g1/ppermute | solution.py:624
  133.0 5.5 %enc_attn_back.1 = (f32[256,768]{1,0:T(8,128)S(1)}, f32[256,768]{1,0:T(8,128)S(1)}, f32[2,768]{1,0:T(2,128)S(1)}, f32[256,2304]{1,0:T(8,128)S(1)}, bf16[256,2304]{1,0:T(8,128)(2,1)S(1)}) custom-call(s32[2]{0:T(128)S(1)} %copy-done.23, f32[256,768]{1,0:T(8,128)S(1)} %get-tuple-element.147.refs_1_, f32[256,768]{1,0:T(8,128)S(1)} %collective-permute-done.14.refs_2_, ...), custom_call_target="tpu_custom_call" | custom-call | flops 345000000 | bytes 1107000 | tf_op jit(solution)/shard_map/enc_attn_back/pallas_call | solution.py:561
  139.8 3.5 %dec_self_back.1 = (f32[128,768]{1,0:T(8,128)S(1)}, f32[128,768]{1,0:T(8,128)S(1)}, f32[2,768]{1,0:T(2,128)S(1)}, f32[128,2304]{1,0:T(8,128)S(1)}, bf16[128,2304]{1,0:T(8,128)(2,1)S(1)}) custom-call(s32[2]{0:T(128)S(1)} %copy-done.34, f32[128,768]{1,0:T(8,128)S(1)} %query_part.1.refs_2_.refs_1_, f32[128,768]{1,0:T(8,128)S(1)} %collective-permute-done.20.refs_2_, ...), custom_call_target="tpu_custom_call" | custom-call | flops 3449999872 | bytes 11070000 | tf_op jit(solution)/shard_map/dec_self_back/pallas_call | solution.py:561
  144.1 5.4 %collective-permute-done.24.refs_1_ = f32[192,2048]{1,0:T(8,128)S(1)} collective-permute-done((f32[192,2048]{1,0:T(8,128)S(1)}, f32[192,2048]{1,0:T(8,128)S(1)}, u32[]{:S(2)}, u32[]{:S(2)}) %collective-permute-start.24) | collective-permute-done | bytes 1572896 | tf_op jit(solution)/shard_map/swap_f_p/ppermute | solution.py:635
  155.8 4.4 %collective-permute-start.30 = (f32[96,1024]{1,0:T(8,128)S(1)}, f32[96,1024]{1,0:T(8,128)S(1)}, u32[]{:S(2)}, u32[]{:S(2)}) collective-permute-start(f32[96,1024]{1,0:T(8,128)S(1)} %get-tuple-element.171.refs_4_), channel_id=1, source_target_pairs={{0,8},{2,10},{4,12},{6,14},{8,0},{10,2},{12,4},{14,6},{16,24},{18,... | collective-permute-start | bytes 1179656 | tf_op jit(solution)/shard_map/swap_fo_p/ppermute | solution.py:635
  166.8 3.7 %collective-permute-done.30.refs_1_ = f32[96,1024]{1,0:T(8,128)S(1)} collective-permute-done((f32[96,1024]{1,0:T(8,128)S(1)}, f32[96,1024]{1,0:T(8,128)S(1)}, u32[]{:S(2)}, u32[]{:S(2)}) %collective-permute-start.30) | collective-permute-done | bytes 393248 | tf_op jit(solution)/shard_map/swap_fo_p/ppermute | solution.py:635
  174.1 17.8 %collective-permute-start.38 = (f32[48,1536]{1,0:T(8,128)S(1)}, f32[48,1536]{1,0:T(8,128)S(1)}, u32[]{:S(2)}, u32[]{:S(2)}) collective-permute-start(f32[48,1536]{1,0:T(8,128)S(1)} %get-tuple-element.188.refs_2_), channel_id=1, source_target_pairs={{0,8},{2,10},{4,12},{6,14},{8,0},{10,2},{12,4},{14,6},{16,24},{18,... | collective-permute-start | bytes 884744 | tf_op jit(solution)/shard_map/swap_c_e/ppermute | solution.py:635
  191.9 3.9 %collective-permute-done.32.refs_1_ = f32[192,1536]{1,0:T(8,128)S(1)} collective-permute-done((f32[192,1536]{1,0:T(8,128)S(1)}, f32[192,1536]{1,0:T(8,128)S(1)}, u32[]{:S(2)}, u32[]{:S(2)}) %collective-permute-start.32) | collective-permute-done | bytes 1179680 | tf_op jit(solution)/shard_map/swap_s_p/ppermute | solution.py:635
  200.4 3.1 %collective-permute-start.43 = (f32[96,1664]{1,0:T(8,128)S(1)}, f32[96,1664]{1,0:T(8,128)S(1)}, u32[]{:S(2)}, u32[]{:S(2)}) collective-permute-start(f32[96,1664]{1,0:T(8,128)S(1)} %get-tuple-element.191.refs_4_), channel_id=1, source_target_pairs={{0,8},{2,10},{4,12},{6,14},{8,0},{10,2},{12,4},{14,6},{16,24},{18,... | collective-permute-start | bytes 1916936 | tf_op jit(solution)/shard_map/swap_a_p/ppermute | solution.py:635
  206.4 4.6 %collective-permute-done.37.refs_1_ = f32[96,1536]{1,0:T(8,128)S(1)} collective-permute-done((f32[96,1536]{1,0:T(8,128)S(1)}, f32[96,1536]{1,0:T(8,128)S(1)}, u32[]{:S(2)}, u32[]{:S(2)}) %collective-permute-start.37) | collective-permute-done | bytes 589856 | tf_op jit(solution)/shard_map/swap_s_x/ppermute | solution.py:635
  212.8 4.4 %collective-permute-start.41 = (f32[48,2048]{1,0:T(8,128)S(1)}, f32[48,2048]{1,0:T(8,128)S(1)}, u32[]{:S(2)}, u32[]{:S(2)}) collective-permute-start(f32[48,2048]{1,0:T(8,128)S(1)} %get-tuple-element.198.refs_2_), channel_id=1, source_target_pairs={{0,8},{2,10},{4,12},{6,14},{8,0},{10,2},{12,4},{14,6},{16,24},{18,... | collective-permute-start | bytes 1179656 | tf_op jit(solution)/shard_map/swap_f_e/ppermute | solution.py:635
  217.2 2.8 %collective-permute-done.43.refs_1_ = f32[96,1664]{1,0:T(8,128)S(1)} collective-permute-done((f32[96,1664]{1,0:T(8,128)S(1)}, f32[96,1664]{1,0:T(8,128)S(1)}, u32[]{:S(2)}, u32[]{:S(2)}) %collective-permute-start.43) | collective-permute-done | bytes 639008 | tf_op jit(solution)/shard_map/swap_a_p/ppermute | solution.py:635
  220.8 4.6 %collective-permute-start.48 = (f32[48,1024]{1,0:T(8,128)S(1)}, f32[48,1024]{1,0:T(8,128)S(1)}, u32[]{:S(2)}, u32[]{:S(2)}) collective-permute-start(f32[48,1024]{1,0:T(8,128)S(1)} %get-tuple-element.160.refs_2_), channel_id=1, source_target_pairs={{0,8},{2,10},{4,12},{6,14},{8,0},{10,2},{12,4},{14,6},{16,24},{18,... | collective-permute-start | bytes 589832 | tf_op jit(solution)/shard_map/swap_mo_e/ppermute | solution.py:635
  225.4 3.0 %collective-permute-done.41.refs_1_ = f32[48,2048]{1,0:T(8,128)S(1)} collective-permute-done((f32[48,2048]{1,0:T(8,128)S(1)}, f32[48,2048]{1,0:T(8,128)S(1)}, u32[]{:S(2)}, u32[]{:S(2)}) %collective-permute-start.41) | collective-permute-done | bytes 393248 | tf_op jit(solution)/shard_map/swap_f_e/ppermute | solution.py:635
  233.7 2.6 %collective-permute-done.36.refs_1_ = f32[512,768]{1,0:T(8,128)S(1)} collective-permute-done((f32[512,768]{1,0:T(8,128)S(1)}, f32[512,768]{1,0:T(8,128)S(1)}, u32[]{:S(2)}, u32[]{:S(2)}) %collective-permute-start.36) | collective-permute-done | bytes 1572896 | tf_op jit(solution)/shard_map/pair_tail/ppermute | solution.py:624
  238.7 5.3 %collective-permute-start.45 = (f32[48,1664]{1,0:T(8,128)S(1)}, f32[48,1664]{1,0:T(8,128)S(1)}, u32[]{:S(2)}, u32[]{:S(2)}) collective-permute-start(f32[48,1664]{1,0:T(8,128)S(1)} %get-tuple-element.207.refs_4_), channel_id=1, source_target_pairs={{0,8},{2,10},{4,12},{6,14},{8,0},{10,2},{12,4},{14,6},{16,24},{18,... | collective-permute-start | bytes 958472 | tf_op jit(solution)/shard_map/swap_a_e/ppermute | solution.py:635
  244.8 2.6 %collective-permute-done.46.refs_1_ = f32[48,1536]{1,0:T(8,128)S(1)} collective-permute-done((f32[48,1536]{1,0:T(8,128)S(1)}, f32[48,1536]{1,0:T(8,128)S(1)}, u32[]{:S(2)}, u32[]{:S(2)}) %collective-permute-start.46) | collective-permute-done | bytes 294944 | tf_op jit(solution)/shard_map/swap_s_e/ppermute | solution.py:635
  250.0 3.2 %collective-permute-done.45.refs_1_ = f32[48,1664]{1,0:T(8,128)S(1)} collective-permute-done((f32[48,1664]{1,0:T(8,128)S(1)}, f32[48,1664]{1,0:T(8,128)S(1)}, u32[]{:S(2)}, u32[]{:S(2)}) %collective-permute-start.45) | collective-permute-done | bytes 319520 | tf_op jit(solution)/shard_map/swap_a_e/ppermute | solution.py:635
  (211 shorter events, 100.8 us)
Async XLA Ops:
  12.0 15.4 %collective-permute-start.3 = (f32[128,768]{1,0:T(8,128)}, f32[128,768]{1,0:T(8,128)}, u32[]{:S(2)}, u32[]{:S(2)}) collective-permute-start(f32[128,768]{1,0:T(8,128)} %get-tuple-element.119.refs_5_.refs_1_), channel_id=1, source_target_pairs={{0,1},{1,0},{2,3},{3,2},{4,5},{5,4},{6,7},{7,6},{8,9},{9,8},{10,11... | collective-permute-start | bytes 1179656 | tf_op jit(solution)/shard_map/pair_e1/ppermute | solution.py:624
  14.6 21.2 %collective-permute-start.2 = (f32[128,768]{1,0:T(8,128)}, f32[128,768]{1,0:T(8,128)}, u32[]{:S(2)}, u32[]{:S(2)}) collective-permute-start(f32[128,768]{1,0:T(8,128)} %get-tuple-element.120.refs_1_.refs_6_), channel_id=1, source_target_pairs={{0,1},{1,0},{2,3},{3,2},{4,5},{5,4},{6,7},{7,6},{8,9},{9,8},{10,11... | collective-permute-start | bytes 1179656 | tf_op jit(solution)/shard_map/pair_d1/ppermute | solution.py:624
  21.6 22.6 %collective-permute-start.1 = (f32[128,768]{1,0:T(8,128)S(1)}, f32[128,768]{1,0:T(8,128)S(1)}, u32[]{:S(2)}, u32[]{:S(2)}) collective-permute-start(f32[128,768]{1,0:T(8,128)S(1)} %get-tuple-element.122.refs_6_.refs_2_), channel_id=1, source_target_pairs={{0,1},{1,0},{2,3},{3,2},{4,5},{5,4},{6,7},{7,6},{8,9},{9,8},{10,11... | collective-permute-start | bytes 1179656 | tf_op jit(solution)/shard_map/pair_e2/ppermute | solution.py:624
  29.9 22.7 %collective-permute-start.4 = (f32[128,768]{1,0:T(8,128)S(1)}, f32[128,768]{1,0:T(8,128)S(1)}, u32[]{:S(2)}, u32[]{:S(2)}) collective-permute-start(f32[128,768]{1,0:T(8,128)S(1)} %get-tuple-element.123.refs_1_.refs_2_), channel_id=1, source_target_pairs={{0,1},{1,0},{2,3},{3,2},{4,5},{5,4},{6,7},{7,6},{8,9},{9,8},{10,11... | collective-permute-start | bytes 1179656 | tf_op jit(solution)/shard_map/pair_e2/ppermute | solution.py:624
  68.0 19.9 %collective-permute-start.13 = (f32[192,1024]{1,0:T(8,128)S(1)}, f32[192,1024]{1,0:T(8,128)S(1)}, u32[]{:S(2)}, u32[]{:S(2)}) collective-permute-start(f32[192,1024]{1,0:T(8,128)S(1)} %get-tuple-element.135.refs_18_), channel_id=1, source_target_pairs={{0,4},{2,6},{4,0},{6,2},{8,12},{10,14},{12,8},{14,10},{16,20},{18,... | collective-permute-start | bytes 2359304 | tf_op jit(solution)/shard_map/swap_mo_x/ppermute | solution.py:635
  70.0 37.3 %collective-permute-start.18 = (f32[192,2048]{1,0:T(8,128)S(1)}, f32[192,2048]{1,0:T(8,128)S(1)}, u32[]{:S(2)}, u32[]{:S(2)}) collective-permute-start(f32[192,2048]{1,0:T(8,128)S(1)} %get-tuple-element.156), channel_id=1, source_target_pairs={{0,8},{2,10},{4,12},{6,14},{8,0},{10,2},{12,4},{14,6},{16,24},{18,... | collective-permute-start | bytes 4718600 | tf_op jit(solution)/shard_map/swap_m_p/ppermute | solution.py:635
  79.7 19.4 %collective-permute-start.9 = (f32[256,768]{1,0:T(8,128)S(1)}, f32[256,768]{1,0:T(8,128)S(1)}, u32[]{:S(2)}, u32[]{:S(2)}) collective-permute-start(f32[256,768]{1,0:T(8,128)S(1)} %get-tuple-element.136.refs_0_), channel_id=1, source_target_pairs={{0,1},{1,0},{2,3},{3,2},{4,5},{5,4},{6,7},{7,6},{8,9},{9,8},{10,11... | collective-permute-start | bytes 2359304 | tf_op jit(solution)/shard_map/pair_m/ppermute | solution.py:624
  88.0 27.8 %collective-permute-start.16 = (f32[96,1024]{1,0:T(8,128)S(1)}, f32[96,1024]{1,0:T(8,128)S(1)}, u32[]{:S(2)}, u32[]{:S(2)}) collective-permute-start(f32[96,1024]{1,0:T(8,128)S(1)} %get-tuple-element.145.refs_4_), channel_id=1, source_target_pairs={{0,8},{2,10},{4,12},{6,14},{8,0},{10,2},{12,4},{14,6},{16,24},{18,... | collective-permute-start | bytes 1179656 | tf_op jit(solution)/shard_map/swap_mo_p/ppermute | solution.py:635
  90.8 28.9 %collective-permute-start.15 = (f32[192,1536]{1,0:T(8,128)S(1)}, f32[192,1536]{1,0:T(8,128)S(1)}, u32[]{:S(2)}, u32[]{:S(2)}) collective-permute-start(f32[192,1536]{1,0:T(8,128)S(1)} %get-tuple-element.146.refs_13_), channel_id=1, source_target_pairs={{0,4},{2,6},{4,0},{6,2},{8,12},{10,14},{12,8},{14,10},{16,20},{18,... | collective-permute-start | bytes 3538952 | tf_op jit(solution)/shard_map/swap_c_x/ppermute | solution.py:635
  110.4 39.1 %collective-permute-start.24 = (f32[192,2048]{1,0:T(8,128)S(1)}, f32[192,2048]{1,0:T(8,128)S(1)}, u32[]{:S(2)}, u32[]{:S(2)}) collective-permute-start(f32[192,2048]{1,0:T(8,128)S(1)} %get-tuple-element.173), channel_id=1, source_target_pairs={{0,8},{2,10},{4,12},{6,14},{8,0},{10,2},{12,4},{14,6},{16,24},{18,... | collective-permute-start | bytes 4718600 | tf_op jit(solution)/shard_map/swap_f_p/ppermute | solution.py:635
  112.1 20.4 %collective-permute-start.14 = (f32[256,768]{1,0:T(8,128)S(1)}, f32[256,768]{1,0:T(8,128)S(1)}, u32[]{:S(2)}, u32[]{:S(2)}) collective-permute-start(f32[256,768]{1,0:T(8,128)S(1)} %get-tuple-element.147.refs_1_), channel_id=1, source_target_pairs={{0,1},{1,0},{2,3},{3,2},{4,5},{5,4},{6,7},{7,6},{8,9},{9,8},{10,11... | collective-permute-start | bytes 2359304 | tf_op jit(solution)/shard_map/pair_g1/ppermute | solution.py:624
  116.7 26.8 %collective-permute-start.22 = (f32[192,1024]{1,0:T(8,128)S(1)}, f32[192,1024]{1,0:T(8,128)S(1)}, u32[]{:S(2)}, u32[]{:S(2)}) collective-permute-start(f32[192,1024]{1,0:T(8,128)S(1)} %get-tuple-element.159.refs_2_), channel_id=1, source_target_pairs={{0,4},{2,6},{4,0},{6,2},{8,12},{10,14},{12,8},{14,10},{16,20},{18,... | collective-permute-start | bytes 2359304 | tf_op jit(solution)/shard_map/swap_fo_x/ppermute | solution.py:635
  116.8 23.0 %collective-permute-start.20 = (f32[128,768]{1,0:T(8,128)S(1)}, f32[128,768]{1,0:T(8,128)S(1)}, u32[]{:S(2)}, u32[]{:S(2)}) collective-permute-start(f32[128,768]{1,0:T(8,128)S(1)} %query_part.1.refs_2_.refs_1_), channel_id=1, source_target_pairs={{0,1},{1,0},{2,3},{3,2},{4,5},{5,4},{6,7},{7,6},{8,9},{9,8},{10,11... | collective-permute-start | bytes 1179656 | tf_op jit(solution)/shard_map/pair_q/ppermute | solution.py:624
  119.7 35.3 %collective-permute-start.27 = (f32[96,2048]{1,0:T(8,128)S(1)}, f32[96,2048]{1,0:T(8,128)S(1)}, u32[]{:S(2)}, u32[]{:S(2)}) collective-permute-start(f32[96,2048]{1,0:T(8,128)S(1)} %get-tuple-element.158.refs_2_), channel_id=1, source_target_pairs={{0,4},{2,6},{4,0},{6,2},{8,12},{10,14},{12,8},{14,10},{16,20},{18,... | collective-permute-start | bytes 2359304 | tf_op jit(solution)/shard_map/swap_m_x/ppermute | solution.py:635
  132.5 29.6 %collective-permute-start.26 = (f32[96,1536]{1,0:T(8,128)S(1)}, f32[96,1536]{1,0:T(8,128)S(1)}, u32[]{:S(2)}, u32[]{:S(2)}) collective-permute-start(f32[96,1536]{1,0:T(8,128)S(1)} %get-tuple-element.161.refs_13_), channel_id=1, source_target_pairs={{0,8},{2,10},{4,12},{6,14},{8,0},{10,2},{12,4},{14,6},{16,24},{18,... | collective-permute-start | bytes 1769480 | tf_op jit(solution)/shard_map/swap_c_p/ppermute | solution.py:635
  143.5 21.7 %collective-permute-start.21 = (f32[256,2304]{1,0:T(8,128)S(1)}, f32[256,2304]{1,0:T(8,128)S(1)}, u32[]{:S(2)}, u32[]{:S(2)}) collective-permute-start(f32[256,2304]{1,0:T(8,128)S(1)} %get-tuple-element.168), channel_id=1, source_target_pairs={{0,2},{2,0},{4,6},{6,4},{8,10},{10,8},{12,14},{14,12},{16,18},{18,... | collective-permute-start | bytes 7077896 | tf_op jit(solution)/shard_map/swap_a_0/ppermute | solution.py:635
  153.3 19.1 %collective-permute-start.35 = (f32[96,2048]{1,0:T(8,128)S(1)}, f32[96,2048]{1,0:T(8,128)S(1)}, u32[]{:S(2)}, u32[]{:S(2)}) collective-permute-start(f32[96,2048]{1,0:T(8,128)S(1)} %get-tuple-element.174.refs_3_), channel_id=1, source_target_pairs={{0,4},{2,6},{4,0},{6,2},{8,12},{10,14},{12,8},{14,10},{16,20},{18,... | collective-permute-start | bytes 2359304 | tf_op jit(solution)/shard_map/swap_f_x/ppermute | solution.py:635
  155.1 18.0 %collective-permute-start.34 = (f32[96,2048]{1,0:T(8,128)S(1)}, f32[96,2048]{1,0:T(8,128)S(1)}, u32[]{:S(2)}, u32[]{:S(2)}) collective-permute-start(f32[96,2048]{1,0:T(8,128)S(1)} %halve_m.4.refs_2_.refs_0_), channel_id=1, source_target_pairs={{8,16},{10,18},{12,20},{14,22},{16,8},{18,10},{20,12},{22,14},{9,1... | collective-permute-start | bytes 2359304 | tf_op jit(solution)/shard_map/swap_m_m/ppermute | solution.py:635
  163.5 32.3 %collective-permute-start.32 = (f32[192,1536]{1,0:T(8,128)S(1)}, f32[192,1536]{1,0:T(8,128)S(1)}, u32[]{:S(2)}, u32[]{:S(2)}) collective-permute-start(f32[192,1536]{1,0:T(8,128)S(1)} %get-tuple-element.181.refs_2_), channel_id=1, source_target_pairs={{0,8},{2,10},{4,12},{6,14},{8,0},{10,2},{12,4},{14,6},{16,24},{18,... | collective-permute-start | bytes 3538952 | tf_op jit(solution)/shard_map/swap_s_p/ppermute | solution.py:635
  170.5 29.7 %collective-permute-start.29 = (f32[192,1664]{1,0:T(8,128)S(1)}, f32[192,1664]{1,0:T(8,128)S(1)}, u32[]{:S(2)}, u32[]{:S(2)}) collective-permute-start(f32[192,1664]{1,0:T(8,128)S(1)} %get-tuple-element.183.refs_2_), channel_id=1, source_target_pairs={{0,4},{2,6},{4,0},{6,2},{8,12},{10,14},{12,8},{14,10},{16,20},{18,... | collective-permute-start | bytes 3833864 | tf_op jit(solution)/shard_map/swap_a_x/ppermute | solution.py:635
  172.4 25.4 %collective-permute-start.31 = (f32[96,1024]{1,0:T(8,128)S(1)}, f32[96,1024]{1,0:T(8,128)S(1)}, u32[]{:S(2)}, u32[]{:S(2)}) collective-permute-start(f32[96,1024]{1,0:T(8,128)S(1)} %halve_fo.4.refs_2_.refs_0_), channel_id=1, source_target_pairs={{8,16},{10,18},{12,20},{14,22},{16,8},{18,10},{20,12},{22,14},{9,1... | collective-permute-start | bytes 1179656 | tf_op jit(solution)/shard_map/swap_fo_m/ppermute | solution.py:635
  173.2 39.5 %collective-permute-start.40 = (f32[96,2048]{1,0:T(8,128)S(1)}, f32[96,2048]{1,0:T(8,128)S(1)}, u32[]{:S(2)}, u32[]{:S(2)}) collective-permute-start(f32[96,2048]{1,0:T(8,128)S(1)} %halve_f.4.refs_2_.refs_0_), channel_id=1, source_target_pairs={{8,16},{10,18},{12,20},{14,22},{16,8},{18,10},{20,12},{22,14},{9,1... | collective-permute-start | bytes 2359304 | tf_op jit(solution)/shard_map/swap_f_m/ppermute | solution.py:635
  174.1 30.0 %collective-permute-start.38 = (f32[48,1536]{1,0:T(8,128)S(1)}, f32[48,1536]{1,0:T(8,128)S(1)}, u32[]{:S(2)}, u32[]{:S(2)}) collective-permute-start(f32[48,1536]{1,0:T(8,128)S(1)} %get-tuple-element.188.refs_2_), channel_id=1, source_target_pairs={{0,8},{2,10},{4,12},{6,14},{8,0},{10,2},{12,4},{14,6},{16,24},{18,... | collective-permute-start | bytes 884744 | tf_op jit(solution)/shard_map/swap_c_e/ppermute | solution.py:635
  197.8 23.0 %collective-permute-start.42 = (f32[48,1024]{1,0:T(8,128)S(1)}, f32[48,1024]{1,0:T(8,128)S(1)}, u32[]{:S(2)}, u32[]{:S(2)}) collective-permute-start(f32[48,1024]{1,0:T(8,128)S(1)} %get-tuple-element.190.refs_2_), channel_id=1, source_target_pairs={{0,8},{2,10},{4,12},{6,14},{8,0},{10,2},{12,4},{14,6},{16,24},{18,... | collective-permute-start | bytes 589832 | tf_op jit(solution)/shard_map/swap_fo_e/ppermute | solution.py:635
  200.4 19.6 %collective-permute-start.43 = (f32[96,1664]{1,0:T(8,128)S(1)}, f32[96,1664]{1,0:T(8,128)S(1)}, u32[]{:S(2)}, u32[]{:S(2)}) collective-permute-start(f32[96,1664]{1,0:T(8,128)S(1)} %get-tuple-element.191.refs_4_), channel_id=1, source_target_pairs={{0,8},{2,10},{4,12},{6,14},{8,0},{10,2},{12,4},{14,6},{16,24},{18,... | collective-permute-start | bytes 1916936 | tf_op jit(solution)/shard_map/swap_a_p/ppermute | solution.py:635
  204.1 32.2 %collective-permute-start.36 = (f32[512,768]{1,0:T(8,128)S(1)}, f32[512,768]{1,0:T(8,128)S(1)}, u32[]{:S(2)}, u32[]{:S(2)}) collective-permute-start(f32[512,768]{1,0:T(8,128)S(1)} %tail_parts.1.refs_2_.refs_0_), channel_id=1, source_target_pairs={{0,1},{1,0},{2,3},{3,2},{4,5},{5,4},{6,7},{7,6},{8,9},{9,8},{10,11... | collective-permute-start | bytes 4718600 | tf_op jit(solution)/shard_map/pair_tail/ppermute | solution.py:624
  212.0 19.1 %collective-permute-start.39 = (f32[96,1536]{1,0:T(8,128)S(1)}, f32[96,1536]{1,0:T(8,128)S(1)}, u32[]{:S(2)}, u32[]{:S(2)}) collective-permute-start(f32[96,1536]{1,0:T(8,128)S(1)} %halve_s.4.refs_2_.refs_0_), channel_id=1, source_target_pairs={{8,16},{10,18},{12,20},{14,22},{16,8},{18,10},{20,12},{22,14},{9,1... | collective-permute-start | bytes 1769480 | tf_op jit(solution)/shard_map/swap_s_m/ppermute | solution.py:635
  212.8 15.7 %collective-permute-start.41 = (f32[48,2048]{1,0:T(8,128)S(1)}, f32[48,2048]{1,0:T(8,128)S(1)}, u32[]{:S(2)}, u32[]{:S(2)}) collective-permute-start(f32[48,2048]{1,0:T(8,128)S(1)} %get-tuple-element.198.refs_2_), channel_id=1, source_target_pairs={{0,8},{2,10},{4,12},{6,14},{8,0},{10,2},{12,4},{14,6},{16,24},{18,... | collective-permute-start | bytes 1179656 | tf_op jit(solution)/shard_map/swap_f_e/ppermute | solution.py:635
  220.1 17.5 %collective-permute-start.44 = (f32[96,1664]{1,0:T(8,128)S(1)}, f32[96,1664]{1,0:T(8,128)S(1)}, u32[]{:S(2)}, u32[]{:S(2)}) collective-permute-start(f32[96,1664]{1,0:T(8,128)S(1)} %halve_a.4.refs_4_.refs_0_), channel_id=1, source_target_pairs={{8,16},{10,18},{12,20},{14,22},{16,8},{18,10},{20,12},{22,14},{9,1... | collective-permute-start | bytes 1916936 | tf_op jit(solution)/shard_map/swap_a_m/ppermute | solution.py:635
  220.8 23.1 %collective-permute-start.48 = (f32[48,1024]{1,0:T(8,128)S(1)}, f32[48,1024]{1,0:T(8,128)S(1)}, u32[]{:S(2)}, u32[]{:S(2)}) collective-permute-start(f32[48,1024]{1,0:T(8,128)S(1)} %get-tuple-element.160.refs_2_), channel_id=1, source_target_pairs={{0,8},{2,10},{4,12},{6,14},{8,0},{10,2},{12,4},{14,6},{16,24},{18,... | collective-permute-start | bytes 589832 | tf_op jit(solution)/shard_map/swap_mo_e/ppermute | solution.py:635
  228.5 15.5 %collective-permute-start.47 = (f32[48,2048]{1,0:T(8,128)S(1)}, f32[48,2048]{1,0:T(8,128)S(1)}, u32[]{:S(2)}, u32[]{:S(2)}) collective-permute-start(f32[48,2048]{1,0:T(8,128)S(1)} %get-tuple-element.187.refs_1_), channel_id=1, source_target_pairs={{0,8},{2,10},{4,12},{6,14},{8,0},{10,2},{12,4},{14,6},{16,24},{18,... | collective-permute-start | bytes 1179656 | tf_op jit(solution)/shard_map/swap_m_e/ppermute | solution.py:635
  232.1 15.3 %collective-permute-start.46 = (f32[48,1536]{1,0:T(8,128)S(1)}, f32[48,1536]{1,0:T(8,128)S(1)}, u32[]{:S(2)}, u32[]{:S(2)}) collective-permute-start(f32[48,1536]{1,0:T(8,128)S(1)} %get-tuple-element.202.refs_9_), channel_id=1, source_target_pairs={{0,8},{2,10},{4,12},{6,14},{8,0},{10,2},{12,4},{14,6},{16,24},{18,... | collective-permute-start | bytes 884744 | tf_op jit(solution)/shard_map/swap_s_e/ppermute | solution.py:635
  (60 other events, 388.0 us)
